TPU v7x, 32 devices: a whole 2x2x4 slice. The times are simulated.
32 devices in a mesh: seq: 4 (over z), batch: 2 (over core), head: 4 (over y, x).
Axes of the slice: x: 2, y: 2, z: 4, core: 2. Of those that a mesh axis runs over, the one named last changes fastest.
Arguments:
- tokens: bfloat16 [4, 2048, 1024], P('batch', 'seq'), may hold values from -6 to 6
- starts: int32 [4], P('batch'), may hold values from 0 to 511
- attn_gain: float32 [1024], P(('seq', 'batch')), may hold values from 0.5 to 1.5
- w_in: float32 [1024, 8, 768], P(('seq', 'batch'), 'head'), may hold values from -0.1875 to 0.1875
- w_rates: float32 [1024, 8, 2], P(('seq', 'batch'), 'head'), may hold values from -0.1875 to 0.1875
- conv_w: float32 [4, 8, 512], P(None, 'head', ('seq', 'batch')), may hold values from -3 to 3
- decay_par: float32 [2, 8], P(None, 'head'), as said below
- o_gain: float32 [256], P(('seq', 'batch')), may hold values from 0.5 to 1.5
- w_out: float32 [8, 256, 1024], P('head', None, ('seq', 'batch')), may hold values from -0.125 to 0.125
- ffn_gain: float32 [1024], P(('seq', 'batch')), may hold values from 0.5 to 1.5
- w_gu: float32 [1024, 2, 2816], P(('seq', 'batch'), None, 'head'), may hold values from -0.1875 to 0.1875
- w_down: float32 [2816, 1024], P('head', ('seq', 'batch')), may hold values from -0.109375 to 0.109375
- cotangent: bfloat16 [4, 2048, 1024], P('batch', 'seq'), may hold values from -6 to 6
Outputs:
- out: bfloat16 [4, 2048, 1024], P('batch', 'seq')
- input_grad: bfloat16 [4, 2048, 1024], P('batch', 'seq')
- grad_attn_gain: float32 [1024], P(('seq', 'batch'))
- grad_w_in: float32 [1024, 8, 768], P(('seq', 'batch'), 'head')
- grad_w_rates: float32 [1024, 8, 2], P(('seq', 'batch'), 'head')
- grad_conv_w: float32 [4, 8, 512], P(None, 'head', ('seq', 'batch'))
- grad_decay_par: float32 [2, 8], P(None, 'head')
- grad_o_gain: float32 [256], P(('seq', 'batch'))
- grad_w_out: float32 [8, 256, 1024], P('head', None, ('seq', 'batch'))
- grad_ffn_gain: float32 [1024], P(('seq', 'batch'))
- grad_w_gu: float32 [1024, 2, 2816], P(('seq', 'batch'), None, 'head')
- grad_w_down: float32 [2816, 1024], P('head', ('seq', 'batch'))
Inputs may be any that keep to these rules, and one draw needn't show every extreme that they name: `starts`: a sequence's tokens before its start position are padding; every start lies among the first 512 positions. `decay_par`: row 0 holds logarithms of positive decay rates, row 1 biases added before softplus.
All inputs are finite; a program needn't handle non-finite values.
Results may differ from a plain program's by a relative error of at most 0.025.
Values may be sent and summed in bfloat16 or wider, within the bound.
A program may use at most 320 MiB of HBM per device.

v0:
```python
import jax
import jax.numpy as jnp
from jax import lax
from jax.sharding import PartitionSpec as P

DK = 128
DV = 256
CONV = 4
STRETCH = 64


top_precision = lax.Precision.HIGHEST
epsilon = 1e-06


def shifted(shard, axis, by):
    count = lax.axis_size(axis)
    pairs = [(i, i + by) for i in range(count) if 0 <= i + by < count]
    return lax.ppermute(shard, axis, pairs)


def carried_in(shard, axis, join, neutral):
    place = lax.axis_index(axis)
    gathered = jax.tree.map(
        lambda a, kind: lax.all_gather(a.astype(kind), axis), shard, (jnp.bfloat16, jnp.bfloat16)
    )
    state = jax.tree.map(lambda a, e: jnp.zeros_like(a) + jnp.asarray(e, a.dtype), shard, neutral)

    def one(lap, state):
        return join(
            state,
            jax.tree.map(
                lambda a, own: lax.dynamic_index_in_dim(a, lap, 0, False).astype(own.dtype),
                gathered,
                shard,
            ),
        )

    return lax.fori_loop(0, place, one, state)


def entering(shard, axis, combine, identity):
    count, place = (lax.axis_size(axis), lax.axis_index(axis))
    everything = jax.tree.map(
        lambda part, kind: lax.all_gather(part.astype(kind), axis),
        shard,
        jax.tree.map(lambda a: jnp.bfloat16 if a.dtype == jnp.float32 else a.dtype, shard),
    )
    start = jax.tree.map(
        lambda part, zero: jnp.broadcast_to(jnp.asarray(zero, part.dtype), part.shape),
        shard,
        identity,
    )

    def lap(k, before):
        at = count - 1 - k
        reached = at > place
        new = combine(
            before, jax.tree.map(lambda part, own: part[at].astype(own.dtype), everything, shard)
        )
        return jax.tree.map(lambda a, b: jnp.where(reached, a, b), new, before)

    return lax.fori_loop(0, count, lap, start)


def root_scale(value_rows):
    return lax.rsqrt(jnp.mean(value_rows * value_rows, axis=-1, keepdims=True) + epsilon)


def norm_backward(grad_normed, scaled, inverse, gain):
    weighted = grad_normed * gain
    return inverse * (weighted - scaled * jnp.mean(weighted * scaled, axis=-1, keepdims=True))


def features(extended, conv_weight):
    tap_count = conv_weight.shape[0]
    span_rows = extended.shape[1] - tap_count + 1
    convolved = extended[:, 0:span_rows] * conv_weight[0]
    for offset in range(1, tap_count):
        convolved = convolved + extended[:, offset : offset + span_rows] * conv_weight[offset]
    active = jax.nn.silu(convolved)
    query_rows = active[..., :DK]
    incoming_keys = active[..., DK : 2 * DK]
    value_rows = active[..., 2 * DK :]
    query_rows = (
        query_rows
        * lax.rsqrt(jnp.sum(query_rows * query_rows, axis=-1, keepdims=True) + epsilon)
        * DK ** (-0.5)
    )
    incoming_keys = incoming_keys * lax.rsqrt(
        jnp.sum(incoming_keys * incoming_keys, axis=-1, keepdims=True) + epsilon
    )
    return (query_rows, incoming_keys, value_rows)


def decay_terms(rate_logits, decay_par):
    log_gate = -jnp.exp(decay_par[0]) * jax.nn.softplus(rate_logits[..., 0] + decay_par[1])
    write_strength = jax.nn.sigmoid(rate_logits[..., 1])
    return (log_gate, write_strength)


def gated_norm(mixed, gain, gate_in):
    return mixed * root_scale(mixed) * gain * jax.nn.silu(gate_in)


def diagonal_blocks(matrix, groups, widths):
    return jnp.einsum("gagb->gab", matrix.reshape(groups, widths, groups, widths))


def place_blocks(blocks, groups, widths):
    return jnp.einsum("gab,gh->gahb", blocks, jnp.eye(groups, dtype=jnp.float32)).reshape(
        groups * widths, groups * widths
    )


def unit_lower_inverse(matrix):
    span = matrix.shape[0]
    inverse = jnp.eye(span, dtype=jnp.float32)
    half_width = 1
    while half_width < span:
        widths = 2 * half_width
        groups = span // widths
        matrix_blocks = diagonal_blocks(matrix, groups, widths)
        inverse_blocks = diagonal_blocks(inverse, groups, widths)
        upper_inv = inverse_blocks[:, :half_width, :half_width]
        lower_inv = inverse_blocks[:, half_width:, half_width:]
        coupled = matrix_blocks[:, half_width:, :half_width]
        corner = -jnp.matmul(
            jnp.matmul(lower_inv, coupled, precision=top_precision),
            upper_inv,
            precision=top_precision,
        )
        top_rows = jnp.concatenate([upper_inv, jnp.zeros_like(corner)], axis=2)
        bottom_rows = jnp.concatenate([corner, lower_inv], axis=2)
        inverse = place_blocks(jnp.concatenate([top_rows, bottom_rows], axis=1), groups, widths)
        half_width = widths
    return inverse


def stretch_step(memory, segment):
    query_rows, incoming_keys, value_rows, write_strength, log_gate = segment
    span = log_gate.shape[0]
    row_ids = lax.broadcasted_iota(jnp.int32, (span, span), 0)
    col_ids = lax.broadcasted_iota(jnp.int32, (span, span), 1)
    below = row_ids >= col_ids
    cumul = jnp.cumsum(log_gate)
    ratios = jnp.where(below, jnp.exp(jnp.where(below, cumul[:, None] - cumul[None, :], 0.0)), 0.0)
    products = jnp.dot(incoming_keys, incoming_keys.T, precision=top_precision)
    coupling = jnp.where(row_ids > col_ids, write_strength[:, None] * ratios * products, 0.0)
    growth = jnp.exp(cumul)
    target = write_strength[:, None] * (
        value_rows - growth[:, None] * jnp.dot(incoming_keys, memory, precision=top_precision)
    )
    solver_inverse = unit_lower_inverse(coupling + jnp.eye(span, dtype=jnp.float32))
    pseudo = jnp.dot(solver_inverse, target, precision=top_precision)
    scores = ratios * jnp.dot(query_rows, incoming_keys.T, precision=top_precision)
    output = growth[:, None] * jnp.dot(query_rows, memory, precision=top_precision) + jnp.dot(
        scores, pseudo, precision=top_precision
    )
    remain = jnp.exp(cumul[-1] - cumul)
    updated = jnp.exp(cumul[-1]) * memory + jnp.dot(
        incoming_keys.T * remain[None, :], pseudo, precision=top_precision
    )
    return (updated, output)


def local_rule(query_rows, incoming_keys, value_rows, write_strength, log_gate):
    length = query_rows.shape[0]
    count = length // STRETCH
    key_width = incoming_keys.shape[1]
    widened = jnp.concatenate([jnp.zeros((length, key_width), jnp.float32), value_rows], axis=1)
    start_state = jnp.concatenate(
        [
            jnp.eye(key_width, dtype=jnp.float32),
            jnp.zeros((key_width, value_rows.shape[1]), jnp.float32),
        ],
        axis=1,
    )
    pieces = tuple(
        (
            member.reshape((count, STRETCH) + member.shape[1:])
            for member in (query_rows, incoming_keys, widened, write_strength, log_gate)
        )
    )
    ending, outputs = lax.scan(stretch_step, start_state, pieces)
    return (outputs.reshape(length, -1), ending[:, :key_width], ending[:, key_width:])


def compose(earlier, later):
    return (
        jnp.matmul(later[0], earlier[0], precision=top_precision),
        jnp.matmul(later[0], earlier[1], precision=top_precision) + later[1],
    )


def heads_first(array):
    return jnp.swapaxes(array, 1, 2)


def per_device(
    tokens,
    starts,
    attn_gain,
    w_in,
    w_rates,
    conv_w,
    decay_par,
    o_gain,
    w_out,
    ffn_gain,
    w_gu,
    w_down,
    cotangent,
):
    gathered = (
        lax.all_gather(attn_gain.astype(jnp.bfloat16), ("seq", "batch"), axis=0, tiled=True),
        lax.all_gather(w_in.astype(jnp.bfloat16), ("seq", "batch"), axis=0, tiled=True),
        lax.all_gather(w_rates.astype(jnp.bfloat16), ("seq", "batch"), axis=0, tiled=True),
        lax.all_gather(conv_w.astype(jnp.bfloat16), ("seq", "batch"), axis=2, tiled=True),
        lax.all_gather(o_gain.astype(jnp.bfloat16), ("seq", "batch"), axis=0, tiled=True),
        lax.all_gather(w_out.astype(jnp.bfloat16), ("seq", "batch"), axis=2, tiled=True),
        lax.all_gather(ffn_gain.astype(jnp.bfloat16), ("seq", "batch"), axis=0, tiled=True),
        lax.all_gather(w_gu.astype(jnp.bfloat16), ("seq", "batch"), axis=0, tiled=True),
        lax.all_gather(w_down.astype(jnp.bfloat16), ("seq", "batch"), axis=1, tiled=True),
    )
    (
        attn_full,
        in_full,
        rates_full,
        conv_full,
        onorm_full,
        out_full,
        ffn_full,
        gu_full,
        down_full,
    ) = gathered
    span_rows = tokens.shape[1]
    qkv_cols = 2 * DK + DV
    inputs = tokens.astype(jnp.float32)
    inverse_in = root_scale(inputs)
    scaled_in = inputs * inverse_in
    attn_gain_f = attn_full.astype(jnp.float32)
    normed_in = (scaled_in * attn_gain_f).astype(jnp.bfloat16)
    projected = jnp.einsum("std,dhc->sthc", normed_in, in_full, preferred_element_type=jnp.float32)
    rate_logits = jnp.einsum(
        "std,dhc->sthc", normed_in, rates_full, preferred_element_type=jnp.float32
    )
    positions = lax.axis_index("seq") * span_rows + jnp.arange(span_rows, dtype=jnp.int32)
    live_mask = (positions[None, :] >= starts[:, None]).astype(jnp.float32)
    conv_input = (projected[..., :qkv_cols] * live_mask[:, :, None, None]).astype(jnp.bfloat16)
    received = shifted(conv_input[:, span_rows - CONV + 1 :], "seq", 1)
    extended = jnp.concatenate([received, conv_input], axis=1).astype(jnp.float32)
    (query_rows, incoming_keys, value_rows), feature_pull = jax.vjp(
        features, extended, conv_full.astype(jnp.float32)
    )
    query_rows = query_rows.astype(jnp.bfloat16).astype(jnp.float32)
    incoming_keys = incoming_keys.astype(jnp.bfloat16).astype(jnp.float32)
    value_rows = value_rows.astype(jnp.bfloat16).astype(jnp.float32)
    (log_gate, write_strength), decay_pull = jax.vjp(decay_terms, rate_logits, decay_par)
    rule_all = jax.vmap(jax.vmap(local_rule))
    (widened_out, transfer_mat, carried), rule_pull = jax.vjp(
        rule_all,
        heads_first(query_rows),
        heads_first(incoming_keys),
        heads_first(value_rows),
        heads_first(write_strength),
        heads_first(log_gate),
    )
    eye_block = jnp.broadcast_to(jnp.eye(DK, dtype=jnp.float32), transfer_mat.shape)
    zero_block = jnp.zeros_like(carried)
    prefix = carried_in((transfer_mat, carried), "seq", compose, (eye_block, zero_block))
    state_in = prefix[1]
    moved_queries = widened_out[..., :DK]
    local_out = widened_out[..., DK:]
    mixed = heads_first(
        local_out + jnp.einsum("shtk,shkv->shtv", moved_queries, state_in, precision=top_precision)
    )
    gate_out = projected[..., qkv_cols:]
    normed, norm_pull = jax.vjp(gated_norm, mixed, onorm_full.astype(jnp.float32), gate_out)
    normed_low = normed.astype(jnp.bfloat16)
    mixer_part = jnp.einsum(
        "sthv,hvd->std", normed_low, out_full, preferred_element_type=jnp.float32
    )
    ffn_gain_f = ffn_full.astype(jnp.float32)
    upstream = cotangent.astype(jnp.float32)
    hidden = inputs + lax.psum(mixer_part.astype(jnp.bfloat16), "head").astype(jnp.float32)
    inverse_mid = root_scale(hidden)
    scaled_mid = hidden * inverse_mid
    normed_mid = (scaled_mid * ffn_gain_f).astype(jnp.bfloat16)
    gate_up = jnp.einsum("std,dgf->stgf", normed_mid, gu_full, preferred_element_type=jnp.float32)
    gate_vals = gate_up[:, :, 0]
    up_vals = gate_up[:, :, 1]
    sig_gate = jax.nn.sigmoid(gate_vals)
    activated = (gate_vals * sig_gate * up_vals).astype(jnp.bfloat16)
    ffn_part = jnp.einsum("stf,fd->std", activated, down_full, preferred_element_type=jnp.float32)
    result = (hidden + lax.psum(ffn_part.astype(jnp.bfloat16), "head").astype(jnp.float32)).astype(
        jnp.bfloat16
    )
    down_grad = jnp.einsum("stf,std->fd", activated, cotangent, preferred_element_type=jnp.float32)
    act_grad = jnp.einsum("std,fd->stf", cotangent, down_full, preferred_element_type=jnp.float32)
    gate_grad = act_grad * up_vals * sig_gate * (1.0 + gate_vals * (1.0 - sig_gate))
    up_grad = act_grad * gate_vals * sig_gate
    gate_up_grad = jnp.stack([gate_grad, up_grad], axis=2).astype(jnp.bfloat16)
    gu_grad = jnp.einsum(
        "std,stgf->dgf", normed_mid, gate_up_grad, preferred_element_type=jnp.float32
    )
    mid_part = jnp.einsum(
        "stgf,dgf->std", gate_up_grad, gu_full, preferred_element_type=jnp.float32
    )
    mid_grad = lax.psum(mid_part.astype(jnp.bfloat16), "head").astype(jnp.float32)
    ffn_gain_part = jnp.sum(mid_grad * scaled_mid, axis=(0, 1))
    hidden_grad = upstream + norm_backward(mid_grad, scaled_mid, inverse_mid, ffn_gain_f)
    mixer_grad_low = hidden_grad.astype(jnp.bfloat16)
    out_grad = jnp.einsum(
        "sthv,std->hvd", normed_low, mixer_grad_low, preferred_element_type=jnp.float32
    )
    normed_grad = jnp.einsum(
        "std,hvd->sthv", mixer_grad_low, out_full, preferred_element_type=jnp.float32
    )
    mixed_grad, onorm_grad, gate_out_grad = norm_pull(normed_grad)
    out_heads = heads_first(mixed_grad)
    moved_grad = jnp.einsum("shtv,shkv->shtk", out_heads, state_in, precision=top_precision)
    own_term = jnp.einsum("shtk,shtv->shkv", moved_queries, out_heads, precision=top_precision)
    suffix = entering(
        (jnp.swapaxes(transfer_mat, 2, 3), own_term), "seq", compose, (eye_block, zero_block)
    )
    later_grad = suffix[1]
    transfer_grad = jnp.einsum("shkv,shjv->shkj", later_grad, state_in, precision=top_precision)
    query_grad, key_grad, value_grad, strength_grad, gate_log_grad = rule_pull(
        (jnp.concatenate([moved_grad, out_heads], axis=-1), transfer_grad, later_grad)
    )
    feature_grads = (
        heads_first(query_grad).astype(jnp.bfloat16).astype(jnp.float32),
        heads_first(key_grad).astype(jnp.bfloat16).astype(jnp.float32),
        heads_first(value_grad).astype(jnp.bfloat16).astype(jnp.float32),
    )
    extended_grad, conv_grad = feature_pull(feature_grads)
    returned = shifted(extended_grad[:, : CONV - 1], "seq", -1)
    own_rows = extended_grad[:, CONV - 1 :]
    input_part_grad = (
        jnp.concatenate(
            [own_rows[:, : span_rows - CONV + 1], own_rows[:, span_rows - CONV + 1 :] + returned],
            axis=1,
        )
        * live_mask[:, :, None, None]
    )
    rate_grad, decay_part = decay_pull((heads_first(gate_log_grad), heads_first(strength_grad)))
    projected_grad = jnp.concatenate([input_part_grad, gate_out_grad], axis=-1).astype(jnp.bfloat16)
    rate_grad_low = rate_grad.astype(jnp.bfloat16)
    in_grad = jnp.einsum(
        "std,sthc->dhc", normed_in, projected_grad, preferred_element_type=jnp.float32
    )
    rates_grad = jnp.einsum(
        "std,sthc->dhc", normed_in, rate_grad_low, preferred_element_type=jnp.float32
    )
    normed_in_part = jnp.einsum(
        "sthc,dhc->std", projected_grad, in_full, preferred_element_type=jnp.float32
    ) + jnp.einsum("sthc,dhc->std", rate_grad_low, rates_full, preferred_element_type=jnp.float32)
    normed_in_grad, onorm_sum = (
        lax.psum(normed_in_part.astype(jnp.bfloat16), "head").astype(jnp.float32),
        lax.psum(onorm_grad.astype(jnp.bfloat16), "head").astype(jnp.float32),
    )
    attn_gain_grad = jnp.sum(normed_in_grad * scaled_in, axis=(0, 1))
    input_grad = (
        hidden_grad + norm_backward(normed_in_grad, scaled_in, inverse_in, attn_gain_f)
    ).astype(jnp.bfloat16)
    decay_grad = lax.psum(decay_part, ("seq", "batch"))
    reduced = tuple(
        (
            lax.psum_scatter(
                attn_gain_grad.astype(jnp.bfloat16),
                ("seq", "batch"),
                scatter_dimension=0,
                tiled=True,
            ).astype(jnp.float32),
            lax.psum_scatter(
                in_grad.astype(jnp.bfloat16), ("seq", "batch"), scatter_dimension=0, tiled=True
            ).astype(jnp.float32),
            lax.psum_scatter(
                rates_grad.astype(jnp.bfloat16), ("seq", "batch"), scatter_dimension=0, tiled=True
            ).astype(jnp.float32),
            lax.psum_scatter(
                conv_grad.astype(jnp.bfloat16), ("seq", "batch"), scatter_dimension=2, tiled=True
            ).astype(jnp.float32),
            lax.psum_scatter(
                onorm_sum.astype(jnp.bfloat16), ("seq", "batch"), scatter_dimension=0, tiled=True
            ).astype(jnp.float32),
            lax.psum_scatter(
                out_grad.astype(jnp.bfloat16), ("seq", "batch"), scatter_dimension=2, tiled=True
            ).astype(jnp.float32),
            lax.psum_scatter(
                ffn_gain_part.astype(jnp.bfloat16),
                ("seq", "batch"),
                scatter_dimension=0,
                tiled=True,
            ).astype(jnp.float32),
            lax.psum_scatter(
                gu_grad.astype(jnp.bfloat16), ("seq", "batch"), scatter_dimension=0, tiled=True
            ).astype(jnp.float32),
            lax.psum_scatter(
                down_grad.astype(jnp.bfloat16), ("seq", "batch"), scatter_dimension=1, tiled=True
            ).astype(jnp.float32),
        )
    )
    return (
        result,
        input_grad,
        reduced[0],
        reduced[1],
        reduced[2],
        reduced[3],
        decay_grad,
        reduced[4],
        reduced[5],
        reduced[6],
        reduced[7],
        reduced[8],
    )


def solution(mesh):
    return jax.shard_map(
        per_device,
        mesh=mesh,
        in_specs=(
            P("batch", "seq", None),
            P("batch"),
            P(("seq", "batch")),
            P(("seq", "batch"), "head", None),
            P(("seq", "batch"), "head", None),
            P(None, "head", ("seq", "batch")),
            P(None, "head"),
            P(("seq", "batch")),
            P("head", None, ("seq", "batch")),
            P(("seq", "batch")),
            P(("seq", "batch"), None, "head"),
            P("head", ("seq", "batch")),
            P("batch", "seq", None),
        ),
        out_specs=(
            P("batch", "seq", None),
            P("batch", "seq", None),
            P(("seq", "batch")),
            P(("seq", "batch"), "head", None),
            P(("seq", "batch"), "head", None),
            P(None, "head", ("seq", "batch")),
            P(None, "head"),
            P(("seq", "batch")),
            P("head", None, ("seq", "batch")),
            P(("seq", "batch")),
            P(("seq", "batch"), None, "head"),
            P("head", ("seq", "batch")),
        ),
        check_vma=False,
    )
```

profile of v0, /device:TPU:0, one launch (start us, length us, event | category | flops | bytes accessed | tf_op | source)
XLA Modules:
  0.0 1923.8 jit_solution(12103422027456400405)
XLA Ops:
  10.0 13.4 all-gather.4
  24.9 15.4 all_gather.54
  40.3 8.9 all_gather.52
  94.6 507.1 %while.166 = (s32[]{:T(128)}, f32[2,2,128,384]{3,2,1,0:T(8,128)S(1)}, f32[8,2,2,64,384]{4,3,2,1,0:T(8,128)}, f32[8,2,2,64,64]{4,3,2,1,0:T(8,128)}, f32[8,2,2,128...) while((s32[]{:T(128)}, ...), condition=%wide.region_15.16_spmd.clone.clone.clone, body=%wide.region_4.15_spmd.clone.clone.sunk.clone | while | flops 660436736 | bytes 19017480 | solution.py:185
  607.1 14.0 all-reduce.43
  625.1 15.9 all-gather
  649.1 7.8 all-gather.15.cloned.1.call-done
  664.9 10.8 all-gather.5
  675.7 53.7 %all-reduce.53.cloned.1.call-done = bf16[2,512,1024]{2,1,0:T(8,128)(2,1)} async-done(((bf16[2,512,1024]{2,1,0:T(8,128)(2,1)}), bf16[2,512,1024]{2,1,0:T(8,128)(2,1)}) %all-reduce.53.cloned.1.call-update) | async-done | bytes 2097168 | tf_op jit(solution)/shard_map/psum | solution.py:286
  731.8 36.8 %all-gather.17.cloned.1.call-done = bf16[1024,2,704]{0,2,1:T(8,128)(2,1)} async-done(((bf16[128,2,704]{0,2,1:T(8,128)(2,1)}), bf16[1024,2,704]{0,2,1:T(8,128)(2,1)}) %all-gather.17.cloned.1.call-update) | async-done | bytes 2883600 | tf_op jit(solution)/shard_map/all_gather | solution.py:223
  768.6 8.2 fusion.356
  776.8 18.7 all-gather.19.cloned.1.call-done
  795.5 7.7 fusion.386
  809.7 68.5 %all-reduce.55.cloned.1.call-done = bf16[2,512,1024]{2,1,0:T(8,128)(2,1)} async-done(((bf16[2,512,1024]{2,1,0:T(8,128)(2,1)}), bf16[2,512,1024]{2,1,0:T(8,128)(2,1)}) %all-reduce.55.cloned.1.call-update) | async-done | bytes 2097168 | tf_op jit(solution)/shard_map/psum | solution.py:310
  900.3 22.6 %all-gather.2 = bf16[8,2,128,128]{3,2,1,0:T(8,128)(2,1)S(1)} all-gather(bf16[2,2,128,128]{3,2,1,0:T(8,128)(2,1)S(1)} %copy.409), channel_id=4, replica_groups=mesh['seq'=4,'batch'=2,'head'=4] {'seq'}, dimensions={0}, use_global_device_ids=true | all-gather | bytes 655360 | tf_op jit(solution)/shard_map/all_gather | solution.py:45
  944.6 670.4 %while.167 = (s32[]{:T(128)}, f32[2,2,128,384]{3,2,1,0:T(8,128)S(1)}, bf16[8,2,2,64,128]{4,3,2,1,0:T(8,128)(2,1)}, bf16[8,2,2,64,128]{4,3,2,1,0:T(8,128)(2,1)}, ...) while((s32[]{:T(128)}, ...), condition=%wide.region_38.39_spmd.clone.clone.clone, body=%wide.region_27.38_spmd.clone.clone.sunk.clone | while | flops 1320805632 | bytes 25953648 | solution.py:185
  1640.9 7.5 bitcast_convert_fusion.1
  1658.2 8.0 broadcast_multiply_fusion
  1671.2 7.6 pad_add_fusion.1
  1702.4 14.3 psum.46
  1727.0 37.2 %reduce-scatter.25.cloned.1.call-done = bf16[128,1408]{1,0:T(8,128)(2,1)} async-done(((bf16[1024,1408]{1,0:T(8,128)(2,1)}), bf16[128,1408]{1,0:T(8,128)(2,1)}) %reduce-scatter.25.cloned.1.call-update) | async-done | bytes 360464
  1765.4 106.3 %all-reduce.57.cloned.1.call-done = (bf16[2,512,1024]{2,1,0:T(8,128)(2,1)}, bf16[2,512,1024]{2,1,0:T(8,128)(2,1)}) async-done(((bf16[2,512,1024]{2,1,0:T(8,128)(2,1)}, bf16[2,512,1024]{2,1,0:T(8,128)(2,1)}), (bf16[2,512,1024]{2,1,0:T(8,128)(2,1)}, bf16[2,512,1024]{2,1,0:T(8,128)(2,1)})) %all-reduce.57.cloned.1.call-update) | async-done | bytes 4194320 | tf_op jit(solution)/shard_map/psum | solution.py:296
  1875.0 17.4 all-reduce.47
  1893.4 9.0 psum.48
  (2158 shorter events, 1381.8 us)
Async XLA Ops:
  7.2 47.2 %copy-start.1 = (bf16[2,512,1024]{2,1,0:T(8,128)(2,1)S(1)}, bf16[2,512,1024]{2,1,0:T(8,128)(2,1)}, u32[]{:S(2)}) copy-start(bf16[2,512,1024]{2,1,0:T(8,128)(2,1)} %param.21) | copy-start | bytes 6291460
  7.2 51.1 %all-gather.13.cloned.1.call-start = ((), (), s32[]{:S(2)}) async-start(), calls=%async_computation.6 | async-start | bytes 3538944 | tf_op jit(solution)/shard_map/all_gather | solution.py:217
  9.3 631.7 %all-gather.21.cloned.1.call-start = ((), (), s32[]{:S(2)}) async-start(), calls=%async_computation.13 | async-start | bytes 1310720 | tf_op jit(solution)/shard_map/all_gather | solution.py:25
  66.4 7.9 collective-permute-start
  602.5 54.4 %all-gather.15.cloned.1.call-start = ((), (), s32[]{:S(2)}) async-start(), calls=%async_computation.7 | async-start | bytes 1179648 | tf_op jit(solution)/shard_map/all_gather | solution.py:221
  604.2 125.3 %all-reduce.53.cloned.1.call-start = ((), (), s32[]{:S(2)}) async-start(), calls=%async_computation.8 | async-start | bytes 4194304 | tf_op jit(solution)/shard_map/psum | solution.py:286
  661.0 68.5 %copy-start.2 = (bf16[2,512,1024]{2,1,0:T(8,128)(2,1)S(1)}, bf16[2,512,1024]{2,1,0:T(8,128)(2,1)}, u32[]{:S(2)}) copy-start(bf16[2,512,1024]{2,1,0:T(8,128)(2,1)} %param.21) | copy-start | bytes 6291460
  661.0 107.6 %all-gather.17.cloned.1.call-start = ((), (), s32[]{:S(2)}) async-start(), calls=%async_computation.9 | async-start | bytes 3244032 | tf_op jit(solution)/shard_map/all_gather | solution.py:223
  663.1 132.4 %all-gather.19.cloned.1.call-start = ((), (), s32[]{:S(2)}) async-start(), calls=%async_computation.10 | async-start | bytes 1622016 | tf_op jit(solution)/shard_map/all_gather | solution.py:224
  664.9 213.3 %all-reduce.55.cloned.1.call-start = ((), (), s32[]{:S(2)}) async-start(), calls=%async_computation.11 | async-start | bytes 4194304 | tf_op jit(solution)/shard_map/psum | solution.py:310
  675.7 207.3 %copy-start.43 = (f32[8,1,128]{2,1,0:T(1,128)}, f32[8,1,128]{2,1,0:T(1,128)S(1)}, u32[]{:S(2)}) copy-start(f32[8,1,128]{2,1,0:T(1,128)S(1)} %convert_element_type.377) | copy-start | bytes 12292
  731.8 151.2 %copy-start.45 = (f32[2,512]{1,0:T(2,128)}, f32[2,512]{1,0:T(2,128)S(1)}, u32[]{:S(2)}) copy-start(f32[2,512]{1,0:T(2,128)S(1)} %add_rsqrt_fusion.2) | copy-start | bytes 12292
  809.6 125.1 %all-gather.23.cloned.1.call-start = ((), (), s32[]{:S(2)}) async-start(), calls=%async_computation.14 | async-start | bytes 1310720 | tf_op jit(solution)/shard_map/all_gather | solution.py:45
  897.1 803.4 %reduce-scatter.27.cloned.1.call-start = ((), (), s32[]{:S(2)}) async-start(), calls=%async_computation.19 | async-start | bytes 1769472
  930.3 786.4 %reduce-scatter.21.cloned.1.call-start = ((), (), s32[]{:S(2)}) async-start(), calls=%async_computation.16 | async-start | bytes 147456
  1631.5 86.7 %reduce-scatter.19.cloned.1.call-start = ((), (), s32[]{:S(2)}) async-start(), calls=%async_computation.15 | async-start | bytes 294912
  1633.2 92.0 %reduce-scatter.23.cloned.1.call-start = ((), (), s32[]{:S(2)}) async-start(), calls=%async_computation.17 | async-start | bytes 1179648
  1640.9 123.4 %reduce-scatter.25.cloned.1.call-start = ((), (), s32[]{:S(2)}) async-start(), calls=%async_computation.18 | async-start | bytes 3244032
  1653.0 218.7 %all-reduce.57.cloned.1.call-start = ((), (), s32[]{:S(2)}) async-start(), calls=%async_computation.20 | async-start | bytes 8388608 | tf_op jit(solution)/shard_map/psum | solution.py:296
  1667.1 14.9 collective-permute-start.1
  1692.4 222.3 %reduce-scatter.17.cloned.1.call-start = ((), (), s32[]{:S(2)}) async-start(), calls=%async_computation.12 | async-start | bytes 3538944 | tf_op jit(solution)/shard_map/reduce_scatter | solution.py:376
  1702.4 172.6 %copy-start.69 = (bf16[1024]{0:T(1024)(128)(2,1)S(1)}, bf16[1024]{0:T(1024)(128)(2,1)}, u32[]{:S(2)}) copy-start(bf16[1024]{0:T(1024)(128)(2,1)} %get-tuple-element.3851) | copy-start | bytes 6148
  1702.4 172.6 %copy-start.75 = (bf16[256]{0:T(256)(128)(2,1)S(1)}, bf16[256]{0:T(256)(128)(2,1)}, u32[]{:S(2)}) copy-start(bf16[256]{0:T(256)(128)(2,1)} %get-tuple-element.3845) | copy-start | bytes 1540
  1726.3 177.8 %copy-start.55 = (f32[2,512]{1,0:T(2,128)S(1)}, f32[2,512]{1,0:T(2,128)}, u32[]{:S(2)}) copy-start(f32[2,512]{1,0:T(2,128)} %copy-done.54) | copy-start | bytes 12292
  (148 other events, 830.9 us)
Sparse Core Ops, SparseCore 0:
  10.2 43.1 all-gather.12
  602.6 28.6 all-gather.20
  633.5 23.3 all-gather.14
  661.1 68.2 all-reduce.52
  731.5 37.0 all-gather.16
  770.7 24.7 all-gather.18
  809.7 68.3 all-reduce.54
  897.2 33.2 all-gather.22
  932.8 34.1 reduce-scatter.26
  1631.6 29.1 reduce-scatter.20
  1663.7 28.5 reduce-scatter.18
  1694.4 30.7 reduce-scatter.22
  1727.5 36.6 reduce-scatter.24
  1768.2 103.4 all-reduce.56
  1874.0 40.7 reduce-scatter.16
where the time goes:
time: 1950 us; the launch traced here: 1920 us
  matrix products  669 us (34%)
  local copies, waits for them, and re-layouts  415 us (21%)
  waiting for transfers between devices  338 us (17%)
  other arithmetic  315 us (16%)
  blocking collectives  142 us (7%)
  loops' own time  21.1 us (1%)
    dot_general x120, matrix products, unit_lower_inverse(): jnp.matmul(lower_inv, coupled, precision=top_precision)  136 us
    reshape x72, local copies, waits for them, and re-layouts, diagonal_blocks(): matrix.reshape(groups, widths, groups, widths)  113 us
    dot_general x120, matrix products, unit_lower_inverse(): jnp.matmul(jnp.matmul(lower_inv, coupled, precision=top_precision), upper...  109 us
    psum x1, waiting for transfers between devices, per_device(): lax.psum(ffn_part.astype(jnp.bfloat16), 'head').astype(jnp.float32)  106 us
    select_n x72, local copies, waits for them, and re-layouts, diagonal_blocks(): jnp.einsum('gagb->gab', matrix.reshape(groups, widths, groups, widths))  83.6 us
    dynamic_update_slice x96, local copies, waits for them, and re-layouts, local_rule(): ending, outputs = lax.scan(stretch_step, start_state, pieces)  73.4 us
    psum x1, waiting for transfers between devices, per_device(): lax.psum(mid_part.astype(jnp.bfloat16), 'head').astype(jnp.float32)  68.5 us
    dot_general x24, matrix products, stretch_step(): jnp.dot(incoming_keys, memory, precision=top_precision)  59.2 us
  transfers between devices with their start and end apart: 17, of which 9 were waited for; matrix products, arithmetic and copies ran while one was open for 43% of the time, Pallas kernels for 0%

commit v1 on v0

v1 whole, which is shorter than its diff:
```python
import functools

import jax
import jax.numpy as jnp
from jax import lax
from jax.experimental import pallas as pl
from jax.experimental.pallas import tpu as pltpu
from jax.sharding import PartitionSpec as P

DK = 128
DV = 256
CONV = 4
QKV = 2 * DK + DV
CHUNK = 128
HALO = 16
PAD = 128

bf16 = jnp.bfloat16
f32 = jnp.float32
epsilon = 1e-06
NN = ((1,), (0,))
NT = ((1,), (1,))
TN = ((0,), (0,))


def mm(a, b, dims=NN):
    return lax.dot_general(
        a.astype(bf16), b.astype(bf16), (dims, ((), ())), preferred_element_type=f32
    )


def split_mm(a, b):
    a_high, b_high = a.astype(bf16), b.astype(bf16)
    a_low = (a - a_high.astype(f32)).astype(bf16)
    b_low = (b - b_high.astype(f32)).astype(bf16)
    return mm(a_high, b_high) + (mm(a_high, b_low) + mm(a_low, b_high))


def iotas(n):
    return (
        lax.broadcasted_iota(jnp.int32, (n, n), 0),
        lax.broadcasted_iota(jnp.int32, (n, n), 1),
    )


def unit_lower_inverses(mats):
    n = mats[0].shape[0]
    rows, cols = iotas(n)
    eye = (rows == cols).astype(f32)
    pair = ((rows >> 1) == (cols >> 1)) & (rows > cols)
    inverses = [eye - jnp.where(pair, a, 0.0) for a in mats]
    shift = 1
    while (1 << shift) < n:
        corner = ((rows >> (shift + 1)) == (cols >> (shift + 1))) & (
            (rows >> shift) > (cols >> shift)
        )
        firsts = [mm(jnp.where(corner, a, 0.0), x) for a, x in zip(mats, inverses)]
        inverses = [x - mm(x, y) for x, y in zip(inverses, firsts)]
        shift += 1
    residuals = [eye - x - split_mm(a, x) for a, x in zip(mats, inverses)]
    return [x + mm(x, r) for x, r in zip(inverses, residuals)]


def sigmoid(v):
    return 1.0 / (1.0 + jnp.exp(-v))


def softplus(v):
    small = jnp.exp(-jnp.abs(v))
    one_more = 1.0 + small
    gap = one_more - 1.0
    exact = gap == 0.0
    tail = jnp.where(exact, small, jnp.log(one_more) * small / jnp.where(exact, 1.0, gap))
    return jnp.maximum(v, 0.0) + tail


def to_row(column, eye):
    return jnp.sum(jnp.where(eye, column, 0.0), axis=0, keepdims=True)


def pick(block, lane):
    lanes = lax.broadcasted_iota(jnp.int32, block.shape, 1)
    return jnp.sum(jnp.where(lanes == lane, block, 0.0), axis=1, keepdims=True)


def gates(logits, decay_ref, head):
    rate = jnp.exp(jnp.full((1, 1), decay_ref[0, head], f32))
    shifted_logit = pick(logits, 2 * head) + decay_ref[1, head]
    strength = sigmoid(pick(logits, 2 * head + 1))
    log_gate = -rate * softplus(shifted_logit)
    return log_gate, strength, rate, shifted_logit


def decays(log_gate, lower, upper, eye):
    gate_row = to_row(log_gate, eye)
    column = jnp.sum(jnp.where(lower, gate_row, 0.0), axis=1, keepdims=True)
    row = jnp.sum(jnp.where(upper, log_gate, 0.0), axis=0, keepdims=True)
    ratio = jnp.where(lower, jnp.exp(jnp.where(lower, column - row, 0.0)), 0.0)
    total = jnp.sum(log_gate, axis=0, keepdims=True)
    return column, total, ratio


def load_conv_input(main_ref, halo_ref, start_ref, x_scr, seq_place):
    length = main_ref.shape[0]
    s = pl.program_id(1)
    positions = seq_place * length + lax.broadcasted_iota(jnp.int32, (length, 1), 0)
    live = (positions >= start_ref[s]).astype(f32)
    x_scr[pl.ds(0, HALO), :] = halo_ref[0].astype(f32)
    x_scr[pl.ds(HALO, length), :] = (main_ref[...] * live).astype(bf16).astype(f32)


def convolve(x_scr, conv, at):
    total = x_scr[pl.ds(at + HALO - CONV + 1, CHUNK), :] * conv[0:1]
    for j in range(1, CONV):
        total = total + x_scr[pl.ds(at + HALO - CONV + 1 + j, CHUNK), :] * conv[j : j + 1]
    return total


def unit(rows):
    return rows * lax.rsqrt(jnp.sum(rows * rows, axis=1, keepdims=True) + epsilon)


def chunk_kernel(
    place_ref, start_ref, decay_ref, main_ref, halo_ref, rate_ref, conv_ref,
    qkv_ref, inv_ref, n_ref, b_ref, qe_ref, o_ref, tot_ref, map_ref, x_scr,
):
    head = pl.program_id(0)
    load_conv_input(main_ref, halo_ref, start_ref, x_scr, place_ref[0])
    conv = conv_ref[...]
    length = main_ref.shape[0]
    count = length // CHUNK
    rows, cols = iotas(CHUNK)
    lower, upper, eye = rows >= cols, rows <= cols, rows == cols
    parts = []
    for c in range(count):
        at = c * CHUNK
        convolved = convolve(x_scr, conv, at)
        active = convolved * sigmoid(convolved)
        q = (unit(active[:, :DK]) * DK ** (-0.5)).astype(bf16)
        k = unit(active[:, DK : 2 * DK]).astype(bf16)
        v = active[:, 2 * DK :].astype(bf16)
        qkv_ref[pl.ds(at, CHUNK), 0:DK] = q
        qkv_ref[pl.ds(at, CHUNK), DK : 2 * DK] = k
        qkv_ref[pl.ds(at, CHUNK), 2 * DK :] = v
        log_gate, strength, _, _ = gates(rate_ref[pl.ds(at, CHUNK), :], decay_ref, head)
        column, total, ratio = decays(log_gate, lower, upper, eye)
        products = mm(jnp.concatenate([k, q], axis=0), k, NT)
        coupling = jnp.where(rows > cols, strength * ratio * products[:CHUNK], 0.0)
        scores = (ratio * products[CHUNK:]).astype(bf16)
        parts.append((q, k, v, strength, column, total, coupling, scores))
    inverses = unit_lower_inverses([p[6] for p in parts])
    maps = []
    for c in range(count):
        q, k, v, strength, column, total, _, scores = parts[c]
        growth = jnp.exp(column)
        kf, vf, qf = k.astype(f32), v.astype(f32), q.astype(f32)
        inverse = inverses[c].astype(bf16)
        inv_ref[0, 0, c] = inverse
        target = jnp.concatenate([(strength * growth) * kf, strength * vf], axis=1)
        solved = mm(inverse, target).astype(bf16)
        read = mm(scores, solved)
        qe_ref[0, 0, c] = (growth * qf - read[:, :DK]).astype(bf16)
        o_ref[pl.ds(c * CHUNK, CHUNK), :] = read[:, DK:]
        kept = jnp.exp(total - column) * kf
        written = mm(kept, solved, TN)
        low_n = written[:, :DK].astype(bf16)
        n_ref[0, 0, c] = low_n
        b_ref[0, 0, c] = written[:, DK:]
        whole = jnp.exp(total)
        tot_ref[0, 0, pl.ds(c, 1), :] = jnp.broadcast_to(whole, (1, DK))
        maps.append((low_n, written[:, DK:], whole))
    low_n, b, whole = maps[0]
    eye_f = eye.astype(f32)
    trans = whole * eye_f - low_n.astype(f32)
    carried = b
    for low_n, b, whole in maps[1:]:
        both = jnp.concatenate([trans, carried], axis=1)
        moved = whole * both - mm(low_n, both)
        trans = moved[:, :DK]
        carried = moved[:, DK:] + b
    map_ref[0, 0, :, 0:DK] = trans.astype(bf16)
    map_ref[0, 0, :, DK:] = carried.astype(bf16)


def state_kernel(
    place_ref, maps_ref, n_ref, b_ref, qe_ref, o_ref, tot_ref, og_ref, gain_ref,
    s_ref, mixed_ref, normed_ref,
):
    count = n_ref.shape[2]

    def lap(z, state):
        stage = maps_ref[z, 0, 0]
        return mm(stage[:, :DK], state) + stage[:, DK:].astype(f32)

    state = lax.fori_loop(0, place_ref[0], lap, jnp.zeros((DK, DV), f32))
    for c in range(count):
        low_state = state.astype(bf16)
        s_ref[0, 0, c] = low_state
        both = mm(jnp.concatenate([n_ref[0, 0, c], qe_ref[0, 0, c]], axis=0), low_state)
        whole = tot_ref[0, 0, c, 0]
        state = whole * state - both[:DK] + b_ref[0, 0, c]
        at = pl.ds(c * CHUNK, CHUNK)
        mixed = o_ref[at, :] + both[DK:]
        mixed_ref[at, :] = mixed
        og = og_ref[at, :]
        inverse = lax.rsqrt(jnp.mean(mixed * mixed, axis=1, keepdims=True) + epsilon)
        normed_ref[at, :] = (mixed * inverse * gain_ref[0:1] * (og * sigmoid(og))).astype(bf16)


def norm_grad_kernel(
    dn_ref, mixed_ref, og_ref, gain_ref, qe_ref, n_ref, tot_ref,
    do_ref, dog_ref, gg_ref, own_ref,
):
    count = n_ref.shape[2]
    gain = gain_ref[0:1]
    state = jnp.zeros((DK, DV), f32)
    total = jnp.zeros((1, DV), f32)
    for c in reversed(range(count)):
        at = pl.ds(c * CHUNK, CHUNK)
        mixed, og, dn = mixed_ref[at, :], og_ref[at, :], dn_ref[at, :]
        inverse = lax.rsqrt(jnp.mean(mixed * mixed, axis=1, keepdims=True) + epsilon)
        scaled = mixed * inverse
        sig = sigmoid(og)
        silu = og * sig
        through = dn * scaled
        total = total + jnp.sum(through * silu, axis=0, keepdims=True)
        dog_ref[at, :] = (through * gain * sig * (1.0 + og * (1.0 - sig))).astype(bf16)
        weighted = dn * gain * silu
        dmixed = inverse * (
            weighted - scaled * jnp.mean(weighted * scaled, axis=1, keepdims=True)
        )
        dmixed = dmixed.astype(bf16)
        do_ref[at, :] = dmixed
        whole = tot_ref[0, 0, c, 0]
        state = whole * state - mm(n_ref[0, 0, c], state, TN) + mm(qe_ref[0, 0, c], dmixed, TN)
    gg_ref[0, 0] = jnp.broadcast_to(total, (8, DV))
    own_ref[0, 0] = state.astype(bf16)


def rule_grad_kernel(
    place_ref, start_ref, decay_ref, owns_ref, maps_ref, qkv_ref, inv_ref, n_ref, qe_ref,
    tot_ref, s_ref, do_ref, main_ref, halo_ref, rate_ref, conv_ref,
    dci_ref, dhalo_ref, dconv_ref, drate_ref, ddecay_ref, x_scr, g_scr,
):
    head = pl.program_id(0)
    length = main_ref.shape[0]
    count = length // CHUNK
    load_conv_input(main_ref, halo_ref, start_ref, x_scr, place_ref[0])
    conv = conv_ref[...]
    rows, cols = iotas(CHUNK)
    lower, upper, eye = rows >= cols, rows <= cols, rows == cols
    strict = rows > cols
    last = owns_ref.shape[0] - 1

    def lap(i, state):
        z = last - i
        return mm(maps_ref[z, 0, 0][:, :DK], state, TN) + owns_ref[z, 0, 0].astype(f32)

    state = lax.fori_loop(0, last - place_ref[0], lap, jnp.zeros((DK, DV), f32))
    leaving = [None] * count
    for c in reversed(range(count)):
        leaving[c] = state
        at = pl.ds(c * CHUNK, CHUNK)
        state = (
            tot_ref[0, 0, c, 0] * state
            - mm(n_ref[0, 0, c], state, TN)
            + mm(qe_ref[0, 0, c], do_ref[at, :], TN)
        )
    g_scr[pl.ds(0, 8), :] = jnp.zeros((8, QKV), f32)
    g_scr[pl.ds(8 + length, 8), :] = jnp.zeros((8, QKV), f32)
    rate_total = jnp.zeros((1, 1), f32)
    bias_total = jnp.zeros((1, 1), f32)
    conv_total = [jnp.zeros((1, QKV), f32) for _ in range(CONV)]
    lanes = lax.broadcasted_iota(jnp.int32, (CHUNK, PAD), 1)
    for c in range(count):
        at = pl.ds(c * CHUNK, CHUNK)
        q, k, v = qkv_ref[at, 0:DK], qkv_ref[at, DK : 2 * DK], qkv_ref[at, 2 * DK :]
        kf, vf = k.astype(f32), v.astype(f32)
        log_gate, strength, rate, logit = gates(rate_ref[at, :], decay_ref, head)
        column, total, ratio = decays(log_gate, lower, upper, eye)
        growth = jnp.exp(column)
        remain = jnp.exp(total - column)
        whole = jnp.exp(total)
        inverse = inv_ref[0, 0, c]
        s0 = s_ref[0, 0, c]
        do = do_ref[at, :]
        grad_state = leaving[c]
        low_grad_state = grad_state.astype(bf16)
        kq = jnp.concatenate([k, q], axis=0)
        products = mm(kq, k, NT)
        kk, qk = products[:CHUNK], products[CHUNK:]
        reads = mm(kq, s0)
        ks, qs = reads[:CHUNK], reads[CHUNK:]
        fresh = vf - growth * ks
        pseudo = mm(inverse, strength * fresh).astype(bf16)
        scores = (ratio * qk).astype(bf16)
        dpseudo = mm(scores, do, TN) + mm(remain * kf, low_grad_state)
        dtarget = mm(inverse, dpseudo, TN)
        low_dtarget = dtarget.astype(bf16)
        dstrength = jnp.sum(dtarget * fresh, axis=1, keepdims=True)
        dlog = -(strength * growth) * jnp.sum(dtarget * ks, axis=1, keepdims=True)
        dv = strength * dtarget
        outer = mm(jnp.concatenate([low_dtarget, do], axis=0), pseudo, NT)
        dcoupling = jnp.where(strict, -outer[:CHUNK] * ratio, 0.0)
        by_strength = dcoupling * kk
        dstrength = dstrength + jnp.sum(by_strength, axis=1, keepdims=True)
        exponent = strength * by_strength
        dkk = (dcoupling * strength).astype(bf16)
        dqk_f = jnp.where(lower, outer[CHUNK:] * ratio, 0.0)
        exponent = exponent + dqk_f * qk
        dqk = dqk_f.astype(bf16)
        back = mm(jnp.concatenate([low_dtarget, do], axis=0), s0, NT)
        wide = mm(jnp.concatenate([dkk, dqk], axis=0), k)
        dq = growth * back[CHUNK:] + wide[CHUNK:]
        dkept = mm(pseudo, low_grad_state, NT)
        dk = (
            wide[:CHUNK]
            - (strength * growth) * back[:CHUNK]
            + mm(jnp.concatenate([dkk, dqk], axis=0), kq, TN)
            + remain * dkept
        )
        dlog = dlog + growth * jnp.sum(do.astype(f32) * qs, axis=1, keepdims=True)
        from_kept = remain * jnp.sum(kf * dkept, axis=1, keepdims=True)
        dlog = dlog - from_kept + jnp.sum(exponent, axis=1, keepdims=True)
        dlog_row = to_row(dlog, eye) - jnp.sum(exponent, axis=0, keepdims=True)
        tail = jnp.sum(from_kept, axis=0, keepdims=True) + whole * jnp.sum(
            jnp.sum(grad_state * s0.astype(f32), axis=1, keepdims=True), axis=0, keepdims=True
        )
        dgate = jnp.sum(jnp.where(upper, dlog_row, 0.0), axis=1, keepdims=True) + tail
        slope = sigmoid(logit)
        drate0 = -rate * slope * dgate
        drate1 = dstrength * strength * (1.0 - strength)
        rate_total = rate_total + jnp.sum(dgate * log_gate, axis=0, keepdims=True)
        bias_total = bias_total + jnp.sum(drate0, axis=0, keepdims=True)
        drate_ref[at, :] = jnp.where(
            lanes == 2 * head, drate0, jnp.where(lanes == 2 * head + 1, drate1, 0.0)
        )
        convolved = convolve(x_scr, conv, c * CHUNK)
        sig = sigmoid(convolved)
        active = convolved * sig
        slope_conv = sig * (1.0 + convolved * (1.0 - sig))

        def unit_grad(rows_in, grad):
            inv_norm = lax.rsqrt(jnp.sum(rows_in * rows_in, axis=1, keepdims=True) + epsilon)
            y = rows_in * inv_norm
            return inv_norm * (grad - y * jnp.sum(y * grad, axis=1, keepdims=True))

        dq = dq.astype(bf16).astype(f32) * DK ** (-0.5)
        dk = dk.astype(bf16).astype(f32)
        dv = dv.astype(bf16).astype(f32)
        dconv = (
            jnp.concatenate(
                [unit_grad(active[:, :DK], dq), unit_grad(active[:, DK : 2 * DK], dk), dv], axis=1
            )
            * slope_conv
        )
        g_scr[pl.ds(8 + c * CHUNK, CHUNK), :] = dconv
        for j in range(CONV):
            shifted_in = x_scr[pl.ds(c * CHUNK + HALO - CONV + 1 + j, CHUNK), :]
            conv_total[j] = conv_total[j] + jnp.sum(dconv * shifted_in, axis=0, keepdims=True)
    for j in range(CONV):
        dconv_ref[0, 0, pl.ds(j, 1), :] = conv_total[j]
    for c in range(count):
        grad = g_scr[pl.ds(8 + c * CHUNK + CONV - 1, CHUNK), :] * conv[0:1]
        for j in range(1, CONV):
            grad = grad + g_scr[pl.ds(8 + c * CHUNK + CONV - 1 - j, CHUNK), :] * conv[j : j + 1]
        dci_ref[pl.ds(c * CHUNK, CHUNK), :] = grad
    grad = g_scr[pl.ds(CONV - 1, 8), :] * conv[0:1]
    for j in range(1, CONV):
        grad = grad + g_scr[pl.ds(CONV - 1 - j, 8), :] * conv[j : j + 1]
    dhalo_ref[0] = grad
    row8 = lax.broadcasted_iota(jnp.int32, (8, PAD), 0)
    ddecay_ref[0, 0] = jnp.where(row8 == 0, rate_total, jnp.where(row8 == 1, bias_total, 0.0))


def params():
    return pltpu.CompilerParams(
        dimension_semantics=("arbitrary", "arbitrary"), vmem_limit_bytes=48 * 2**20
    )


def smem():
    return pl.BlockSpec(memory_space=pltpu.SMEM)


class Rule:
    def __init__(self, seqs, length, heads, places):
        self.seqs, self.length, self.heads, self.places = seqs, length, heads, places
        self.count = length // CHUNK
        self.grid = (heads, seqs)

    def per_chain(self, *dims):
        zeros = (0,) * len(dims)
        return pl.BlockSpec((1, 1) + dims, lambda h, s: (s, h) + zeros)

    def chain_shape(self, dims, kind):
        return jax.ShapeDtypeStruct((self.seqs, self.heads) + dims, kind)

    def rows(self, width, first):
        return pl.BlockSpec((self.length, width), lambda h, s: (s, first + h))

    def rates(self):
        at = self.heads * (QKV + DV) // PAD
        return pl.BlockSpec((self.length, PAD), lambda h, s: (s, at))

    def og(self):
        return self.rows(DV, self.heads * QKV // DV)

    def halo(self):
        return pl.BlockSpec((1, HALO, QKV), lambda h, s: (s, 0, h))

    def conv(self):
        return pl.BlockSpec((CONV, QKV), lambda h, s: (0, h))

    def gain(self):
        return pl.BlockSpec((1, DV), lambda h, s: (0, 0))

    def everyones(self, width):
        return pl.BlockSpec((self.places, 1, 1, DK, width), lambda h, s: (0, s, h, 0, 0))

    def row_shape(self, width, kind):
        return jax.ShapeDtypeStruct((self.seqs * self.length, self.heads * width), kind)

    def chunks(self, place, starts, decay_par, projected, halo, conv_w):
        c = self.count
        return pl.pallas_call(
            chunk_kernel,
            grid=self.grid,
            in_specs=[
                smem(), smem(), smem(), self.rows(QKV, 0), self.halo(), self.rates(), self.conv(),
            ],
            out_specs=[
                self.rows(QKV, 0), self.per_chain(c, CHUNK, CHUNK), self.per_chain(c, DK, DK),
                self.per_chain(c, DK, DV), self.per_chain(c, CHUNK, DK), self.rows(DV, 0),
                self.per_chain(c, DK), self.per_chain(DK, DK + DV),
            ],
            out_shape=[
                self.row_shape(QKV, bf16), self.chain_shape((c, CHUNK, CHUNK), bf16),
                self.chain_shape((c, DK, DK), bf16), self.chain_shape((c, DK, DV), f32),
                self.chain_shape((c, CHUNK, DK), bf16), self.row_shape(DV, f32),
                self.chain_shape((c, DK), f32), self.chain_shape((DK, DK + DV), bf16),
            ],
            scratch_shapes=[pltpu.VMEM((HALO + self.length, QKV), f32)],
            compiler_params=params(),
            name="chunk_maps",
        )(place, starts, decay_par, projected, halo, projected, conv_w)

    def states(self, place, maps, n, b, qe, o, tot, projected, gain):
        c = self.count
        return pl.pallas_call(
            state_kernel,
            grid=self.grid,
            in_specs=[
                smem(), self.everyones(DK + DV), self.per_chain(c, DK, DK),
                self.per_chain(c, DK, DV), self.per_chain(c, CHUNK, DK), self.rows(DV, 0),
                self.per_chain(c, DK), self.og(), self.gain(),
            ],
            out_specs=[self.per_chain(c, DK, DV), self.rows(DV, 0), self.rows(DV, 0)],
            out_shape=[
                self.chain_shape((c, DK, DV), bf16), self.row_shape(DV, f32),
                self.row_shape(DV, bf16),
            ],
            compiler_params=params(),
            name="states_and_norm",
        )(place, maps, n, b, qe, o, tot, projected, gain)

    def norm_grads(self, dn, mixed, projected, gain, qe, n, tot):
        c = self.count
        return pl.pallas_call(
            norm_grad_kernel,
            grid=self.grid,
            in_specs=[
                self.rows(DV, 0), self.rows(DV, 0), self.og(), self.gain(),
                self.per_chain(c, CHUNK, DK), self.per_chain(c, DK, DK), self.per_chain(c, DK),
            ],
            out_specs=[
                self.rows(DV, 0), self.rows(DV, 0), self.per_chain(8, DV), self.per_chain(DK, DV),
            ],
            out_shape=[
                self.row_shape(DV, bf16), self.row_shape(DV, bf16), self.chain_shape((8, DV), f32),
                self.chain_shape((DK, DV), bf16),
            ],
            compiler_params=params(),
            name="norm_grads",
        )(dn, mixed, projected, gain, qe, n, tot)

    def rule_grads(
        self, place, starts, decay_par, owns, maps, qkv, inv, n, qe, tot, s, do, projected, halo, conv_w
    ):
        c = self.count
        return pl.pallas_call(
            rule_grad_kernel,
            grid=self.grid,
            in_specs=[
                smem(), smem(), smem(), self.everyones(DV), self.everyones(DK + DV),
                self.rows(QKV, 0), self.per_chain(c, CHUNK, CHUNK), self.per_chain(c, DK, DK),
                self.per_chain(c, CHUNK, DK), self.per_chain(c, DK), self.per_chain(c, DK, DV),
                self.rows(DV, 0), self.rows(QKV, 0), self.halo(), self.rates(), self.conv(),
            ],
            out_specs=[
                self.rows(QKV, 0), pl.BlockSpec((1, 8, QKV), lambda h, s: (s, 0, h)),
                self.per_chain(CONV, QKV), self.rows(PAD, 0), self.per_chain(8, PAD),
            ],
            out_shape=[
                self.row_shape(QKV, f32),
                jax.ShapeDtypeStruct((self.seqs, 8, self.heads * QKV), f32),
                self.chain_shape((CONV, QKV), f32), self.row_shape(PAD, f32),
                self.chain_shape((8, PAD), f32),
            ],
            scratch_shapes=[
                pltpu.VMEM((HALO + self.length, QKV), f32),
                pltpu.VMEM((16 + self.length, QKV), f32),
            ],
            compiler_params=params(),
            name="rule_grads",
        )(
            place, starts, decay_par, owns, maps, qkv, inv, n, qe, tot, s, do, projected, halo,
            projected, conv_w,
        )


MESH = pl.DeviceIdType.MESH
SUB = 128


def head_copy(src, dst, send_sem, recv_sem, peer):
    return pltpu.make_async_remote_copy(
        src_ref=src, dst_ref=dst, send_sem=send_sem, recv_sem=recv_sem,
        device_id={"head": peer}, device_id_type=MESH,
    )


def greet_heads(me, peers):
    barrier = pltpu.get_barrier_semaphore()
    for k in range(1, peers):
        pl.semaphore_signal(barrier, inc=1, device_id={"head": me ^ k}, device_id_type=MESH)
    pl.semaphore_wait(barrier, peers - 1)


def part(ref, start, size):
    return ref.at[pl.ds(pl.multiple_of(start, size), size)]


def mixer_ffn_kernel(
    peers, normed_hbm, wout_hbm, ffn_hbm, x_hbm, ct_hbm, gain_ref,
    grads_hbm, ffnp_hbm, ng_hbm, hidden_ref, hgrad_ref, gpart_ref,
    normed_v, wout_v, ffn_v, x_v, ct_v, send1, recv1, nm, act, dgu, send2, recv2, dm, ffnp_v,
    grads_v, ng_v, in_sem, out_sem, ss1, rs1, ss2, rs2, ss3, rs3, ss4, rs4,
):
    me = lax.axis_index("head")
    total, width = ct_hbm.shape
    own_rows = total // peers
    subs = own_rows // SUB
    cells = act.shape[1]
    tile = 256
    loads = [
        pltpu.make_async_copy(normed_hbm, normed_v, in_sem.at[0]),
        pltpu.make_async_copy(wout_hbm, wout_v, in_sem.at[1]),
        pltpu.make_async_copy(part(x_hbm, me * own_rows, own_rows), x_v, in_sem.at[2]),
        pltpu.make_async_copy(ffn_hbm, ffn_v, in_sem.at[3]),
        pltpu.make_async_copy(ct_hbm, ct_v, in_sem.at[4]),
    ]
    for load in loads:
        load.start()
    greet_heads(me, peers)
    loads[0].wait()
    loads[1].wait()

    def sub_copy(k, t):
        rows = pl.ds(pl.multiple_of(t * SUB, SUB), SUB)
        return head_copy(
            send1.at[k, rows], recv1.at[k, rows], ss1.at[k, t], rs1.at[k, t], me ^ k
        )

    def project(i, carry):
        k = peers - 1 - i
        rows = pl.ds(pl.multiple_of((me ^ k) * own_rows, own_rows), own_rows)
        send1[k] = mm(normed_v[rows, :], wout_v[...], NT).astype(bf16)

        @pl.when(k > 0)
        def _():
            for t in range(subs):
                sub_copy(k, t).start()

        return carry

    lax.fori_loop(0, peers, project, 0)
    loads[2].wait()
    gain = gain_ref[...]

    def sub_gather(k, t, owner, buffer, send_sem, recv_sem):
        at = part(buffer, owner * own_rows + t * SUB, SUB)
        return head_copy(at, at, send_sem.at[k, t], recv_sem.at[k, t], me ^ k)

    def normalise(t, carry):
        rows = pl.ds(pl.multiple_of(t * SUB, SUB), SUB)
        hidden = x_v[rows, :].astype(f32) + send1[0, rows, :].astype(f32)
        for k in range(1, peers):
            sub_copy(k, t).wait_recv()
            hidden = hidden + recv1[k, rows, :].astype(f32)
        hidden_ref[rows, :] = hidden
        inverse = lax.rsqrt(jnp.mean(hidden * hidden, axis=1, keepdims=True) + epsilon)
        part(nm, me * own_rows + t * SUB, SUB)[...] = (hidden * inverse * gain).astype(bf16)
        for k in range(peers - 1, 0, -1):
            sub_gather(k, t, me, nm, ss2, rs2).start()
        return carry

    lax.fori_loop(0, subs, normalise, 0)
    loads[3].wait()
    loads[4].wait()

    def mid_copy(k, t):
        rows = pl.ds(pl.multiple_of(t * SUB, SUB), SUB)
        return head_copy(
            send2.at[k, rows], recv2.at[k, rows], ss3.at[k, t], rs3.at[k, t], me ^ k
        )

    def feed_forward(k, carry):
        owner = me ^ k

        @pl.when(k > 0)
        def _():
            for t in range(subs):
                sub_gather(k, t, owner, nm, ss2, rs2).wait_recv()

        rows = pl.ds(pl.multiple_of(owner * own_rows, own_rows), own_rows)

        def cell_tile(j, carry):
            at = pl.ds(pl.multiple_of(j * tile, tile), tile)
            at_up = pl.ds(pl.multiple_of(cells + j * tile, tile), tile)
            at_down = pl.ds(pl.multiple_of(2 * cells + j * tile, tile), tile)
            gate = mm(nm[rows, :], ffn_v[:, at])
            up = mm(nm[rows, :], ffn_v[:, at_up])
            dact = mm(ct_v[rows, :], ffn_v[:, at_down])
            sig = sigmoid(gate)
            silu = gate * sig
            act[rows, at] = (silu * up).astype(bf16)
            dgu[rows, at] = (dact * up * sig * (1.0 + gate * (1.0 - sig))).astype(bf16)
            dgu[rows, at_up] = (dact * silu).astype(bf16)
            return carry

        lax.fori_loop(0, cells // tile, cell_tile, 0)

        def mid_tile(j, carry):
            at = pl.ds(pl.multiple_of(j * tile, tile), tile)
            send2[k, :, at] = mm(dgu[rows, :], ffn_v[at, 0 : 2 * cells], NT).astype(bf16)
            return carry

        lax.fori_loop(0, width // tile, mid_tile, 0)

        @pl.when(k > 0)
        def _():
            for t in range(subs):
                mid_copy(k, t).start()

        return carry

    lax.fori_loop(0, peers, feed_forward, 0)

    def middle_grad(t, carry):
        rows = pl.ds(pl.multiple_of(t * SUB, SUB), SUB)
        dmid = send2[0, rows, :].astype(f32)
        for k in range(1, peers):
            mid_copy(k, t).wait_recv()
            dmid = dmid + recv2[k, rows, :].astype(f32)
        hidden = hidden_ref[rows, :]
        inverse = lax.rsqrt(jnp.mean(hidden * hidden, axis=1, keepdims=True) + epsilon)
        scaled = hidden * inverse
        weighted = dmid * gain
        grad = part(ct_v, me * own_rows + t * SUB, SUB)[...].astype(f32) + inverse * (
            weighted - scaled * jnp.mean(weighted * scaled, axis=1, keepdims=True)
        )
        hgrad_ref[rows, :] = grad
        part(dm, me * own_rows + t * SUB, SUB)[...] = grad.astype(bf16)
        for k in range(peers - 1, 0, -1):
            sub_gather(k, t, me, dm, ss4, rs4).start()
        return carry + jnp.sum(dmid * scaled, axis=0, keepdims=True)

    gain_part = lax.fori_loop(0, subs, middle_grad, jnp.zeros((1, width), f32))
    gpart_ref[...] = jnp.broadcast_to(gain_part, gpart_ref.shape)

    def block_store(i, size, source, target, sem):
        return pltpu.make_async_copy(
            part(source, i * size, size), part(target, i * size, size), sem.at[i]
        )

    def cell_grads(i, carry):
        at = pl.ds(pl.multiple_of(i * tile, tile), tile)
        grads_v[at, 0 : 2 * cells] = mm(nm[:, at], dgu[...], TN).astype(bf16)
        grads_v[at, 2 * cells : 3 * cells] = mm(ct_v[:, at], act[...], TN).astype(bf16)
        return carry

    lax.fori_loop(0, width // tile, cell_grads, 0)

    def ffn_rows(i, carry):
        rows = pl.ds(pl.multiple_of(i * own_rows, own_rows), own_rows)
        ffnp_v[rows, :] = mm(act[rows, :], ffn_v[:, 2 * cells :], NT).astype(bf16)
        block_store(i, own_rows, ffnp_v, ffnp_hbm, out_sem.at[0]).start()
        return carry

    lax.fori_loop(0, peers, ffn_rows, 0)

    def norm_rows(k, carry):
        owner = me ^ k

        @pl.when(k > 0)
        def _():
            for t in range(subs):
                sub_gather(k, t, owner, dm, ss4, rs4).wait_recv()

        rows = pl.ds(pl.multiple_of(owner * own_rows, own_rows), own_rows)
        ng_v[rows, :] = mm(dm[rows, :], wout_v[...])
        block_store(owner, own_rows, ng_v, ng_hbm, out_sem.at[1]).start()
        return carry

    lax.fori_loop(0, peers, norm_rows, 0)

    def out_grads(i, carry):
        at = pl.ds(pl.multiple_of(i * tile, tile), tile)
        grads_v[at, 3 * cells :] = mm(dm[:, at], normed_v[...], TN).astype(bf16)
        block_store(i, tile, grads_v, grads_hbm, out_sem.at[2]).start()
        return carry

    lax.fori_loop(0, width // tile, out_grads, 0)
    for i in range(peers):
        block_store(i, own_rows, ffnp_v, ffnp_hbm, out_sem.at[0]).wait()
        block_store(i, own_rows, ng_v, ng_hbm, out_sem.at[1]).wait()
    for i in range(width // tile):
        block_store(i, tile, grads_v, grads_hbm, out_sem.at[2]).wait()
    for k in range(1, peers):
        for t in range(subs):
            sub_copy(k, t).wait_send()
            sub_gather(k, t, me, nm, ss2, rs2).wait_send()
            mid_copy(k, t).wait_send()
            sub_gather(k, t, me, dm, ss4, rs4).wait_send()


def anywhere():
    return pl.BlockSpec(memory_space=pl.ANY)


def vmem():
    return pl.BlockSpec(memory_space=pltpu.VMEM)


def mixer_ffn(normed, out_full, ffn_full, x, ct, gain):
    peers = lax.axis_size("head")
    total, width = ct.shape
    own_rows = total // peers
    subs = own_rows // SUB
    values = normed.shape[1]
    cells = ffn_full.shape[1] // 3
    sems = pltpu.SemaphoreType.DMA((peers, subs))
    return pl.pallas_call(
        functools.partial(mixer_ffn_kernel, peers),
        in_specs=[anywhere()] * 5 + [vmem()],
        out_specs=[anywhere()] * 3 + [vmem()] * 3,
        out_shape=[
            jax.ShapeDtypeStruct((width, 3 * cells + values), bf16),
            jax.ShapeDtypeStruct((total, width), bf16),
            jax.ShapeDtypeStruct((total, values), f32),
            jax.ShapeDtypeStruct((own_rows, width), f32),
            jax.ShapeDtypeStruct((own_rows, width), f32),
            jax.ShapeDtypeStruct((8, width), f32),
        ],
        scratch_shapes=[
            pltpu.VMEM((total, values), bf16),
            pltpu.VMEM((width, values), bf16),
            pltpu.VMEM((width, 3 * cells), bf16),
            pltpu.VMEM((own_rows, width), bf16),
            pltpu.VMEM((total, width), bf16),
            pltpu.VMEM((peers, own_rows, width), bf16),
            pltpu.VMEM((peers, own_rows, width), bf16),
            pltpu.VMEM((total, width), bf16),
            pltpu.VMEM((total, cells), bf16),
            pltpu.VMEM((total, 2 * cells), bf16),
            pltpu.VMEM((peers, own_rows, width), bf16),
            pltpu.VMEM((peers, own_rows, width), bf16),
            pltpu.VMEM((total, width), bf16),
            pltpu.VMEM((total, width), bf16),
            pltpu.VMEM((width, 3 * cells + values), bf16),
            pltpu.VMEM((total, values), f32),
            pltpu.SemaphoreType.DMA((5,)),
            pltpu.SemaphoreType.DMA((3, max(peers, width // 256))),
        ]
        + [sems] * 8,
        compiler_params=pltpu.CompilerParams(
            collective_id=1, has_side_effects=True, vmem_limit_bytes=56 * 2**20
        ),
        name="mixer_ffn",
    )(normed, out_full, ffn_full, x, ct, gain)


def input_grad_kernel(
    peers, dp_hbm, win_hbm, x_hbm, hgrad_ref, gain_ref,
    out_hbm, gpart_ref,
    dp_v, win_v, x_v, send1, recv1, whole, in_sem, out_sem, ss1, rs1, ss2, rs2,
):
    me = lax.axis_index("head")
    total, width = whole.shape
    own_rows = total // peers
    subs = own_rows // SUB
    loads = [
        pltpu.make_async_copy(dp_hbm, dp_v, in_sem.at[0]),
        pltpu.make_async_copy(win_hbm, win_v, in_sem.at[1]),
        pltpu.make_async_copy(part(x_hbm, me * own_rows, own_rows), x_v, in_sem.at[2]),
    ]
    for load in loads:
        load.start()
    greet_heads(me, peers)
    loads[0].wait()
    loads[1].wait()

    def sub_copy(k, t):
        rows = pl.ds(pl.multiple_of(t * SUB, SUB), SUB)
        return head_copy(
            send1.at[k, rows], recv1.at[k, rows], ss1.at[k, t], rs1.at[k, t], me ^ k
        )

    def project(i, carry):
        k = peers - 1 - i
        rows = pl.ds(pl.multiple_of((me ^ k) * own_rows, own_rows), own_rows)
        send1[k] = mm(dp_v[rows, :], win_v[...], NT).astype(bf16)

        @pl.when(k > 0)
        def _():
            for t in range(subs):
                sub_copy(k, t).start()

        return carry

    lax.fori_loop(0, peers, project, 0)
    loads[2].wait()
    gain = gain_ref[...]

    def sub_gather(k, t, owner):
        at = part(whole, owner * own_rows + t * SUB, SUB)
        return head_copy(at, at, ss2.at[k, t], rs2.at[k, t], me ^ k)

    def input_rows(t, carry):
        rows = pl.ds(pl.multiple_of(t * SUB, SUB), SUB)
        din = send1[0, rows, :].astype(f32)
        for k in range(1, peers):
            sub_copy(k, t).wait_recv()
            din = din + recv1[k, rows, :].astype(f32)
        x = x_v[rows, :].astype(f32)
        inverse = lax.rsqrt(jnp.mean(x * x, axis=1, keepdims=True) + epsilon)
        scaled = x * inverse
        weighted = din * gain
        grad = hgrad_ref[rows, :] + inverse * (
            weighted - scaled * jnp.mean(weighted * scaled, axis=1, keepdims=True)
        )
        part(whole, me * own_rows + t * SUB, SUB)[...] = grad.astype(bf16)
        for k in range(peers - 1, 0, -1):
            sub_gather(k, t, me).start()
        return carry + jnp.sum(din * scaled, axis=0, keepdims=True)

    gain_part = lax.fori_loop(0, subs, input_rows, jnp.zeros((1, width), f32))
    gpart_ref[...] = jnp.broadcast_to(gain_part, gpart_ref.shape)

    def store(i):
        return pltpu.make_async_copy(
            part(whole, i * own_rows, own_rows), part(out_hbm, i * own_rows, own_rows),
            out_sem.at[i],
        )

    store(me).start()
    for k in range(1, peers):
        for t in range(subs):
            sub_gather(k, t, me ^ k).wait_recv()
        store(me ^ k).start()
    for k in range(peers):
        store(me ^ k).wait()
    for k in range(1, peers):
        for t in range(subs):
            sub_copy(k, t).wait_send()
            sub_gather(k, t, me).wait_send()


def input_grads(dp, in_full, x, hgrad, gain):
    peers = lax.axis_size("head")
    total, width = x.shape
    cols = dp.shape[1]
    own_rows = total // peers
    subs = own_rows // SUB
    sems = pltpu.SemaphoreType.DMA((peers, subs))
    return pl.pallas_call(
        functools.partial(input_grad_kernel, peers),
        in_specs=[anywhere()] * 3 + [vmem()] * 2,
        out_specs=[anywhere(), vmem()],
        out_shape=[
            jax.ShapeDtypeStruct((total, width), bf16),
            jax.ShapeDtypeStruct((8, width), f32),
        ],
        scratch_shapes=[
            pltpu.VMEM((total, cols), bf16),
            pltpu.VMEM((width, cols), bf16),
            pltpu.VMEM((own_rows, width), bf16),
            pltpu.VMEM((peers, own_rows, width), bf16),
            pltpu.VMEM((peers, own_rows, width), bf16),
            pltpu.VMEM((total, width), bf16),
            pltpu.SemaphoreType.DMA((3,)),
            pltpu.SemaphoreType.DMA((peers,)),
        ]
        + [sems] * 4,
        compiler_params=pltpu.CompilerParams(
            collective_id=2, has_side_effects=True, vmem_limit_bytes=48 * 2**20
        ),
        name="input_grads",
    )(dp, in_full, x, hgrad, gain)


def shifted(shard, axis, by):
    count = lax.axis_size(axis)
    pairs = [(i, i + by) for i in range(count) if 0 <= i + by < count]
    return lax.ppermute(shard, axis, pairs)


def root_scale(value_rows):
    return lax.rsqrt(jnp.mean(value_rows * value_rows, axis=-1, keepdims=True) + epsilon)


def matmul(a, b, dims=NN):
    return lax.dot_general(a, b, (dims, ((), ())), preferred_element_type=f32)


ALL = ("seq", "batch")


def per_device(
    tokens, starts, attn_gain, w_in, w_rates, conv_w, decay_par, o_gain, w_out, ffn_gain, w_gu,
    w_down, cotangent,
):
    seqs, length, width = tokens.shape
    shard, heads = w_in.shape[:2]
    shards = width // shard
    total = seqs * length
    conv_cols = heads * QKV
    value_cols = heads * DV
    in_cols = conv_cols + value_cols
    units = w_down.shape[0]
    cells = -(-units // 256) * 256
    spare = cells - units

    conv_flat = conv_w.reshape(-1)
    small = jnp.concatenate([attn_gain, ffn_gain, conv_flat, o_gain]).astype(bf16)
    packed_in = jnp.concatenate(
        [
            w_in[:, :, :QKV].reshape(shard, conv_cols),
            w_in[:, :, QKV:].reshape(shard, value_cols),
            w_rates.reshape(shard, 2 * heads),
            jnp.zeros((shard, PAD - 2 * heads), f32),
        ],
        axis=1,
    ).astype(bf16)
    packed_ffn = jnp.pad(
        jnp.stack([w_gu[:, 0], w_gu[:, 1], w_down.T], axis=1).astype(bf16),
        ((0, 0), (0, 0), (0, spare)),
    ).reshape(shard, 3 * cells)
    in_full = lax.all_gather(packed_in, ALL, axis=0, tiled=True)
    small_full = lax.all_gather(small, ALL, axis=0)
    out_full = lax.all_gather(
        w_out.reshape(value_cols, -1).T.astype(bf16), ALL, axis=0, tiled=True
    )
    ffn_full = lax.all_gather(packed_ffn, ALL, axis=0, tiled=True)
    attn_gain_f = small_full[:, :shard].reshape(1, width).astype(f32)
    ffn_gain_f = small_full[:, shard : 2 * shard].reshape(1, width).astype(f32)
    conv_end = 2 * shard + conv_flat.shape[0]
    conv_full = (
        small_full[:, 2 * shard : conv_end]
        .reshape(shards, CONV, heads, -1)
        .transpose(1, 2, 0, 3)
        .reshape(CONV, conv_cols)
        .astype(f32)
    )
    o_gain_full = small_full[:, conv_end:].reshape(1, DV).astype(f32)

    place = lax.axis_index("seq").astype(jnp.int32).reshape(1)
    rule = Rule(seqs, length, heads, lax.axis_size("seq"))

    x = tokens.reshape(total, width)
    ct = cotangent.reshape(total, width)
    inputs = x.astype(f32)
    normed_in = (inputs * root_scale(inputs) * attn_gain_f).astype(bf16)
    projected = matmul(normed_in, in_full)
    ends = projected.reshape(seqs, length, -1)[:, length - CONV + 1 :, :conv_cols]
    end_live = (
        place * length + length - CONV + 1 + jnp.arange(CONV - 1, dtype=jnp.int32)
    )[None, :] >= starts[:, None]
    received = shifted((ends * end_live.astype(f32)[:, :, None]).astype(bf16), "seq", 1)
    halo = jnp.pad(received, ((0, 0), (HALO - CONV + 1, 0), (0, 0)))
    qkv, inv, n, b, qe, o, tot, own_map = rule.chunks(
        place, starts, decay_par, projected, halo, conv_full
    )
    maps = lax.all_gather(own_map, "seq")
    states, mixed, normed = rule.states(place, maps, n, b, qe, o, tot, projected, o_gain_full)

    late_grads, ffn_part, normed_grad, hidden, hidden_grad, ffn_gain_part = mixer_ffn(
        normed, out_full, ffn_full, x, ct, ffn_gain_f
    )
    own_rows = total // lax.axis_size("head")
    ffn_out = lax.psum_scatter(ffn_part, "head", scatter_dimension=0, tiled=True)
    result = lax.all_gather(
        (hidden + ffn_out.astype(f32)).astype(bf16), "head", axis=0, tiled=True
    )
    do, dog, onorm_grads, own = rule.norm_grads(
        normed_grad, mixed, projected, o_gain_full, qe, n, tot
    )
    owns = lax.all_gather(own, "seq")
    dci, dhalo, dconv, drate, ddecay = rule.rule_grads(
        place, starts, decay_par, owns, maps, qkv, inv, n, qe, tot, states, do, projected, halo,
        conv_full,
    )
    returned = shifted(dhalo[:, 8 - CONV + 1 :], "seq", -1)
    positions = place * length + jnp.arange(length, dtype=jnp.int32)
    live = (positions[None, :] >= starts[:, None]).astype(f32)
    dci = (
        dci.reshape(seqs, length, conv_cols)
        + jnp.pad(returned, ((0, 0), (length - CONV + 1, 0), (0, 0)))
    ) * live[:, :, None]
    rate_grad = jnp.sum(drate.reshape(total, heads, PAD), axis=1)
    projected_grad = jnp.concatenate(
        [dci.reshape(total, conv_cols).astype(bf16), dog, rate_grad.astype(bf16)], axis=1
    )
    in_grad = matmul(normed_in, projected_grad, TN)
    input_grad, attn_gain_part = input_grads(
        projected_grad, in_full, x, hidden_grad, attn_gain_f
    )
    onorm_grad = jnp.sum(onorm_grads[:, :, 0], axis=(0, 1))
    decay_part = jnp.sum(ddecay[:, :, :2, 0], axis=0).T
    conv_grad = jnp.sum(dconv, axis=0).transpose(1, 0, 2)

    def scatter(grad, dim=0):
        return lax.psum_scatter(
            grad.astype(bf16), ALL, scatter_dimension=dim, tiled=True
        ).astype(f32)

    late_own = scatter(late_grads)
    in_own = scatter(in_grad)
    gains = lax.psum(
        jnp.concatenate([attn_gain_part[0], ffn_gain_part[0], onorm_grad]), ("head",) + ALL
    )
    at = lax.axis_index(ALL)
    attn_own = lax.dynamic_slice(gains, (at * shard,), (shard,))
    ffn_own = lax.dynamic_slice(gains, (width + at * shard,), (shard,))
    onorm_own = lax.dynamic_slice(gains, (2 * width + at * (DV // shards),), (DV // shards,))
    channels = lax.psum(
        jnp.concatenate([conv_grad.reshape(-1), decay_part.reshape(-1)]), ALL
    )
    conv_own = lax.dynamic_slice(
        channels[: CONV * conv_cols].reshape(CONV, heads, QKV),
        (0, 0, at * (QKV // shards)),
        (CONV, heads, QKV // shards),
    )
    in_main = jnp.concatenate(
        [
            in_own[:, :conv_cols].reshape(shard, heads, QKV),
            in_own[:, conv_cols:in_cols].reshape(shard, heads, DV),
        ],
        axis=2,
    )
    return (
        result.reshape(tokens.shape),
        input_grad.reshape(tokens.shape),
        attn_own,
        in_main,
        in_own[:, in_cols : in_cols + 2 * heads].reshape(shard, heads, 2),
        conv_own,
        channels[CONV * conv_cols :].reshape(2, heads),
        onorm_own,
        late_own[:, 3 * cells :].T.reshape(heads, DV, -1),
        ffn_own,
        late_own[:, : 2 * cells].reshape(shard, 2, cells)[:, :, :units],
        late_own[:, 2 * cells : 2 * cells + units].T,
    )


def solution(mesh):
    weights = P(ALL)
    in_specs = (
        P("batch", "seq", None),
        P("batch"),
        weights,
        P(ALL, "head", None),
        P(ALL, "head", None),
        P(None, "head", ALL),
        P(None, "head"),
        weights,
        P("head", None, ALL),
        weights,
        P(ALL, None, "head"),
        P("head", ALL),
        P("batch", "seq", None),
    )
    out_specs = (
        P("batch", "seq", None),
        P("batch", "seq", None),
        weights,
        P(ALL, "head", None),
        P(ALL, "head", None),
        P(None, "head", ALL),
        P(None, "head"),
        weights,
        P("head", None, ALL),
        weights,
        P(ALL, None, "head"),
        P("head", ALL),
    )
    return jax.shard_map(
        per_device, mesh=mesh, in_specs=in_specs, out_specs=out_specs, check_vma=False
    )
```

time: 1950 us -> 574 us (0.29); the launches traced: 1920 us -> 573 us
  matrix products: 669 us -> 12.7 us
  local copies, waits for them, and re-layouts: 415 us -> 37.8 us
  other arithmetic: 315 us -> 16.8 us
  Pallas kernels: 0 us -> 224 us
  waiting for transfers between devices: 338 us -> 182 us
  blocking collectives: 142 us -> 82.2 us
  loops' own time: 21.1 us -> 0 us
    dot_general x471 -> x2, matrix products: 669 us -> 12.7 us  [matmul(): return lax.dot_general(a, b, (dims, ((), ())), preferred_element_type=f32)]
    psum x3 -> x0, waiting for transfers between devices: 228 us -> none  [the longest x1 106 us: per_device(): lax.psum(ffn_part.astype(jnp.bfloat16), 'head').astype(jnp.float32)]
    pallas_call x0 -> x6, Pallas kernels: none -> 224 us  [the longest x1 110 us: mixer_ffn(): pl.pallas_call(functools.partial(mixer_ffn_kernel, peers), in_specs=[anyw...]
    reshape x79 -> x9, local copies, waits for them, and re-layouts: 116 us -> 4.56 us  [the longest x1 1.74 us: per_device(): rate_grad = jnp.sum(drate.reshape(total, heads, PAD), axis=1)]
    reduce_sum x79 -> x4, other arithmetic: 106 us -> 2.2 us  [the longest x1 2.08 us: per_device(): rate_grad = jnp.sum(drate.reshape(total, heads, PAD), axis=1)]
    all_gather x6, waiting for transfers between devices: 63.3 us -> 156 us  [the longest x1 53.4 us: per_device(): ffn_full = lax.all_gather(packed_ffn, ALL, axis=0, tiled=True)]
    select_n x72 -> x0, local copies, waits for them, and re-layouts: 83.6 us -> none  [diagonal_blocks(): jnp.einsum('gagb->gab', matrix.reshape(groups, widths, groups, widths))]
    dynamic_update_slice x96 -> x0, local copies, waits for them, and re-layouts: 73.4 us -> none  [local_rule(): ending, outputs = lax.scan(stretch_step, start_state, pieces)]
  transfers between devices with their start and end apart: 17 -> 11, of which waited for: 9 -> 8; matrix products, arithmetic and copies ran while one was open for 43% -> 5% of each run, Pallas kernels for 0% -> 16%
where the time goes in v1:
time: 574 us; the launch traced here: 573 us
  Pallas kernels  224 us (39%)
  waiting for transfers between devices  182 us (32%)
  blocking collectives  82.2 us (14%)
  local copies, waits for them, and re-layouts  37.8 us (7%)
  other arithmetic  16.8 us (3%)
  between operations  14.4 us (3%)
  matrix products  12.7 us (2%)
    pallas_call x1, Pallas kernels, mixer_ffn(): pl.pallas_call(functools.partial(mixer_ffn_kernel, peers), in_specs=[anyw...  110 us
    all_gather x1, waiting for transfers between devices, per_device(): ffn_full = lax.all_gather(packed_ffn, ALL, axis=0, tiled=True)  53.4 us
    pallas_call x1, Pallas kernels, input_grads(): pl.pallas_call(functools.partial(input_grad_kernel, peers), in_specs=[any...  49.3 us
    psum x1, blocking collectives, per_device(): lax.psum(jnp.concatenate([attn_gain_part[0], ffn_gain_part[0], onorm_grad...  38.9 us
    all_gather x1, waiting for transfers between devices, per_device(): maps = lax.all_gather(own_map, 'seq')  35.5 us
    pallas_call x1, Pallas kernels, rule_grads(): pl.pallas_call(rule_grad_kernel, grid=self.grid, in_specs=[smem(), smem()...  30.8 us
    psum x1, blocking collectives, per_device(): lax.psum(jnp.concatenate([conv_grad.reshape(-1), decay_part.reshape(-1)])...  27.5 us
    all_gather x1, waiting for transfers between devices, per_device(): owns = lax.all_gather(own, 'seq')  27.4 us
  transfers between devices with their start and end apart: 11, of which 8 were waited for; matrix products, arithmetic and copies ran while one was open for 5% of the time, Pallas kernels for 16%

profile of v1, /device:TPU:0, one launch (start us, length us, event | category | flops | bytes accessed | tf_op | source)
XLA Modules:
  0.0 573.4 jit_solution(2789275535567407410)
XLA Ops:
  11.1 15.7 %all-gather.2 = bf16[8,1,800]{2,1,0:T(2,128)(2,1)S(1)} all-gather(bf16[1,1,800]{2,1,0:T(2,128)(2,1)S(1)} %maximum_bitcast_fusion), channel_id=1, replica_groups=mesh['seq'=4,'batch'=2,'head'=4] {'seq','batch'}, dimensions={0}, use_global_device_ids=true | all-gather | bytes 14400 | tf_op jit(solution)/shard_map/all_gather | solution.py:961
  28.1 26.2 %all-gather.10.cloned.1.call-done.win_hbm = bf16[1024,1664]{1,0:T(8,128)(2,1)} async-done(((bf16[128,1664]{1,0:T(8,128)(2,1)}), bf16[1024,1664]{1,0:T(8,128)(2,1)}) %all-gather.10.cloned.1.call-update) | async-done | bytes 3407888 | tf_op jit(solution)/shard_map/all_gather | solution.py:960
  54.2 6.0 %fusion.2.main_ref.rate_ref.og_ref = f32[1024,1664]{1,0:T(8,128)S(1)} fusion(bf16[1024,1664]{1,0:T(8,128)(2,1)} %all-gather.10.cloned.1.call-done.win_hbm, bf16[1024,1024]{1,0:T(8,128)(2,1)S(1)} %bitcast.64, f32[1024]{0:T(1024)S(1)} %get-tuple-element.117, f32[1024]{0:T(1024)S(1)} %bitcast.99), kind=kOutput, calls=%fused_computation.10 | convolution fusion | flops 3493855232 | bytes 12328960 | tf_op jit(solution)/shard_map/dot_general | solution.py:924
  60.3 2.8 copy-done.21
  63.1 2.3 collective-permute-start
  66.9 20.9 %chunk_maps.1 = (bf16[1024,1024]{1,0:T(8,128)(2,1)S(1)}, bf16[2,2,4,128,128]{4,3,2,1,0:T(8,128)(2,1)S(1)}, bf16[2,2,4,128,128]{4,3,2,1,0:T(8,128)(2,1)S(1)}, f32...) custom-call(s32[1]{0:T(128)} %bitcast.place_ref, ...), custom_call_target="tpu_custom_call" | custom-call | tf_op jit(solution)/shard_map/chunk_maps/pallas_call | solution.py:426
  92.4 35.5 %all-gather.18.cloned.1.call-done = bf16[8,2,128,384]{3,2,1,0:T(8,128)(2,1)} async-done(((bf16[2,2,128,384]{3,2,1,0:T(8,128)(2,1)}), bf16[8,2,128,384]{3,2,1,0:T(8,128)(2,1)}) %all-gather.18.cloned.1.call-update) | async-done | bytes 1572880 | tf_op jit(solution)/shard_map/all_gather | solution.py:995
  129.3 6.1 %states_and_norm.1 = (bf16[2,2,4,128,256]{4,3,2,1,0:T(8,128)(2,1)S(1)}, f32[1024,512]{1,0:T(8,128)}, bf16[1024,512]{1,0:T(8,128)(2,1)S(1)}) custom-call(s32[1]{0:T(128)} %bitcast.place_ref, bf16[4,2,2,128,384]{4,3,2,1,0:T(8,128)(2,1)S(1)} %bitcast.68, bf16[2,2,4,128,128]{4,3,2,1,0:T(8,128)(2,1)S(1)} %get-tuple-element.41.n_ref, ...), custom_call_target="tpu_custom_call" | custom-call | tf_op jit(solution)/shard_map/states_and_norm/pallas_call | solution.py:450
  137.4 13.7 %all-gather.12.cloned.1.call-done.wout_hbm = bf16[1024,512]{1,0:T(8,128)(2,1)} async-done(((bf16[128,512]{1,0:T(8,128)(2,1)}), bf16[1024,512]{1,0:T(8,128)(2,1)}) %all-gather.12.cloned.1.call-update) | async-done | bytes 1048592 | tf_op jit(solution)/shard_map/all_gather | solution.py:962
  151.1 53.4 %all-gather.14.cloned.1.call-done.ffn_hbm = bf16[1024,2304]{1,0:T(8,128)(2,1)} async-done(((bf16[128,2304]{1,0:T(8,128)(2,1)}), bf16[1024,2304]{1,0:T(8,128)(2,1)}) %all-gather.14.cloned.1.call-update) | async-done | bytes 4718608 | tf_op jit(solution)/shard_map/all_gather | solution.py:965
  204.5 110.3 %mixer_ffn.1 = (bf16[1024,2816]{1,0:T(8,128)(2,1)}, bf16[1024,1024]{1,0:T(8,128)(2,1)}, f32[1024,512]{1,0:T(8,128)}, f32[256,1024]{1,0:T(8,128)}, f32[256,1024]{1,0:T(8,128)}, /*index=5*/f32[8,1024]{1,0:T(8,128)}) custom-call(bf16[1024,512]{1,0:T(8,128)(2,1)} %copy-done.13, bf16[1024,512]{1,0:T(8,128)(2,1)} %all-gather.12.cloned.1.call-done.wout_hbm, ...), custom_call_target="tpu_custom_call" | custom-call | tf_op jit(solution)/shard_map/mixer_ffn/pallas_call | solution.py:754
  316.4 6.2 %norm_grads.1 = (bf16[1024,512]{1,0:T(8,128)(2,1)S(1)}, bf16[1024,512]{1,0:T(8,128)(2,1)S(1)}, f32[2,2,8,256]{3,2,1,0:T(8,128)S(1)}, bf16[2,2,128,256]{3,2,1,0:T(8,128)(2,1)}) custom-call(f32[1024,512]{1,0:T(8,128)S(1)} %copy-done.6, f32[1024,512]{1,0:T(8,128)} %get-tuple-element.50.mixed_ref, f32[1024,1664]{1,0:T(8,128)} %copy-done.21, ...), custom_call_target="tpu_custom_call" | custom-call | tf_op jit(solution)/shard_map/norm_grads/pallas_call | solution.py:469
  324.7 22.7 %reduce-scatter.4.cloned.1.call-done = bf16[256,1024]{1,0:T(8,128)(2,1)} async-done(((bf16[1024,1024]{1,0:T(8,128)(2,1)}), bf16[256,1024]{1,0:T(8,128)(2,1)}) %reduce-scatter.4.cloned.1.call-update) | async-done | bytes 524304 | tf_op jit(solution)/shard_map/reduce_scatter | solution.py:1002
  347.5 2.3 add_convert_fusion
  350.1 27.4 %all-gather.20.cloned.1.call-done = bf16[8,2,128,256]{3,2,1,0:T(8,128)(2,1)} async-done(((bf16[2,2,128,256]{3,2,1,0:T(8,128)(2,1)}), bf16[8,2,128,256]{3,2,1,0:T(8,128)(2,1)}) %all-gather.20.cloned.1.call-update) | async-done | bytes 1048592 | tf_op jit(solution)/shard_map/all_gather | solution.py:1009
  379.8 30.8 %rule_grads.1 = (f32[1024,1024]{1,0:T(8,128)}, f32[2,8,1024]{2,1,0:T(8,128)S(1)}, f32[2,2,4,512]{3,2,1,0:T(4,128)S(1)}, f32[1024,256]{1,0:T(8,128)S(1)}, f32[2,2,8,128]{3,2,1,0:T(8,128)S(1)}) custom-call(s32[1]{0:T(128)} %bitcast.place_ref, s32[2]{0:T(128)S(1)} %copy-done.19, f32[2,2]{1,0:T(2,128)S(1)} %copy-done.20, ...), custom_call_target="tpu_custom_call" | custom-call | tf_op jit(solution)/shard_map/rule_grads/pallas_call | solution.py:491
  414.7 2.1 reduce_sum.46
  417.4 2.8 multiply_convert_fusion
  421.5 6.7 %convolution_convert_fusion = bf16[1024,1664]{1,0:T(8,128)(2,1)} fusion(bf16[1024,1024]{1,0:T(8,128)(2,1)S(1)} %bitcast.65, f32[1024]{0:T(1024)S(1)} %get-tuple-element.117, f32[1024]{0:T(1024)S(1)} %bitcast.100, bf16[1024,128]{1,0:T(8,128)(2,1)S(1)} %copy-done.24, bf16[1024,512]{1,0:T(8,128)(2,1)S(1)} %copy-done.16, bf16[1024,1024]{1,0:T(8,128)(2,1)S(1)} %bitcast.73), kind=kOutput, calls=%fused_computation.3 | convolution fusion | flops 3505782784 | bytes 8921088 | tf_op jit(solution)/shard_map/dot_general | solution.py:924
  430.1 27.5 %psum.15 = f32[4100]{0:T(1024)S(1)} all-reduce(f32[4100]{0:T(1024)S(1)} %pad_maximum_fusion.2), channel_id=1, replica_groups=mesh['seq'=4,'batch'=2,'head'=4] {'seq','batch'}, use_global_device_ids=true, to_apply=%region_8.9 | all-reduce | flops 4100 | bytes 32800 | tf_op jit(solution)/shard_map/psum | solution.py:1047
  458.9 3.3 pad_maximum_fusion.dp_hbm
  462.2 49.3 %input_grads.1 = (bf16[1024,1024]{1,0:T(8,128)(2,1)S(1)}, f32[8,1024]{1,0:T(8,128)S(1)}) custom-call(bf16[1024,1664]{1,0:T(8,128)(2,1)} %pad_maximum_fusion.dp_hbm, bf16[1024,1664]{1,0:T(8,128)(2,1)} %all-gather.10.cloned.1.call-done.win_hbm, bf16[1024,1024]{1,0:T(8,128)(2,1)S(1)} %bitcast.66, f32[256,1024]{1,0:T(8,128)S(1)} %copy-done.7, f32[1,1024]{1,0:T(1,128)S(1)} %bitcast.71), custom_call_target="tpu_custom_call" | custom-call | tf_op jit(solution)/shard_map/input_grads/pallas_call | solution.py:887
  512.8 38.9 %psum.14 = f32[2304]{0:T(1024)S(1)} all-reduce(f32[2304]{0:T(1024)S(1)} %pad_maximum_fusion.3), channel_id=1, replica_groups=mesh['seq'=4,'batch'=2,'head'=4] {'head','seq','batch'}, use_global_device_ids=true, to_apply=%region_4.5 | all-reduce | flops 2304 | bytes 18432 | tf_op jit(solution)/shard_map/psum | solution.py:1040
  562.5 3.1 copy.77
  (160 shorter events, 43.0 us)
Async XLA Ops:
  7.2 3.9 copy-start.31
  7.2 19.6 %copy-start = (bf16[2,512,1024]{2,1,0:T(8,128)(2,1)S(1)}, bf16[2,512,1024]{2,1,0:T(8,128)(2,1)}, u32[]{:S(2)}) copy-start(bf16[2,512,1024]{2,1,0:T(8,128)(2,1)} %param.13) | copy-start | bytes 6291460
  7.2 20.2 %copy-start.19 = (s32[2]{0:T(128)S(1)}, s32[2]{0:T(128)}, u32[]{:S(2)}) copy-start(s32[2]{0:T(128)} %start_ref.3) | copy-start | bytes 28
  7.2 47.0 %all-gather.10.cloned.1.call-start = ((), (), s32[]{:S(2)}) async-start(), calls=%async_computation.3 | async-start | bytes 3833856 | tf_op jit(solution)/shard_map/all_gather | solution.py:960
  10.9 117.0 %all-gather.18.cloned.1.call-start = ((), (), s32[]{:S(2)}) async-start(), calls=%async_computation.10 | async-start | bytes 1966080 | tf_op jit(solution)/shard_map/all_gather | solution.py:995
  54.2 12.6 %copy-start.20 = (f32[2,2]{1,0:T(2,128)S(1)}, f32[2,2]{1,0:T(2,128)}, u32[]{:S(2)}) copy-start(f32[2,2]{1,0:T(2,128)} %decay_ref.3) | copy-start | bytes 52
  63.1 3.7 collective-permute-start
  66.8 23.1 %copy-start.27 = (f32[2,256,128]{2,1,0:T(8,128)S(1)}, f32[2,256,128]{2,1,0:T(8,128)}, u32[]{:S(2)}) copy-start(f32[2,256,128]{2,1,0:T(8,128)} %param.21) | copy-start | bytes 786436
  66.9 24.0 %copy-start.25 = (f32[128,2,704]{0,2,1:T(8,128)S(1)}, f32[128,2,704]{0,2,1:T(8,128)}, u32[]{:S(2)}) copy-start(f32[128,2,704]{0,2,1:T(8,128)} %param.23) | copy-start | bytes 2162692
  66.9 24.0 %copy-start.26 = (f32[704,128]{1,0:T(8,128)S(1)}, f32[704,128]{1,0:T(8,128)}, u32[]{:S(2)}) copy-start(f32[704,128]{1,0:T(8,128)} %param.24) | copy-start | bytes 1081348
  89.9 61.2 %all-gather.12.cloned.1.call-start = ((), (), s32[]{:S(2)}) async-start(), calls=%async_computation.4 | async-start | bytes 1179648 | tf_op jit(solution)/shard_map/all_gather | solution.py:962
  90.8 113.7 %all-gather.14.cloned.1.call-start = ((), (), s32[]{:S(2)}) async-start(), calls=%async_computation.5 | async-start | bytes 5308416 | tf_op jit(solution)/shard_map/all_gather | solution.py:965
  92.1 255.4 %reduce-scatter.4.cloned.1.call-start = ((), (), s32[]{:S(2)}) async-start(), calls=%async_computation.6 | async-start | bytes 2621440 | tf_op jit(solution)/shard_map/reduce_scatter | solution.py:1002
  314.9 62.6 %all-gather.20.cloned.1.call-start = ((), (), s32[]{:S(2)}) async-start(), calls=%async_computation.11 | async-start | bytes 1310720 | tf_op jit(solution)/shard_map/all_gather | solution.py:1009
  324.7 52.8 %copy-start.9 = (bf16[2,2,4,128,256]{4,3,2,1,0:T(8,128)(2,1)S(1)}, bf16[2,2,4,128,256]{4,3,2,1,0:T(8,128)(2,1)}, u32[]{:S(2)}) copy-start(bf16[2,2,4,128,256]{4,3,2,1,0:T(8,128)(2,1)} %copy-done.8) | copy-start | bytes 3145732
  324.7 52.8 %copy-start.11 = (bf16[1024,512]{1,0:T(8,128)(2,1)S(1)}, bf16[1024,512]{1,0:T(8,128)(2,1)}, u32[]{:S(2)}) copy-start(bf16[1024,512]{1,0:T(8,128)(2,1)} %copy-done.10) | copy-start | bytes 3145732
  324.7 228.3 %all-gather.16.cloned.1.call-start = ((), (), s32[]{:S(2)}) async-start(), calls=%async_computation.7 | async-start | bytes 2621440 | tf_op jit(solution)/shard_map/all_gather | solution.py:1003
  349.8 203.2 %reduce-scatter.6.cloned.1.call-start = ((), (), s32[]{:S(2)}) async-start(), calls=%async_computation.8 | async-start | bytes 3833856 | tf_op jit(solution)/shard_map/reduce_scatter | solution.py:1034
  411.6 5.8 %collective-permute-start.1 = (f32[2,3,1024]{2,1,0:T(4,128)S(1)}, f32[2,3,1024]{2,1,0:T(4,128)S(1)}, u32[]{:S(2)}, u32[]{:S(2)}) collective-permute-start(f32[2,3,1024]{2,1,0:T(4,128)S(1)} %slice.83), channel_id=1, source_target_pairs={{8,0},{16,8},{24,16},{9,1},{17,9},{25,17},{10,2},{18,10},{26,18},{... | collective-permute-start | bytes 73736 | tf_op jit(solution)/shard_map/ppermute | solution.py:916
  416.8 4.7 copy-start.1
  416.8 4.7 copy-start.16
  416.8 4.7 copy-start.24
  428.2 130.0 %reduce-scatter.8.cloned.1.call-start = ((), (), s32[]{:S(2)}) async-start(), calls=%async_computation.9 | async-start | bytes 6488064 | tf_op jit(solution)/shard_map/reduce_scatter | solution.py:1034
  559.9 5.7 %copy-start.5 = (bf16[1024,1024]{1,0:T(8,128)(2,1)S(1)}, bf16[1024,1024]{1,0:T(8,128)(2,1)}, u32[]{:S(2)}) copy-start(bf16[1024,1024]{1,0:T(8,128)(2,1)} %copy-done.4) | copy-start | bytes 6291460
  (19 other events, 33.9 us)
Sparse Core Ops, SparseCore 0:
  11.0 43.1 all-gather.9
  90.0 37.8 all-gather.17
  130.1 20.9 all-gather.11
  153.2 51.3 all-gather.13
  315.0 32.4 reduce-scatter.3
  349.5 27.9 all-gather.19
  380.1 34.8 all-gather.15
  428.3 42.6 reduce-scatter.5
  473.5 64.2 reduce-scatter.7

commit v2 on v1

--- a/solution.py
+++ b/solution.py
@@ -100,11 +100,10 @@
     return column, total, ratio
 
 
-def load_conv_input(main_ref, halo_ref, start_ref, x_scr, seq_place):
+def load_conv_input(main_ref, halo_ref, start, x_scr, first):
     length = main_ref.shape[0]
-    s = pl.program_id(1)
-    positions = seq_place * length + lax.broadcasted_iota(jnp.int32, (length, 1), 0)
-    live = (positions >= start_ref[s]).astype(f32)
+    positions = first + lax.broadcasted_iota(jnp.int32, (length, 1), 0)
+    live = (positions >= start).astype(f32)
     x_scr[pl.ds(0, HALO), :] = halo_ref[0].astype(f32)
     x_scr[pl.ds(HALO, length), :] = (main_ref[...] * live).astype(bf16).astype(f32)
 
@@ -120,405 +119,6 @@
     return rows * lax.rsqrt(jnp.sum(rows * rows, axis=1, keepdims=True) + epsilon)
 
 
-def chunk_kernel(
-    place_ref, start_ref, decay_ref, main_ref, halo_ref, rate_ref, conv_ref,
-    qkv_ref, inv_ref, n_ref, b_ref, qe_ref, o_ref, tot_ref, map_ref, x_scr,
-):
-    head = pl.program_id(0)
-    load_conv_input(main_ref, halo_ref, start_ref, x_scr, place_ref[0])
-    conv = conv_ref[...]
-    length = main_ref.shape[0]
-    count = length // CHUNK
-    rows, cols = iotas(CHUNK)
-    lower, upper, eye = rows >= cols, rows <= cols, rows == cols
-    parts = []
-    for c in range(count):
-        at = c * CHUNK
-        convolved = convolve(x_scr, conv, at)
-        active = convolved * sigmoid(convolved)
-        q = (unit(active[:, :DK]) * DK ** (-0.5)).astype(bf16)
-        k = unit(active[:, DK : 2 * DK]).astype(bf16)
-        v = active[:, 2 * DK :].astype(bf16)
-        qkv_ref[pl.ds(at, CHUNK), 0:DK] = q
-        qkv_ref[pl.ds(at, CHUNK), DK : 2 * DK] = k
-        qkv_ref[pl.ds(at, CHUNK), 2 * DK :] = v
-        log_gate, strength, _, _ = gates(rate_ref[pl.ds(at, CHUNK), :], decay_ref, head)
-        column, total, ratio = decays(log_gate, lower, upper, eye)
-        products = mm(jnp.concatenate([k, q], axis=0), k, NT)
-        coupling = jnp.where(rows > cols, strength * ratio * products[:CHUNK], 0.0)
-        scores = (ratio * products[CHUNK:]).astype(bf16)
-        parts.append((q, k, v, strength, column, total, coupling, scores))
-    inverses = unit_lower_inverses([p[6] for p in parts])
-    maps = []
-    for c in range(count):
-        q, k, v, strength, column, total, _, scores = parts[c]
-        growth = jnp.exp(column)
-        kf, vf, qf = k.astype(f32), v.astype(f32), q.astype(f32)
-        inverse = inverses[c].astype(bf16)
-        inv_ref[0, 0, c] = inverse
-        target = jnp.concatenate([(strength * growth) * kf, strength * vf], axis=1)
-        solved = mm(inverse, target).astype(bf16)
-        read = mm(scores, solved)
-        qe_ref[0, 0, c] = (growth * qf - read[:, :DK]).astype(bf16)
-        o_ref[pl.ds(c * CHUNK, CHUNK), :] = read[:, DK:]
-        kept = jnp.exp(total - column) * kf
-        written = mm(kept, solved, TN)
-        low_n = written[:, :DK].astype(bf16)
-        n_ref[0, 0, c] = low_n
-        b_ref[0, 0, c] = written[:, DK:]
-        whole = jnp.exp(total)
-        tot_ref[0, 0, pl.ds(c, 1), :] = jnp.broadcast_to(whole, (1, DK))
-        maps.append((low_n, written[:, DK:], whole))
-    low_n, b, whole = maps[0]
-    eye_f = eye.astype(f32)
-    trans = whole * eye_f - low_n.astype(f32)
-    carried = b
-    for low_n, b, whole in maps[1:]:
-        both = jnp.concatenate([trans, carried], axis=1)
-        moved = whole * both - mm(low_n, both)
-        trans = moved[:, :DK]
-        carried = moved[:, DK:] + b
-    map_ref[0, 0, :, 0:DK] = trans.astype(bf16)
-    map_ref[0, 0, :, DK:] = carried.astype(bf16)
-
-
-def state_kernel(
-    place_ref, maps_ref, n_ref, b_ref, qe_ref, o_ref, tot_ref, og_ref, gain_ref,
-    s_ref, mixed_ref, normed_ref,
-):
-    count = n_ref.shape[2]
-
-    def lap(z, state):
-        stage = maps_ref[z, 0, 0]
-        return mm(stage[:, :DK], state) + stage[:, DK:].astype(f32)
-
-    state = lax.fori_loop(0, place_ref[0], lap, jnp.zeros((DK, DV), f32))
-    for c in range(count):
-        low_state = state.astype(bf16)
-        s_ref[0, 0, c] = low_state
-        both = mm(jnp.concatenate([n_ref[0, 0, c], qe_ref[0, 0, c]], axis=0), low_state)
-        whole = tot_ref[0, 0, c, 0]
-        state = whole * state - both[:DK] + b_ref[0, 0, c]
-        at = pl.ds(c * CHUNK, CHUNK)
-        mixed = o_ref[at, :] + both[DK:]
-        mixed_ref[at, :] = mixed
-        og = og_ref[at, :]
-        inverse = lax.rsqrt(jnp.mean(mixed * mixed, axis=1, keepdims=True) + epsilon)
-        normed_ref[at, :] = (mixed * inverse * gain_ref[0:1] * (og * sigmoid(og))).astype(bf16)
-
-
-def norm_grad_kernel(
-    dn_ref, mixed_ref, og_ref, gain_ref, qe_ref, n_ref, tot_ref,
-    do_ref, dog_ref, gg_ref, own_ref,
-):
-    count = n_ref.shape[2]
-    gain = gain_ref[0:1]
-    state = jnp.zeros((DK, DV), f32)
-    total = jnp.zeros((1, DV), f32)
-    for c in reversed(range(count)):
-        at = pl.ds(c * CHUNK, CHUNK)
-        mixed, og, dn = mixed_ref[at, :], og_ref[at, :], dn_ref[at, :]
-        inverse = lax.rsqrt(jnp.mean(mixed * mixed, axis=1, keepdims=True) + epsilon)
-        scaled = mixed * inverse
-        sig = sigmoid(og)
-        silu = og * sig
-        through = dn * scaled
-        total = total + jnp.sum(through * silu, axis=0, keepdims=True)
-        dog_ref[at, :] = (through * gain * sig * (1.0 + og * (1.0 - sig))).astype(bf16)
-        weighted = dn * gain * silu
-        dmixed = inverse * (
-            weighted - scaled * jnp.mean(weighted * scaled, axis=1, keepdims=True)
-        )
-        dmixed = dmixed.astype(bf16)
-        do_ref[at, :] = dmixed
-        whole = tot_ref[0, 0, c, 0]
-        state = whole * state - mm(n_ref[0, 0, c], state, TN) + mm(qe_ref[0, 0, c], dmixed, TN)
-    gg_ref[0, 0] = jnp.broadcast_to(total, (8, DV))
-    own_ref[0, 0] = state.astype(bf16)
-
-
-def rule_grad_kernel(
-    place_ref, start_ref, decay_ref, owns_ref, maps_ref, qkv_ref, inv_ref, n_ref, qe_ref,
-    tot_ref, s_ref, do_ref, main_ref, halo_ref, rate_ref, conv_ref,
-    dci_ref, dhalo_ref, dconv_ref, drate_ref, ddecay_ref, x_scr, g_scr,
-):
-    head = pl.program_id(0)
-    length = main_ref.shape[0]
-    count = length // CHUNK
-    load_conv_input(main_ref, halo_ref, start_ref, x_scr, place_ref[0])
-    conv = conv_ref[...]
-    rows, cols = iotas(CHUNK)
-    lower, upper, eye = rows >= cols, rows <= cols, rows == cols
-    strict = rows > cols
-    last = owns_ref.shape[0] - 1
-
-    def lap(i, state):
-        z = last - i
-        return mm(maps_ref[z, 0, 0][:, :DK], state, TN) + owns_ref[z, 0, 0].astype(f32)
-
-    state = lax.fori_loop(0, last - place_ref[0], lap, jnp.zeros((DK, DV), f32))
-    leaving = [None] * count
-    for c in reversed(range(count)):
-        leaving[c] = state
-        at = pl.ds(c * CHUNK, CHUNK)
-        state = (
-            tot_ref[0, 0, c, 0] * state
-            - mm(n_ref[0, 0, c], state, TN)
-            + mm(qe_ref[0, 0, c], do_ref[at, :], TN)
-        )
-    g_scr[pl.ds(0, 8), :] = jnp.zeros((8, QKV), f32)
-    g_scr[pl.ds(8 + length, 8), :] = jnp.zeros((8, QKV), f32)
-    rate_total = jnp.zeros((1, 1), f32)
-    bias_total = jnp.zeros((1, 1), f32)
-    conv_total = [jnp.zeros((1, QKV), f32) for _ in range(CONV)]
-    lanes = lax.broadcasted_iota(jnp.int32, (CHUNK, PAD), 1)
-    for c in range(count):
-        at = pl.ds(c * CHUNK, CHUNK)
-        q, k, v = qkv_ref[at, 0:DK], qkv_ref[at, DK : 2 * DK], qkv_ref[at, 2 * DK :]
-        kf, vf = k.astype(f32), v.astype(f32)
-        log_gate, strength, rate, logit = gates(rate_ref[at, :], decay_ref, head)
-        column, total, ratio = decays(log_gate, lower, upper, eye)
-        growth = jnp.exp(column)
-        remain = jnp.exp(total - column)
-        whole = jnp.exp(total)
-        inverse = inv_ref[0, 0, c]
-        s0 = s_ref[0, 0, c]
-        do = do_ref[at, :]
-        grad_state = leaving[c]
-        low_grad_state = grad_state.astype(bf16)
-        kq = jnp.concatenate([k, q], axis=0)
-        products = mm(kq, k, NT)
-        kk, qk = products[:CHUNK], products[CHUNK:]
-        reads = mm(kq, s0)
-        ks, qs = reads[:CHUNK], reads[CHUNK:]
-        fresh = vf - growth * ks
-        pseudo = mm(inverse, strength * fresh).astype(bf16)
-        scores = (ratio * qk).astype(bf16)
-        dpseudo = mm(scores, do, TN) + mm(remain * kf, low_grad_state)
-        dtarget = mm(inverse, dpseudo, TN)
-        low_dtarget = dtarget.astype(bf16)
-        dstrength = jnp.sum(dtarget * fresh, axis=1, keepdims=True)
-        dlog = -(strength * growth) * jnp.sum(dtarget * ks, axis=1, keepdims=True)
-        dv = strength * dtarget
-        outer = mm(jnp.concatenate([low_dtarget, do], axis=0), pseudo, NT)
-        dcoupling = jnp.where(strict, -outer[:CHUNK] * ratio, 0.0)
-        by_strength = dcoupling * kk
-        dstrength = dstrength + jnp.sum(by_strength, axis=1, keepdims=True)
-        exponent = strength * by_strength
-        dkk = (dcoupling * strength).astype(bf16)
-        dqk_f = jnp.where(lower, outer[CHUNK:] * ratio, 0.0)
-        exponent = exponent + dqk_f * qk
-        dqk = dqk_f.astype(bf16)
-        back = mm(jnp.concatenate([low_dtarget, do], axis=0), s0, NT)
-        wide = mm(jnp.concatenate([dkk, dqk], axis=0), k)
-        dq = growth * back[CHUNK:] + wide[CHUNK:]
-        dkept = mm(pseudo, low_grad_state, NT)
-        dk = (
-            wide[:CHUNK]
-            - (strength * growth) * back[:CHUNK]
-            + mm(jnp.concatenate([dkk, dqk], axis=0), kq, TN)
-            + remain * dkept
-        )
-        dlog = dlog + growth * jnp.sum(do.astype(f32) * qs, axis=1, keepdims=True)
-        from_kept = remain * jnp.sum(kf * dkept, axis=1, keepdims=True)
-        dlog = dlog - from_kept + jnp.sum(exponent, axis=1, keepdims=True)
-        dlog_row = to_row(dlog, eye) - jnp.sum(exponent, axis=0, keepdims=True)
-        tail = jnp.sum(from_kept, axis=0, keepdims=True) + whole * jnp.sum(
-            jnp.sum(grad_state * s0.astype(f32), axis=1, keepdims=True), axis=0, keepdims=True
-        )
-        dgate = jnp.sum(jnp.where(upper, dlog_row, 0.0), axis=1, keepdims=True) + tail
-        slope = sigmoid(logit)
-        drate0 = -rate * slope * dgate
-        drate1 = dstrength * strength * (1.0 - strength)
-        rate_total = rate_total + jnp.sum(dgate * log_gate, axis=0, keepdims=True)
-        bias_total = bias_total + jnp.sum(drate0, axis=0, keepdims=True)
-        drate_ref[at, :] = jnp.where(
-            lanes == 2 * head, drate0, jnp.where(lanes == 2 * head + 1, drate1, 0.0)
-        )
-        convolved = convolve(x_scr, conv, c * CHUNK)
-        sig = sigmoid(convolved)
-        active = convolved * sig
-        slope_conv = sig * (1.0 + convolved * (1.0 - sig))
-
-        def unit_grad(rows_in, grad):
-            inv_norm = lax.rsqrt(jnp.sum(rows_in * rows_in, axis=1, keepdims=True) + epsilon)
-            y = rows_in * inv_norm
-            return inv_norm * (grad - y * jnp.sum(y * grad, axis=1, keepdims=True))
-
-        dq = dq.astype(bf16).astype(f32) * DK ** (-0.5)
-        dk = dk.astype(bf16).astype(f32)
-        dv = dv.astype(bf16).astype(f32)
-        dconv = (
-            jnp.concatenate(
-                [unit_grad(active[:, :DK], dq), unit_grad(active[:, DK : 2 * DK], dk), dv], axis=1
-            )
-            * slope_conv
-        )
-        g_scr[pl.ds(8 + c * CHUNK, CHUNK), :] = dconv
-        for j in range(CONV):
-            shifted_in = x_scr[pl.ds(c * CHUNK + HALO - CONV + 1 + j, CHUNK), :]
-            conv_total[j] = conv_total[j] + jnp.sum(dconv * shifted_in, axis=0, keepdims=True)
-    for j in range(CONV):
-        dconv_ref[0, 0, pl.ds(j, 1), :] = conv_total[j]
-    for c in range(count):
-        grad = g_scr[pl.ds(8 + c * CHUNK + CONV - 1, CHUNK), :] * conv[0:1]
-        for j in range(1, CONV):
-            grad = grad + g_scr[pl.ds(8 + c * CHUNK + CONV - 1 - j, CHUNK), :] * conv[j : j + 1]
-        dci_ref[pl.ds(c * CHUNK, CHUNK), :] = grad
-    grad = g_scr[pl.ds(CONV - 1, 8), :] * conv[0:1]
-    for j in range(1, CONV):
-        grad = grad + g_scr[pl.ds(CONV - 1 - j, 8), :] * conv[j : j + 1]
-    dhalo_ref[0] = grad
-    row8 = lax.broadcasted_iota(jnp.int32, (8, PAD), 0)
-    ddecay_ref[0, 0] = jnp.where(row8 == 0, rate_total, jnp.where(row8 == 1, bias_total, 0.0))
-
-
-def params():
-    return pltpu.CompilerParams(
-        dimension_semantics=("arbitrary", "arbitrary"), vmem_limit_bytes=48 * 2**20
-    )
-
-
-def smem():
-    return pl.BlockSpec(memory_space=pltpu.SMEM)
-
-
-class Rule:
-    def __init__(self, seqs, length, heads, places):
-        self.seqs, self.length, self.heads, self.places = seqs, length, heads, places
-        self.count = length // CHUNK
-        self.grid = (heads, seqs)
-
-    def per_chain(self, *dims):
-        zeros = (0,) * len(dims)
-        return pl.BlockSpec((1, 1) + dims, lambda h, s: (s, h) + zeros)
-
-    def chain_shape(self, dims, kind):
-        return jax.ShapeDtypeStruct((self.seqs, self.heads) + dims, kind)
-
-    def rows(self, width, first):
-        return pl.BlockSpec((self.length, width), lambda h, s: (s, first + h))
-
-    def rates(self):
-        at = self.heads * (QKV + DV) // PAD
-        return pl.BlockSpec((self.length, PAD), lambda h, s: (s, at))
-
-    def og(self):
-        return self.rows(DV, self.heads * QKV // DV)
-
-    def halo(self):
-        return pl.BlockSpec((1, HALO, QKV), lambda h, s: (s, 0, h))
-
-    def conv(self):
-        return pl.BlockSpec((CONV, QKV), lambda h, s: (0, h))
-
-    def gain(self):
-        return pl.BlockSpec((1, DV), lambda h, s: (0, 0))
-
-    def everyones(self, width):
-        return pl.BlockSpec((self.places, 1, 1, DK, width), lambda h, s: (0, s, h, 0, 0))
-
-    def row_shape(self, width, kind):
-        return jax.ShapeDtypeStruct((self.seqs * self.length, self.heads * width), kind)
-
-    def chunks(self, place, starts, decay_par, projected, halo, conv_w):
-        c = self.count
-        return pl.pallas_call(
-            chunk_kernel,
-            grid=self.grid,
-            in_specs=[
-                smem(), smem(), smem(), self.rows(QKV, 0), self.halo(), self.rates(), self.conv(),
-            ],
-            out_specs=[
-                self.rows(QKV, 0), self.per_chain(c, CHUNK, CHUNK), self.per_chain(c, DK, DK),
-                self.per_chain(c, DK, DV), self.per_chain(c, CHUNK, DK), self.rows(DV, 0),
-                self.per_chain(c, DK), self.per_chain(DK, DK + DV),
-            ],
-            out_shape=[
-                self.row_shape(QKV, bf16), self.chain_shape((c, CHUNK, CHUNK), bf16),
-                self.chain_shape((c, DK, DK), bf16), self.chain_shape((c, DK, DV), f32),
-                self.chain_shape((c, CHUNK, DK), bf16), self.row_shape(DV, f32),
-                self.chain_shape((c, DK), f32), self.chain_shape((DK, DK + DV), bf16),
-            ],
-            scratch_shapes=[pltpu.VMEM((HALO + self.length, QKV), f32)],
-            compiler_params=params(),
-            name="chunk_maps",
-        )(place, starts, decay_par, projected, halo, projected, conv_w)
-
-    def states(self, place, maps, n, b, qe, o, tot, projected, gain):
-        c = self.count
-        return pl.pallas_call(
-            state_kernel,
-            grid=self.grid,
-            in_specs=[
-                smem(), self.everyones(DK + DV), self.per_chain(c, DK, DK),
-                self.per_chain(c, DK, DV), self.per_chain(c, CHUNK, DK), self.rows(DV, 0),
-                self.per_chain(c, DK), self.og(), self.gain(),
-            ],
-            out_specs=[self.per_chain(c, DK, DV), self.rows(DV, 0), self.rows(DV, 0)],
-            out_shape=[
-                self.chain_shape((c, DK, DV), bf16), self.row_shape(DV, f32),
-                self.row_shape(DV, bf16),
-            ],
-            compiler_params=params(),
-            name="states_and_norm",
-        )(place, maps, n, b, qe, o, tot, projected, gain)
-
-    def norm_grads(self, dn, mixed, projected, gain, qe, n, tot):
-        c = self.count
-        return pl.pallas_call(
-            norm_grad_kernel,
-            grid=self.grid,
-            in_specs=[
-                self.rows(DV, 0), self.rows(DV, 0), self.og(), self.gain(),
-                self.per_chain(c, CHUNK, DK), self.per_chain(c, DK, DK), self.per_chain(c, DK),
-            ],
-            out_specs=[
-                self.rows(DV, 0), self.rows(DV, 0), self.per_chain(8, DV), self.per_chain(DK, DV),
-            ],
-            out_shape=[
-                self.row_shape(DV, bf16), self.row_shape(DV, bf16), self.chain_shape((8, DV), f32),
-                self.chain_shape((DK, DV), bf16),
-            ],
-            compiler_params=params(),
-            name="norm_grads",
-        )(dn, mixed, projected, gain, qe, n, tot)
-
-    def rule_grads(
-        self, place, starts, decay_par, owns, maps, qkv, inv, n, qe, tot, s, do, projected, halo, conv_w
-    ):
-        c = self.count
-        return pl.pallas_call(
-            rule_grad_kernel,
-            grid=self.grid,
-            in_specs=[
-                smem(), smem(), smem(), self.everyones(DV), self.everyones(DK + DV),
-                self.rows(QKV, 0), self.per_chain(c, CHUNK, CHUNK), self.per_chain(c, DK, DK),
-                self.per_chain(c, CHUNK, DK), self.per_chain(c, DK), self.per_chain(c, DK, DV),
-                self.rows(DV, 0), self.rows(QKV, 0), self.halo(), self.rates(), self.conv(),
-            ],
-            out_specs=[
-                self.rows(QKV, 0), pl.BlockSpec((1, 8, QKV), lambda h, s: (s, 0, h)),
-                self.per_chain(CONV, QKV), self.rows(PAD, 0), self.per_chain(8, PAD),
-            ],
-            out_shape=[
-                self.row_shape(QKV, f32),
-                jax.ShapeDtypeStruct((self.seqs, 8, self.heads * QKV), f32),
-                self.chain_shape((CONV, QKV), f32), self.row_shape(PAD, f32),
-                self.chain_shape((8, PAD), f32),
-            ],
-            scratch_shapes=[
-                pltpu.VMEM((HALO + self.length, QKV), f32),
-                pltpu.VMEM((16 + self.length, QKV), f32),
-            ],
-            compiler_params=params(),
-            name="rule_grads",
-        )(
-            place, starts, decay_par, owns, maps, qkv, inv, n, qe, tot, s, do, projected, halo,
-            projected, conv_w,
-        )
-
-
 MESH = pl.DeviceIdType.MESH
 SUB = 128
 
@@ -539,6 +139,646 @@
 
 def part(ref, start, size):
     return ref.at[pl.ds(pl.multiple_of(start, size), size)]
+
+
+def anywhere():
+    return pl.BlockSpec(memory_space=pl.ANY)
+
+
+def vmem():
+    return pl.BlockSpec(memory_space=pltpu.VMEM)
+
+
+def along(axis, source, target, send_sem, recv_sem, to):
+    return pltpu.make_async_remote_copy(
+        src_ref=source, dst_ref=target, send_sem=send_sem, recv_sem=recv_sem,
+        device_id={axis: to}, device_id_type=MESH,
+    )
+
+
+def forward_kernel(
+    seqs, places, start_ref, decay_ref, main_ref, halo_ref, rate_ref, conv_ref, og_ref, gain_ref,
+    qkv_ref, inv_ref, n_ref, qe_ref, tot_ref, trans_ref, s_ref, mixed_ref, normed_ref,
+    x_scr, b_scr, o_scr, carried_scr, send, recv, send_sem, recv_sem,
+):
+    step = pl.program_id(0)
+    chains = n_ref.shape[0]
+    count = n_ref.shape[1]
+    length = main_ref.shape[0]
+    place = lax.axis_index("seq")
+    lag = jnp.minimum(place, chains - 1)
+
+    @pl.when(step == 0)
+    def _():
+        barrier = pltpu.get_barrier_semaphore()
+
+        @pl.when(place > 0)
+        def _():
+            pl.semaphore_signal(
+                barrier, inc=1, device_id={"seq": place - 1}, device_id_type=MESH
+            )
+
+        @pl.when(place == 0)
+        def _():
+            recv[...] = jnp.zeros_like(recv)
+
+        @pl.when(place < places - 1)
+        def _():
+            pl.semaphore_wait(barrier, 1)
+
+    @pl.when(step < chains)
+    def _():
+        head = step // seqs
+        load_conv_input(
+            main_ref, halo_ref, start_ref[step % seqs], x_scr, place * length
+        )
+        conv = conv_ref[...]
+        rows, cols = iotas(CHUNK)
+        lower, upper, eye = rows >= cols, rows <= cols, rows == cols
+        parts = []
+        for c in range(count):
+            at = c * CHUNK
+            convolved = convolve(x_scr, conv, at)
+            active = convolved * sigmoid(convolved)
+            q = (unit(active[:, :DK]) * DK ** (-0.5)).astype(bf16)
+            k = unit(active[:, DK : 2 * DK]).astype(bf16)
+            v = active[:, 2 * DK :].astype(bf16)
+            qkv_ref[pl.ds(at, CHUNK), 0:DK] = q
+            qkv_ref[pl.ds(at, CHUNK), DK : 2 * DK] = k
+            qkv_ref[pl.ds(at, CHUNK), 2 * DK :] = v
+            log_gate, strength, _, _ = gates(rate_ref[pl.ds(at, CHUNK), :], decay_ref, head)
+            column, total, ratio = decays(log_gate, lower, upper, eye)
+            products = mm(jnp.concatenate([k, q], axis=0), k, NT)
+            coupling = jnp.where(rows > cols, strength * ratio * products[:CHUNK], 0.0)
+            scores = (ratio * products[CHUNK:]).astype(bf16)
+            parts.append((q, k, v, strength, column, total, coupling, scores))
+        inverses = unit_lower_inverses([p[6] for p in parts])
+        maps = []
+        for c in range(count):
+            q, k, v, strength, column, total, _, scores = parts[c]
+            growth = jnp.exp(column)
+            kf, vf, qf = k.astype(f32), v.astype(f32), q.astype(f32)
+            inverse = inverses[c].astype(bf16)
+            inv_ref[0, c] = inverse
+            target = jnp.concatenate([(strength * growth) * kf, strength * vf], axis=1)
+            solved = mm(inverse, target).astype(bf16)
+            read = mm(scores, solved)
+            qe_ref[step, c] = (growth * qf - read[:, :DK]).astype(bf16)
+            o_scr[step, pl.ds(c * CHUNK, CHUNK), :] = read[:, DK:]
+            written = mm(jnp.exp(total - column) * kf, solved, TN)
+            low_n = written[:, :DK].astype(bf16)
+            n_ref[step, c] = low_n
+            b_scr[step, c] = written[:, DK:]
+            whole = jnp.exp(total)
+            tot_ref[step, pl.ds(c, 1), :] = jnp.broadcast_to(whole, (1, DK))
+            maps.append((low_n, written[:, DK:], whole))
+        low_n, b, whole = maps[0]
+        trans = whole * eye.astype(f32) - low_n.astype(f32)
+        carried = b
+        for low_n, b, whole in maps[1:]:
+            both = jnp.concatenate([trans, carried], axis=1)
+            moved = whole * both - mm(low_n, both)
+            trans = moved[:, :DK]
+            carried = moved[:, DK:] + b
+        trans_ref[step] = trans.astype(bf16)
+        carried_scr[step] = carried
+
+    @pl.when(step >= chains)
+    def _():
+        chain = jnp.maximum(step - chains, 0)
+        state = recv[chain].astype(f32)
+        for c in range(count):
+            low_state = state.astype(bf16)
+            s_ref[0, c] = low_state
+            both = mm(jnp.concatenate([n_ref[chain, c], qe_ref[chain, c]], axis=0), low_state)
+            whole = tot_ref[chain, pl.ds(c, 1), 0:1]
+            state = whole * state - both[:DK] + b_scr[chain, c]
+            at = pl.ds(c * CHUNK, CHUNK)
+            mixed = o_scr[chain, at, :] + both[DK:]
+            mixed_ref[at, :] = mixed
+            og = og_ref[at, :]
+            inverse = lax.rsqrt(jnp.mean(mixed * mixed, axis=1, keepdims=True) + epsilon)
+            normed_ref[at, :] = (
+                mixed * inverse * gain_ref[0:1] * (og * sigmoid(og))
+            ).astype(bf16)
+
+    def passed(chain):
+        return along(
+            "seq", send.at[chain], recv.at[chain], send_sem.at[chain], recv_sem.at[chain],
+            jnp.minimum(place + 1, places - 1),
+        )
+
+    relayed = step - lag
+
+    @pl.when((relayed >= 0) & (relayed < chains))
+    def _():
+        chain = jnp.clip(relayed, 0, chains - 1)
+
+        @pl.when(place > 0)
+        def _():
+            passed(chain).wait_recv()
+
+        @pl.when(place < places - 1)
+        def _():
+            leaving = mm(trans_ref[chain], recv[chain]) + carried_scr[chain]
+            send[chain] = leaving.astype(bf16)
+            passed(chain).start()
+
+    @pl.when((step == 2 * chains - 1) & (place < places - 1))
+    def _():
+        for chain in range(chains):
+            passed(chain).wait_send()
+
+
+def early(chains, make):
+    return lambda j: make(jnp.minimum(j, chains - 1))
+
+
+def late(chains, make):
+    return lambda j: make(jnp.maximum(j - chains, 0))
+
+
+def forward_rule(starts, decay_par, projected, halo, conv_w, gain, seqs, heads):
+    places = lax.axis_size("seq")
+    chains = seqs * heads
+    length = projected.shape[0] // seqs
+    count = length // CHUNK
+    rates_at = heads * (QKV + DV) // PAD
+    og_at = heads * QKV // DV
+    row = lambda first: lambda i: (i % seqs, first + i // seqs)
+    whole = lambda *dims: pl.BlockSpec(dims, lambda j: (0,) * len(dims))
+    shape = jax.ShapeDtypeStruct
+    return pl.pallas_call(
+        functools.partial(forward_kernel, seqs, places),
+        grid=(2 * chains,),
+        in_specs=[
+            smem(),
+            smem(),
+            pl.BlockSpec((length, QKV), early(chains, row(0))),
+            pl.BlockSpec((1, HALO, QKV), early(chains, lambda i: (i % seqs, 0, i // seqs))),
+            pl.BlockSpec((length, PAD), early(chains, lambda i: (i % seqs, rates_at))),
+            pl.BlockSpec((CONV, QKV), early(chains, lambda i: (0, i // seqs))),
+            pl.BlockSpec((length, DV), late(chains, row(og_at))),
+            whole(1, DV),
+        ],
+        out_specs=[
+            pl.BlockSpec((length, QKV), early(chains, row(0))),
+            pl.BlockSpec((1, count, CHUNK, CHUNK), early(chains, lambda i: (i, 0, 0, 0))),
+            whole(chains, count, DK, DK),
+            whole(chains, count, CHUNK, DK),
+            whole(chains, count, DK),
+            whole(chains, DK, DK),
+            pl.BlockSpec((1, count, DK, DV), late(chains, lambda i: (i, 0, 0, 0))),
+            pl.BlockSpec((length, DV), late(chains, row(0))),
+            pl.BlockSpec((length, DV), late(chains, row(0))),
+        ],
+        out_shape=[
+            shape((seqs * length, heads * QKV), bf16),
+            shape((chains, count, CHUNK, CHUNK), bf16),
+            shape((chains, count, DK, DK), bf16),
+            shape((chains, count, CHUNK, DK), bf16),
+            shape((chains, count, DK), f32),
+            shape((chains, DK, DK), bf16),
+            shape((chains, count, DK, DV), bf16),
+            shape((seqs * length, heads * DV), f32),
+            shape((seqs * length, heads * DV), bf16),
+        ],
+        scratch_shapes=[
+            pltpu.VMEM((HALO + length, QKV), f32),
+            pltpu.VMEM((chains, count, DK, DV), f32),
+            pltpu.VMEM((chains, length, DV), f32),
+            pltpu.VMEM((chains, DK, DV), f32),
+            pltpu.VMEM((chains, DK, DV), bf16),
+            pltpu.VMEM((chains, DK, DV), bf16),
+            pltpu.SemaphoreType.DMA((chains,)),
+            pltpu.SemaphoreType.DMA((chains,)),
+        ],
+        compiler_params=pltpu.CompilerParams(
+            dimension_semantics=("arbitrary",), collective_id=3, has_side_effects=True,
+            vmem_limit_bytes=48 * 2**20,
+        ),
+        name="forward_rule",
+    )(starts, decay_par, projected, halo, projected, conv_w, projected, gain)
+
+
+def backward_kernel(
+    seqs, places, peers, start_ref, decay_ref,
+    dn_ref, mixed_ref, og_ref, gain_ref, n_ref, qe_ref, tot_ref, trans_ref,
+    qkv_ref, inv_ref, s_ref, main_ref, halo_ref, rate_ref, conv_ref, hidden_ref, ffnp_hbm,
+    dp_ref, dconv_ref, ddecay_ref, gg_ref, out_hbm,
+    x_scr, g_scr, do_scr, own_scr, send, recv, tail_scr, halo_send, halo_recv,
+    parts, whole_out, send_sem, recv_sem, halo_send_sem, halo_recv_sem, own_sem, out_sem,
+    ss1, rs1, ss2, rs2,
+):
+    step = pl.program_id(0)
+    chains = n_ref.shape[0]
+    count = n_ref.shape[1]
+    length = main_ref.shape[0]
+    heads = chains // seqs
+    conv_cols = heads * QKV
+    in_cols = conv_cols + heads * DV
+    place = lax.axis_index("seq")
+    lag = jnp.minimum(places - 1 - place, chains - 1)
+    me = lax.axis_index("head")
+    own_rows = hidden_ref.shape[0]
+    subs = own_rows // SUB
+
+    def ffn_copy(k):
+        return head_copy(
+            part(ffnp_hbm, (me ^ k) * own_rows, own_rows), parts.at[k], ss1.at[k], rs1.at[k],
+            me ^ k,
+        )
+
+    def own_copy():
+        return pltpu.make_async_copy(
+            part(ffnp_hbm, me * own_rows, own_rows), parts.at[0], own_sem.at[0]
+        )
+
+    def out_copy(k, owner):
+        at = part(whole_out, owner * own_rows, own_rows)
+        return head_copy(at, at, ss2.at[k], rs2.at[k], me ^ k)
+
+    def out_store(k):
+        owner = me ^ k
+        return pltpu.make_async_copy(
+            part(whole_out, owner * own_rows, own_rows), part(out_hbm, owner * own_rows, own_rows),
+            out_sem.at[k],
+        )
+
+    def passed(chain):
+        return along(
+            "seq", send.at[chain], recv.at[chain], send_sem.at[chain], recv_sem.at[chain],
+            jnp.maximum(place - 1, 0),
+        )
+
+    def returned(chain):
+        return along(
+            "seq", halo_send.at[chain], halo_recv.at[chain], halo_send_sem.at[chain],
+            halo_recv_sem.at[chain], jnp.maximum(place - 1, 0),
+        )
+
+    @pl.when(step == 0)
+    def _():
+        barrier = pltpu.get_barrier_semaphore()
+        for k in range(1, peers):
+            pl.semaphore_signal(barrier, inc=1, device_id={"head": me ^ k}, device_id_type=MESH)
+
+        @pl.when(place < places - 1)
+        def _():
+            pl.semaphore_signal(
+                barrier, inc=1, device_id={"seq": place + 1}, device_id_type=MESH
+            )
+
+        @pl.when(place == places - 1)
+        def _():
+            recv[...] = jnp.zeros_like(recv)
+            halo_recv[...] = jnp.zeros_like(halo_recv)
+
+        @pl.when(place > 0)
+        def _():
+            pl.semaphore_wait(barrier, peers)
+
+        @pl.when(place == 0)
+        def _():
+            pl.semaphore_wait(barrier, peers - 1)
+
+        own_copy().start()
+        for k in range(peers - 1, 0, -1):
+            ffn_copy(k).start()
+
+    @pl.when(step < chains)
+    def _():
+        gain = gain_ref[0:1]
+        first = (step % seqs) * length
+        og_at = pl.ds(pl.multiple_of(conv_cols + (step // seqs) * DV, DV), DV)
+        state = jnp.zeros((DK, DV), f32)
+        total = jnp.zeros((1, DV), f32)
+        for c in reversed(range(count)):
+            at = pl.ds(c * CHUNK, CHUNK)
+            mixed, og, dn = mixed_ref[at, :], og_ref[at, :], dn_ref[at, :]
+            inverse = lax.rsqrt(jnp.mean(mixed * mixed, axis=1, keepdims=True) + epsilon)
+            scaled = mixed * inverse
+            sig = sigmoid(og)
+            silu = og * sig
+            through = dn * scaled
+            total = total + jnp.sum(through * silu, axis=0, keepdims=True)
+            dp_ref[pl.ds(pl.multiple_of(first + c * CHUNK, CHUNK), CHUNK), og_at] = (
+                through * gain * sig * (1.0 + og * (1.0 - sig))
+            ).astype(bf16)
+            weighted = dn * gain * silu
+            dmixed = inverse * (
+                weighted - scaled * jnp.mean(weighted * scaled, axis=1, keepdims=True)
+            )
+            dmixed = dmixed.astype(bf16)
+            do_scr[step, at, :] = dmixed
+            decay = tot_ref[step, pl.ds(c, 1), 0:1]
+            state = (
+                decay * state - mm(n_ref[step, c], state, TN) + mm(qe_ref[step, c], dmixed, TN)
+            )
+        gg_ref[0] = jnp.broadcast_to(total, (8, DV))
+        own_scr[step] = state
+
+    @pl.when(step >= chains)
+    def _():
+        chain = jnp.maximum(step - chains, 0)
+        head, seq = chain // seqs, chain % seqs
+        first = seq * length
+        start = start_ref[seq]
+        load_conv_input(main_ref, halo_ref, start, x_scr, place * length)
+        conv = conv_ref[...]
+        rows, cols = iotas(CHUNK)
+        lower, upper, eye = rows >= cols, rows <= cols, rows == cols
+        strict = rows > cols
+        state = recv[chain].astype(f32)
+        leaving = [None] * count
+        for c in reversed(range(count)):
+            leaving[c] = state
+            state = (
+                tot_ref[chain, pl.ds(c, 1), 0:1] * state
+                - mm(n_ref[chain, c], state, TN)
+                + mm(qe_ref[chain, c], do_scr[chain, pl.ds(c * CHUNK, CHUNK), :], TN)
+            )
+        g_scr[pl.ds(0, 8), :] = jnp.zeros((8, QKV), f32)
+        g_scr[pl.ds(8 + length, 8), :] = jnp.zeros((8, QKV), f32)
+        rate_total = jnp.zeros((1, 1), f32)
+        bias_total = jnp.zeros((1, 1), f32)
+        conv_total = [jnp.zeros((1, QKV), f32) for _ in range(CONV)]
+        lanes = lax.broadcasted_iota(jnp.int32, (CHUNK, PAD), 1)
+        for c in range(count):
+            at = pl.ds(c * CHUNK, CHUNK)
+            q, k, v = qkv_ref[at, 0:DK], qkv_ref[at, DK : 2 * DK], qkv_ref[at, 2 * DK :]
+            kf, vf = k.astype(f32), v.astype(f32)
+            log_gate, strength, rate, logit = gates(rate_ref[at, :], decay_ref, head)
+            column, total, ratio = decays(log_gate, lower, upper, eye)
+            growth = jnp.exp(column)
+            remain = jnp.exp(total - column)
+            whole = jnp.exp(total)
+            inverse = inv_ref[0, c]
+            s0 = s_ref[0, c]
+            do = do_scr[chain, at, :]
+            grad_state = leaving[c]
+            low_grad_state = grad_state.astype(bf16)
+            kq = jnp.concatenate([k, q], axis=0)
+            products = mm(kq, k, NT)
+            kk, qk = products[:CHUNK], products[CHUNK:]
+            reads = mm(kq, s0)
+            ks, qs = reads[:CHUNK], reads[CHUNK:]
+            fresh = vf - growth * ks
+            pseudo = mm(inverse, strength * fresh).astype(bf16)
+            scores = (ratio * qk).astype(bf16)
+            dpseudo = mm(scores, do, TN) + mm(remain * kf, low_grad_state)
+            dtarget = mm(inverse, dpseudo, TN)
+            low_dtarget = dtarget.astype(bf16)
+            dstrength = jnp.sum(dtarget * fresh, axis=1, keepdims=True)
+            dlog = -(strength * growth) * jnp.sum(dtarget * ks, axis=1, keepdims=True)
+            dv = strength * dtarget
+            both = jnp.concatenate([low_dtarget, do], axis=0)
+            outer = mm(both, pseudo, NT)
+            dcoupling = jnp.where(strict, -outer[:CHUNK] * ratio, 0.0)
+            by_strength = dcoupling * kk
+            dstrength = dstrength + jnp.sum(by_strength, axis=1, keepdims=True)
+            exponent = strength * by_strength
+            dqk_f = jnp.where(lower, outer[CHUNK:] * ratio, 0.0)
+            exponent = exponent + dqk_f * qk
+            pair = jnp.concatenate([(dcoupling * strength).astype(bf16), dqk_f.astype(bf16)], axis=0)
+            back = mm(both, s0, NT)
+            wide = mm(pair, k)
+            dq = growth * back[CHUNK:] + wide[CHUNK:]
+            dkept = mm(pseudo, low_grad_state, NT)
+            dk = (
+                wide[:CHUNK]
+                - (strength * growth) * back[:CHUNK]
+                + mm(pair, kq, TN)
+                + remain * dkept
+            )
+            dlog = dlog + growth * jnp.sum(do.astype(f32) * qs, axis=1, keepdims=True)
+            from_kept = remain * jnp.sum(kf * dkept, axis=1, keepdims=True)
+            dlog = dlog - from_kept + jnp.sum(exponent, axis=1, keepdims=True)
+            dlog_row = to_row(dlog, eye) - jnp.sum(exponent, axis=0, keepdims=True)
+            tail = jnp.sum(from_kept, axis=0, keepdims=True) + whole * jnp.sum(
+                jnp.sum(grad_state * s0.astype(f32), axis=1, keepdims=True), axis=0, keepdims=True
+            )
+            dgate = jnp.sum(jnp.where(upper, dlog_row, 0.0), axis=1, keepdims=True) + tail
+            slope = sigmoid(logit)
+            drate0 = -rate * slope * dgate
+            drate1 = dstrength * strength * (1.0 - strength)
+            rate_total = rate_total + jnp.sum(dgate * log_gate, axis=0, keepdims=True)
+            bias_total = bias_total + jnp.sum(drate0, axis=0, keepdims=True)
+            here = pl.ds(pl.multiple_of(first + c * CHUNK, CHUNK), CHUNK)
+            others = jnp.where(head == 0, 0.0, dp_ref[here, in_cols:].astype(f32))
+            dp_ref[here, in_cols:] = jnp.where(
+                lanes == 2 * head, drate0, jnp.where(lanes == 2 * head + 1, drate1, others)
+            ).astype(bf16)
+            convolved = convolve(x_scr, conv, c * CHUNK)
+            sig = sigmoid(convolved)
+            active = convolved * sig
+            slope_conv = sig * (1.0 + convolved * (1.0 - sig))
+
+            def unit_grad(rows_in, grad):
+                inv_norm = lax.rsqrt(jnp.sum(rows_in * rows_in, axis=1, keepdims=True) + epsilon)
+                y = rows_in * inv_norm
+                return inv_norm * (grad - y * jnp.sum(y * grad, axis=1, keepdims=True))
+
+            dq = dq.astype(bf16).astype(f32) * DK ** (-0.5)
+            dk = dk.astype(bf16).astype(f32)
+            dv = dv.astype(bf16).astype(f32)
+            dconv = (
+                jnp.concatenate(
+                    [unit_grad(active[:, :DK], dq), unit_grad(active[:, DK : 2 * DK], dk), dv],
+                    axis=1,
+                )
+                * slope_conv
+            )
+            g_scr[pl.ds(8 + c * CHUNK, CHUNK), :] = dconv
+            for j in range(CONV):
+                shifted_in = x_scr[pl.ds(c * CHUNK + HALO - CONV + 1 + j, CHUNK), :]
+                conv_total[j] = conv_total[j] + jnp.sum(dconv * shifted_in, axis=0, keepdims=True)
+        for j in range(CONV):
+            dconv_ref[0, pl.ds(j, 1), :] = conv_total[j]
+        row8 = lax.broadcasted_iota(jnp.int32, (8, PAD), 0)
+        ddecay_ref[0] = jnp.where(row8 == 0, rate_total, jnp.where(row8 == 1, bias_total, 0.0))
+
+        def conv_back(at, size):
+            grad = g_scr[pl.ds(at + CONV - 1, size), :] * conv[0:1]
+            for j in range(1, CONV):
+                grad = grad + g_scr[pl.ds(at + CONV - 1 - j, size), :] * conv[j : j + 1]
+            return grad
+
+        halo_send[chain] = conv_back(0, 8)
+
+        @pl.when(place > 0)
+        def _():
+            returned(chain).start()
+
+        conv_at = pl.ds(pl.multiple_of(head * QKV, QKV), QKV)
+        for c in range(count):
+            grad = conv_back(8 + c * CHUNK, CHUNK)
+            positions = place * length + c * CHUNK + lax.broadcasted_iota(
+                jnp.int32, (CHUNK, 1), 0
+            )
+            live = (positions >= start).astype(f32)
+            if c == count - 1:
+                tail_scr[chain] = grad[CHUNK - HALO :]
+            dp_ref[pl.ds(pl.multiple_of(first + c * CHUNK, CHUNK), CHUNK), conv_at] = (
+                grad * live
+            ).astype(bf16)
+
+    relayed = step - lag
+
+    @pl.when((relayed >= 0) & (relayed < chains))
+    def _():
+        chain = jnp.clip(relayed, 0, chains - 1)
+
+        @pl.when(place < places - 1)
+        def _():
+            passed(chain).wait_recv()
+
+        @pl.when(place > 0)
+        def _():
+            earlier = mm(trans_ref[chain], recv[chain], TN) + own_scr[chain]
+            send[chain] = earlier.astype(bf16)
+            passed(chain).start()
+
+    @pl.when(step == chains)
+    def _():
+        own_copy().wait()
+        for k in range(1, peers):
+            ffn_copy(k).wait_recv()
+
+        def out_rows(t, carry):
+            rows = pl.ds(pl.multiple_of(t * SUB, SUB), SUB)
+            value = hidden_ref[rows, :]
+            for k in range(peers):
+                value = value + parts[k, rows, :].astype(f32)
+            part(whole_out, me * own_rows + t * SUB, SUB)[...] = value.astype(bf16)
+            return carry
+
+        lax.fori_loop(0, subs, out_rows, 0)
+        for k in range(peers - 1, 0, -1):
+            out_copy(k, me).start()
+        out_store(0).start()
+
+    @pl.when(step == 2 * chains - 1)
+    def _():
+        for chain in range(chains):
+            @pl.when(place < places - 1)
+            def _():
+                returned(chain).wait_recv()
+
+            head, seq = chain // seqs, chain % seqs
+            positions = (place + 1) * length - HALO + lax.broadcasted_iota(
+                jnp.int32, (HALO, 1), 0
+            )
+            live = (positions >= start_ref[seq]).astype(f32)
+            grad = tail_scr[chain] + jnp.concatenate(
+                [jnp.zeros((HALO - 8, QKV), f32), halo_recv[chain]], axis=0
+            )
+            dp_ref[pl.ds((seq + 1) * length - HALO, HALO), pl.ds(head * QKV, QKV)] = (
+                grad * live
+            ).astype(bf16)
+
+            @pl.when(place > 0)
+            def _():
+                returned(chain).wait_send()
+                passed(chain).wait_send()
+
+        for k in range(1, peers):
+            out_copy(k, me ^ k).wait_recv()
+            out_store(k).start()
+        for k in range(peers):
+            out_store(k).wait()
+        for k in range(1, peers):
+            ffn_copy(k).wait_send()
+            out_copy(k, me).wait_send()
+
+
+def backward_rule(
+    starts, decay_par, dn, mixed, projected, gain, n, qe, tot, trans, qkv, inv, states, halo, conv_w,
+    hidden, ffn_part, seqs, heads,
+):
+    places, peers = lax.axis_size("seq"), lax.axis_size("head")
+    chains = seqs * heads
+    rows = projected.shape[0]
+    length = rows // seqs
+    count = length // CHUNK
+    width = hidden.shape[1]
+    own_rows = hidden.shape[0]
+    rates_at = heads * (QKV + DV) // PAD
+    og_at = heads * QKV // DV
+    row = lambda first: lambda i: (i % seqs, first + i // seqs)
+    whole = lambda *dims: pl.BlockSpec(dims, lambda j: (0,) * len(dims))
+    chain4 = lambda i: (i, 0, 0, 0)
+    chain3 = lambda i: (i, 0, 0)
+    shape = jax.ShapeDtypeStruct
+    per_chain = pltpu.SemaphoreType.DMA((chains,))
+    per_peer = pltpu.SemaphoreType.DMA((peers,))
+    return pl.pallas_call(
+        functools.partial(backward_kernel, seqs, places, peers),
+        grid=(2 * chains,),
+        in_specs=[
+            smem(),
+            smem(),
+            pl.BlockSpec((length, DV), early(chains, row(0))),
+            pl.BlockSpec((length, DV), early(chains, row(0))),
+            pl.BlockSpec((length, DV), early(chains, row(og_at))),
+            whole(1, DV),
+            whole(chains, count, DK, DK),
+            whole(chains, count, CHUNK, DK),
+            whole(chains, count, DK),
+            whole(chains, DK, DK),
+            pl.BlockSpec((length, QKV), late(chains, row(0))),
+            pl.BlockSpec((1, count, CHUNK, CHUNK), late(chains, chain4)),
+            pl.BlockSpec((1, count, DK, DV), late(chains, chain4)),
+            pl.BlockSpec((length, QKV), late(chains, row(0))),
+            pl.BlockSpec((1, HALO, QKV), late(chains, lambda i: (i % seqs, 0, i // seqs))),
+            pl.BlockSpec((length, PAD), late(chains, lambda i: (i % seqs, rates_at))),
+            pl.BlockSpec((CONV, QKV), late(chains, lambda i: (0, i // seqs))),
+            whole(own_rows, width),
+            anywhere(),
+        ],
+        out_specs=[
+            whole(rows, heads * (QKV + DV) + PAD),
+            pl.BlockSpec((1, CONV, QKV), late(chains, chain3)),
+            pl.BlockSpec((1, 8, PAD), late(chains, chain3)),
+            pl.BlockSpec((1, 8, DV), early(chains, chain3)),
+            anywhere(),
+        ],
+        out_shape=[
+            shape((rows, heads * (QKV + DV) + PAD), bf16),
+            shape((chains, CONV, QKV), f32),
+            shape((chains, 8, PAD), f32),
+            shape((chains, 8, DV), f32),
+            shape((rows, width), bf16),
+        ],
+        scratch_shapes=[
+            pltpu.VMEM((HALO + length, QKV), f32),
+            pltpu.VMEM((16 + length, QKV), f32),
+            pltpu.VMEM((chains, length, DV), bf16),
+            pltpu.VMEM((chains, DK, DV), f32),
+            pltpu.VMEM((chains, DK, DV), bf16),
+            pltpu.VMEM((chains, DK, DV), bf16),
+            pltpu.VMEM((chains, HALO, QKV), f32),
+            pltpu.VMEM((chains, 8, QKV), f32),
+            pltpu.VMEM((chains, 8, QKV), f32),
+            pltpu.VMEM((peers, own_rows, width), bf16),
+            pltpu.VMEM((rows, width), bf16),
+            per_chain, per_chain, per_chain, per_chain,
+            pltpu.SemaphoreType.DMA((1,)),
+            per_peer, per_peer, per_peer, per_peer, per_peer,
+        ],
+        compiler_params=pltpu.CompilerParams(
+            dimension_semantics=("arbitrary",), collective_id=4, has_side_effects=True,
+            vmem_limit_bytes=52 * 2**20,
+        ),
+        name="backward_rule",
+    )(
+        starts, decay_par, dn, mixed, projected, gain, n, qe, tot, trans, qkv, inv, states, projected,
+        halo, projected, conv_w, hidden, ffn_part,
+    )
+
+
+def smem():
+    return pl.BlockSpec(memory_space=pltpu.SMEM)
 
 
 def mixer_ffn_kernel(
@@ -733,14 +973,6 @@
             sub_gather(k, t, me, nm, ss2, rs2).wait_send()
             mid_copy(k, t).wait_send()
             sub_gather(k, t, me, dm, ss4, rs4).wait_send()
-
-
-def anywhere():
-    return pl.BlockSpec(memory_space=pl.ANY)
-
-
-def vmem():
-    return pl.BlockSpec(memory_space=pltpu.VMEM)
 
 
 def mixer_ffn(normed, out_full, ffn_full, x, ct, gain):
@@ -975,9 +1207,7 @@
     )
     o_gain_full = small_full[:, conv_end:].reshape(1, DV).astype(f32)
 
-    place = lax.axis_index("seq").astype(jnp.int32).reshape(1)
-    rule = Rule(seqs, length, heads, lax.axis_size("seq"))
-
+    place = lax.axis_index("seq")
     x = tokens.reshape(total, width)
     ct = cotangent.reshape(total, width)
     inputs = x.astype(f32)
@@ -989,46 +1219,23 @@
     )[None, :] >= starts[:, None]
     received = shifted((ends * end_live.astype(f32)[:, :, None]).astype(bf16), "seq", 1)
     halo = jnp.pad(received, ((0, 0), (HALO - CONV + 1, 0), (0, 0)))
-    qkv, inv, n, b, qe, o, tot, own_map = rule.chunks(
-        place, starts, decay_par, projected, halo, conv_full
-    )
-    maps = lax.all_gather(own_map, "seq")
-    states, mixed, normed = rule.states(place, maps, n, b, qe, o, tot, projected, o_gain_full)
-
+    qkv, inv, n, qe, tot, trans, states, mixed, normed = forward_rule(
+        starts, decay_par, projected, halo, conv_full, o_gain_full, seqs, heads
+    )
     late_grads, ffn_part, normed_grad, hidden, hidden_grad, ffn_gain_part = mixer_ffn(
         normed, out_full, ffn_full, x, ct, ffn_gain_f
     )
-    own_rows = total // lax.axis_size("head")
-    ffn_out = lax.psum_scatter(ffn_part, "head", scatter_dimension=0, tiled=True)
-    result = lax.all_gather(
-        (hidden + ffn_out.astype(f32)).astype(bf16), "head", axis=0, tiled=True
-    )
-    do, dog, onorm_grads, own = rule.norm_grads(
-        normed_grad, mixed, projected, o_gain_full, qe, n, tot
-    )
-    owns = lax.all_gather(own, "seq")
-    dci, dhalo, dconv, drate, ddecay = rule.rule_grads(
-        place, starts, decay_par, owns, maps, qkv, inv, n, qe, tot, states, do, projected, halo,
-        conv_full,
-    )
-    returned = shifted(dhalo[:, 8 - CONV + 1 :], "seq", -1)
-    positions = place * length + jnp.arange(length, dtype=jnp.int32)
-    live = (positions[None, :] >= starts[:, None]).astype(f32)
-    dci = (
-        dci.reshape(seqs, length, conv_cols)
-        + jnp.pad(returned, ((0, 0), (length - CONV + 1, 0), (0, 0)))
-    ) * live[:, :, None]
-    rate_grad = jnp.sum(drate.reshape(total, heads, PAD), axis=1)
-    projected_grad = jnp.concatenate(
-        [dci.reshape(total, conv_cols).astype(bf16), dog, rate_grad.astype(bf16)], axis=1
+    projected_grad, dconv, ddecay, onorm_grads, result = backward_rule(
+        starts, decay_par, normed_grad, mixed, projected, o_gain_full, n, qe, tot, trans, qkv, inv,
+        states, halo, conv_full, hidden, ffn_part, seqs, heads,
     )
     in_grad = matmul(normed_in, projected_grad, TN)
     input_grad, attn_gain_part = input_grads(
         projected_grad, in_full, x, hidden_grad, attn_gain_f
     )
-    onorm_grad = jnp.sum(onorm_grads[:, :, 0], axis=(0, 1))
-    decay_part = jnp.sum(ddecay[:, :, :2, 0], axis=0).T
-    conv_grad = jnp.sum(dconv, axis=0).transpose(1, 0, 2)
+    onorm_grad = jnp.sum(onorm_grads[:, 0], axis=0)
+    decay_part = jnp.sum(ddecay[:, :2, 0].reshape(heads, seqs, 2), axis=1).T
+    conv_grad = jnp.sum(dconv.reshape(heads, seqs, CONV, QKV), axis=1).transpose(1, 0, 2)
 
     def scatter(grad, dim=0):
         return lax.psum_scatter(

time: 574 us -> 453 us (0.79)
  waiting for transfers between devices: 182 us -> 55.6 us
  Pallas kernels: 224 us -> 242 us
  local copies, waits for them, and re-layouts: 37.8 us -> 28.7 us
  other arithmetic: 16.8 us -> 8.4 us
    all_gather x3 -> x0, waiting for transfers between devices: 62.9 us -> none  [the longest x1 35.5 us: per_device(): maps = lax.all_gather(own_map, 'seq')]
    reduce_scatter x1 -> x0, waiting for transfers between devices: 22.7 us -> none  [per_device(): lax.psum_scatter(ffn_part, 'head', scatter_dimension=0, tiled=True)]
    all_gather x1, waiting for transfers between devices: 53.4 us -> 32.1 us  [per_device(): ffn_full = lax.all_gather(packed_ffn, ALL, axis=0, tiled=True)]
    pallas_call x4 -> x2, Pallas kernels: 64 us -> 84 us  [the longest x1 55.6 us: backward_rule(): pl.pallas_call(functools.partial(backward_kernel, seqs, places, peers), g...]
    all_gather x1, waiting for transfers between devices: 13.7 us -> 0.01 us  [per_device(): lax.all_gather(w_out.reshape(value_cols, -1).T.astype(bf16), ALL, axis=0,...]
    unnamed x73 -> x47, local copies, waits for them, and re-layouts: 23.9 us -> 14.5 us
  transfers between devices with their start and end apart: 11 -> 6, of which waited for: 8 -> 3; matrix products, arithmetic and copies ran while one was open for 5% -> 5% of each run, Pallas kernels for 16% -> 17%
where the time goes in v2:
time: 453 us; the launch traced here: 452 us
  Pallas kernels  242 us (53%)
  blocking collectives  86.4 us (19%)
  waiting for transfers between devices  55.6 us (12%)
  local copies, waits for them, and re-layouts  28.7 us (6%)
  between operations  14.3 us (3%)
  matrix products  13.6 us (3%)
  other arithmetic  8.4 us (2%)
    pallas_call x1, Pallas kernels, mixer_ffn(): pl.pallas_call(functools.partial(mixer_ffn_kernel, peers), in_specs=[anyw...  110 us
    pallas_call x1, Pallas kernels, backward_rule(): pl.pallas_call(functools.partial(backward_kernel, seqs, places, peers), g...  55.6 us
    pallas_call x1, Pallas kernels, input_grads(): pl.pallas_call(functools.partial(input_grad_kernel, peers), in_specs=[any...  47.7 us
    psum x1, blocking collectives, per_device(): lax.psum(jnp.concatenate([attn_gain_part[0], ffn_gain_part[0], onorm_grad...  39.7 us
    all_gather x1, waiting for transfers between devices, per_device(): ffn_full = lax.all_gather(packed_ffn, ALL, axis=0, tiled=True)  32.1 us
    psum x1, blocking collectives, per_device(): lax.psum(jnp.concatenate([conv_grad.reshape(-1), decay_part.reshape(-1)])...  30.9 us
    pallas_call x1, Pallas kernels, forward_rule(): pl.pallas_call(functools.partial(forward_kernel, seqs, places), grid=(2 *...  28.3 us
    all_gather x1, waiting for transfers between devices, per_device(): in_full = lax.all_gather(packed_in, ALL, axis=0, tiled=True)  22 us
  transfers between devices with their start and end apart: 6, of which 3 were waited for; matrix products, arithmetic and copies ran while one was open for 5% of the time, Pallas kernels for 17%

profile of v2, /device:TPU:0, one launch (start us, length us, event | category | flops | bytes accessed | tf_op | source)
XLA Modules:
  0.0 451.7 jit_solution(9359997722288269325)
XLA Ops:
  7.2 1.4 convert.49
  11.9 1.2 convert.51
  14.1 1.1 copy.56
  15.4 15.8 %all-gather = bf16[8,1,800]{2,1,0:T(2,128)(2,1)S(1)} all-gather(bf16[1,1,800]{2,1,0:T(2,128)(2,1)S(1)} %maximum_bitcast_fusion), channel_id=1, replica_groups=mesh['seq'=4,'batch'=2,'head'=4] {'seq','batch'}, dimensions={0}, use_global_device_ids=true | all-gather | bytes 14400 | tf_op jit(solution)/shard_map/all_gather | solution.py:1193
  32.4 22.0 %all-gather.5.cloned.1.call-done.win_hbm = bf16[1024,1664]{1,0:T(8,128)(2,1)} async-done(((bf16[128,1664]{1,0:T(8,128)(2,1)}), bf16[1024,1664]{1,0:T(8,128)(2,1)}) %all-gather.5.cloned.1.call-update) | async-done | bytes 3407888 | tf_op jit(solution)/shard_map/all_gather | solution.py:1192
  54.4 6.0 %fusion.2.main_ref.rate_ref.og_ref = f32[1024,1664]{1,0:T(8,128)S(1)} fusion(bf16[1024,1664]{1,0:T(8,128)(2,1)} %all-gather.5.cloned.1.call-done.win_hbm, bf16[1024,1024]{1,0:T(8,128)(2,1)S(1)} %bitcast.62, f32[1024]{0:T(1024)S(1)} %get-tuple-element.105, f32[1024]{0:T(1024)S(1)} %bitcast.90), kind=kOutput, calls=%fused_computation.7 | convolution fusion | flops 3493855232 | bytes 12328960 | tf_op jit(solution)/shard_map/dot_general | solution.py:1156
  60.4 2.8 copy-done.12
  63.3 2.5 collective-permute-start
  67.1 28.3 %forward_rule.1 = (bf16[1024,1024]{1,0:T(8,128)(2,1)S(1)}, bf16[4,4,128,128]{3,2,1,0:T(8,128)(2,1)S(1)}, bf16[4,4,128,128]{3,2,1,0:T(8,128)(2,1)S(1)}, bf16[4,4,...) custom-call(s32[2]{0:T(128)S(1)} %copy-done.10, ...), custom_call_target="tpu_custom_call" | custom-call | tf_op jit(solution)/shard_map/forward_rule/pallas_call | solution.py:311
  95.4 1.3 copy-done.2
  99.5 32.1 %all-gather.9.cloned.1.call-done.ffn_hbm = bf16[1024,2304]{1,0:T(8,128)(2,1)} async-done(((bf16[128,2304]{1,0:T(8,128)(2,1)}), bf16[1024,2304]{1,0:T(8,128)(2,1)}) %all-gather.9.cloned.1.call-update) | async-done | bytes 4718608 | tf_op jit(solution)/shard_map/all_gather | solution.py:1197
  131.6 110.3 %mixer_ffn.1 = (bf16[1024,2816]{1,0:T(8,128)(2,1)}, bf16[1024,1024]{1,0:T(8,128)(2,1)}, f32[1024,512]{1,0:T(8,128)}, f32[256,1024]{1,0:T(8,128)}, f32[256,1024]{1,0:T(8,128)}, /*index=5*/f32[8,1024]{1,0:T(8,128)}) custom-call(bf16[1024,512]{1,0:T(8,128)(2,1)} %copy-done.7, bf16[1024,512]{1,0:T(8,128)(2,1)} %all-gather.7.cloned.1.call-done.wout_hbm, ...), custom_call_target="tpu_custom_call" | custom-call | tf_op jit(solution)/shard_map/mixer_ffn/pallas_call | solution.py:986
  242.0 55.6 %backward_rule.1 = (bf16[1024,1664]{1,0:T(8,128)(2,1)}, f32[4,4,512]{2,1,0:T(4,128)S(1)}, f32[4,8,128]{2,1,0:T(8,128)S(1)}, f32[4,8,256]{2,1,0:T(8,128)S(1)}, bf16[1024,1024]{1,0:T(8,128)(2,1)}) custom-call(s32[2]{0:T(128)S(1)} %copy-done.10, f32[2,2]{1,0:T(2,128)S(1)} %copy-done.11, f32[1024,512]{1,0:T(8,128)} %get-tuple-element.35.dn_ref, ...), custom_call_target="tpu_custom_call" | custom-call | tf_op jit(solution)/shard_map/backward_rule/pallas_call | solution.py:715
  297.6 7.6 %convolution_convert_fusion = bf16[1024,1664]{1,0:T(8,128)(2,1)} fusion(bf16[1024,1664]{1,0:T(8,128)(2,1)} %get-tuple-element.47.dp_hbm, bf16[1024,1024]{1,0:T(8,128)(2,1)S(1)} %bitcast.63, f32[1024]{0:T(1024)S(1)} %get-tuple-element.105, f32[1024]{0:T(1024)S(1)} %bitcast.91), kind=kOutput, calls=%fused_computation.2 | convolution fusion | flops 3495559168 | bytes 8921088 | tf_op jit(solution)/shard_map/dot_general | solution.py:1156
  306.3 30.9 %psum.15 = f32[4100]{0:T(1024)S(1)} all-reduce(f32[4100]{0:T(1024)S(1)} %pad_maximum_fusion.1), channel_id=1, replica_groups=mesh['seq'=4,'batch'=2,'head'=4] {'seq','batch'}, use_global_device_ids=true, to_apply=%region_6.7 | all-reduce | flops 4100 | bytes 32800 | tf_op jit(solution)/shard_map/psum | solution.py:1254
  337.9 47.7 %input_grads.1 = (bf16[1024,1024]{1,0:T(8,128)(2,1)S(1)}, f32[8,1024]{1,0:T(8,128)S(1)}) custom-call(bf16[1024,1664]{1,0:T(8,128)(2,1)} %get-tuple-element.47.dp_hbm, bf16[1024,1664]{1,0:T(8,128)(2,1)} %all-gather.5.cloned.1.call-done.win_hbm, bf16[1024,1024]{1,0:T(8,128)(2,1)S(1)} %bitcast.64, f32[256,1024]{1,0:T(8,128)S(1)} %copy-done.5, ...), custom_call_target="tpu_custom_call" | custom-call | tf_op jit(solution)/shard_map/input_grads/pallas_call | solution.py:1119
  385.6 1.3 copy-done.3
  387.7 39.7 %psum.14 = f32[2304]{0:T(1024)S(1)} all-reduce(f32[2304]{0:T(1024)S(1)} %pad_maximum_fusion.2), channel_id=1, replica_groups=mesh['seq'=4,'batch'=2,'head'=4] {'head','seq','batch'}, use_global_device_ids=true, to_apply=%region_2.3 | all-reduce | flops 2304 | bytes 18432 | tf_op jit(solution)/shard_map/psum | solution.py:1247
  433.2 1.2 pad_maximum_fusion
  434.5 1.3 convert_element_type.101
  437.6 1.1 copy.65
  438.8 2.0 slice.107
  440.8 3.1 copy.79
  443.9 1.3 copy.80
  (112 shorter events, 19.7 us)
Async XLA Ops:
  7.2 3.8 copy-start.14
  7.2 47.2 %all-gather.5.cloned.1.call-start = ((), (), s32[]{:S(2)}) async-start(), calls=%async_computation.2 | async-start | bytes 3833856 | tf_op jit(solution)/shard_map/all_gather | solution.py:1192
  9.0 6.2 %copy-start.15 = (f32[4,2,64]{2,1,0:T(2,128)S(1)}, f32[4,2,64]{2,1,0:T(2,128)}, u32[]{:S(2)}) copy-start(f32[4,2,64]{2,1,0:T(2,128)} %param.18) | copy-start | bytes 6148
  9.0 6.3 %copy-start.18 = (f32[32]{0:T(128)S(1)}, f32[32]{0:T(128)}, u32[]{:S(2)}) copy-start(f32[32]{0:T(128)} %param.20) | copy-start | bytes 388
  9.1 6.3 %copy-start.16 = (f32[128]{0:T(128)S(1)}, f32[128]{0:T(128)}, u32[]{:S(2)}) copy-start(f32[128]{0:T(128)} %param.22) | copy-start | bytes 1540
  9.1 6.3 %copy-start.17 = (f32[128]{0:T(128)S(1)}, f32[128]{0:T(128)}, u32[]{:S(2)}) copy-start(f32[128]{0:T(128)} %param.15) | copy-start | bytes 1540
  9.1 22.1 %copy-start = (bf16[2,512,1024]{2,1,0:T(8,128)(2,1)S(1)}, bf16[2,512,1024]{2,1,0:T(8,128)(2,1)}, u32[]{:S(2)}) copy-start(bf16[2,512,1024]{2,1,0:T(8,128)(2,1)} %param.13) | copy-start | bytes 6291460
  11.0 88.6 %all-gather.7.cloned.1.call-start = ((), (), s32[]{:S(2)}) async-start(), calls=%async_computation.3 | async-start | bytes 1179648 | tf_op jit(solution)/shard_map/all_gather | solution.py:1194
  11.8 19.9 %copy-start.10 = (s32[2]{0:T(128)S(1)}, s32[2]{0:T(128)}, u32[]{:S(2)}) copy-start(s32[2]{0:T(128)} %start_ref.3) | copy-start | bytes 28
  11.8 119.8 %all-gather.9.cloned.1.call-start = ((), (), s32[]{:S(2)}) async-start(), calls=%async_computation.4 | async-start | bytes 5308416 | tf_op jit(solution)/shard_map/all_gather | solution.py:1197
  15.2 414.1 %reduce-scatter.3.cloned.1.call-start = ((), (), s32[]{:S(2)}) async-start(), calls=%async_computation.5 | async-start | bytes 3833856 | tf_op jit(solution)/shard_map/reduce_scatter | solution.py:1241
  54.4 12.7 %copy-start.11 = (f32[2,2]{1,0:T(2,128)S(1)}, f32[2,2]{1,0:T(2,128)}, u32[]{:S(2)}) copy-start(f32[2,2]{1,0:T(2,128)} %decay_ref.3) | copy-start | bytes 52
  60.4 2.8 copy-start.12
  63.3 3.8 collective-permute-start
  95.4 1.3 copy-start.2
  96.8 1.0 copy-start.6
  97.8 1.0 copy-start.7
  131.6 110.3 %copy-start.9 = (bf16[4,4,128,128]{3,2,1,0:T(8,128)(2,1)S(1)}, bf16[4,4,128,128]{3,2,1,0:T(8,128)(2,1)}, u32[]{:S(2)}) copy-start(bf16[4,4,128,128]{3,2,1,0:T(8,128)(2,1)} %copy-done.8) | copy-start | bytes 1572868
  242.0 55.7 %copy-start.1 = (bf16[2,512,1024]{2,1,0:T(8,128)(2,1)S(1)}, bf16[2,512,1024]{2,1,0:T(8,128)(2,1)}, u32[]{:S(2)}) copy-start(bf16[2,512,1024]{2,1,0:T(8,128)(2,1)} %param.13) | copy-start | bytes 6291460
  305.3 32.6 %copy-start.5 = (f32[256,1024]{1,0:T(8,128)S(1)}, f32[256,1024]{1,0:T(8,128)}, u32[]{:S(2)}) copy-start(f32[256,1024]{1,0:T(8,128)} %get-tuple-element.48.hgrad_ref) | copy-start | bytes 3145732
  305.3 129.2 %reduce-scatter.5.cloned.1.call-start = ((), (), s32[]{:S(2)}) async-start(), calls=%async_computation.6 | async-start | bytes 6488064 | tf_op jit(solution)/shard_map/reduce_scatter | solution.py:1241
  385.6 1.3 copy-start.3
  434.5 3.1 copy-start.13
  437.6 6.3 %copy-start.4 = (bf16[1024,1024]{1,0:T(8,128)(2,1)S(1)}, bf16[1024,1024]{1,0:T(8,128)(2,1)}, u32[]{:S(2)}) copy-start(bf16[1024,1024]{1,0:T(8,128)(2,1)} %copy-done.3) | copy-start | bytes 6291460
  (1 other events, 0.8 us)
Sparse Core Ops, SparseCore 0:
  11.1 43.2 all-gather.4
  56.5 21.1 all-gather.6
  80.0 51.5 all-gather.8
  305.4 43.9 reduce-scatter.2
  351.6 64.2 reduce-scatter.4

commit v3 on v2

--- a/solution.py
+++ b/solution.py
@@ -104,7 +104,9 @@
     length = main_ref.shape[0]
     positions = first + lax.broadcasted_iota(jnp.int32, (length, 1), 0)
     live = (positions >= start).astype(f32)
-    x_scr[pl.ds(0, HALO), :] = halo_ref[0].astype(f32)
+    before = first - HALO + lax.broadcasted_iota(jnp.int32, (HALO, 1), 0)
+    lived = (before >= start).astype(f32)
+    x_scr[pl.ds(0, HALO), :] = (halo_ref[0] * lived).astype(bf16).astype(f32)
     x_scr[pl.ds(HALO, length), :] = (main_ref[...] * live).astype(bf16).astype(f32)
 
 
@@ -141,6 +143,43 @@
     return ref.at[pl.ds(pl.multiple_of(start, size), size)]
 
 
+class Spread:
+    def __init__(self, buffer, size, me, send_sem, recv_sem, piece=None):
+        self.buffer, self.size, self.me = buffer, size, me
+        self.piece = size if piece is None else piece
+        self.send_sem, self.recv_sem = send_sem, recv_sem
+
+    def region(self, owner, t, half):
+        rows = pl.ds(pl.multiple_of(owner * self.size + t * self.piece, self.piece), self.piece)
+        middle = self.buffer.shape[1] // 2
+        if half is None:
+            return self.buffer.at[rows]
+        return self.buffer.at[rows, pl.ds(half * middle, middle)]
+
+    def copy(self, kind, t, owner):
+        at = self.region(owner, t, None if kind < 2 else kind - 2)
+        to = self.me ^ (1 if kind in (0, 3) else 2)
+        return head_copy(at, at, self.send_sem.at[kind, t], self.recv_sem.at[kind, t], to)
+
+    def start(self, t):
+        self.copy(0, t, self.me).start()
+        self.copy(1, t, self.me).start()
+
+    def forward(self, t):
+        self.copy(0, t, self.me ^ 1).wait_recv()
+        self.copy(2, t, self.me ^ 1).start()
+        self.copy(1, t, self.me ^ 2).wait_recv()
+        self.copy(3, t, self.me ^ 2).start()
+
+    def finish(self, t):
+        self.copy(2, t, self.me ^ 3).wait_recv()
+        self.copy(3, t, self.me ^ 3).wait_recv()
+
+    def drain(self, t):
+        for kind, owner in enumerate((0, 0, 1, 2)):
+            self.copy(kind, t, self.me ^ owner).wait_send()
+
+
 def anywhere():
     return pl.BlockSpec(memory_space=pl.ANY)
 
@@ -157,8 +196,8 @@
 
 
 def forward_kernel(
-    seqs, places, start_ref, decay_ref, main_ref, halo_ref, rate_ref, conv_ref, og_ref, gain_ref,
-    qkv_ref, inv_ref, n_ref, qe_ref, tot_ref, trans_ref, s_ref, mixed_ref, normed_ref,
+    seqs, places, start_ref, decay_ref, main_ref, halo_ref, rate_ref, conv_ref,
+    qkv_ref, inv_ref, n_ref, qe_ref, tot_ref, trans_ref, s_ref, mixed_ref,
     x_scr, b_scr, o_scr, carried_scr, send, recv, send_sem, recv_sem,
 ):
     step = pl.program_id(0)
@@ -254,13 +293,7 @@
             whole = tot_ref[chain, pl.ds(c, 1), 0:1]
             state = whole * state - both[:DK] + b_scr[chain, c]
             at = pl.ds(c * CHUNK, CHUNK)
-            mixed = o_scr[chain, at, :] + both[DK:]
-            mixed_ref[at, :] = mixed
-            og = og_ref[at, :]
-            inverse = lax.rsqrt(jnp.mean(mixed * mixed, axis=1, keepdims=True) + epsilon)
-            normed_ref[at, :] = (
-                mixed * inverse * gain_ref[0:1] * (og * sigmoid(og))
-            ).astype(bf16)
+            mixed_ref[at, :] = o_scr[chain, at, :] + both[DK:]
 
     def passed(chain):
         return along(
@@ -298,13 +331,12 @@
     return lambda j: make(jnp.maximum(j - chains, 0))
 
 
-def forward_rule(starts, decay_par, projected, halo, conv_w, gain, seqs, heads):
+def forward_rule(starts, decay_par, projected, halo, conv_w, seqs, heads):
     places = lax.axis_size("seq")
     chains = seqs * heads
     length = projected.shape[0] // seqs
     count = length // CHUNK
-    rates_at = heads * (QKV + DV) // PAD
-    og_at = heads * QKV // DV
+    rates_at = heads * QKV // PAD
     row = lambda first: lambda i: (i % seqs, first + i // seqs)
     whole = lambda *dims: pl.BlockSpec(dims, lambda j: (0,) * len(dims))
     shape = jax.ShapeDtypeStruct
@@ -318,8 +350,6 @@
             pl.BlockSpec((1, HALO, QKV), early(chains, lambda i: (i % seqs, 0, i // seqs))),
             pl.BlockSpec((length, PAD), early(chains, lambda i: (i % seqs, rates_at))),
             pl.BlockSpec((CONV, QKV), early(chains, lambda i: (0, i // seqs))),
-            pl.BlockSpec((length, DV), late(chains, row(og_at))),
-            whole(1, DV),
         ],
         out_specs=[
             pl.BlockSpec((length, QKV), early(chains, row(0))),
@@ -329,7 +359,6 @@
             whole(chains, count, DK),
             whole(chains, DK, DK),
             pl.BlockSpec((1, count, DK, DV), late(chains, lambda i: (i, 0, 0, 0))),
-            pl.BlockSpec((length, DV), late(chains, row(0))),
             pl.BlockSpec((length, DV), late(chains, row(0))),
         ],
         out_shape=[
@@ -341,7 +370,6 @@
             shape((chains, DK, DK), bf16),
             shape((chains, count, DK, DV), bf16),
             shape((seqs * length, heads * DV), f32),
-            shape((seqs * length, heads * DV), bf16),
         ],
         scratch_shapes=[
             pltpu.VMEM((HALO + length, QKV), f32),
@@ -358,7 +386,7 @@
             vmem_limit_bytes=48 * 2**20,
         ),
         name="forward_rule",
-    )(starts, decay_par, projected, halo, projected, conv_w, projected, gain)
+    )(starts, decay_par, projected, halo, projected, conv_w)
 
 
 def backward_kernel(
@@ -368,7 +396,7 @@
     dp_ref, dconv_ref, ddecay_ref, gg_ref, out_hbm,
     x_scr, g_scr, do_scr, own_scr, send, recv, tail_scr, halo_send, halo_recv,
     parts, whole_out, send_sem, recv_sem, halo_send_sem, halo_recv_sem, own_sem, out_sem,
-    ss1, rs1, ss2, rs2,
+    ss1, rs1, gather_send, gather_recv,
 ):
     step = pl.program_id(0)
     chains = n_ref.shape[0]
@@ -394,9 +422,7 @@
             part(ffnp_hbm, me * own_rows, own_rows), parts.at[0], own_sem.at[0]
         )
 
-    def out_copy(k, owner):
-        at = part(whole_out, owner * own_rows, own_rows)
-        return head_copy(at, at, ss2.at[k], rs2.at[k], me ^ k)
+    ring = Spread(whole_out, own_rows, me, gather_send, gather_recv)
 
     def out_store(k):
         owner = me ^ k
@@ -654,9 +680,12 @@
             return carry
 
         lax.fori_loop(0, subs, out_rows, 0)
-        for k in range(peers - 1, 0, -1):
-            out_copy(k, me).start()
+        ring.start(0)
         out_store(0).start()
+
+    @pl.when(step == chains + 2)
+    def _():
+        ring.forward(0)
 
     @pl.when(step == 2 * chains - 1)
     def _():
@@ -682,18 +711,18 @@
                 returned(chain).wait_send()
                 passed(chain).wait_send()
 
+        ring.finish(0)
         for k in range(1, peers):
-            out_copy(k, me ^ k).wait_recv()
             out_store(k).start()
         for k in range(peers):
             out_store(k).wait()
         for k in range(1, peers):
             ffn_copy(k).wait_send()
-            out_copy(k, me).wait_send()
+        ring.drain(0)
 
 
 def backward_rule(
-    starts, decay_par, dn, mixed, projected, gain, n, qe, tot, trans, qkv, inv, states, halo, conv_w,
+    starts, decay_par, dn, mixed, og, projected, gain, n, qe, tot, trans, qkv, inv, states, halo, conv_w,
     hidden, ffn_part, seqs, heads,
 ):
     places, peers = lax.axis_size("seq"), lax.axis_size("head")
@@ -703,8 +732,7 @@
     count = length // CHUNK
     width = hidden.shape[1]
     own_rows = hidden.shape[0]
-    rates_at = heads * (QKV + DV) // PAD
-    og_at = heads * QKV // DV
+    rates_at = heads * QKV // PAD
     row = lambda first: lambda i: (i % seqs, first + i // seqs)
     whole = lambda *dims: pl.BlockSpec(dims, lambda j: (0,) * len(dims))
     chain4 = lambda i: (i, 0, 0, 0)
@@ -720,7 +748,7 @@
             smem(),
             pl.BlockSpec((length, DV), early(chains, row(0))),
             pl.BlockSpec((length, DV), early(chains, row(0))),
-            pl.BlockSpec((length, DV), early(chains, row(og_at))),
+            pl.BlockSpec((length, DV), early(chains, row(0))),
             whole(1, DV),
             whole(chains, count, DK, DK),
             whole(chains, count, CHUNK, DK),
@@ -764,7 +792,9 @@
             pltpu.VMEM((rows, width), bf16),
             per_chain, per_chain, per_chain, per_chain,
             pltpu.SemaphoreType.DMA((1,)),
-            per_peer, per_peer, per_peer, per_peer, per_peer,
+            per_peer, per_peer, per_peer,
+            pltpu.SemaphoreType.DMA((4, 1)),
+            pltpu.SemaphoreType.DMA((4, 1)),
         ],
         compiler_params=pltpu.CompilerParams(
             dimension_semantics=("arbitrary",), collective_id=4, has_side_effects=True,
@@ -772,7 +802,7 @@
         ),
         name="backward_rule",
     )(
-        starts, decay_par, dn, mixed, projected, gain, n, qe, tot, trans, qkv, inv, states, projected,
+        starts, decay_par, dn, mixed, og, gain, n, qe, tot, trans, qkv, inv, states, projected,
         halo, projected, conv_w, hidden, ffn_part,
     )
 
@@ -781,89 +811,182 @@
     return pl.BlockSpec(memory_space=pltpu.SMEM)
 
 
-def mixer_ffn_kernel(
-    peers, normed_hbm, wout_hbm, ffn_hbm, x_hbm, ct_hbm, gain_ref,
-    grads_hbm, ffnp_hbm, ng_hbm, hidden_ref, hgrad_ref, gpart_ref,
-    normed_v, wout_v, ffn_v, x_v, ct_v, send1, recv1, nm, act, dgu, send2, recv2, dm, ffnp_v,
-    grads_v, ng_v, in_sem, out_sem, ss1, rs1, ss2, rs2, ss3, rs3, ss4, rs4,
+def rows_of(t):
+    return pl.ds(pl.multiple_of(t * SUB, SUB), SUB)
+
+
+class Summed:
+    def __init__(self, send, recv, me, send_sem, recv_sem):
+        self.send, self.recv, self.me = send, recv, me
+        self.send_sem, self.recv_sem = send_sem, recv_sem
+
+    def copy(self, k, t):
+        return head_copy(
+            self.send.at[k, rows_of(t)], self.recv.at[k, rows_of(t)], self.send_sem.at[k, t],
+            self.recv_sem.at[k, t], self.me ^ k,
+        )
+
+    def collect(self, t, peers):
+        total = self.send[0, rows_of(t), :].astype(f32)
+        for k in range(1, peers):
+            self.copy(k, t).wait_recv()
+            total = total + self.recv[k, rows_of(t), :].astype(f32)
+        return total
+
+
+def block_store(i, size, source, target, sem):
+    return pltpu.make_async_copy(
+        part(source, i * size, size), part(target, i * size, size), sem.at[i]
+    )
+
+
+def mixer_kernel(
+    peers, nin_hbm, mixed_hbm, weights_hbm, x_hbm, gain_ref, o_gain_ref,
+    og_hbm, normed_hbm, nm_hbm, hidden_ref,
+    nin, mixed, weights, x_v, og_v, normed_v, send1, recv1, nm, in_sem, out_sem,
+    ss1, rs1, gather_send, gather_recv,
 ):
     me = lax.axis_index("head")
-    total, width = ct_hbm.shape
+    total, width = nm.shape
+    values = mixed.shape[1]
+    own_rows = total // peers
+    subs = own_rows // SUB
+    loads = [
+        pltpu.make_async_copy(weights_hbm, weights, in_sem.at[0]),
+        pltpu.make_async_copy(nin_hbm, nin, in_sem.at[1]),
+        pltpu.make_async_copy(mixed_hbm, mixed, in_sem.at[2]),
+        pltpu.make_async_copy(part(x_hbm, me * own_rows, own_rows), x_v, in_sem.at[3]),
+    ]
+    for load in loads:
+        load.start()
+    greet_heads(me, peers)
+    for load in loads[:3]:
+        load.wait()
+    sums = Summed(send1, recv1, me, ss1, rs1)
+
+    def project(i, carry):
+        k = peers - 1 - i
+        owner = me ^ k
+        rows = pl.ds(pl.multiple_of(owner * own_rows, own_rows), own_rows)
+        og = mm(nin[rows, :], weights[:, 0:values])
+        og_v[rows, :] = og
+        gated = og * sigmoid(og)
+        for first in range(0, values, DV):
+            at = pl.ds(first, DV)
+            own = mixed[rows, at]
+            inverse = lax.rsqrt(jnp.mean(own * own, axis=1, keepdims=True) + epsilon)
+            normed_v[rows, at] = (
+                own * inverse * o_gain_ref[0:1] * gated[:, first : first + DV]
+            ).astype(bf16)
+        send1[k] = mm(normed_v[rows, :], weights[:, values:], NT).astype(bf16)
+
+        @pl.when(k > 0)
+        def _():
+            for t in range(subs):
+                sums.copy(k, t).start()
+
+        block_store(owner, own_rows, og_v, og_hbm, out_sem.at[0]).start()
+        block_store(owner, own_rows, normed_v, normed_hbm, out_sem.at[1]).start()
+        return carry
+
+    lax.fori_loop(0, peers, project, 0)
+    loads[3].wait()
+    gain = gain_ref[...]
+    ring = Spread(nm, own_rows, me, gather_send, gather_recv, SUB)
+    for t in range(subs):
+        rows = rows_of(t)
+        hidden = x_v[rows, :].astype(f32) + sums.collect(t, peers)
+        hidden_ref[rows, :] = hidden
+        inverse = lax.rsqrt(jnp.mean(hidden * hidden, axis=1, keepdims=True) + epsilon)
+        part(nm, me * own_rows + t * SUB, SUB)[...] = (hidden * inverse * gain).astype(bf16)
+        ring.start(t)
+    for t in range(subs):
+        ring.forward(t)
+    for k in range(peers):
+        if k == peers - 1:
+            for t in range(subs):
+                ring.finish(t)
+        block_store(me ^ k, own_rows, nm, nm_hbm, out_sem.at[2]).start()
+    for i in range(peers):
+        block_store(i, own_rows, og_v, og_hbm, out_sem.at[0]).wait()
+        block_store(i, own_rows, normed_v, normed_hbm, out_sem.at[1]).wait()
+        block_store(i, own_rows, nm, nm_hbm, out_sem.at[2]).wait()
+    for t in range(subs):
+        for k in range(1, peers):
+            sums.copy(k, t).wait_send()
+        ring.drain(t)
+
+
+def mixer(nin, mixed, weights, x, gain, o_gain):
+    peers = lax.axis_size("head")
+    total, width = x.shape
+    values = mixed.shape[1]
+    own_rows = total // peers
+    subs = own_rows // SUB
+    shape = jax.ShapeDtypeStruct
+    sems = pltpu.SemaphoreType.DMA((peers, subs))
+    return pl.pallas_call(
+        functools.partial(mixer_kernel, peers),
+        in_specs=[anywhere()] * 4 + [vmem()] * 2,
+        out_specs=[anywhere()] * 3 + [vmem()],
+        out_shape=[
+            shape((total, values), f32),
+            shape((total, values), bf16),
+            shape((total, width), bf16),
+            shape((own_rows, width), f32),
+        ],
+        scratch_shapes=[
+            pltpu.VMEM((total, width), bf16),
+            pltpu.VMEM((total, values), f32),
+            pltpu.VMEM((width, 2 * values), bf16),
+            pltpu.VMEM((own_rows, width), bf16),
+            pltpu.VMEM((total, values), f32),
+            pltpu.VMEM((total, values), bf16),
+            pltpu.VMEM((peers, own_rows, width), bf16),
+            pltpu.VMEM((peers, own_rows, width), bf16),
+            pltpu.VMEM((total, width), bf16),
+            pltpu.SemaphoreType.DMA((4,)),
+            pltpu.SemaphoreType.DMA((3, peers)),
+        ]
+        + [sems] * 4,
+        compiler_params=pltpu.CompilerParams(
+            collective_id=1, has_side_effects=True, vmem_limit_bytes=48 * 2**20
+        ),
+        name="mixer",
+    )(nin, mixed, weights, x, gain, o_gain)
+
+
+def ffn_kernel(
+    peers, nm_hbm, ffn_hbm, ct_hbm, normed_hbm, weights_hbm, hidden_ref, gain_ref,
+    grads_hbm, ffnp_hbm, ng_hbm, hgrad_ref, gpart_ref,
+    nm, ffn_v, ct_v, normed_v, wout_v, act, dgu, send2, recv2, dm, ffnp_v, grads_v, ng_v,
+    in_sem, out_sem, ss, rs, gather_send, gather_recv,
+):
+    me = lax.axis_index("head")
+    total, width = nm.shape
+    values = normed_v.shape[1]
     own_rows = total // peers
     subs = own_rows // SUB
     cells = act.shape[1]
     tile = 256
     loads = [
-        pltpu.make_async_copy(normed_hbm, normed_v, in_sem.at[0]),
-        pltpu.make_async_copy(wout_hbm, wout_v, in_sem.at[1]),
-        pltpu.make_async_copy(part(x_hbm, me * own_rows, own_rows), x_v, in_sem.at[2]),
-        pltpu.make_async_copy(ffn_hbm, ffn_v, in_sem.at[3]),
-        pltpu.make_async_copy(ct_hbm, ct_v, in_sem.at[4]),
+        pltpu.make_async_copy(ffn_hbm, ffn_v, in_sem.at[0]),
+        pltpu.make_async_copy(nm_hbm, nm, in_sem.at[1]),
+        pltpu.make_async_copy(ct_hbm, ct_v, in_sem.at[2]),
+        pltpu.make_async_copy(normed_hbm, normed_v, in_sem.at[3]),
+        pltpu.make_async_copy(weights_hbm.at[:, pl.ds(values, values)], wout_v, in_sem.at[4]),
     ]
     for load in loads:
         load.start()
     greet_heads(me, peers)
-    loads[0].wait()
-    loads[1].wait()
-
-    def sub_copy(k, t):
-        rows = pl.ds(pl.multiple_of(t * SUB, SUB), SUB)
-        return head_copy(
-            send1.at[k, rows], recv1.at[k, rows], ss1.at[k, t], rs1.at[k, t], me ^ k
-        )
-
-    def project(i, carry):
-        k = peers - 1 - i
+    for load in loads[:3]:
+        load.wait()
+    gain = gain_ref[...]
+    sums = Summed(send2, recv2, me, ss, rs)
+
+    def feed_forward(i, carry):
+        k = lax.rem(i + peers - 1, peers)
         rows = pl.ds(pl.multiple_of((me ^ k) * own_rows, own_rows), own_rows)
-        send1[k] = mm(normed_v[rows, :], wout_v[...], NT).astype(bf16)
-
-        @pl.when(k > 0)
-        def _():
-            for t in range(subs):
-                sub_copy(k, t).start()
-
-        return carry
-
-    lax.fori_loop(0, peers, project, 0)
-    loads[2].wait()
-    gain = gain_ref[...]
-
-    def sub_gather(k, t, owner, buffer, send_sem, recv_sem):
-        at = part(buffer, owner * own_rows + t * SUB, SUB)
-        return head_copy(at, at, send_sem.at[k, t], recv_sem.at[k, t], me ^ k)
-
-    def normalise(t, carry):
-        rows = pl.ds(pl.multiple_of(t * SUB, SUB), SUB)
-        hidden = x_v[rows, :].astype(f32) + send1[0, rows, :].astype(f32)
-        for k in range(1, peers):
-            sub_copy(k, t).wait_recv()
-            hidden = hidden + recv1[k, rows, :].astype(f32)
-        hidden_ref[rows, :] = hidden
-        inverse = lax.rsqrt(jnp.mean(hidden * hidden, axis=1, keepdims=True) + epsilon)
-        part(nm, me * own_rows + t * SUB, SUB)[...] = (hidden * inverse * gain).astype(bf16)
-        for k in range(peers - 1, 0, -1):
-            sub_gather(k, t, me, nm, ss2, rs2).start()
-        return carry
-
-    lax.fori_loop(0, subs, normalise, 0)
-    loads[3].wait()
-    loads[4].wait()
-
-    def mid_copy(k, t):
-        rows = pl.ds(pl.multiple_of(t * SUB, SUB), SUB)
-        return head_copy(
-            send2.at[k, rows], recv2.at[k, rows], ss3.at[k, t], rs3.at[k, t], me ^ k
-        )
-
-    def feed_forward(k, carry):
-        owner = me ^ k
-
-        @pl.when(k > 0)
-        def _():
-            for t in range(subs):
-                sub_gather(k, t, owner, nm, ss2, rs2).wait_recv()
-
-        rows = pl.ds(pl.multiple_of(owner * own_rows, own_rows), own_rows)
 
         def cell_tile(j, carry):
             at = pl.ds(pl.multiple_of(j * tile, tile), tile)
@@ -891,18 +1014,24 @@
         @pl.when(k > 0)
         def _():
             for t in range(subs):
-                mid_copy(k, t).start()
+                sums.copy(k, t).start()
 
         return carry
 
     lax.fori_loop(0, peers, feed_forward, 0)
 
-    def middle_grad(t, carry):
-        rows = pl.ds(pl.multiple_of(t * SUB, SUB), SUB)
-        dmid = send2[0, rows, :].astype(f32)
-        for k in range(1, peers):
-            mid_copy(k, t).wait_recv()
-            dmid = dmid + recv2[k, rows, :].astype(f32)
+    def ffn_rows(i, carry):
+        rows = pl.ds(pl.multiple_of(i * own_rows, own_rows), own_rows)
+        ffnp_v[rows, :] = mm(act[rows, :], ffn_v[:, 2 * cells :], NT).astype(bf16)
+        block_store(i, own_rows, ffnp_v, ffnp_hbm, out_sem.at[0]).start()
+        return carry
+
+    lax.fori_loop(0, peers, ffn_rows, 0)
+    ring = Spread(dm, own_rows, me, gather_send, gather_recv, SUB)
+    gain_part = jnp.zeros((1, width), f32)
+    for t in range(subs):
+        rows = rows_of(t)
+        dmid = sums.collect(t, peers)
         hidden = hidden_ref[rows, :]
         inverse = lax.rsqrt(jnp.mean(hidden * hidden, axis=1, keepdims=True) + epsilon)
         scaled = hidden * inverse
@@ -912,17 +1041,9 @@
         )
         hgrad_ref[rows, :] = grad
         part(dm, me * own_rows + t * SUB, SUB)[...] = grad.astype(bf16)
-        for k in range(peers - 1, 0, -1):
-            sub_gather(k, t, me, dm, ss4, rs4).start()
-        return carry + jnp.sum(dmid * scaled, axis=0, keepdims=True)
-
-    gain_part = lax.fori_loop(0, subs, middle_grad, jnp.zeros((1, width), f32))
+        ring.start(t)
+        gain_part = gain_part + jnp.sum(dmid * scaled, axis=0, keepdims=True)
     gpart_ref[...] = jnp.broadcast_to(gain_part, gpart_ref.shape)
-
-    def block_store(i, size, source, target, sem):
-        return pltpu.make_async_copy(
-            part(source, i * size, size), part(target, i * size, size), sem.at[i]
-        )
 
     def cell_grads(i, carry):
         at = pl.ds(pl.multiple_of(i * tile, tile), tile)
@@ -930,23 +1051,21 @@
         grads_v[at, 2 * cells : 3 * cells] = mm(ct_v[:, at], act[...], TN).astype(bf16)
         return carry
 
-    lax.fori_loop(0, width // tile, cell_grads, 0)
-
-    def ffn_rows(i, carry):
-        rows = pl.ds(pl.multiple_of(i * own_rows, own_rows), own_rows)
-        ffnp_v[rows, :] = mm(act[rows, :], ffn_v[:, 2 * cells :], NT).astype(bf16)
-        block_store(i, own_rows, ffnp_v, ffnp_hbm, out_sem.at[0]).start()
-        return carry
-
-    lax.fori_loop(0, peers, ffn_rows, 0)
+    half = width // tile // 2
+    lax.fori_loop(0, half, cell_grads, 0)
+    loads[3].wait()
+    loads[4].wait()
+    for t in range(subs):
+        ring.forward(t)
+    lax.fori_loop(half, width // tile, cell_grads, 0)
 
     def norm_rows(k, carry):
         owner = me ^ k
 
-        @pl.when(k > 0)
+        @pl.when(k == peers - 1)
         def _():
             for t in range(subs):
-                sub_gather(k, t, owner, dm, ss4, rs4).wait_recv()
+                ring.finish(t)
 
         rows = pl.ds(pl.multiple_of(owner * own_rows, own_rows), own_rows)
         ng_v[rows, :] = mm(dm[rows, :], wout_v[...])
@@ -967,43 +1086,38 @@
         block_store(i, own_rows, ng_v, ng_hbm, out_sem.at[1]).wait()
     for i in range(width // tile):
         block_store(i, tile, grads_v, grads_hbm, out_sem.at[2]).wait()
-    for k in range(1, peers):
-        for t in range(subs):
-            sub_copy(k, t).wait_send()
-            sub_gather(k, t, me, nm, ss2, rs2).wait_send()
-            mid_copy(k, t).wait_send()
-            sub_gather(k, t, me, dm, ss4, rs4).wait_send()
-
-
-def mixer_ffn(normed, out_full, ffn_full, x, ct, gain):
+    for t in range(subs):
+        for k in range(1, peers):
+            sums.copy(k, t).wait_send()
+        ring.drain(t)
+
+
+def feed_forward_block(nm, ffn_full, ct, normed, weights, hidden, gain):
     peers = lax.axis_size("head")
     total, width = ct.shape
     own_rows = total // peers
     subs = own_rows // SUB
     values = normed.shape[1]
     cells = ffn_full.shape[1] // 3
+    shape = jax.ShapeDtypeStruct
     sems = pltpu.SemaphoreType.DMA((peers, subs))
     return pl.pallas_call(
-        functools.partial(mixer_ffn_kernel, peers),
-        in_specs=[anywhere()] * 5 + [vmem()],
-        out_specs=[anywhere()] * 3 + [vmem()] * 3,
+        functools.partial(ffn_kernel, peers),
+        in_specs=[anywhere()] * 5 + [vmem()] * 2,
+        out_specs=[anywhere()] * 3 + [vmem()] * 2,
         out_shape=[
-            jax.ShapeDtypeStruct((width, 3 * cells + values), bf16),
-            jax.ShapeDtypeStruct((total, width), bf16),
-            jax.ShapeDtypeStruct((total, values), f32),
-            jax.ShapeDtypeStruct((own_rows, width), f32),
-            jax.ShapeDtypeStruct((own_rows, width), f32),
-            jax.ShapeDtypeStruct((8, width), f32),
+            shape((width, 3 * cells + values), bf16),
+            shape((total, width), bf16),
+            shape((total, values), f32),
+            shape((own_rows, width), f32),
+            shape((8, width), f32),
         ],
         scratch_shapes=[
+            pltpu.VMEM((total, width), bf16),
+            pltpu.VMEM((width, 3 * cells), bf16),
+            pltpu.VMEM((total, width), bf16),
             pltpu.VMEM((total, values), bf16),
             pltpu.VMEM((width, values), bf16),
-            pltpu.VMEM((width, 3 * cells), bf16),
-            pltpu.VMEM((own_rows, width), bf16),
-            pltpu.VMEM((total, width), bf16),
-            pltpu.VMEM((peers, own_rows, width), bf16),
-            pltpu.VMEM((peers, own_rows, width), bf16),
-            pltpu.VMEM((total, width), bf16),
             pltpu.VMEM((total, cells), bf16),
             pltpu.VMEM((total, 2 * cells), bf16),
             pltpu.VMEM((peers, own_rows, width), bf16),
@@ -1015,66 +1129,89 @@
             pltpu.SemaphoreType.DMA((5,)),
             pltpu.SemaphoreType.DMA((3, max(peers, width // 256))),
         ]
-        + [sems] * 8,
+        + [sems] * 4,
         compiler_params=pltpu.CompilerParams(
-            collective_id=1, has_side_effects=True, vmem_limit_bytes=56 * 2**20
+            collective_id=5, has_side_effects=True, vmem_limit_bytes=56 * 2**20
         ),
-        name="mixer_ffn",
-    )(normed, out_full, ffn_full, x, ct, gain)
+        name="feed_forward",
+    )(nm, ffn_full, ct, normed, weights, hidden, gain)
 
 
 def input_grad_kernel(
-    peers, dp_hbm, win_hbm, x_hbm, hgrad_ref, gain_ref,
-    out_hbm, gpart_ref,
-    dp_v, win_v, x_v, send1, recv1, whole, in_sem, out_sem, ss1, rs1, ss2, rs2,
+    peers, places, cores, dp_hbm, win_hbm, wog_hbm, x_hbm, hgrad_ref, gain_ref, gains_ref,
+    channels_ref,
+    out_hbm, gains_out, channels_out,
+    dp_v, win_v, wog_v, x_v, send1, recv1, whole, gains_v, gains_recv, gains_sum, gains_all,
+    channels_all, in_sem, out_sem, ss1, rs1, gather_send, gather_recv,
+    hs, hr, gs, gr, cs, cr,
 ):
     me = lax.axis_index("head")
+    place, core = lax.axis_index("seq"), lax.axis_index("batch")
     total, width = whole.shape
     own_rows = total // peers
     subs = own_rows // SUB
+    values = wog_v.shape[1]
+    conv_cols = win_v.shape[1] - PAD
+    group = places * cores
+    flat = place * cores + core
     loads = [
         pltpu.make_async_copy(dp_hbm, dp_v, in_sem.at[0]),
         pltpu.make_async_copy(win_hbm, win_v, in_sem.at[1]),
-        pltpu.make_async_copy(part(x_hbm, me * own_rows, own_rows), x_v, in_sem.at[2]),
+        pltpu.make_async_copy(wog_hbm.at[:, pl.ds(0, values)], wog_v, in_sem.at[2]),
+        pltpu.make_async_copy(part(x_hbm, me * own_rows, own_rows), x_v, in_sem.at[3]),
     ]
     for load in loads:
         load.start()
-    greet_heads(me, peers)
-    loads[0].wait()
-    loads[1].wait()
-
-    def sub_copy(k, t):
-        rows = pl.ds(pl.multiple_of(t * SUB, SUB), SUB)
-        return head_copy(
-            send1.at[k, rows], recv1.at[k, rows], ss1.at[k, t], rs1.at[k, t], me ^ k
+
+    def to_group(d, source, target, send_sem, recv_sem):
+        to = lax.rem(flat + d, group)
+        return pltpu.make_async_remote_copy(
+            src_ref=source, dst_ref=target.at[d], send_sem=send_sem.at[d],
+            recv_sem=recv_sem.at[d], device_id={"seq": to // cores, "batch": lax.rem(to, cores)},
+            device_id_type=MESH,
         )
+
+    barrier = pltpu.get_barrier_semaphore()
+    for k in range(1, peers):
+        pl.semaphore_signal(barrier, inc=1, device_id={"head": me ^ k}, device_id_type=MESH)
+    for d in range(1, group):
+        to = lax.rem(flat + d, group)
+        pl.semaphore_signal(
+            barrier, inc=1, device_id={"seq": to // cores, "batch": lax.rem(to, cores)},
+            device_id_type=MESH,
+        )
+    pl.semaphore_wait(barrier, peers + group - 2)
+    for load in loads[:3]:
+        load.wait()
+    sums = Summed(send1, recv1, me, ss1, rs1)
 
     def project(i, carry):
         k = peers - 1 - i
         rows = pl.ds(pl.multiple_of((me ^ k) * own_rows, own_rows), own_rows)
-        send1[k] = mm(dp_v[rows, :], win_v[...], NT).astype(bf16)
+        partial = mm(dp_v[rows, 0:conv_cols], win_v[:, 0:conv_cols], NT)
+        partial = partial + mm(
+            dp_v[rows, conv_cols : conv_cols + values], wog_v[...], NT
+        )
+        partial = partial + mm(dp_v[rows, conv_cols + values :], win_v[:, conv_cols:], NT)
+        send1[k] = partial.astype(bf16)
 
         @pl.when(k > 0)
         def _():
             for t in range(subs):
-                sub_copy(k, t).start()
+                sums.copy(k, t).start()
 
         return carry
 
     lax.fori_loop(0, peers, project, 0)
-    loads[2].wait()
+    for d in range(1, group):
+        to_group(d, channels_ref, channels_all, cs, cr).start()
+    loads[3].wait()
     gain = gain_ref[...]
-
-    def sub_gather(k, t, owner):
-        at = part(whole, owner * own_rows + t * SUB, SUB)
-        return head_copy(at, at, ss2.at[k, t], rs2.at[k, t], me ^ k)
-
-    def input_rows(t, carry):
-        rows = pl.ds(pl.multiple_of(t * SUB, SUB), SUB)
-        din = send1[0, rows, :].astype(f32)
-        for k in range(1, peers):
-            sub_copy(k, t).wait_recv()
-            din = din + recv1[k, rows, :].astype(f32)
+    ring = Spread(whole, own_rows, me, gather_send, gather_recv, SUB)
+    gain_part = jnp.zeros((1, width), f32)
+    for t in range(subs):
+        rows = rows_of(t)
+        din = sums.collect(t, peers)
         x = x_v[rows, :].astype(f32)
         inverse = lax.rsqrt(jnp.mean(x * x, axis=1, keepdims=True) + epsilon)
         scaled = x * inverse
@@ -1083,63 +1220,96 @@
             weighted - scaled * jnp.mean(weighted * scaled, axis=1, keepdims=True)
         )
         part(whole, me * own_rows + t * SUB, SUB)[...] = grad.astype(bf16)
-        for k in range(peers - 1, 0, -1):
-            sub_gather(k, t, me).start()
-        return carry + jnp.sum(din * scaled, axis=0, keepdims=True)
-
-    gain_part = lax.fori_loop(0, subs, input_rows, jnp.zeros((1, width), f32))
-    gpart_ref[...] = jnp.broadcast_to(gain_part, gpart_ref.shape)
-
-    def store(i):
-        return pltpu.make_async_copy(
-            part(whole, i * own_rows, own_rows), part(out_hbm, i * own_rows, own_rows),
-            out_sem.at[i],
-        )
-
-    store(me).start()
+        ring.start(t)
+        gain_part = gain_part + jnp.sum(din * scaled, axis=0, keepdims=True)
+    row8 = lax.broadcasted_iota(jnp.int32, (8, width), 0)
+    gains_v[...] = jnp.where(row8 == 0, gain_part, gains_ref[...])
+
+    def gains_copy(k):
+        return head_copy(gains_v, gains_recv.at[k], hs.at[k], hr.at[k], me ^ k)
+
     for k in range(1, peers):
-        for t in range(subs):
-            sub_gather(k, t, me ^ k).wait_recv()
-        store(me ^ k).start()
+        gains_copy(k).start()
+    block_store(me, own_rows, whole, out_hbm, out_sem).start()
+    gathered = gains_v[...]
+    for k in range(1, peers):
+        gains_copy(k).wait_recv()
+        gathered = gathered + gains_recv[k]
+    gains_sum[...] = gathered
+    for d in range(1, group):
+        to_group(d, gains_sum, gains_all, gs, gr).start()
+    for t in range(subs):
+        ring.forward(t)
+    block_store(me ^ 1, own_rows, whole, out_hbm, out_sem).start()
+    block_store(me ^ 2, own_rows, whole, out_hbm, out_sem).start()
+    channels = channels_ref[...]
+    for d in range(1, group):
+        to_group(d, channels_ref, channels_all, cs, cr).wait_recv()
+        channels = channels + channels_all[d]
+    channels_out[...] = channels
+    for d in range(1, group):
+        to_group(d, gains_sum, gains_all, gs, gr).wait_recv()
+        gathered = gathered + gains_all[d]
+    gains_out[...] = gathered
+    for t in range(subs):
+        ring.finish(t)
+    block_store(me ^ 3, own_rows, whole, out_hbm, out_sem).start()
     for k in range(peers):
-        store(me ^ k).wait()
+        block_store(k, own_rows, whole, out_hbm, out_sem).wait()
+    for t in range(subs):
+        for k in range(1, peers):
+            sums.copy(k, t).wait_send()
+        ring.drain(t)
     for k in range(1, peers):
-        for t in range(subs):
-            sub_copy(k, t).wait_send()
-            sub_gather(k, t, me).wait_send()
-
-
-def input_grads(dp, in_full, x, hgrad, gain):
-    peers = lax.axis_size("head")
+        gains_copy(k).wait_send()
+    for d in range(1, group):
+        to_group(d, channels_ref, channels_all, cs, cr).wait_send()
+        to_group(d, gains_sum, gains_all, gs, gr).wait_send()
+
+
+def input_grads(dp, in_full, gate_full, x, hgrad, gain, gains, channels):
+    peers, places, cores = lax.axis_size("head"), lax.axis_size("seq"), lax.axis_size("batch")
+    group = places * cores
     total, width = x.shape
     cols = dp.shape[1]
+    values = gate_full.shape[1] // 2
     own_rows = total // peers
     subs = own_rows // SUB
+    shape = jax.ShapeDtypeStruct
     sems = pltpu.SemaphoreType.DMA((peers, subs))
+    per_peer = pltpu.SemaphoreType.DMA((peers,))
+    per_member = pltpu.SemaphoreType.DMA((group,))
     return pl.pallas_call(
-        functools.partial(input_grad_kernel, peers),
-        in_specs=[anywhere()] * 3 + [vmem()] * 2,
-        out_specs=[anywhere(), vmem()],
+        functools.partial(input_grad_kernel, peers, places, cores),
+        in_specs=[anywhere()] * 4 + [vmem()] * 4,
+        out_specs=[anywhere(), vmem(), vmem()],
         out_shape=[
-            jax.ShapeDtypeStruct((total, width), bf16),
-            jax.ShapeDtypeStruct((8, width), f32),
+            shape((total, width), bf16), shape(gains.shape, f32), shape(channels.shape, f32),
         ],
         scratch_shapes=[
             pltpu.VMEM((total, cols), bf16),
-            pltpu.VMEM((width, cols), bf16),
+            pltpu.VMEM((width, cols - values), bf16),
+            pltpu.VMEM((width, values), bf16),
             pltpu.VMEM((own_rows, width), bf16),
             pltpu.VMEM((peers, own_rows, width), bf16),
             pltpu.VMEM((peers, own_rows, width), bf16),
             pltpu.VMEM((total, width), bf16),
-            pltpu.SemaphoreType.DMA((3,)),
+            pltpu.VMEM(gains.shape, f32),
+            pltpu.VMEM((peers,) + gains.shape, f32),
+            pltpu.VMEM(gains.shape, f32),
+            pltpu.VMEM((group,) + gains.shape, f32),
+            pltpu.VMEM((group,) + channels.shape, f32),
+            pltpu.SemaphoreType.DMA((4,)),
             pltpu.SemaphoreType.DMA((peers,)),
         ]
-        + [sems] * 4,
+        + [sems] * 4
+        + [per_peer] * 2
+        + [per_member] * 4,
         compiler_params=pltpu.CompilerParams(
             collective_id=2, has_side_effects=True, vmem_limit_bytes=48 * 2**20
         ),
         name="input_grads",
-    )(dp, in_full, x, hgrad, gain)
+    )(dp, in_full, gate_full, x, hgrad, gain, gains, channels)
 
 
 def shifted(shard, axis, by):
@@ -1169,31 +1339,34 @@
     total = seqs * length
     conv_cols = heads * QKV
     value_cols = heads * DV
-    in_cols = conv_cols + value_cols
     units = w_down.shape[0]
     cells = -(-units // 256) * 256
     spare = cells - units
 
-    conv_flat = conv_w.reshape(-1)
-    small = jnp.concatenate([attn_gain, ffn_gain, conv_flat, o_gain]).astype(bf16)
     packed_in = jnp.concatenate(
         [
             w_in[:, :, :QKV].reshape(shard, conv_cols),
-            w_in[:, :, QKV:].reshape(shard, value_cols),
             w_rates.reshape(shard, 2 * heads),
             jnp.zeros((shard, PAD - 2 * heads), f32),
         ],
         axis=1,
     ).astype(bf16)
+    packed_gate = jnp.concatenate(
+        [w_in[:, :, QKV:].reshape(shard, value_cols), w_out.reshape(value_cols, -1).T], axis=1
+    ).astype(bf16)
     packed_ffn = jnp.pad(
         jnp.stack([w_gu[:, 0], w_gu[:, 1], w_down.T], axis=1).astype(bf16),
         ((0, 0), (0, 0), (0, spare)),
     ).reshape(shard, 3 * cells)
+    conv_flat = conv_w.reshape(-1)
+    small = jnp.concatenate([attn_gain, ffn_gain, conv_flat, o_gain]).astype(bf16)
+
+    x = tokens.reshape(total, width)
+    ct = cotangent.reshape(total, width)
+    before = shifted(tokens[:, length - HALO :], "seq", 1).reshape(seqs * HALO, width)
     in_full = lax.all_gather(packed_in, ALL, axis=0, tiled=True)
     small_full = lax.all_gather(small, ALL, axis=0)
-    out_full = lax.all_gather(
-        w_out.reshape(value_cols, -1).T.astype(bf16), ALL, axis=0, tiled=True
-    )
+    gate_full = lax.all_gather(packed_gate, ALL, axis=0, tiled=True)
     ffn_full = lax.all_gather(packed_ffn, ALL, axis=0, tiled=True)
     attn_gain_f = small_full[:, :shard].reshape(1, width).astype(f32)
     ffn_gain_f = small_full[:, shard : 2 * shard].reshape(1, width).astype(f32)
@@ -1207,76 +1380,79 @@
     )
     o_gain_full = small_full[:, conv_end:].reshape(1, DV).astype(f32)
 
-    place = lax.axis_index("seq")
-    x = tokens.reshape(total, width)
-    ct = cotangent.reshape(total, width)
-    inputs = x.astype(f32)
-    normed_in = (inputs * root_scale(inputs) * attn_gain_f).astype(bf16)
+    def normed_rows(rows):
+        rows = rows.astype(f32)
+        return (rows * root_scale(rows) * attn_gain_f).astype(bf16)
+
+    normed_in = normed_rows(x)
     projected = matmul(normed_in, in_full)
-    ends = projected.reshape(seqs, length, -1)[:, length - CONV + 1 :, :conv_cols]
-    end_live = (
-        place * length + length - CONV + 1 + jnp.arange(CONV - 1, dtype=jnp.int32)
-    )[None, :] >= starts[:, None]
-    received = shifted((ends * end_live.astype(f32)[:, :, None]).astype(bf16), "seq", 1)
-    halo = jnp.pad(received, ((0, 0), (HALO - CONV + 1, 0), (0, 0)))
-    qkv, inv, n, qe, tot, trans, states, mixed, normed = forward_rule(
-        starts, decay_par, projected, halo, conv_full, o_gain_full, seqs, heads
-    )
-    late_grads, ffn_part, normed_grad, hidden, hidden_grad, ffn_gain_part = mixer_ffn(
-        normed, out_full, ffn_full, x, ct, ffn_gain_f
-    )
+    halo = matmul(normed_rows(before), in_full[:, :conv_cols]).reshape(seqs, HALO, conv_cols)
+    qkv, inv, n, qe, tot, trans, states, mixed = forward_rule(
+        starts, decay_par, projected, halo, conv_full, seqs, heads
+    )
+    og, normed, nm, hidden = mixer(
+        normed_in, mixed, gate_full, x, ffn_gain_f, o_gain_full
+    )
+    late_grads, ffn_part, normed_grad, hidden_grad, ffn_gain_part = feed_forward_block(
+        nm, ffn_full, ct, normed, gate_full, hidden, ffn_gain_f
+    )
+    late_own = lax.psum_scatter(late_grads, ALL, scatter_dimension=0, tiled=True)
     projected_grad, dconv, ddecay, onorm_grads, result = backward_rule(
-        starts, decay_par, normed_grad, mixed, projected, o_gain_full, n, qe, tot, trans, qkv, inv,
-        states, halo, conv_full, hidden, ffn_part, seqs, heads,
-    )
-    in_grad = matmul(normed_in, projected_grad, TN)
-    input_grad, attn_gain_part = input_grads(
-        projected_grad, in_full, x, hidden_grad, attn_gain_f
-    )
+        starts, decay_par, normed_grad, mixed, og, projected, o_gain_full, n, qe, tot, trans, qkv,
+        inv, states, halo, conv_full, hidden, ffn_part, seqs, heads,
+    )
+    in_grad = matmul(normed_in, projected_grad, TN).astype(bf16)
+    in_grad, late_own = lax.optimization_barrier((in_grad, late_own))
+    in_own = lax.psum_scatter(in_grad, ALL, scatter_dimension=0, tiled=True)
+
     onorm_grad = jnp.sum(onorm_grads[:, 0], axis=0)
     decay_part = jnp.sum(ddecay[:, :2, 0].reshape(heads, seqs, 2), axis=1).T
     conv_grad = jnp.sum(dconv.reshape(heads, seqs, CONV, QKV), axis=1).transpose(1, 0, 2)
-
-    def scatter(grad, dim=0):
-        return lax.psum_scatter(
-            grad.astype(bf16), ALL, scatter_dimension=dim, tiled=True
-        ).astype(f32)
-
-    late_own = scatter(late_grads)
-    in_own = scatter(in_grad)
-    gains = lax.psum(
-        jnp.concatenate([attn_gain_part[0], ffn_gain_part[0], onorm_grad]), ("head",) + ALL
+    gains = jnp.concatenate(
+        [
+            jnp.zeros((1, width), f32),
+            ffn_gain_part[:1],
+            jnp.pad(onorm_grad, (0, width - DV))[None],
+            jnp.zeros((5, width), f32),
+        ]
+    )
+    taps = CONV * heads
+    channels = jnp.concatenate(
+        [
+            conv_grad.reshape(taps, QKV),
+            jnp.pad(decay_part.reshape(1, 2 * heads), ((0, 7), (0, QKV - 2 * heads))),
+        ]
+    )
+    input_grad, gains, channels = input_grads(
+        projected_grad, in_full, gate_full, x, hidden_grad, attn_gain_f, gains, channels
     )
     at = lax.axis_index(ALL)
-    attn_own = lax.dynamic_slice(gains, (at * shard,), (shard,))
-    ffn_own = lax.dynamic_slice(gains, (width + at * shard,), (shard,))
-    onorm_own = lax.dynamic_slice(gains, (2 * width + at * (DV // shards),), (DV // shards,))
-    channels = lax.psum(
-        jnp.concatenate([conv_grad.reshape(-1), decay_part.reshape(-1)]), ALL
-    )
+    own_gains = lax.dynamic_slice(gains, (0, at * shard), (2, shard))
+    onorm_own = lax.dynamic_slice(gains, (2, at * (DV // shards)), (1, DV // shards))
     conv_own = lax.dynamic_slice(
-        channels[: CONV * conv_cols].reshape(CONV, heads, QKV),
-        (0, 0, at * (QKV // shards)),
-        (CONV, heads, QKV // shards),
-    )
+        channels, (0, at * (QKV // shards)), (taps, QKV // shards)
+    ).reshape(CONV, heads, -1)
+    in_own = in_own.astype(f32)
+    late_own = late_own.astype(f32)
     in_main = jnp.concatenate(
         [
             in_own[:, :conv_cols].reshape(shard, heads, QKV),
-            in_own[:, conv_cols:in_cols].reshape(shard, heads, DV),
+            in_own[:, conv_cols : conv_cols + value_cols].reshape(shard, heads, DV),
         ],
         axis=2,
     )
+    rates_at = conv_cols + value_cols
     return (
         result.reshape(tokens.shape),
         input_grad.reshape(tokens.shape),
-        attn_own,
+        own_gains[0],
         in_main,
-        in_own[:, in_cols : in_cols + 2 * heads].reshape(shard, heads, 2),
+        in_own[:, rates_at : rates_at + 2 * heads].reshape(shard, heads, 2),
         conv_own,
-        channels[CONV * conv_cols :].reshape(2, heads),
-        onorm_own,
+        channels[taps, : 2 * heads].reshape(2, heads),
+        onorm_own[0],
         late_own[:, 3 * cells :].T.reshape(heads, DV, -1),
-        ffn_own,
+        own_gains[1],
         late_own[:, : 2 * cells].reshape(shard, 2, cells)[:, :, :units],
         late_own[:, 2 * cells : 2 * cells + units].T,
     )

time: 453 us -> 339 us (0.75)
  blocking collectives: 86.4 us -> 14.5 us
  waiting for transfers between devices: 55.6 us -> 19.2 us
  Pallas kernels: 242 us -> 235 us
    psum x2 -> x0, blocking collectives: 70.6 us -> none  [the longest x1 39.7 us: per_device(): lax.psum(jnp.concatenate([attn_gain_part[0], ffn_gain_part[0], onorm_grad...]
    all_gather x1, waiting for transfers between devices: 32.1 us -> 0.01 us  [per_device(): ffn_full = lax.all_gather(packed_ffn, ALL, axis=0, tiled=True)]
    all_gather x1, waiting for transfers between devices: 22 us -> 9.52 us  [per_device(): in_full = lax.all_gather(packed_in, ALL, axis=0, tiled=True)]
    reduce_scatter x2, waiting for transfers between devices: 0.01 us -> 9.57 us  [the longest x1 9.57 us: per_device(): lax.psum_scatter(late_grads, ALL, scatter_dimension=0, tiled=True)]
    pallas_call x2 -> x3, Pallas kernels: 158 us -> 152 us  [the longest x1 54.9 us: feed_forward_block(): pl.pallas_call(functools.partial(ffn_kernel, peers), in_specs=[anywhere()...]
    dot_general x2 -> x3, matrix products: 13.6 us -> 16.2 us  [matmul(): return lax.dot_general(a, b, (dims, ((), ())), preferred_element_type=f32)]
    unnamed x47 -> x60, local copies, waits for them, and re-layouts: 14.5 us -> 12.9 us
  transfers between devices with their start and end apart: 6 -> 6, of which waited for: 3 -> 2; matrix products, arithmetic and copies ran while one was open for 5% -> 9% of each run, Pallas kernels for 17% -> 53%
where the time goes in v3:
time: 339 us
  Pallas kernels  235 us (69%)
  local copies, waits for them, and re-layouts  27.7 us (8%)
  waiting for transfers between devices  19.2 us (6%)
  matrix products  16.2 us (5%)
  blocking collectives  14.5 us (4%)
  between operations  14.3 us (4%)
  other arithmetic  6.33 us (2%)
  starting transfers between devices  5.12 us (2%)
    pallas_call x1, Pallas kernels, backward_rule(): pl.pallas_call(functools.partial(backward_kernel, seqs, places, peers), g...  57.7 us
    pallas_call x1, Pallas kernels, feed_forward_block(): pl.pallas_call(functools.partial(ffn_kernel, peers), in_specs=[anywhere()...  54.9 us
    pallas_call x1, Pallas kernels, input_grads(): pl.pallas_call(functools.partial(input_grad_kernel, peers, places, cores)...  49.2 us
    pallas_call x1, Pallas kernels, mixer(): pl.pallas_call(functools.partial(mixer_kernel, peers), in_specs=[anywhere...  47.6 us
    pallas_call x1, Pallas kernels, forward_rule(): pl.pallas_call(functools.partial(forward_kernel, seqs, places), grid=(2 *...  25.9 us
    dot_general x3, matrix products, matmul(): return lax.dot_general(a, b, (dims, ((), ())), preferred_element_type=f32)  16.2 us
    all_gather x1, blocking collectives, per_device(): small_full = lax.all_gather(small, ALL, axis=0)  14.5 us
    unnamed x60, local copies, waits for them, and re-layouts  12.9 us
  transfers between devices with their start and end apart: 6, of which 2 were waited for; matrix products, arithmetic and copies ran while one was open for 9% of the time, Pallas kernels for 53%

profile of v3, /device:TPU:0, one launch (start us, length us, event | category | flops | bytes accessed | tf_op | source)
XLA Modules:
  0.0 338.6 jit_solution(4104330761890346467)
XLA Ops:
  7.2 1.4 convert.54
  12.8 4.9 %collective-permute-start = (bf16[2,16,1024]{2,1,0:T(8,128)(2,1)S(1)}, bf16[2,16,1024]{2,1,0:T(8,128)(2,1)S(1)}, u32[]{:S(2)}, u32[]{:S(2)}) collective-permute-start(bf16[2,16,1024]{2,1,0:T(8,128)(2,1)S(1)} %slice.70), channel_id=1, source_target_pairs={{0,8},{8,16},{16,24},{1,9},{9,17},{17,25},{2,10},{10,18},{18,26},{... | collective-permute-start | bytes 196616 | tf_op jit(solution)/shard_map/ppermute | solution.py:1318
  17.9 14.5 %all-gather = bf16[8,1,800]{2,1,0:T(2,128)(2,1)S(1)} all-gather(bf16[1,1,800]{2,1,0:T(2,128)(2,1)S(1)} %maximum_bitcast_fusion), channel_id=1, replica_groups=mesh['seq'=4,'batch'=2,'head'=4] {'seq','batch'}, dimensions={0}, use_global_device_ids=true | all-gather | bytes 14400 | tf_op jit(solution)/shard_map/all_gather | solution.py:1368
  33.0 1.9 multiply_convert_fusion.nin_hbm
  35.3 9.5 %all-gather.5.cloned.1.call-done.win_hbm = bf16[1024,1152]{1,0:T(8,128)(2,1)} async-done(((bf16[128,1152]{1,0:T(8,128)(2,1)}), bf16[1024,1152]{1,0:T(8,128)(2,1)}) %all-gather.5.cloned.1.call-update) | async-done | bytes 2359312 | tf_op jit(solution)/shard_map/all_gather | solution.py:1367
  44.8 2.2 fusion.halo_ref
  47.1 6.4 %fusion.11.main_ref.rate_ref = f32[1024,1152]{1,0:T(8,128)} fusion(bf16[1024,1024]{1,0:T(8,128)(2,1)S(1)} %copy-done.14, bf16[1024,1152]{1,0:T(8,128)(2,1)} %all-gather.5.cloned.1.call-done.win_hbm), kind=kOutput, calls=%fused_computation.45 | convolution fusion | flops 2415919104 | bytes 9175040 | tf_op jit(solution)/shard_map/dot_general | solution.py:1326
  53.5 25.9 %forward_rule.1 = (bf16[1024,1024]{1,0:T(8,128)(2,1)S(1)}, bf16[4,4,128,128]{3,2,1,0:T(8,128)(2,1)S(1)}, bf16[4,4,128,128]{3,2,1,0:T(8,128)(2,1)S(1)}, bf16[4,4,...) custom-call(s32[2]{0:T(128)S(1)} %copy-done.11, ...), custom_call_target="tpu_custom_call" | custom-call | tf_op jit(solution)/shard_map/forward_rule/pallas_call | solution.py:343
  79.4 1.4 copy-done.2
  81.8 47.6 %mixer.1 = (f32[1024,512]{1,0:T(8,128)S(1)}, bf16[1024,512]{1,0:T(8,128)(2,1)S(1)}, bf16[1024,1024]{1,0:T(8,128)(2,1)}, f32[256,1024]{1,0:T(8,128)S(1)}) custom-call(bf16[1024,1024]{1,0:T(8,128)(2,1)} %multiply_convert_fusion.nin_hbm, f32[1024,512]{1,0:T(8,128)} %get-tuple-element.39.mixed_hbm.mixed_ref, ...), custom_call_target="tpu_custom_call" | custom-call | tf_op jit(solution)/shard_map/mixer/pallas_call | solution.py:928
  130.3 1.3 copy-done.3
  132.6 54.9 %feed_forward.1 = (bf16[1024,2816]{1,0:T(8,128)(2,1)}, bf16[1024,1024]{1,0:T(8,128)(2,1)}, f32[1024,512]{1,0:T(8,128)}, f32[256,1024]{1,0:T(8,128)}, f32[8,1024]{1,0:T(8,128)}) custom-call(bf16[1024,1024]{1,0:T(8,128)(2,1)} %get-tuple-element.40.nm_hbm, bf16[1024,2304]{1,0:T(8,128)(2,1)} %all-gather.9.cloned.1.call-done.ffn_hbm, ...), custom_call_target="tpu_custom_call" | custom-call | tf_op jit(solution)/shard_map/feed_forward/pallas_call | solution.py:1104
  187.6 57.7 %backward_rule.1 = (bf16[1024,1664]{1,0:T(8,128)(2,1)}, f32[4,4,512]{2,1,0:T(4,128)S(1)}, f32[4,8,128]{2,1,0:T(8,128)S(1)}, f32[4,8,256]{2,1,0:T(8,128)S(1)}, bf16[1024,1024]{1,0:T(8,128)(2,1)}) custom-call(s32[2]{0:T(128)S(1)} %copy-done.11, f32[2,2]{1,0:T(2,128)S(1)} %copy-done.10, f32[1024,512]{1,0:T(8,128)} %get-tuple-element.43.dn_ref, ...), custom_call_target="tpu_custom_call" | custom-call | tf_op jit(solution)/shard_map/backward_rule/pallas_call | solution.py:743
  245.3 7.5 %convolution_convert_fusion = bf16[1024,1664]{1,0:T(8,128)(2,1)} fusion(bf16[1024,1024]{1,0:T(8,128)(2,1)S(1)} %copy-done.15, bf16[1024,1664]{1,0:T(8,128)(2,1)} %get-tuple-element.54.dp_hbm), kind=kOutput, calls=%fused_computation.2 | convolution fusion | flops 3491364864 | bytes 8912896 | tf_op jit(solution)/shard_map/dot_general | solution.py:1326
  252.9 9.6 %reduce-scatter.3.cloned.1.call-done = bf16[128,2816]{1,0:T(8,128)(2,1)} async-done(((bf16[1024,2816]{1,0:T(8,128)(2,1)}), bf16[128,2816]{1,0:T(8,128)(2,1)}) %reduce-scatter.3.cloned.1.call-update) | async-done | bytes 720912 | tf_op jit(solution)/shard_map/reduce_scatter | solution.py:1399
  263.9 49.2 %input_grads.1 = (bf16[1024,1024]{1,0:T(8,128)(2,1)S(1)}, f32[8,1024]{1,0:T(8,128)S(1)}, f32[16,512]{1,0:T(8,128)S(1)}) custom-call(bf16[1024,1664]{1,0:T(8,128)(2,1)} %get-tuple-element.54.dp_hbm, bf16[1024,1152]{1,0:T(8,128)(2,1)} %all-gather.5.cloned.1.call-done.win_hbm, bf16[1024,1024]{1,0:T(8,128)(2,1)S(1)} %copy-done, bf16[1024,1024]{1,0:T(8,128)(2,1)} %bitcast.74, ...), custom_call_target="tpu_custom_call" | custom-call | tf_op jit(solution)/shard_map/input_grads/pallas_call | solution.py:1282
  313.1 1.3 copy-done.4
  316.9 1.1 slice.100
  318.1 1.1 copy.65
  319.2 2.0 slice.101
  324.5 1.1 slice.97
  327.2 1.2 pad_maximum_fusion
  328.4 1.3 copy.76
  330.8 1.3 copy.77
  (129 shorter events, 17.8 us)
Async XLA Ops:
  7.2 2.9 copy-start.20
  7.2 37.6 %all-gather.5.cloned.1.call-start = ((), (), s32[]{:S(2)}) async-start(), calls=%async_computation.2 | async-start | bytes 2654208 | tf_op jit(solution)/shard_map/all_gather | solution.py:1367
  8.7 2.5 copy-start.18
  8.9 2.3 copy-start.19
  9.9 71.8 %all-gather.7.cloned.1.call-start = ((), (), s32[]{:S(2)}) async-start(), calls=%async_computation.3 | async-start | bytes 2359296 | tf_op jit(solution)/shard_map/all_gather | solution.py:1369
  11.0 6.7 %copy-start.21 = (f32[4,2,64]{2,1,0:T(2,128)S(1)}, f32[4,2,64]{2,1,0:T(2,128)}, u32[]{:S(2)}) copy-start(f32[4,2,64]{2,1,0:T(2,128)} %param.18) | copy-start | bytes 6148
  11.1 6.8 %copy-start.25 = (f32[32]{0:T(128)S(1)}, f32[32]{0:T(128)}, u32[]{:S(2)}) copy-start(f32[32]{0:T(128)} %param.20) | copy-start | bytes 388
  11.1 6.8 %copy-start.23 = (f32[128]{0:T(128)S(1)}, f32[128]{0:T(128)}, u32[]{:S(2)}) copy-start(f32[128]{0:T(128)} %param.22) | copy-start | bytes 1540
  11.1 6.8 %copy-start.24 = (f32[128]{0:T(128)S(1)}, f32[128]{0:T(128)}, u32[]{:S(2)}) copy-start(f32[128]{0:T(128)} %param.15) | copy-start | bytes 1540
  11.1 121.5 %all-gather.9.cloned.1.call-start = ((), (), s32[]{:S(2)}) async-start(), calls=%async_computation.4 | async-start | bytes 5308416 | tf_op jit(solution)/shard_map/all_gather | solution.py:1370
  12.4 250.0 %reduce-scatter.3.cloned.1.call-start = ((), (), s32[]{:S(2)}) async-start(), calls=%async_computation.5 | async-start | bytes 6488064 | tf_op jit(solution)/shard_map/reduce_scatter | solution.py:1399
  12.8 22.3 %collective-permute-start = (bf16[2,16,1024]{2,1,0:T(8,128)(2,1)S(1)}, bf16[2,16,1024]{2,1,0:T(8,128)(2,1)S(1)}, u32[]{:S(2)}, u32[]{:S(2)}) collective-permute-start(bf16[2,16,1024]{2,1,0:T(8,128)(2,1)S(1)} %slice.70), channel_id=1, source_target_pairs={{0,8},{8,16},{16,24},{1,9},{9,17},{17,25},{2,10},{10,18},{18,26},{... | collective-permute-start | bytes 196616 | tf_op jit(solution)/shard_map/ppermute | solution.py:1318
  17.9 15.1 %copy-start.13 = (bf16[2,512,1024]{2,1,0:T(8,128)(2,1)S(1)}, bf16[2,512,1024]{2,1,0:T(8,128)(2,1)}, u32[]{:S(2)}) copy-start(bf16[2,512,1024]{2,1,0:T(8,128)(2,1)} %param.13) | copy-start | bytes 6291460
  33.0 48.8 %copy-start.9 = (f32[8,128]{1,0:T(8,128)}, f32[8,128]{1,0:T(8,128)S(1)}, u32[]{:S(2)}) copy-start(f32[8,128]{1,0:T(8,128)S(1)} %get-tuple-element.116) | copy-start | bytes 12292
  44.8 2.2 copy-start.14
  47.1 6.5 %copy-start.10 = (f32[2,2]{1,0:T(2,128)S(1)}, f32[2,2]{1,0:T(2,128)}, u32[]{:S(2)}) copy-start(f32[2,2]{1,0:T(2,128)} %decay_ref.3) | copy-start | bytes 52
  47.1 6.4 %copy-start.11 = (s32[2]{0:T(128)S(1)}, s32[2]{0:T(128)}, u32[]{:S(2)}) copy-start(s32[2]{0:T(128)} %start_ref.3) | copy-start | bytes 28
  187.5 135.5 %reduce-scatter.5.cloned.1.call-start = ((), (), s32[]{:S(2)}) async-start(), calls=%async_computation.6 | async-start | bytes 3833856 | tf_op jit(solution)/shard_map/reduce_scatter | solution.py:1406
  187.6 57.7 %copy-start.15 = (bf16[1024,1024]{1,0:T(8,128)(2,1)S(1)}, bf16[1024,1024]{1,0:T(8,128)(2,1)}, u32[]{:S(2)}) copy-start(bf16[1024,1024]{1,0:T(8,128)(2,1)} %multiply_convert_fusion.nin_hbm) | copy-start | bytes 6291460
  252.9 11.0 %copy-start = (bf16[1024,1024]{1,0:T(8,128)(2,1)S(1)}, bf16[1024,1024]{1,0:T(8,128)(2,1)}, u32[]{:S(2)}) copy-start(bf16[1024,1024]{1,0:T(8,128)(2,1)} %all-gather.7.cloned.1.call-done.weights_hbm.wog_hbm) | copy-start | bytes 6291460
  252.9 11.0 %copy-start.6 = (f32[256,1024]{1,0:T(8,128)S(1)}, f32[256,1024]{1,0:T(8,128)}, u32[]{:S(2)}) copy-start(f32[256,1024]{1,0:T(8,128)} %get-tuple-element.55.hgrad_ref) | copy-start | bytes 3145732
  314.4 3.5 %copy-start.16 = (bf16[128,2816]{1,0:T(8,128)(2,1)S(1)}, bf16[128,2816]{1,0:T(8,128)(2,1)}, u32[]{:S(2)}) copy-start(bf16[128,2816]{1,0:T(8,128)(2,1)} %reduce-scatter.3.cloned.1.call-done) | copy-start | bytes 2162692
  324.0 4.4 %copy-start.17 = (bf16[1024,1024]{1,0:T(8,128)(2,1)S(1)}, bf16[1024,1024]{1,0:T(8,128)(2,1)}, u32[]{:S(2)}) copy-start(bf16[1024,1024]{1,0:T(8,128)(2,1)} %get-tuple-element.53) | copy-start | bytes 6291460
  328.4 2.3 copy-start.5
  (8 other events, 10.6 us)
Sparse Core Ops, SparseCore 0:
  10.2 34.5 all-gather.4
  47.0 28.2 all-gather.6
  77.5 53.8 all-gather.8
  187.7 74.7 reduce-scatter.2
  264.6 45.3 reduce-scatter.4

commit v4 on v3

--- a/solution.py
+++ b/solution.py
@@ -178,6 +178,140 @@
     def drain(self, t):
         for kind, owner in enumerate((0, 0, 1, 2)):
             self.copy(kind, t, self.me ^ owner).wait_send()
+
+
+class Combine:
+    def __init__(self, send, recv, relay, me, send_sem, recv_sem, piece):
+        self.send, self.recv, self.relay, self.me = send, recv, relay, me
+        self.send_sem, self.recv_sem, self.piece = send_sem, recv_sem, piece
+        self.middle = send.shape[2] // 2
+
+    def rows(self, t):
+        return pl.ds(pl.multiple_of(t * self.piece, self.piece), self.piece)
+
+    def copy(self, kind, t):
+        rows, low, high = self.rows(t), pl.ds(0, self.middle), pl.ds(self.middle, self.middle)
+        source, target, to = (
+            (self.send.at[3, rows, low], self.relay.at[0, rows], 1),
+            (self.send.at[3, rows, high], self.relay.at[1, rows], 2),
+            (self.send.at[1, rows, low], self.recv.at[0, rows, low], 1),
+            (self.send.at[2, rows, high], self.recv.at[1, rows, high], 2),
+            (self.send.at[1, rows, high], self.recv.at[0, rows, high], 1),
+            (self.send.at[2, rows, low], self.recv.at[1, rows, low], 2),
+        )[kind]
+        return head_copy(
+            source, target, self.send_sem.at[kind, t], self.recv_sem.at[kind, t], self.me ^ to
+        )
+
+    def start(self, k, t):
+        if k == 3:
+            self.copy(0, t).start()
+            self.copy(1, t).start()
+        else:
+            self.copy(k + 1, t).start()
+
+    def combine(self, t):
+        rows = self.rows(t)
+        for k, at in ((1, pl.ds(self.middle, self.middle)), (2, pl.ds(0, self.middle))):
+            self.copy(2 - k, t).wait_recv()
+            both = self.send[k, rows, at].astype(f32) + self.relay[2 - k, rows, :].astype(f32)
+            self.send[k, rows, at] = both.astype(bf16)
+            self.copy(3 + k, t).start()
+
+    def collect(self, t):
+        for kind in range(2, 6):
+            self.copy(kind, t).wait_recv()
+        return self.total(self.rows(t))
+
+    def total(self, rows):
+        return (
+            self.send[0, rows, :].astype(f32)
+            + self.recv[0, rows, :].astype(f32)
+            + self.recv[1, rows, :].astype(f32)
+        )
+
+    def drain(self, t):
+        for kind in range(6):
+            self.copy(kind, t).wait_send()
+
+
+def sum_buffers(rows, width, pieces):
+    return [
+        pltpu.VMEM((4, rows, width), bf16),
+        pltpu.VMEM((2, rows, width), bf16),
+        pltpu.VMEM((2, rows, width // 2), bf16),
+        pltpu.SemaphoreType.DMA((6, pieces)),
+        pltpu.SemaphoreType.DMA((6, pieces)),
+        pltpu.SemaphoreType.DMA((4, pieces)),
+        pltpu.SemaphoreType.DMA((4, pieces)),
+    ]
+
+
+class GroupScatter:
+    def __init__(self, source, columns, core_recv, seq_send, seq_recv, sems):
+        self.source, self.columns = source, columns
+        self.core_recv, self.seq_send, self.seq_recv, self.sems = core_recv, seq_send, seq_recv, sems
+        self.place, self.core = lax.axis_index("seq"), lax.axis_index("batch")
+        self.places, self.shard = core_recv.shape[0], core_recv.shape[1]
+
+    def rows(self, k, core):
+        at = ((self.place ^ k) * 2 + core) * self.shard
+        return pl.ds(pl.multiple_of(at, self.shard), self.shard)
+
+    def core_copy(self, k):
+        return along(
+            "batch", self.source.at[self.rows(k, 1 - self.core), self.columns],
+            self.core_recv.at[k], self.sems.at[0, k], self.sems.at[1, k], 1 - self.core,
+        )
+
+    def seq_copy(self, k):
+        return along(
+            "seq", self.seq_send.at[k], self.seq_recv.at[k], self.sems.at[2, k],
+            self.sems.at[3, k], self.place ^ k,
+        )
+
+    def pass_on(self, k):
+        self.core_copy(k).wait_recv()
+        own = self.source[self.rows(k, self.core), self.columns].astype(f32)
+        self.seq_send[k] = (own + self.core_recv[k].astype(f32)).astype(bf16)
+
+        @pl.when(k > 0)
+        def _():
+            self.seq_copy(k).start()
+
+    def finish(self):
+        total = self.seq_send[0].astype(f32)
+        for k in range(1, self.places):
+            self.seq_copy(k).wait_recv()
+            total = total + self.seq_recv[k].astype(f32)
+        return total
+
+    def drain(self):
+        for k in range(self.places):
+            self.core_copy(k).wait_send()
+        for k in range(1, self.places):
+            self.seq_copy(k).wait_send()
+
+
+def scatter_buffers(places, shard, columns):
+    return [pltpu.VMEM((places, shard, columns), bf16)] * 3 + [
+        pltpu.SemaphoreType.DMA((4, places))
+    ]
+
+
+def greet_group(me, peers, places, cores):
+    barrier = pltpu.get_barrier_semaphore()
+    group = places * cores
+    flat = lax.axis_index("seq") * cores + lax.axis_index("batch")
+    for k in range(1, peers):
+        pl.semaphore_signal(barrier, inc=1, device_id={"head": me ^ k}, device_id_type=MESH)
+    for d in range(1, group):
+        to = lax.rem(flat + d, group)
+        pl.semaphore_signal(
+            barrier, inc=1, device_id={"seq": to // cores, "batch": lax.rem(to, cores)},
+            device_id_type=MESH,
+        )
+    pl.semaphore_wait(barrier, peers + group - 2)
 
 
 def anywhere():
@@ -395,8 +529,8 @@
     qkv_ref, inv_ref, s_ref, main_ref, halo_ref, rate_ref, conv_ref, hidden_ref, ffnp_hbm,
     dp_ref, dconv_ref, ddecay_ref, gg_ref, out_hbm,
     x_scr, g_scr, do_scr, own_scr, send, recv, tail_scr, halo_send, halo_recv,
-    parts, whole_out, send_sem, recv_sem, halo_send_sem, halo_recv_sem, own_sem, out_sem,
-    ss1, rs1, gather_send, gather_recv,
+    whole_out, send_sem, recv_sem, halo_send_sem, halo_recv_sem, load_sem, out_sem,
+    sent, got, relay, sum_send, sum_recv, gather_send, gather_recv,
 ):
     step = pl.program_id(0)
     chains = n_ref.shape[0]
@@ -411,15 +545,11 @@
     own_rows = hidden_ref.shape[0]
     subs = own_rows // SUB
 
-    def ffn_copy(k):
-        return head_copy(
-            part(ffnp_hbm, (me ^ k) * own_rows, own_rows), parts.at[k], ss1.at[k], rs1.at[k],
-            me ^ k,
-        )
-
-    def own_copy():
+    sums = Combine(sent, got, relay, me, sum_send, sum_recv, own_rows)
+
+    def ffn_load(k):
         return pltpu.make_async_copy(
-            part(ffnp_hbm, me * own_rows, own_rows), parts.at[0], own_sem.at[0]
+            part(ffnp_hbm, (me ^ k) * own_rows, own_rows), sent.at[k], load_sem.at[k]
         )
 
     ring = Spread(whole_out, own_rows, me, gather_send, gather_recv)
@@ -445,6 +575,8 @@
 
     @pl.when(step == 0)
     def _():
+        for k in range(peers):
+            ffn_load(k).start()
         barrier = pltpu.get_barrier_semaphore()
         for k in range(1, peers):
             pl.semaphore_signal(barrier, inc=1, device_id={"head": me ^ k}, device_id_type=MESH)
@@ -468,9 +600,10 @@
         def _():
             pl.semaphore_wait(barrier, peers - 1)
 
-        own_copy().start()
         for k in range(peers - 1, 0, -1):
-            ffn_copy(k).start()
+            ffn_load(k).wait()
+            sums.start(k, 0)
+        ffn_load(0).wait()
 
     @pl.when(step < chains)
     def _():
@@ -665,18 +798,20 @@
             send[chain] = earlier.astype(bf16)
             passed(chain).start()
 
+    @pl.when(step == chains - 1)
+    def _():
+        sums.combine(0)
+
     @pl.when(step == chains)
     def _():
-        own_copy().wait()
-        for k in range(1, peers):
-            ffn_copy(k).wait_recv()
+        for kind in range(2, 6):
+            sums.copy(kind, 0).wait_recv()
 
         def out_rows(t, carry):
             rows = pl.ds(pl.multiple_of(t * SUB, SUB), SUB)
-            value = hidden_ref[rows, :]
-            for k in range(peers):
-                value = value + parts[k, rows, :].astype(f32)
-            part(whole_out, me * own_rows + t * SUB, SUB)[...] = value.astype(bf16)
+            part(whole_out, me * own_rows + t * SUB, SUB)[...] = (
+                hidden_ref[rows, :] + sums.total(rows)
+            ).astype(bf16)
             return carry
 
         lax.fori_loop(0, subs, out_rows, 0)
@@ -716,8 +851,7 @@
             out_store(k).start()
         for k in range(peers):
             out_store(k).wait()
-        for k in range(1, peers):
-            ffn_copy(k).wait_send()
+        sums.drain(0)
         ring.drain(0)
 
 
@@ -788,14 +922,11 @@
             pltpu.VMEM((chains, HALO, QKV), f32),
             pltpu.VMEM((chains, 8, QKV), f32),
             pltpu.VMEM((chains, 8, QKV), f32),
-            pltpu.VMEM((peers, own_rows, width), bf16),
             pltpu.VMEM((rows, width), bf16),
             per_chain, per_chain, per_chain, per_chain,
-            pltpu.SemaphoreType.DMA((1,)),
-            per_peer, per_peer, per_peer,
-            pltpu.SemaphoreType.DMA((4, 1)),
-            pltpu.SemaphoreType.DMA((4, 1)),
-        ],
+            per_peer, per_peer,
+        ]
+        + sum_buffers(own_rows, width, 1),
         compiler_params=pltpu.CompilerParams(
             dimension_semantics=("arbitrary",), collective_id=4, has_side_effects=True,
             vmem_limit_bytes=52 * 2**20,
@@ -815,25 +946,6 @@
     return pl.ds(pl.multiple_of(t * SUB, SUB), SUB)
 
 
-class Summed:
-    def __init__(self, send, recv, me, send_sem, recv_sem):
-        self.send, self.recv, self.me = send, recv, me
-        self.send_sem, self.recv_sem = send_sem, recv_sem
-
-    def copy(self, k, t):
-        return head_copy(
-            self.send.at[k, rows_of(t)], self.recv.at[k, rows_of(t)], self.send_sem.at[k, t],
-            self.recv_sem.at[k, t], self.me ^ k,
-        )
-
-    def collect(self, t, peers):
-        total = self.send[0, rows_of(t), :].astype(f32)
-        for k in range(1, peers):
-            self.copy(k, t).wait_recv()
-            total = total + self.recv[k, rows_of(t), :].astype(f32)
-        return total
-
-
 def block_store(i, size, source, target, sem):
     return pltpu.make_async_copy(
         part(source, i * size, size), part(target, i * size, size), sem.at[i]
@@ -842,9 +954,9 @@
 
 def mixer_kernel(
     peers, nin_hbm, mixed_hbm, weights_hbm, x_hbm, gain_ref, o_gain_ref,
-    og_hbm, normed_hbm, nm_hbm, hidden_ref,
-    nin, mixed, weights, x_v, og_v, normed_v, send1, recv1, nm, in_sem, out_sem,
-    ss1, rs1, gather_send, gather_recv,
+    og_hbm, normed_hbm, nm_hbm, turned_hbm, hidden_ref,
+    nin, turned, mixed, weights, x_v, og_v, normed_v, nm, in_sem, out_sem,
+    send, recv, relay, sum_send, sum_recv, gather_send, gather_recv,
 ):
     me = lax.axis_index("head")
     total, width = nm.shape
@@ -862,10 +974,10 @@
     greet_heads(me, peers)
     for load in loads[:3]:
         load.wait()
-    sums = Summed(send1, recv1, me, ss1, rs1)
+    sums = Combine(send, recv, relay, me, sum_send, sum_recv, SUB)
 
     def project(i, carry):
-        k = peers - 1 - i
+        k = jnp.where(i == 0, peers - 1, lax.rem(i, peers - 1))
         owner = me ^ k
         rows = pl.ds(pl.multiple_of(owner * own_rows, own_rows), own_rows)
         og = mm(nin[rows, :], weights[:, 0:values])
@@ -878,24 +990,33 @@
             normed_v[rows, at] = (
                 own * inverse * o_gain_ref[0:1] * gated[:, first : first + DV]
             ).astype(bf16)
-        send1[k] = mm(normed_v[rows, :], weights[:, values:], NT).astype(bf16)
-
-        @pl.when(k > 0)
-        def _():
-            for t in range(subs):
-                sums.copy(k, t).start()
+        send[k] = mm(normed_v[rows, :], weights[:, values:], NT).astype(bf16)
+
+        for kk in range(1, peers):
+
+            @pl.when(k == kk)
+            def _():
+                for t in range(subs):
+                    sums.start(kk, t)
 
         block_store(owner, own_rows, og_v, og_hbm, out_sem.at[0]).start()
         block_store(owner, own_rows, normed_v, normed_hbm, out_sem.at[1]).start()
         return carry
 
     lax.fori_loop(0, peers, project, 0)
+    tile = 256
+    for first in range(0, width, tile):
+        turned[first : first + tile, :] = nin[:, first : first + tile].T
+    for t in range(subs):
+        sums.combine(t)
+    turned_store = pltpu.make_async_copy(turned, turned_hbm, in_sem.at[4])
+    turned_store.start()
     loads[3].wait()
     gain = gain_ref[...]
     ring = Spread(nm, own_rows, me, gather_send, gather_recv, SUB)
     for t in range(subs):
         rows = rows_of(t)
-        hidden = x_v[rows, :].astype(f32) + sums.collect(t, peers)
+        hidden = x_v[rows, :].astype(f32) + sums.collect(t)
         hidden_ref[rows, :] = hidden
         inverse = lax.rsqrt(jnp.mean(hidden * hidden, axis=1, keepdims=True) + epsilon)
         part(nm, me * own_rows + t * SUB, SUB)[...] = (hidden * inverse * gain).astype(bf16)
@@ -907,13 +1028,13 @@
             for t in range(subs):
                 ring.finish(t)
         block_store(me ^ k, own_rows, nm, nm_hbm, out_sem.at[2]).start()
+    turned_store.wait()
     for i in range(peers):
         block_store(i, own_rows, og_v, og_hbm, out_sem.at[0]).wait()
         block_store(i, own_rows, normed_v, normed_hbm, out_sem.at[1]).wait()
         block_store(i, own_rows, nm, nm_hbm, out_sem.at[2]).wait()
     for t in range(subs):
-        for k in range(1, peers):
-            sums.copy(k, t).wait_send()
+        sums.drain(t)
         ring.drain(t)
 
 
@@ -924,31 +1045,30 @@
     own_rows = total // peers
     subs = own_rows // SUB
     shape = jax.ShapeDtypeStruct
-    sems = pltpu.SemaphoreType.DMA((peers, subs))
     return pl.pallas_call(
         functools.partial(mixer_kernel, peers),
         in_specs=[anywhere()] * 4 + [vmem()] * 2,
-        out_specs=[anywhere()] * 3 + [vmem()],
+        out_specs=[anywhere()] * 4 + [vmem()],
         out_shape=[
             shape((total, values), f32),
             shape((total, values), bf16),
             shape((total, width), bf16),
+            shape((width, total), bf16),
             shape((own_rows, width), f32),
         ],
         scratch_shapes=[
             pltpu.VMEM((total, width), bf16),
+            pltpu.VMEM((width, total), bf16),
             pltpu.VMEM((total, values), f32),
             pltpu.VMEM((width, 2 * values), bf16),
             pltpu.VMEM((own_rows, width), bf16),
             pltpu.VMEM((total, values), f32),
             pltpu.VMEM((total, values), bf16),
-            pltpu.VMEM((peers, own_rows, width), bf16),
-            pltpu.VMEM((peers, own_rows, width), bf16),
             pltpu.VMEM((total, width), bf16),
-            pltpu.SemaphoreType.DMA((4,)),
+            pltpu.SemaphoreType.DMA((5,)),
             pltpu.SemaphoreType.DMA((3, peers)),
         ]
-        + [sems] * 4,
+        + sum_buffers(own_rows, width, subs),
         compiler_params=pltpu.CompilerParams(
             collective_id=1, has_side_effects=True, vmem_limit_bytes=48 * 2**20
         ),
@@ -957,10 +1077,11 @@
 
 
 def ffn_kernel(
-    peers, nm_hbm, ffn_hbm, ct_hbm, normed_hbm, weights_hbm, hidden_ref, gain_ref,
-    grads_hbm, ffnp_hbm, ng_hbm, hgrad_ref, gpart_ref,
-    nm, ffn_v, ct_v, normed_v, wout_v, act, dgu, send2, recv2, dm, ffnp_v, grads_v, ng_v,
-    in_sem, out_sem, ss, rs, gather_send, gather_recv,
+    peers, places, cores, nm_hbm, ffn_hbm, ct_hbm, normed_hbm, weights_hbm, hidden_ref, gain_ref,
+    grads_hbm, ffnp_hbm, ng_hbm, hgrad_ref, gpart_ref, down_ref,
+    nm, ffn_v, ct_v, normed_v, wout_v, act, dgu, dm, ffnp_v, grads_v, down_v, ng_v,
+    in_sem, out_sem, send, recv, relay, sum_send, sum_recv, gather_send, gather_recv,
+    core_recv, seq_send, seq_recv, scatter_sems,
 ):
     me = lax.axis_index("head")
     total, width = nm.shape
@@ -978,14 +1099,14 @@
     ]
     for load in loads:
         load.start()
-    greet_heads(me, peers)
+    greet_group(me, peers, places, cores)
     for load in loads[:3]:
         load.wait()
     gain = gain_ref[...]
-    sums = Summed(send2, recv2, me, ss, rs)
+    sums = Combine(send, recv, relay, me, sum_send, sum_recv, SUB)
 
     def feed_forward(i, carry):
-        k = lax.rem(i + peers - 1, peers)
+        k = jnp.where(i == 0, peers - 1, lax.rem(i, peers - 1))
         rows = pl.ds(pl.multiple_of((me ^ k) * own_rows, own_rows), own_rows)
 
         def cell_tile(j, carry):
@@ -1006,32 +1127,52 @@
 
         def mid_tile(j, carry):
             at = pl.ds(pl.multiple_of(j * tile, tile), tile)
-            send2[k, :, at] = mm(dgu[rows, :], ffn_v[at, 0 : 2 * cells], NT).astype(bf16)
+            send[k, :, at] = mm(dgu[rows, :], ffn_v[at, 0 : 2 * cells], NT).astype(bf16)
             return carry
 
         lax.fori_loop(0, width // tile, mid_tile, 0)
 
-        @pl.when(k > 0)
+        for kk in range(1, peers):
+
+            @pl.when(k == kk)
+            def _():
+                for t in range(subs):
+                    sums.start(kk, t)
+
+        @pl.when(k == 2)
         def _():
             for t in range(subs):
-                sums.copy(k, t).start()
+                sums.combine(t)
 
         return carry
 
     lax.fori_loop(0, peers, feed_forward, 0)
 
-    def ffn_rows(i, carry):
-        rows = pl.ds(pl.multiple_of(i * own_rows, own_rows), own_rows)
-        ffnp_v[rows, :] = mm(act[rows, :], ffn_v[:, 2 * cells :], NT).astype(bf16)
-        block_store(i, own_rows, ffnp_v, ffnp_hbm, out_sem.at[0]).start()
+    def down_grads(i, carry):
+        at = pl.ds(pl.multiple_of(i * tile, tile), tile)
+        down_v[at, :] = mm(ct_v[:, at], act[...], TN).astype(bf16)
         return carry
 
-    lax.fori_loop(0, peers, ffn_rows, 0)
+    lax.fori_loop(0, width // tile, down_grads, 0)
+    scatter = GroupScatter(down_v, pl.ds(0, cells), core_recv, seq_send, seq_recv, scatter_sems)
+    for k in range(places - 1, -1, -1):
+        scatter.core_copy(k).start()
+
+    def cell_grads(i, carry):
+        at = pl.ds(pl.multiple_of(i * tile, tile), tile)
+        grads_v[at, 0 : 2 * cells] = mm(nm[:, at], dgu[...], TN).astype(bf16)
+        return carry
+
+    half = width // tile // 2
+    lax.fori_loop(0, half, cell_grads, 0)
+    for k in range(places - 1, -1, -1):
+        scatter.pass_on(k)
+    lax.fori_loop(half, width // tile, cell_grads, 0)
     ring = Spread(dm, own_rows, me, gather_send, gather_recv, SUB)
     gain_part = jnp.zeros((1, width), f32)
     for t in range(subs):
         rows = rows_of(t)
-        dmid = sums.collect(t, peers)
+        dmid = sums.collect(t)
         hidden = hidden_ref[rows, :]
         inverse = lax.rsqrt(jnp.mean(hidden * hidden, axis=1, keepdims=True) + epsilon)
         scaled = hidden * inverse
@@ -1045,19 +1186,18 @@
         gain_part = gain_part + jnp.sum(dmid * scaled, axis=0, keepdims=True)
     gpart_ref[...] = jnp.broadcast_to(gain_part, gpart_ref.shape)
 
-    def cell_grads(i, carry):
-        at = pl.ds(pl.multiple_of(i * tile, tile), tile)
-        grads_v[at, 0 : 2 * cells] = mm(nm[:, at], dgu[...], TN).astype(bf16)
-        grads_v[at, 2 * cells : 3 * cells] = mm(ct_v[:, at], act[...], TN).astype(bf16)
+    def ffn_rows(i, carry):
+        rows = pl.ds(pl.multiple_of(i * own_rows, own_rows), own_rows)
+        ffnp_v[rows, :] = mm(act[rows, :], ffn_v[:, 2 * cells :], NT).astype(bf16)
+        block_store(i, own_rows, ffnp_v, ffnp_hbm, out_sem.at[0]).start()
         return carry
 
-    half = width // tile // 2
-    lax.fori_loop(0, half, cell_grads, 0)
+    lax.fori_loop(0, peers, ffn_rows, 0)
     loads[3].wait()
     loads[4].wait()
     for t in range(subs):
         ring.forward(t)
-    lax.fori_loop(half, width // tile, cell_grads, 0)
+    down_ref[...] = scatter.finish()
 
     def norm_rows(k, carry):
         owner = me ^ k
@@ -1076,7 +1216,7 @@
 
     def out_grads(i, carry):
         at = pl.ds(pl.multiple_of(i * tile, tile), tile)
-        grads_v[at, 3 * cells :] = mm(dm[:, at], normed_v[...], TN).astype(bf16)
+        grads_v[at, 2 * cells :] = mm(dm[:, at], normed_v[...], TN).astype(bf16)
         block_store(i, tile, grads_v, grads_hbm, out_sem.at[2]).start()
         return carry
 
@@ -1087,30 +1227,31 @@
     for i in range(width // tile):
         block_store(i, tile, grads_v, grads_hbm, out_sem.at[2]).wait()
     for t in range(subs):
-        for k in range(1, peers):
-            sums.copy(k, t).wait_send()
+        sums.drain(t)
         ring.drain(t)
+    scatter.drain()
 
 
 def feed_forward_block(nm, ffn_full, ct, normed, weights, hidden, gain):
-    peers = lax.axis_size("head")
+    peers, places, cores = lax.axis_size("head"), lax.axis_size("seq"), lax.axis_size("batch")
     total, width = ct.shape
     own_rows = total // peers
     subs = own_rows // SUB
     values = normed.shape[1]
     cells = ffn_full.shape[1] // 3
+    shard = width // (places * cores)
     shape = jax.ShapeDtypeStruct
-    sems = pltpu.SemaphoreType.DMA((peers, subs))
     return pl.pallas_call(
-        functools.partial(ffn_kernel, peers),
+        functools.partial(ffn_kernel, peers, places, cores),
         in_specs=[anywhere()] * 5 + [vmem()] * 2,
-        out_specs=[anywhere()] * 3 + [vmem()] * 2,
+        out_specs=[anywhere()] * 3 + [vmem()] * 3,
         out_shape=[
-            shape((width, 3 * cells + values), bf16),
+            shape((width, 2 * cells + values), bf16),
             shape((total, width), bf16),
             shape((total, values), f32),
             shape((own_rows, width), f32),
             shape((8, width), f32),
+            shape((shard, cells), f32),
         ],
         scratch_shapes=[
             pltpu.VMEM((total, width), bf16),
@@ -1120,16 +1261,16 @@
             pltpu.VMEM((width, values), bf16),
             pltpu.VMEM((total, cells), bf16),
             pltpu.VMEM((total, 2 * cells), bf16),
-            pltpu.VMEM((peers, own_rows, width), bf16),
-            pltpu.VMEM((peers, own_rows, width), bf16),
             pltpu.VMEM((total, width), bf16),
             pltpu.VMEM((total, width), bf16),
-            pltpu.VMEM((width, 3 * cells + values), bf16),
+            pltpu.VMEM((width, 2 * cells + values), bf16),
+            pltpu.VMEM((width, cells), bf16),
             pltpu.VMEM((total, values), f32),
             pltpu.SemaphoreType.DMA((5,)),
             pltpu.SemaphoreType.DMA((3, max(peers, width // 256))),
         ]
-        + [sems] * 4,
+        + sum_buffers(own_rows, width, subs)
+        + scatter_buffers(places, shard, cells),
         compiler_params=pltpu.CompilerParams(
             collective_id=5, has_side_effects=True, vmem_limit_bytes=56 * 2**20
         ),
@@ -1138,12 +1279,13 @@
 
 
 def input_grad_kernel(
-    peers, places, cores, dp_hbm, win_hbm, wog_hbm, x_hbm, hgrad_ref, gain_ref, gains_ref,
-    channels_ref,
-    out_hbm, gains_out, channels_out,
-    dp_v, win_v, wog_v, x_v, send1, recv1, whole, gains_v, gains_recv, gains_sum, gains_all,
-    channels_all, in_sem, out_sem, ss1, rs1, gather_send, gather_recv,
-    hs, hr, gs, gr, cs, cr,
+    peers, places, cores, heads, dp_hbm, win_hbm, wog_hbm, nin_hbm, x_hbm, hgrad_ref, gain_ref,
+    gains_ref, extras_ref,
+    out_hbm, gains_out, grad_out, small_out,
+    dp_v, win_v, wog_v, nin_v, x_v, whole, grads_v, gains_v, gains_recv, gains_sum, gains_all,
+    in_sem, out_sem,
+    send, recv, relay, sum_send, sum_recv, gather_send, gather_recv,
+    core_recv, seq_send, seq_recv, scatter_sems, hs, hr, gs, gr,
 ):
     me = lax.axis_index("head")
     place, core = lax.axis_index("seq"), lax.axis_index("batch")
@@ -1152,66 +1294,73 @@
     subs = own_rows // SUB
     values = wog_v.shape[1]
     conv_cols = win_v.shape[1] - PAD
+    cols = dp_v.shape[1]
     group = places * cores
+    pair = cores * (width // group)
     flat = place * cores + core
     loads = [
         pltpu.make_async_copy(dp_hbm, dp_v, in_sem.at[0]),
         pltpu.make_async_copy(win_hbm, win_v, in_sem.at[1]),
         pltpu.make_async_copy(wog_hbm.at[:, pl.ds(0, values)], wog_v, in_sem.at[2]),
-        pltpu.make_async_copy(part(x_hbm, me * own_rows, own_rows), x_v, in_sem.at[3]),
+        pltpu.make_async_copy(nin_hbm, nin_v, in_sem.at[3]),
+        pltpu.make_async_copy(part(x_hbm, me * own_rows, own_rows), x_v, in_sem.at[4]),
     ]
     for load in loads:
         load.start()
-
-    def to_group(d, source, target, send_sem, recv_sem):
-        to = lax.rem(flat + d, group)
-        return pltpu.make_async_remote_copy(
-            src_ref=source, dst_ref=target.at[d], send_sem=send_sem.at[d],
-            recv_sem=recv_sem.at[d], device_id={"seq": to // cores, "batch": lax.rem(to, cores)},
-            device_id_type=MESH,
-        )
-
-    barrier = pltpu.get_barrier_semaphore()
-    for k in range(1, peers):
-        pl.semaphore_signal(barrier, inc=1, device_id={"head": me ^ k}, device_id_type=MESH)
-    for d in range(1, group):
-        to = lax.rem(flat + d, group)
-        pl.semaphore_signal(
-            barrier, inc=1, device_id={"seq": to // cores, "batch": lax.rem(to, cores)},
-            device_id_type=MESH,
-        )
-    pl.semaphore_wait(barrier, peers + group - 2)
+    greet_group(me, peers, places, cores)
     for load in loads[:3]:
         load.wait()
-    sums = Summed(send1, recv1, me, ss1, rs1)
+    sums = Combine(send, recv, relay, me, sum_send, sum_recv, SUB)
 
     def project(i, carry):
-        k = peers - 1 - i
+        k = jnp.where(i == 0, peers - 1, lax.rem(i, peers - 1))
         rows = pl.ds(pl.multiple_of((me ^ k) * own_rows, own_rows), own_rows)
         partial = mm(dp_v[rows, 0:conv_cols], win_v[:, 0:conv_cols], NT)
         partial = partial + mm(
             dp_v[rows, conv_cols : conv_cols + values], wog_v[...], NT
         )
         partial = partial + mm(dp_v[rows, conv_cols + values :], win_v[:, conv_cols:], NT)
-        send1[k] = partial.astype(bf16)
-
-        @pl.when(k > 0)
+        send[k] = partial.astype(bf16)
+
+        for kk in range(1, peers):
+
+            @pl.when(k == kk)
+            def _():
+                for t in range(subs):
+                    sums.start(kk, t)
+
+        return carry
+
+    lax.fori_loop(0, peers - 1, project, 0)
+    loads[3].wait()
+    scatter = GroupScatter(grads_v, pl.ds(0, cols), core_recv, seq_send, seq_recv, scatter_sems)
+
+    def place_grads(i, carry):
+        k = places - 1 - i
+        rows = pl.ds(pl.multiple_of((place ^ k) * pair, pair), pair)
+        grads = mm(nin_v[rows, :], dp_v[...])
+        grads_v[rows, 0 : cols - PAD] = grads[:, : cols - PAD].astype(bf16)
+        grads_v[rows, cols - PAD :] = (grads[:, cols - PAD :] + extras_ref[rows, :]).astype(bf16)
+        scatter.core_copy(k).start()
+
+        @pl.when(i > 0)
         def _():
-            for t in range(subs):
-                sums.copy(k, t).start()
+            scatter.pass_on(jnp.minimum(k + 1, places - 1))
 
         return carry
 
-    lax.fori_loop(0, peers, project, 0)
-    for d in range(1, group):
-        to_group(d, channels_ref, channels_all, cs, cr).start()
-    loads[3].wait()
+    lax.fori_loop(0, places, place_grads, 0)
+    scatter.pass_on(0)
+    for t in range(subs):
+        sums.combine(t)
+    project(peers - 1, 0)
+    loads[4].wait()
     gain = gain_ref[...]
     ring = Spread(whole, own_rows, me, gather_send, gather_recv, SUB)
     gain_part = jnp.zeros((1, width), f32)
     for t in range(subs):
         rows = rows_of(t)
-        din = sums.collect(t, peers)
+        din = sums.collect(t)
         x = x_v[rows, :].astype(f32)
         inverse = lax.rsqrt(jnp.mean(x * x, axis=1, keepdims=True) + epsilon)
         scaled = x * inverse
@@ -1222,11 +1371,19 @@
         part(whole, me * own_rows + t * SUB, SUB)[...] = grad.astype(bf16)
         ring.start(t)
         gain_part = gain_part + jnp.sum(din * scaled, axis=0, keepdims=True)
-    row8 = lax.broadcasted_iota(jnp.int32, (8, width), 0)
-    gains_v[...] = jnp.where(row8 == 0, gain_part, gains_ref[...])
+    gains_v[...] = gains_ref[...]
+    for r in range(width // 128):
+        gains_v[r : r + 1, :] = gain_part[:, r * 128 : (r + 1) * 128]
 
     def gains_copy(k):
         return head_copy(gains_v, gains_recv.at[k], hs.at[k], hr.at[k], me ^ k)
+
+    def to_group(d):
+        to = lax.rem(flat + d, group)
+        return pltpu.make_async_remote_copy(
+            src_ref=gains_sum, dst_ref=gains_all.at[d], send_sem=gs.at[d], recv_sem=gr.at[d],
+            device_id={"seq": to // cores, "batch": lax.rem(to, cores)}, device_id_type=MESH,
+        )
 
     for k in range(1, peers):
         gains_copy(k).start()
@@ -1237,37 +1394,38 @@
         gathered = gathered + gains_recv[k]
     gains_sum[...] = gathered
     for d in range(1, group):
-        to_group(d, gains_sum, gains_all, gs, gr).start()
+        to_group(d).start()
     for t in range(subs):
         ring.forward(t)
     block_store(me ^ 1, own_rows, whole, out_hbm, out_sem).start()
     block_store(me ^ 2, own_rows, whole, out_hbm, out_sem).start()
-    channels = channels_ref[...]
     for d in range(1, group):
-        to_group(d, channels_ref, channels_all, cs, cr).wait_recv()
-        channels = channels + channels_all[d]
-    channels_out[...] = channels
-    for d in range(1, group):
-        to_group(d, gains_sum, gains_all, gs, gr).wait_recv()
+        to_group(d).wait_recv()
         gathered = gathered + gains_all[d]
     gains_out[...] = gathered
     for t in range(subs):
         ring.finish(t)
     block_store(me ^ 3, own_rows, whole, out_hbm, out_sem).start()
+    grad = scatter.finish()
+    for head in range(heads):
+        at = head * (QKV + DV)
+        grad_out[:, at : at + QKV] = grad[:, head * QKV : (head + 1) * QKV]
+        gate_at = conv_cols + head * DV
+        grad_out[:, at + QKV : at + QKV + DV] = grad[:, gate_at : gate_at + DV]
+    small_out[...] = grad[:, conv_cols + values :]
     for k in range(peers):
         block_store(k, own_rows, whole, out_hbm, out_sem).wait()
     for t in range(subs):
-        for k in range(1, peers):
-            sums.copy(k, t).wait_send()
+        sums.drain(t)
         ring.drain(t)
     for k in range(1, peers):
         gains_copy(k).wait_send()
+    scatter.drain()
     for d in range(1, group):
-        to_group(d, channels_ref, channels_all, cs, cr).wait_send()
-        to_group(d, gains_sum, gains_all, gs, gr).wait_send()
-
-
-def input_grads(dp, in_full, gate_full, x, hgrad, gain, gains, channels):
+        to_group(d).wait_send()
+
+
+def input_grads(dp, in_full, gate_full, nin, x, hgrad, gain, gains, extras, heads):
     peers, places, cores = lax.axis_size("head"), lax.axis_size("seq"), lax.axis_size("batch")
     group = places * cores
     total, width = x.shape
@@ -1275,41 +1433,65 @@
     values = gate_full.shape[1] // 2
     own_rows = total // peers
     subs = own_rows // SUB
+    shard = width // group
     shape = jax.ShapeDtypeStruct
-    sems = pltpu.SemaphoreType.DMA((peers, subs))
     per_peer = pltpu.SemaphoreType.DMA((peers,))
     per_member = pltpu.SemaphoreType.DMA((group,))
     return pl.pallas_call(
-        functools.partial(input_grad_kernel, peers, places, cores),
-        in_specs=[anywhere()] * 4 + [vmem()] * 4,
-        out_specs=[anywhere(), vmem(), vmem()],
+        functools.partial(input_grad_kernel, peers, places, cores, heads),
+        in_specs=[anywhere()] * 5 + [vmem()] * 4,
+        out_specs=[anywhere()] + [vmem()] * 3,
         out_shape=[
-            shape((total, width), bf16), shape(gains.shape, f32), shape(channels.shape, f32),
+            shape((total, width), bf16), shape(gains.shape, f32),
+            shape((shard, cols - PAD), f32), shape((shard, PAD), f32),
         ],
         scratch_shapes=[
             pltpu.VMEM((total, cols), bf16),
             pltpu.VMEM((width, cols - values), bf16),
             pltpu.VMEM((width, values), bf16),
+            pltpu.VMEM((width, total), bf16),
             pltpu.VMEM((own_rows, width), bf16),
-            pltpu.VMEM((peers, own_rows, width), bf16),
-            pltpu.VMEM((peers, own_rows, width), bf16),
             pltpu.VMEM((total, width), bf16),
+            pltpu.VMEM((width, cols), bf16),
             pltpu.VMEM(gains.shape, f32),
             pltpu.VMEM((peers,) + gains.shape, f32),
             pltpu.VMEM(gains.shape, f32),
             pltpu.VMEM((group,) + gains.shape, f32),
-            pltpu.VMEM((group,) + channels.shape, f32),
-            pltpu.SemaphoreType.DMA((4,)),
+            pltpu.SemaphoreType.DMA((5,)),
             pltpu.SemaphoreType.DMA((peers,)),
         ]
-        + [sems] * 4
+        + sum_buffers(own_rows, width, subs)
+        + scatter_buffers(places, shard, cols)
         + [per_peer] * 2
-        + [per_member] * 4,
+        + [per_member] * 2,
         compiler_params=pltpu.CompilerParams(
-            collective_id=2, has_side_effects=True, vmem_limit_bytes=48 * 2**20
+            collective_id=2, has_side_effects=True, vmem_limit_bytes=52 * 2**20
         ),
         name="input_grads",
-    )(dp, in_full, gate_full, x, hgrad, gain, gains, channels)
+    )(dp, in_full, gate_full, nin, x, hgrad, gain, gains, extras)
+
+
+def late_kernel(units, cells, late_ref, down_in, gate_ref, up_ref, down_ref, out_ref):
+    gate_ref[...] = late_ref[:, 0:units].astype(f32)
+    up_ref[...] = late_ref[:, cells : cells + units].astype(f32)
+    down_ref[...] = down_in[...].T[0:units]
+    out_ref[...] = late_ref[:, 2 * cells :].astype(f32).T
+
+
+def late_outputs(late, down, units, cells):
+    shard = late.shape[0]
+    values = late.shape[1] - 2 * cells
+    shape = jax.ShapeDtypeStruct
+    return pl.pallas_call(
+        functools.partial(late_kernel, units, cells),
+        in_specs=[vmem()] * 2,
+        out_specs=[vmem()] * 4,
+        out_shape=[
+            shape((shard, units), f32), shape((shard, units), f32), shape((units, shard), f32),
+            shape((values, shard), f32),
+        ],
+        name="late_outputs",
+    )(late, down)
 
 
 def shifted(shard, axis, by):
@@ -1390,10 +1572,10 @@
     qkv, inv, n, qe, tot, trans, states, mixed = forward_rule(
         starts, decay_par, projected, halo, conv_full, seqs, heads
     )
-    og, normed, nm, hidden = mixer(
+    og, normed, nm, turned_in, hidden = mixer(
         normed_in, mixed, gate_full, x, ffn_gain_f, o_gain_full
     )
-    late_grads, ffn_part, normed_grad, hidden_grad, ffn_gain_part = feed_forward_block(
+    late_grads, ffn_part, normed_grad, hidden_grad, ffn_gain_part, down_own = feed_forward_block(
         nm, ffn_full, ct, normed, gate_full, hidden, ffn_gain_f
     )
     late_own = lax.psum_scatter(late_grads, ALL, scatter_dimension=0, tiled=True)
@@ -1401,60 +1583,55 @@
         starts, decay_par, normed_grad, mixed, og, projected, o_gain_full, n, qe, tot, trans, qkv,
         inv, states, halo, conv_full, hidden, ffn_part, seqs, heads,
     )
-    in_grad = matmul(normed_in, projected_grad, TN).astype(bf16)
-    in_grad, late_own = lax.optimization_barrier((in_grad, late_own))
-    in_own = lax.psum_scatter(in_grad, ALL, scatter_dimension=0, tiled=True)
-
+    taps = CONV * heads
+    per_shard = taps * QKV // shards
+    conv_at = 2 * heads
+    conv_end = conv_at + per_shard // shard
     onorm_grad = jnp.sum(onorm_grads[:, 0], axis=0)
-    decay_part = jnp.sum(ddecay[:, :2, 0].reshape(heads, seqs, 2), axis=1).T
+    decay_part = jnp.sum(ddecay[:, :2, 0].reshape(heads, seqs, 2), axis=1).T.reshape(1, 1, -1)
     conv_grad = jnp.sum(dconv.reshape(heads, seqs, CONV, QKV), axis=1).transpose(1, 0, 2)
+    conv_grad = conv_grad.reshape(taps, shards, -1).transpose(1, 0, 2).reshape(shards, -1, shard)
+    decay_part = jnp.pad(decay_part, ((0, 0), (0, 0), (0, shard - 2 * heads)))
+    extras = jnp.concatenate(
+        [
+            jnp.zeros((shards, conv_at, shard), f32),
+            conv_grad,
+            jnp.broadcast_to(decay_part, (shards, 1, shard)),
+            jnp.zeros((shards, PAD - conv_end - 1, shard), f32),
+        ],
+        axis=1,
+    ).transpose(0, 2, 1).reshape(width, PAD)
+    lane_rows = width // 128
     gains = jnp.concatenate(
         [
-            jnp.zeros((1, width), f32),
-            ffn_gain_part[:1],
-            jnp.pad(onorm_grad, (0, width - DV))[None],
-            jnp.zeros((5, width), f32),
+            jnp.zeros((lane_rows, 128), f32),
+            ffn_gain_part[0].reshape(lane_rows, 128),
+            jnp.pad(onorm_grad, (0, width - DV)).reshape(lane_rows, 128),
         ]
     )
-    taps = CONV * heads
-    channels = jnp.concatenate(
-        [
-            conv_grad.reshape(taps, QKV),
-            jnp.pad(decay_part.reshape(1, 2 * heads), ((0, 7), (0, QKV - 2 * heads))),
-        ]
+    input_grad, gains, in_main, in_small = input_grads(
+        projected_grad, in_full, gate_full, turned_in, x, hidden_grad, attn_gain_f, gains, extras,
+        heads,
     )
-    input_grad, gains, channels = input_grads(
-        projected_grad, in_full, gate_full, x, hidden_grad, attn_gain_f, gains, channels
-    )
+    grad_gate, grad_up, grad_down, grad_out = late_outputs(late_own, down_own, units, cells)
     at = lax.axis_index(ALL)
+    gains = gains.reshape(3, width)
     own_gains = lax.dynamic_slice(gains, (0, at * shard), (2, shard))
     onorm_own = lax.dynamic_slice(gains, (2, at * (DV // shards)), (1, DV // shards))
-    conv_own = lax.dynamic_slice(
-        channels, (0, at * (QKV // shards)), (taps, QKV // shards)
-    ).reshape(CONV, heads, -1)
-    in_own = in_own.astype(f32)
-    late_own = late_own.astype(f32)
-    in_main = jnp.concatenate(
-        [
-            in_own[:, :conv_cols].reshape(shard, heads, QKV),
-            in_own[:, conv_cols : conv_cols + value_cols].reshape(shard, heads, DV),
-        ],
-        axis=2,
-    )
-    rates_at = conv_cols + value_cols
+    small_rows = in_small.T
     return (
         result.reshape(tokens.shape),
         input_grad.reshape(tokens.shape),
         own_gains[0],
-        in_main,
-        in_own[:, rates_at : rates_at + 2 * heads].reshape(shard, heads, 2),
-        conv_own,
-        channels[taps, : 2 * heads].reshape(2, heads),
+        in_main.reshape(shard, heads, QKV + DV),
+        in_small[:, : 2 * heads].reshape(shard, heads, 2),
+        small_rows[conv_at:conv_end].reshape(CONV, heads, -1),
+        small_rows[conv_end, : 2 * heads].reshape(2, heads),
         onorm_own[0],
-        late_own[:, 3 * cells :].T.reshape(heads, DV, -1),
+        grad_out.reshape(heads, DV, -1),
         own_gains[1],
-        late_own[:, : 2 * cells].reshape(shard, 2, cells)[:, :, :units],
-        late_own[:, 2 * cells : 2 * cells + units].T,
+        jnp.stack([grad_gate, grad_up], axis=1),
+        grad_down,
     )
 
 

time: 339 us -> 312 us (0.920)
  Pallas kernels: 235 us -> 227 us
  local copies, waits for them, and re-layouts: 27.7 us -> 20.1 us
  matrix products: 16.2 us -> 8.63 us
  waiting for transfers between devices: 19.2 us -> 15 us
    reduce_scatter x1, waiting for transfers between devices: 9.57 us -> 0.01 us  [per_device(): lax.psum_scatter(late_grads, ALL, scatter_dimension=0, tiled=True)]
    dot_general x3 -> x2, matrix products: 16.2 us -> 8.63 us  [matmul(): return lax.dot_general(a, b, (dims, ((), ())), preferred_element_type=f32)]
    pallas_call x1, Pallas kernels: 47.6 us -> 41.1 us  [mixer(): pl.pallas_call(functools.partial(mixer_kernel, peers), in_specs=[anywhere...]
    slice x10 -> x6, local copies, waits for them, and re-layouts: 7.46 us -> 1.77 us  [the longest x1 0.76 us: per_device(): ffn_gain_part[0].reshape(lane_rows, 128)]
    all_gather x1, waiting for transfers between devices: 0.01 us -> 5.39 us  [per_device(): ffn_full = lax.all_gather(packed_ffn, ALL, axis=0, tiled=True)]
    pallas_call x1, Pallas kernels: 57.7 us -> 54.2 us  [backward_rule(): pl.pallas_call(functools.partial(backward_kernel, seqs, places, peers), g...]
    pallas_call x2 -> x3, Pallas kernels: 104 us -> 106 us  [the longest x1 52.1 us: feed_forward_block(): pl.pallas_call(functools.partial(ffn_kernel, peers, places, cores), in_sp...]
    unnamed x60 -> x50, local copies, waits for them, and re-layouts: 12.9 us -> 11.6 us
  transfers between devices with their start and end apart: 6 -> 5, of which waited for: 2 -> 2; matrix products, arithmetic and copies ran while one was open for 9% -> 7% of each run, Pallas kernels for 53% -> 55%
where the time goes in v4:
time: 312 us; the launch traced here: 311 us
  Pallas kernels  227 us (73%)
  local copies, waits for them, and re-layouts  20.1 us (6%)
  waiting for transfers between devices  15 us (5%)
  blocking collectives  14.5 us (5%)
  between operations  14.3 us (5%)
  matrix products  8.63 us (3%)
  other arithmetic  6.51 us (2%)
  starting transfers between devices  5.08 us (2%)
    pallas_call x1, Pallas kernels, backward_rule(): pl.pallas_call(functools.partial(backward_kernel, seqs, places, peers), g...  54.2 us
    pallas_call x1, Pallas kernels, feed_forward_block(): pl.pallas_call(functools.partial(ffn_kernel, peers, places, cores), in_sp...  52.1 us
    pallas_call x1, Pallas kernels, input_grads(): pl.pallas_call(functools.partial(input_grad_kernel, peers, places, cores,...  51.5 us
    pallas_call x1, Pallas kernels, mixer(): pl.pallas_call(functools.partial(mixer_kernel, peers), in_specs=[anywhere...  41.1 us
    pallas_call x1, Pallas kernels, forward_rule(): pl.pallas_call(functools.partial(forward_kernel, seqs, places), grid=(2 *...  25.9 us
    all_gather x1, blocking collectives, per_device(): small_full = lax.all_gather(small, ALL, axis=0)  14.5 us
    unnamed x50, local copies, waits for them, and re-layouts  11.6 us
    all_gather x1, waiting for transfers between devices, per_device(): in_full = lax.all_gather(packed_in, ALL, axis=0, tiled=True)  9.52 us
  transfers between devices with their start and end apart: 5, of which 2 were waited for; matrix products, arithmetic and copies ran while one was open for 7% of the time, Pallas kernels for 55%

profile of v4, /device:TPU:0, one launch (start us, length us, event | category | flops | bytes accessed | tf_op | source)
XLA Modules:
  0.0 311.2 jit_solution(15702707482893941390)
XLA Ops:
  7.2 1.4 convert.54
  11.3 1.1 copy.57
  12.8 4.9 %collective-permute-start = (bf16[2,16,1024]{2,1,0:T(8,128)(2,1)S(1)}, bf16[2,16,1024]{2,1,0:T(8,128)(2,1)S(1)}, u32[]{:S(2)}, u32[]{:S(2)}) collective-permute-start(bf16[2,16,1024]{2,1,0:T(8,128)(2,1)S(1)} %slice.55), channel_id=1, source_target_pairs={{0,8},{8,16},{16,24},{1,9},{9,17},{17,25},{2,10},{10,18},{18,26},{... | collective-permute-start | bytes 196616 | tf_op jit(solution)/shard_map/ppermute | solution.py:1500
  17.9 14.5 %all-gather = bf16[8,1,800]{2,1,0:T(2,128)(2,1)S(1)} all-gather(bf16[1,1,800]{2,1,0:T(2,128)(2,1)S(1)} %maximum_bitcast_fusion), channel_id=1, replica_groups=mesh['seq'=4,'batch'=2,'head'=4] {'seq','batch'}, dimensions={0}, use_global_device_ids=true | all-gather | bytes 14400 | tf_op jit(solution)/shard_map/all_gather | solution.py:1550
  33.0 1.9 multiply_convert_fusion.nin_hbm
  35.3 9.5 %all-gather.5.cloned.1.call-done.win_hbm = bf16[1024,1152]{1,0:T(8,128)(2,1)} async-done(((bf16[128,1152]{1,0:T(8,128)(2,1)}), bf16[1024,1152]{1,0:T(8,128)(2,1)}) %all-gather.5.cloned.1.call-update) | async-done | bytes 2359312 | tf_op jit(solution)/shard_map/all_gather | solution.py:1549
  44.8 2.2 fusion.halo_ref
  47.1 6.4 %fusion.11.main_ref.rate_ref = f32[1024,1152]{1,0:T(8,128)} fusion(bf16[1024,1024]{1,0:T(8,128)(2,1)S(1)} %copy-done.10, bf16[1024,1152]{1,0:T(8,128)(2,1)} %all-gather.5.cloned.1.call-done.win_hbm), kind=kOutput, calls=%fused_computation.42 | convolution fusion | flops 2415919104 | bytes 9175040 | tf_op jit(solution)/shard_map/dot_general | solution.py:1508
  53.5 25.9 %forward_rule.1 = (bf16[1024,1024]{1,0:T(8,128)(2,1)S(1)}, bf16[4,4,128,128]{3,2,1,0:T(8,128)(2,1)S(1)}, bf16[4,4,128,128]{3,2,1,0:T(8,128)(2,1)S(1)}, bf16[4,4,...) custom-call(s32[2]{0:T(128)S(1)} %copy-done.7, ...), custom_call_target="tpu_custom_call" | custom-call | tf_op jit(solution)/shard_map/forward_rule/pallas_call | solution.py:477
  79.4 1.3 copy-done.1
  81.7 41.1 %mixer.1 = (f32[1024,512]{1,0:T(8,128)S(1)}, bf16[1024,512]{1,0:T(8,128)(2,1)S(1)}, bf16[1024,1024]{1,0:T(8,128)(2,1)}, bf16[1024,1024]{1,0:T(8,128)(2,1)}, f32[256,1024]{1,0:T(8,128)S(1)}) custom-call(bf16[1024,1024]{1,0:T(8,128)(2,1)} %multiply_convert_fusion.nin_hbm, f32[1024,512]{1,0:T(8,128)} %get-tuple-element.44.mixed_hbm.mixed_ref, ...), custom_call_target="tpu_custom_call" | custom-call | tf_op jit(solution)/shard_map/mixer/pallas_call | solution.py:1048
  123.8 1.3 copy-done.2
  125.1 1.0 copy-done.4
  126.1 5.4 %all-gather.9.cloned.1.call-done.ffn_hbm = bf16[1024,2304]{1,0:T(8,128)(2,1)} async-done(((bf16[128,2304]{1,0:T(8,128)(2,1)}), bf16[1024,2304]{1,0:T(8,128)(2,1)}) %all-gather.9.cloned.1.call-update) | async-done | bytes 4718608 | tf_op jit(solution)/shard_map/all_gather | solution.py:1552
  131.5 52.1 %feed_forward.1 = (bf16[1024,2048]{1,0:T(8,128)(2,1)}, bf16[1024,1024]{1,0:T(8,128)(2,1)}, f32[1024,512]{1,0:T(8,128)}, f32[256,1024]{1,0:T(8,128)}, f32[8,1024]{1,0:T(8,128)}, /*index=5*/f32[128,768]{1,0:T(8,128)}) custom-call(bf16[1024,1024]{1,0:T(8,128)(2,1)} %get-tuple-element.45.nm_hbm, bf16[1024,2304]{1,0:T(8,128)(2,1)} %all-gather.9.cloned.1.call-done.ffn_hbm, ...), custom_call_target="tpu_custom_call" | custom-call | tf_op jit(solution)/shard_map/feed_forward/pallas_call | solution.py:1244
  183.7 54.2 %backward_rule.1 = (bf16[1024,1664]{1,0:T(8,128)(2,1)}, f32[4,4,512]{2,1,0:T(4,128)S(1)}, f32[4,8,128]{2,1,0:T(8,128)S(1)}, f32[4,8,256]{2,1,0:T(8,128)S(1)}, bf16[1024,1024]{1,0:T(8,128)(2,1)}) custom-call(s32[2]{0:T(128)S(1)} %copy-done.7, f32[2,2]{1,0:T(2,128)S(1)} %copy-done.6, f32[1024,512]{1,0:T(8,128)} %get-tuple-element.48.dn_ref, ...), custom_call_target="tpu_custom_call" | custom-call | tf_op jit(solution)/shard_map/backward_rule/pallas_call | solution.py:877
  240.1 51.5 %input_grads.1 = (bf16[1024,1024]{1,0:T(8,128)(2,1)}, f32[24,128]{1,0:T(8,128)S(1)}, f32[128,1536]{1,0:T(8,128)S(1)}, f32[128,128]{1,0:T(8,128)S(1)}) custom-call(bf16[1024,1664]{1,0:T(8,128)(2,1)} %get-tuple-element.59.dp_hbm, bf16[1024,1152]{1,0:T(8,128)(2,1)} %all-gather.5.cloned.1.call-done.win_hbm, ...), custom_call_target="tpu_custom_call" | custom-call | tf_op jit(solution)/shard_map/input_grads/pallas_call | solution.py:1440
  291.6 1.4 reshape.262
  296.4 2.4 late_outputs.1
  298.7 1.2 pad_maximum_fusion
  299.9 1.1 copy.64
  301.0 1.3 copy.76
  302.4 1.0 copy-done.12
  303.4 1.3 copy.77
  (115 shorter events, 11.5 us)
Async XLA Ops:
  7.2 1.8 copy-start.17
  7.2 2.9 copy-start.15
  7.2 37.6 %all-gather.5.cloned.1.call-start = ((), (), s32[]{:S(2)}) async-start(), calls=%async_computation.1 | async-start | bytes 2654208 | tf_op jit(solution)/shard_map/all_gather | solution.py:1549
  8.7 2.5 copy-start.13
  8.9 2.3 copy-start.14
  9.9 71.7 %all-gather.7.cloned.1.call-start = ((), (), s32[]{:S(2)}) async-start(), calls=%async_computation.2 | async-start | bytes 2359296 | tf_op jit(solution)/shard_map/all_gather | solution.py:1551
  11.0 1.8 copy-start.8
  11.0 6.7 %copy-start.16 = (f32[4,2,64]{2,1,0:T(2,128)S(1)}, f32[4,2,64]{2,1,0:T(2,128)}, u32[]{:S(2)}) copy-start(f32[4,2,64]{2,1,0:T(2,128)} %param.18) | copy-start | bytes 6148
  11.1 6.8 %copy-start.20 = (f32[32]{0:T(128)S(1)}, f32[32]{0:T(128)}, u32[]{:S(2)}) copy-start(f32[32]{0:T(128)} %param.20) | copy-start | bytes 388
  11.1 6.8 %copy-start.18 = (f32[128]{0:T(128)S(1)}, f32[128]{0:T(128)}, u32[]{:S(2)}) copy-start(f32[128]{0:T(128)} %param.22) | copy-start | bytes 1540
  11.1 6.8 %copy-start.19 = (f32[128]{0:T(128)S(1)}, f32[128]{0:T(128)}, u32[]{:S(2)}) copy-start(f32[128]{0:T(128)} %param.15) | copy-start | bytes 1540
  11.1 120.4 %all-gather.9.cloned.1.call-start = ((), (), s32[]{:S(2)}) async-start(), calls=%async_computation.3 | async-start | bytes 5308416 | tf_op jit(solution)/shard_map/all_gather | solution.py:1552
  12.4 284.0 %reduce-scatter.2.cloned.1.call-start = ((), (), s32[]{:S(2)}) async-start(), calls=%async_computation.4 | async-start | bytes 4718592 | tf_op jit(solution)/shard_map/reduce_scatter | solution.py:1581
  12.8 22.3 %collective-permute-start = (bf16[2,16,1024]{2,1,0:T(8,128)(2,1)S(1)}, bf16[2,16,1024]{2,1,0:T(8,128)(2,1)S(1)}, u32[]{:S(2)}, u32[]{:S(2)}) collective-permute-start(bf16[2,16,1024]{2,1,0:T(8,128)(2,1)S(1)} %slice.55), channel_id=1, source_target_pairs={{0,8},{8,16},{16,24},{1,9},{9,17},{17,25},{2,10},{10,18},{18,26},{... | collective-permute-start | bytes 196616 | tf_op jit(solution)/shard_map/ppermute | solution.py:1500
  17.9 15.1 %copy-start.9 = (bf16[2,512,1024]{2,1,0:T(8,128)(2,1)S(1)}, bf16[2,512,1024]{2,1,0:T(8,128)(2,1)}, u32[]{:S(2)}) copy-start(bf16[2,512,1024]{2,1,0:T(8,128)(2,1)} %param.13) | copy-start | bytes 6291460
  33.0 48.7 %copy-start.5 = (f32[8,128]{1,0:T(8,128)}, f32[8,128]{1,0:T(8,128)S(1)}, u32[]{:S(2)}) copy-start(f32[8,128]{1,0:T(8,128)S(1)} %get-tuple-element.126) | copy-start | bytes 12292
  44.8 2.2 copy-start.10
  47.1 6.4 %copy-start.6 = (f32[2,2]{1,0:T(2,128)S(1)}, f32[2,2]{1,0:T(2,128)}, u32[]{:S(2)}) copy-start(f32[2,2]{1,0:T(2,128)} %decay_ref.3) | copy-start | bytes 52
  47.1 6.4 %copy-start.7 = (s32[2]{0:T(128)S(1)}, s32[2]{0:T(128)}, u32[]{:S(2)}) copy-start(s32[2]{0:T(128)} %start_ref.3) | copy-start | bytes 28
  79.4 1.3 copy-start.1
  122.8 1.0 copy-start
  123.7 1.3 copy-start.2
  293.1 8.0 %copy-start.11 = (bf16[1024,1024]{1,0:T(8,128)(2,1)S(1)}, bf16[1024,1024]{1,0:T(8,128)(2,1)}, u32[]{:S(2)}) copy-start(bf16[1024,1024]{1,0:T(8,128)(2,1)} %get-tuple-element.58) | copy-start | bytes 6291460
  301.0 2.3 copy-start.12
  (2 other events, 2.0 us)
Sparse Core Ops, SparseCore 0:
  10.2 34.5 all-gather.4
  47.0 28.2 all-gather.6
  77.5 53.8 all-gather.8
  183.7 55.9 reduce-scatter.1

commit v5 on v4

--- a/solution.py
+++ b/solution.py
@@ -143,18 +143,59 @@
     return ref.at[pl.ds(pl.multiple_of(start, size), size)]
 
 
+def piece_rows(owner, t, total, subs):
+    return pl.ds(pl.multiple_of(t * (total // subs) + owner * SUB, SUB), SUB)
+
+
+def take(ref, owner, subs):
+    total = ref.shape[0]
+    return jnp.concatenate(
+        [ref[piece_rows(owner, t, total, subs), :] for t in range(subs)], axis=0
+    )
+
+
+class Pieces:
+    def __init__(self, source, target, total, subs, sems):
+        self.source, self.target, self.total, self.subs, self.sems = source, target, total, subs, sems
+
+    def at(self, ref, owner, t):
+        rows = piece_rows(owner, t, self.total, self.subs)
+        if ref.shape[0] != self.total:
+            rows = pl.ds(t * SUB, SUB)
+        return ref.at[rows]
+
+    def copies(self, owner):
+        return [
+            pltpu.make_async_copy(
+                self.at(self.source, owner, t), self.at(self.target, owner, t),
+                self.sems.at[owner, t],
+            )
+            for t in range(self.subs)
+        ]
+
+    def start(self, owner):
+        for copy in self.copies(owner):
+            copy.start()
+
+    def wait(self, owner):
+        for copy in self.copies(owner):
+            copy.wait()
+
+
 class Spread:
-    def __init__(self, buffer, size, me, send_sem, recv_sem, piece=None):
-        self.buffer, self.size, self.me = buffer, size, me
-        self.piece = size if piece is None else piece
+    def __init__(self, buffer, subs, me, send_sem, recv_sem):
+        self.buffer, self.subs, self.me = buffer, subs, me
         self.send_sem, self.recv_sem = send_sem, recv_sem
 
     def region(self, owner, t, half):
-        rows = pl.ds(pl.multiple_of(owner * self.size + t * self.piece, self.piece), self.piece)
+        rows = piece_rows(owner, t, self.buffer.shape[0], self.subs)
         middle = self.buffer.shape[1] // 2
         if half is None:
             return self.buffer.at[rows]
         return self.buffer.at[rows, pl.ds(half * middle, middle)]
+
+    def put(self, t, value):
+        self.buffer[piece_rows(self.me, t, self.buffer.shape[0], self.subs), :] = value
 
     def copy(self, kind, t, owner):
         at = self.region(owner, t, None if kind < 2 else kind - 2)
@@ -293,6 +334,101 @@
             self.seq_copy(k).wait_send()
 
 
+class LineScatter:
+    def __init__(self, own, core_recv, recv, sems):
+        self.own, self.core_recv, self.recv, self.sems = own, core_recv, recv, sems
+        self.place, self.core = lax.axis_index("seq"), lax.axis_index("batch")
+        self.places = own.shape[0]
+
+    def clear(self):
+        @pl.when(self.place == 0)
+        def _():
+            self.recv[0] = jnp.zeros_like(self.recv[0])
+
+        @pl.when(self.place == self.places - 1)
+        def _():
+            self.recv[self.places] = jnp.zeros_like(self.recv[0])
+
+    def core_copy(self, d, source):
+        return along(
+            "batch", source, self.core_recv.at[d], self.sems.at[0, d], self.sems.at[1, d],
+            1 - self.core,
+        )
+
+    def add_core(self, d, source):
+        self.core_copy(d, source).wait_recv()
+        self.add(d, self.core_recv[d])
+
+    def add(self, d, other):
+        self.own[d] = (self.own[d].astype(f32) + other.astype(f32)).astype(bf16)
+
+    def move(self, d):
+        right = d > self.place
+        to = jnp.clip(jnp.where(right, self.place + 1, self.place - 1), 0, self.places - 1)
+        slot = jnp.where(right | (to != d), d, self.places)
+        return along(
+            "seq", self.own.at[d], self.recv.at[slot], self.sems.at[2, d], self.sems.at[3, slot], to
+        )
+
+    def arrived(self, slot):
+        return along(
+            "seq", self.own.at[0], self.recv.at[slot], self.sems.at[2, 0], self.sems.at[3, slot],
+            jnp.where(self.place > 0, self.place - 1, self.places - 1),
+        )
+
+    def advance(self, hop):
+        last = self.places - 1
+
+        def towards(d, active, through):
+            @pl.when(active)
+            def _():
+                @pl.when(through)
+                def _():
+                    self.arrived(d).wait_recv()
+                    self.add(d, self.recv[d])
+
+                self.move(d).start()
+
+        turn = hop - self.place
+        d = jnp.clip(last - turn, 0, last)
+        towards(d, (turn >= 0) & (last - turn > self.place), self.place > 0)
+        turn = hop - (last - self.place)
+        d = jnp.clip(turn, 0, last)
+        towards(d, (turn >= 0) & (turn < self.place), self.place < last)
+
+    def finish(self):
+        @pl.when(self.place > 0)
+        def _():
+            self.arrived(self.place).wait_recv()
+
+        @pl.when(self.place < self.places - 1)
+        def _():
+            self.arrived(self.places).wait_recv()
+
+        return (
+            self.own[self.place].astype(f32)
+            + self.recv[self.place].astype(f32)
+            + self.recv[self.places].astype(f32)
+        )
+
+    def drain(self, source):
+        for d in range(self.places):
+            self.core_copy(d, source(d)).wait_send()
+
+            @pl.when(self.place != d)
+            def _():
+                self.move(d).wait_send()
+
+
+def line_buffers(places, shard, columns):
+    return [
+        pltpu.VMEM((places, shard, columns), bf16),
+        pltpu.VMEM((places, shard, columns), bf16),
+        pltpu.VMEM((places + 1, shard, columns), bf16),
+        pltpu.SemaphoreType.DMA((4, places + 1)),
+    ]
+
+
 def scatter_buffers(places, shard, columns):
     return [pltpu.VMEM((places, shard, columns), bf16)] * 3 + [
         pltpu.SemaphoreType.DMA((4, places))
@@ -330,7 +466,7 @@
 
 
 def forward_kernel(
-    seqs, places, start_ref, decay_ref, main_ref, halo_ref, rate_ref, conv_ref,
+    heads, places, start_ref, decay_ref, main_ref, halo_ref, rate_ref, conv_ref,
     qkv_ref, inv_ref, n_ref, qe_ref, tot_ref, trans_ref, s_ref, mixed_ref,
     x_scr, b_scr, o_scr, carried_scr, send, recv, send_sem, recv_sem,
 ):
@@ -361,9 +497,9 @@
 
     @pl.when(step < chains)
     def _():
-        head = step // seqs
+        head = step % heads
         load_conv_input(
-            main_ref, halo_ref, start_ref[step % seqs], x_scr, place * length
+            main_ref, halo_ref, start_ref[jnp.minimum(step, chains - 1) // heads], x_scr, place * length
         )
         conv = conv_ref[...]
         rows, cols = iotas(CHUNK)
@@ -471,19 +607,19 @@
     length = projected.shape[0] // seqs
     count = length // CHUNK
     rates_at = heads * QKV // PAD
-    row = lambda first: lambda i: (i % seqs, first + i // seqs)
+    row = lambda first: lambda i: (i // heads, first + i % heads)
     whole = lambda *dims: pl.BlockSpec(dims, lambda j: (0,) * len(dims))
     shape = jax.ShapeDtypeStruct
     return pl.pallas_call(
-        functools.partial(forward_kernel, seqs, places),
+        functools.partial(forward_kernel, heads, places),
         grid=(2 * chains,),
         in_specs=[
             smem(),
             smem(),
             pl.BlockSpec((length, QKV), early(chains, row(0))),
-            pl.BlockSpec((1, HALO, QKV), early(chains, lambda i: (i % seqs, 0, i // seqs))),
-            pl.BlockSpec((length, PAD), early(chains, lambda i: (i % seqs, rates_at))),
-            pl.BlockSpec((CONV, QKV), early(chains, lambda i: (0, i // seqs))),
+            pl.BlockSpec((1, HALO, QKV), early(chains, lambda i: (i // heads, 0, i % heads))),
+            pl.BlockSpec((length, PAD), early(chains, lambda i: (i // heads, rates_at))),
+            pl.BlockSpec((CONV, QKV), early(chains, lambda i: (0, i % heads))),
         ],
         out_specs=[
             pl.BlockSpec((length, QKV), early(chains, row(0))),
@@ -524,42 +660,84 @@
 
 
 def backward_kernel(
-    seqs, places, peers, start_ref, decay_ref,
-    dn_ref, mixed_ref, og_ref, gain_ref, n_ref, qe_ref, tot_ref, trans_ref,
-    qkv_ref, inv_ref, s_ref, main_ref, halo_ref, rate_ref, conv_ref, hidden_ref, ffnp_hbm,
-    dp_ref, dconv_ref, ddecay_ref, gg_ref, out_hbm,
-    x_scr, g_scr, do_scr, own_scr, send, recv, tail_scr, halo_send, halo_recv,
-    whole_out, send_sem, recv_sem, halo_send_sem, halo_recv_sem, load_sem, out_sem,
+    heads, places, peers, cores, start_ref, decay_ref,
+    dn_ref, mixed_ref, og_ref, o_gain_ref, n_ref, qe_ref, tot_ref, trans_ref,
+    qkv_ref, inv_ref, s_ref, main_ref, halo_ref, rate_ref, conv_ref,
+    hidden_ref, hgrad_ref, gain_ref, ffn_gain_ref, ffnp_hbm, win_hbm, wog_hbm, nin_hbm, x_hbm,
+    late_hbm,
+    out_hbm, igrad_hbm, gains_out, grad_out, small_out, late_out,
+    dp_ref, x_scr, g_scr, do_scr, own_scr, send, recv, tail_scr, halo_send, halo_recv,
+    conv_scr, decay_scr, o_gain_scr, whole_out, whole_in, win_v, wog_v, nin_v, x_v, conv_source,
+    gate_source, extras_v, gains_v, gains_recv, gains_sum, gains_all,
+    send_sem, recv_sem, halo_send_sem, halo_recv_sem, load_sem, in_sem, late_sem, x_sem, out_sem, hs, hr, gs, gr,
     sent, got, relay, sum_send, sum_recv, gather_send, gather_recv,
+    in_sent, in_got, in_relay, in_sum_send, in_sum_recv, in_gather_send, in_gather_recv,
+    conv_own, conv_core, conv_recv, conv_sems,
+    gate_own, gate_core, gate_recv, gate_sems,
+    late_own, late_core, late_recv, late_sems,
 ):
     step = pl.program_id(0)
     chains = n_ref.shape[0]
     count = n_ref.shape[1]
     length = main_ref.shape[0]
-    heads = chains // seqs
+    seqs = chains // heads
+    total, width = whole_out.shape
     conv_cols = heads * QKV
-    in_cols = conv_cols + heads * DV
-    place = lax.axis_index("seq")
+    values = heads * DV
+    in_cols = conv_cols + values
+    place, core = lax.axis_index("seq"), lax.axis_index("batch")
     lag = jnp.minimum(places - 1 - place, chains - 1)
     me = lax.axis_index("head")
     own_rows = hidden_ref.shape[0]
     subs = own_rows // SUB
-
+    group = places * cores
+    shard = width // group
+    pair = cores * shard
+    flat = place * cores + core
+
+    ring = Spread(whole_out, subs, me, gather_send, gather_recv)
     sums = Combine(sent, got, relay, me, sum_send, sum_recv, own_rows)
-
-    def ffn_load(k):
-        return pltpu.make_async_copy(
-            part(ffnp_hbm, (me ^ k) * own_rows, own_rows), sent.at[k], load_sem.at[k]
-        )
-
-    ring = Spread(whole_out, own_rows, me, gather_send, gather_recv)
-
-    def out_store(k):
-        owner = me ^ k
-        return pltpu.make_async_copy(
-            part(whole_out, owner * own_rows, own_rows), part(out_hbm, owner * own_rows, own_rows),
-            out_sem.at[k],
-        )
+    in_ring = Spread(whole_in, subs, me, in_gather_send, in_gather_recv)
+    in_sums = Combine(in_sent, in_got, in_relay, me, in_sum_send, in_sum_recv, SUB)
+    conv_line = LineScatter(conv_own, conv_core, conv_recv, conv_sems)
+    gate_line = LineScatter(gate_own, gate_core, gate_recv, gate_sems)
+    late_line = LineScatter(late_own, late_core, late_recv, late_sems)
+
+    def late_rows(d, at_core):
+        return late_hbm.at[pl.ds(pl.multiple_of((d * cores + at_core) * shard, shard), shard)]
+
+    def late_source(d):
+        return late_rows(d, 1 - core)
+
+    def late_load(d):
+        return pltpu.make_async_copy(late_rows(d, core), late_own.at[d], late_sem.at[d])
+
+    def hops(third):
+        return range(third * (places - 1) // 3, (third + 1) * (places - 1) // 3)
+
+    def far_first(i):
+        return jnp.where(i % 2 == 0, places - 1 - i // 2, i // 2)
+
+    def halves(grads):
+        top, low = grads[:shard], grads[shard:]
+        return jnp.where(core == 0, top, low), jnp.where(core == 0, low, top)
+    out_store = Pieces(whole_out, out_hbm, total, subs, out_sem.at[0])
+    in_store = Pieces(whole_in, igrad_hbm, total, subs, out_sem.at[1])
+    own_x = Pieces(x_hbm, x_v, total, subs, x_sem)
+    loads = [
+        pltpu.make_async_copy(win_hbm, win_v, in_sem.at[0]),
+        pltpu.make_async_copy(wog_hbm.at[:, pl.ds(0, values)], wog_v, in_sem.at[1]),
+        pltpu.make_async_copy(nin_hbm, nin_v, in_sem.at[2]),
+    ]
+
+    def ffn_loads(k):
+        return [
+            pltpu.make_async_copy(
+                ffnp_hbm.at[piece_rows(me ^ k, t, total, subs)], sent.at[k, pl.ds(t * SUB, SUB)],
+                load_sem.at[k, t],
+            )
+            for t in range(subs)
+        ]
 
     def passed(chain):
         return along(
@@ -575,43 +753,42 @@
 
     @pl.when(step == 0)
     def _():
-        for k in range(peers):
-            ffn_load(k).start()
-        barrier = pltpu.get_barrier_semaphore()
-        for k in range(1, peers):
-            pl.semaphore_signal(barrier, inc=1, device_id={"head": me ^ k}, device_id_type=MESH)
-
-        @pl.when(place < places - 1)
-        def _():
-            pl.semaphore_signal(
-                barrier, inc=1, device_id={"seq": place + 1}, device_id_type=MESH
-            )
+        for k in range(peers - 1, -1, -1):
+            for load in ffn_loads(k):
+                load.start()
 
         @pl.when(place == places - 1)
         def _():
             recv[...] = jnp.zeros_like(recv)
             halo_recv[...] = jnp.zeros_like(halo_recv)
 
-        @pl.when(place > 0)
-        def _():
-            pl.semaphore_wait(barrier, peers)
-
-        @pl.when(place == 0)
-        def _():
-            pl.semaphore_wait(barrier, peers - 1)
-
+        decay_scr[...] = jnp.zeros_like(decay_scr)
+        o_gain_scr[...] = jnp.zeros_like(o_gain_scr)
+        extras_v[...] = jnp.zeros_like(extras_v)
+        for line in (conv_line, gate_line, late_line):
+            line.clear()
+        for d in range(places):
+            late_load(d).start()
+        for load in loads:
+            load.start()
+        own_x.start(me)
+        greet_group(me, peers, places, cores)
         for k in range(peers - 1, 0, -1):
-            ffn_load(k).wait()
+            for load in ffn_loads(k):
+                load.wait()
             sums.start(k, 0)
-        ffn_load(0).wait()
+        for load in ffn_loads(0):
+            load.wait()
+        for d in range(places):
+            late_line.core_copy(d, late_source(d)).start()
 
     @pl.when(step < chains)
     def _():
-        gain = gain_ref[0:1]
-        first = (step % seqs) * length
-        og_at = pl.ds(pl.multiple_of(conv_cols + (step // seqs) * DV, DV), DV)
+        gain = o_gain_ref[0:1]
+        first = (step // heads) * length
+        og_at = pl.ds(pl.multiple_of(conv_cols + (step % heads) * DV, DV), DV)
         state = jnp.zeros((DK, DV), f32)
-        total = jnp.zeros((1, DV), f32)
+        gain_total = jnp.zeros((1, DV), f32)
         for c in reversed(range(count)):
             at = pl.ds(c * CHUNK, CHUNK)
             mixed, og, dn = mixed_ref[at, :], og_ref[at, :], dn_ref[at, :]
@@ -620,7 +797,7 @@
             sig = sigmoid(og)
             silu = og * sig
             through = dn * scaled
-            total = total + jnp.sum(through * silu, axis=0, keepdims=True)
+            gain_total = gain_total + jnp.sum(through * silu, axis=0, keepdims=True)
             dp_ref[pl.ds(pl.multiple_of(first + c * CHUNK, CHUNK), CHUNK), og_at] = (
                 through * gain * sig * (1.0 + og * (1.0 - sig))
             ).astype(bf16)
@@ -634,13 +811,13 @@
             state = (
                 decay * state - mm(n_ref[step, c], state, TN) + mm(qe_ref[step, c], dmixed, TN)
             )
-        gg_ref[0] = jnp.broadcast_to(total, (8, DV))
+        o_gain_scr[0:1, :] = o_gain_scr[0:1, :] + gain_total
         own_scr[step] = state
 
     @pl.when(step >= chains)
     def _():
         chain = jnp.maximum(step - chains, 0)
-        head, seq = chain // seqs, chain % seqs
+        seq, head = chain // heads, chain % heads
         first = seq * length
         start = start_ref[seq]
         load_conv_input(main_ref, halo_ref, start, x_scr, place * length)
@@ -753,9 +930,13 @@
                 shifted_in = x_scr[pl.ds(c * CHUNK + HALO - CONV + 1 + j, CHUNK), :]
                 conv_total[j] = conv_total[j] + jnp.sum(dconv * shifted_in, axis=0, keepdims=True)
         for j in range(CONV):
-            dconv_ref[0, pl.ds(j, 1), :] = conv_total[j]
-        row8 = lax.broadcasted_iota(jnp.int32, (8, PAD), 0)
-        ddecay_ref[0] = jnp.where(row8 == 0, rate_total, jnp.where(row8 == 1, bias_total, 0.0))
+            tap = pl.ds(j * heads + head, 1)
+            conv_scr[tap, :] = conv_total[j] + jnp.where(seq == 0, 0.0, conv_scr[tap, :])
+        spots = lax.broadcasted_iota(jnp.int32, decay_scr.shape, 1)
+        top = lax.broadcasted_iota(jnp.int32, decay_scr.shape, 0) == 0
+        decay_scr[...] = decay_scr[...] + jnp.where(
+            top & (spots == 2 * heads + head), rate_total, 0.0
+        ) + jnp.where(top & (spots == 3 * heads + head), bias_total, 0.0)
 
         def conv_back(at, size):
             grad = g_scr[pl.ds(at + CONV - 1, size), :] * conv[0:1]
@@ -782,6 +963,24 @@
                 grad * live
             ).astype(bf16)
 
+    @pl.when(step == chains - 1)
+    def _():
+        loads[2].wait()
+
+        def gate_grads(i, carry):
+            d = far_first(i)
+            rows = pl.ds(pl.multiple_of(d * pair, pair), pair)
+            mine, others = halves(mm(nin_v[rows, :], dp_ref[:, conv_cols:in_cols]))
+            gate_own[d] = mine.astype(bf16)
+            gate_source[d] = others.astype(bf16)
+            gate_line.core_copy(d, gate_source.at[d]).start()
+            return carry
+
+        lax.fori_loop(0, places, gate_grads, 0)
+        for d in range(places):
+            late_load(d).wait()
+            late_line.add_core(d, late_source(d))
+
     relayed = step - lag
 
     @pl.when((relayed >= 0) & (relayed < chains))
@@ -806,30 +1005,42 @@
     def _():
         for kind in range(2, 6):
             sums.copy(kind, 0).wait_recv()
-
-        def out_rows(t, carry):
-            rows = pl.ds(pl.multiple_of(t * SUB, SUB), SUB)
-            part(whole_out, me * own_rows + t * SUB, SUB)[...] = (
-                hidden_ref[rows, :] + sums.total(rows)
-            ).astype(bf16)
-            return carry
-
-        lax.fori_loop(0, subs, out_rows, 0)
-        ring.start(0)
-        out_store(0).start()
+        for t in range(subs):
+            rows = pl.ds(t * SUB, SUB)
+            ring.put(t, (hidden_ref[rows, :] + sums.total(rows)).astype(bf16))
+            ring.start(t)
+        out_store.start(me)
 
     @pl.when(step == chains + 2)
     def _():
-        ring.forward(0)
-
-    @pl.when(step == 2 * chains - 1)
-    def _():
-        for chain in range(chains):
+        for t in range(subs):
+            ring.forward(t)
+
+    for third, at_step in enumerate((chains - 1, chains + 1, 2 * chains - 1)):
+
+        @pl.when(step == at_step)
+        def _():
+            for hop in hops(third):
+                late_line.advance(hop)
+
+    for third, at_step in enumerate((chains, chains + 1, chains + 2)):
+
+        @pl.when(step == at_step)
+        def _():
+            if third == 0:
+                for d in range(places):
+                    gate_line.add_core(d, gate_source.at[d])
+            for hop in hops(third):
+                gate_line.advance(hop)
+
+    def mend_ends(seq):
+        for head in range(heads):
+            chain = seq * heads + head
+
             @pl.when(place < places - 1)
             def _():
                 returned(chain).wait_recv()
 
-            head, seq = chain // seqs, chain % seqs
             positions = (place + 1) * length - HALO + lax.broadcasted_iota(
                 jnp.int32, (HALO, 1), 0
             )
@@ -841,41 +1052,219 @@
                 grad * live
             ).astype(bf16)
 
-            @pl.when(place > 0)
+    def project(t):
+        def one(i, carry):
+            k = jnp.where(i == 0, peers - 1, lax.rem(i, peers - 1))
+            rows = piece_rows(me ^ k, t, total, subs)
+            partial = mm(dp_ref[rows, 0:conv_cols], win_v[:, 0:conv_cols], NT)
+            partial = partial + mm(dp_ref[rows, conv_cols:in_cols], wog_v[...], NT)
+            partial = partial + mm(dp_ref[rows, in_cols:], win_v[:, conv_cols:], NT)
+            in_sent[k, pl.ds(t * SUB, SUB), :] = partial.astype(bf16)
+
+            for kk in range(1, peers):
+
+                @pl.when(k == kk)
+                def _():
+                    in_sums.start(kk, t)
+
+            return carry
+
+        lax.fori_loop(0, peers, one, 0)
+
+    for t in range(seqs - 1):
+
+        @pl.when(step == chains + (t + 1) * heads - 1)
+        def _():
+            mend_ends(t)
+            if t == 0:
+                for load in loads[:2]:
+                    load.wait()
+            project(t)
+
+        @pl.when(step == chains + (t + 1) * heads)
+        def _():
+            in_sums.combine(t)
+
+    def own_input_grads(t):
+        rows = pl.ds(t * SUB, SUB)
+        din = in_sums.collect(t)
+        x = x_v[rows, :].astype(f32)
+        inverse = lax.rsqrt(jnp.mean(x * x, axis=1, keepdims=True) + epsilon)
+        scaled = x * inverse
+        weighted = din * gain_ref[...]
+        grad = hgrad_ref[rows, :] + inverse * (
+            weighted - scaled * jnp.mean(weighted * scaled, axis=1, keepdims=True)
+        )
+        in_ring.put(t, grad.astype(bf16))
+        in_ring.start(t)
+        return jnp.sum(din * scaled, axis=0, keepdims=True)
+
+    @pl.when(step == 2 * chains - 1)
+    def _():
+        own_x.wait(me)
+        gain_part = jnp.zeros((1, width), f32)
+        for t in range(seqs - 1):
+            gain_part = gain_part + own_input_grads(t)
+        mend_ends(seqs - 1)
+        taps = CONV * heads
+        per = QKV // group
+        lanes = lax.broadcasted_iota(jnp.int32, (taps, PAD), 1)
+        for q in range(group):
+            at = per * q // PAD * PAD
+            shift = (PAD // 2 - per * q) % PAD
+            moved = conv_scr[:, at : at + PAD]
+            if shift:
+                moved = pltpu.roll(moved, shift, 1)
+            kept = jnp.where((lanes >= PAD // 2) & (lanes < PAD // 2 + per), moved, 0.0)
+            extras_v[q * shard : q * shard + taps, :] = kept + decay_scr[...]
+        if seqs == 1:
+            for load in loads[:2]:
+                load.wait()
+
+        def place_grads(i, carry):
+            d = far_first(i)
+            rows = pl.ds(pl.multiple_of(d * pair, pair), pair)
+            mine, others = halves(mm(nin_v[rows, :], dp_ref[:, 0:conv_cols]))
+            conv_own[d, :, 0:conv_cols] = mine.astype(bf16)
+            conv_source[d, :, 0:conv_cols] = others.astype(bf16)
+            mine, others = halves(mm(nin_v[rows, :], dp_ref[:, in_cols:]) + extras_v[rows, :])
+            conv_own[d, :, conv_cols:] = mine.astype(bf16)
+            conv_source[d, :, conv_cols:] = others.astype(bf16)
+            conv_line.core_copy(d, conv_source.at[d]).start()
+
+            @pl.when(i > 0)
             def _():
+                before = far_first(jnp.maximum(i - 1, 0))
+                conv_line.add_core(before, conv_source.at[before])
+
+            return carry
+
+        first_places = min(2, places)
+        lax.fori_loop(0, first_places, place_grads, 0)
+        project(seqs - 1)
+        lax.fori_loop(first_places, places, place_grads, 0)
+        before = far_first(places - 1)
+        conv_line.add_core(before, conv_source.at[before])
+        for hop in hops(0):
+            conv_line.advance(hop)
+        in_sums.combine(seqs - 1)
+        gain_part = gain_part + own_input_grads(seqs - 1)
+        lane_rows = width // 128
+        gains_v[...] = jnp.zeros_like(gains_v)
+        for r in range(lane_rows):
+            gains_v[r : r + 1, :] = gain_part[:, r * 128 : (r + 1) * 128]
+            gains_v[lane_rows + r : lane_rows + r + 1, :] = ffn_gain_ref[
+                0:1, r * 128 : (r + 1) * 128
+            ]
+        for r in range(DV // 128):
+            gains_v[2 * lane_rows + r : 2 * lane_rows + r + 1, :] = o_gain_scr[
+                0:1, r * 128 : (r + 1) * 128
+            ]
+
+        def gains_copy(k):
+            return head_copy(gains_v, gains_recv.at[k], hs.at[k], hr.at[k], me ^ k)
+
+        def to_group(d):
+            to = lax.rem(flat + d, group)
+            return pltpu.make_async_remote_copy(
+                src_ref=gains_sum, dst_ref=gains_all.at[d], send_sem=gs.at[d], recv_sem=gr.at[d],
+                device_id={"seq": to // cores, "batch": lax.rem(to, cores)}, device_id_type=MESH,
+            )
+
+        for k in range(1, peers):
+            gains_copy(k).start()
+        for hop in hops(1):
+            conv_line.advance(hop)
+        in_store.start(me)
+        for t in range(subs):
+            ring.finish(t)
+        for k in range(1, peers):
+            out_store.start(me ^ k)
+        gathered = gains_v[...]
+        for k in range(1, peers):
+            gains_copy(k).wait_recv()
+            gathered = gathered + gains_recv[k]
+        gains_sum[...] = gathered
+        for d in range(1, group):
+            to_group(d).start()
+        for t in range(subs):
+            in_ring.forward(t)
+        for hop in hops(2):
+            conv_line.advance(hop)
+        in_store.start(me ^ 1)
+        in_store.start(me ^ 2)
+        for d in range(1, group):
+            to_group(d).wait_recv()
+            gathered = gathered + gains_all[d]
+        gains_out[...] = gathered
+        for t in range(subs):
+            in_ring.finish(t)
+        in_store.start(me ^ 3)
+        late_out[...] = late_line.finish()
+        grad = gate_line.finish()
+        for head in range(heads):
+            at = head * (QKV + DV) + QKV
+            grad_out[:, at : at + DV] = grad[:, head * DV : (head + 1) * DV]
+        grad = conv_line.finish()
+        for head in range(heads):
+            at = head * (QKV + DV)
+            grad_out[:, at : at + QKV] = grad[:, head * QKV : (head + 1) * QKV]
+        small_out[...] = grad[:, conv_cols:]
+        for k in range(peers):
+            out_store.wait(k)
+            in_store.wait(k)
+
+        @pl.when(place > 0)
+        def _():
+            for chain in range(chains):
                 returned(chain).wait_send()
                 passed(chain).wait_send()
 
-        ring.finish(0)
+        sums.drain(0)
+        for t in range(subs):
+            ring.drain(t)
+            in_ring.drain(t)
+            in_sums.drain(t)
         for k in range(1, peers):
-            out_store(k).start()
-        for k in range(peers):
-            out_store(k).wait()
-        sums.drain(0)
-        ring.drain(0)
+            gains_copy(k).wait_send()
+        for d in range(1, group):
+            to_group(d).wait_send()
+        conv_line.drain(lambda d: conv_source.at[d])
+        gate_line.drain(lambda d: gate_source.at[d])
+        late_line.drain(late_source)
 
 
 def backward_rule(
-    starts, decay_par, dn, mixed, og, projected, gain, n, qe, tot, trans, qkv, inv, states, halo, conv_w,
-    hidden, ffn_part, seqs, heads,
+    starts, decay_par, dn, mixed, og, projected, o_gain, n, qe, tot, trans, qkv, inv, states, halo,
+    conv_w, hidden, hidden_grad, gain, ffn_gain_part, ffn_part, in_full, gate_full, turned, x, late_grads,
+    heads,
 ):
-    places, peers = lax.axis_size("seq"), lax.axis_size("head")
-    chains = seqs * heads
+    places, peers, cores = lax.axis_size("seq"), lax.axis_size("head"), lax.axis_size("batch")
+    chains, count = n.shape[:2]
+    seqs = chains // heads
     rows = projected.shape[0]
     length = rows // seqs
-    count = length // CHUNK
     width = hidden.shape[1]
     own_rows = hidden.shape[0]
+    subs = own_rows // SUB
     rates_at = heads * QKV // PAD
-    row = lambda first: lambda i: (i % seqs, first + i // seqs)
+    values = heads * DV
+    cols = heads * (QKV + DV) + PAD
+    group = places * cores
+    shard = width // group
+    gain_rows = 3 * width // 128
+    row = lambda first: lambda i: (i // heads, first + i % heads)
     whole = lambda *dims: pl.BlockSpec(dims, lambda j: (0,) * len(dims))
     chain4 = lambda i: (i, 0, 0, 0)
-    chain3 = lambda i: (i, 0, 0)
     shape = jax.ShapeDtypeStruct
     per_chain = pltpu.SemaphoreType.DMA((chains,))
     per_peer = pltpu.SemaphoreType.DMA((peers,))
+    per_member = pltpu.SemaphoreType.DMA((group,))
+    pieces = pltpu.SemaphoreType.DMA((peers, subs))
+    ffn_sums = sum_buffers(own_rows, width, subs)
+    ffn_sums[3:5] = [pltpu.SemaphoreType.DMA((6, 1))] * 2
     return pl.pallas_call(
-        functools.partial(backward_kernel, seqs, places, peers),
+        functools.partial(backward_kernel, heads, places, peers, cores),
         grid=(2 * chains,),
         in_specs=[
             smem(),
@@ -892,27 +1281,33 @@
             pl.BlockSpec((1, count, CHUNK, CHUNK), late(chains, chain4)),
             pl.BlockSpec((1, count, DK, DV), late(chains, chain4)),
             pl.BlockSpec((length, QKV), late(chains, row(0))),
-            pl.BlockSpec((1, HALO, QKV), late(chains, lambda i: (i % seqs, 0, i // seqs))),
-            pl.BlockSpec((length, PAD), late(chains, lambda i: (i % seqs, rates_at))),
-            pl.BlockSpec((CONV, QKV), late(chains, lambda i: (0, i // seqs))),
+            pl.BlockSpec((1, HALO, QKV), late(chains, lambda i: (i // heads, 0, i % heads))),
+            pl.BlockSpec((length, PAD), late(chains, lambda i: (i // heads, rates_at))),
+            pl.BlockSpec((CONV, QKV), late(chains, lambda i: (0, i % heads))),
             whole(own_rows, width),
+            whole(own_rows, width),
+            whole(1, width),
+            whole(8, width),
+        ]
+        + [anywhere()] * 6,
+        out_specs=[
             anywhere(),
-        ],
-        out_specs=[
-            whole(rows, heads * (QKV + DV) + PAD),
-            pl.BlockSpec((1, CONV, QKV), late(chains, chain3)),
-            pl.BlockSpec((1, 8, PAD), late(chains, chain3)),
-            pl.BlockSpec((1, 8, DV), early(chains, chain3)),
             anywhere(),
+            whole(gain_rows, 128),
+            whole(shard, cols - PAD),
+            whole(shard, PAD),
+            whole(shard, late_grads.shape[1]),
         ],
         out_shape=[
-            shape((rows, heads * (QKV + DV) + PAD), bf16),
-            shape((chains, CONV, QKV), f32),
-            shape((chains, 8, PAD), f32),
-            shape((chains, 8, DV), f32),
             shape((rows, width), bf16),
+            shape((rows, width), bf16),
+            shape((gain_rows, 128), f32),
+            shape((shard, cols - PAD), f32),
+            shape((shard, PAD), f32),
+            shape((shard, late_grads.shape[1]), f32),
         ],
         scratch_shapes=[
+            pltpu.VMEM((rows, cols), bf16),
             pltpu.VMEM((HALO + length, QKV), f32),
             pltpu.VMEM((16 + length, QKV), f32),
             pltpu.VMEM((chains, length, DV), bf16),
@@ -922,19 +1317,44 @@
             pltpu.VMEM((chains, HALO, QKV), f32),
             pltpu.VMEM((chains, 8, QKV), f32),
             pltpu.VMEM((chains, 8, QKV), f32),
+            pltpu.VMEM((CONV * heads, QKV), f32),
+            pltpu.VMEM((CONV * heads, PAD), f32),
+            pltpu.VMEM((8, DV), f32),
             pltpu.VMEM((rows, width), bf16),
+            pltpu.VMEM((rows, width), bf16),
+            pltpu.VMEM((width, cols - values), bf16),
+            pltpu.VMEM((width, values), bf16),
+            pltpu.VMEM((width, rows), bf16),
+            pltpu.VMEM((own_rows, width), bf16),
+            pltpu.VMEM((places, shard, cols - values), bf16),
+            pltpu.VMEM((places, shard, values), bf16),
+            pltpu.VMEM((width, PAD), f32),
+            pltpu.VMEM((gain_rows, 128), f32),
+            pltpu.VMEM((peers, gain_rows, 128), f32),
+            pltpu.VMEM((gain_rows, 128), f32),
+            pltpu.VMEM((group, gain_rows, 128), f32),
             per_chain, per_chain, per_chain, per_chain,
-            per_peer, per_peer,
+            pieces,
+            pltpu.SemaphoreType.DMA((3,)),
+            pltpu.SemaphoreType.DMA((places,)),
+            pieces,
+            pltpu.SemaphoreType.DMA((2, peers, subs)),
+            per_peer, per_peer, per_member, per_member,
         ]
-        + sum_buffers(own_rows, width, 1),
+        + ffn_sums
+        + sum_buffers(own_rows, width, subs)
+        + line_buffers(places, shard, cols - values)
+        + line_buffers(places, shard, values)
+        + line_buffers(places, shard, late_grads.shape[1]),
         compiler_params=pltpu.CompilerParams(
             dimension_semantics=("arbitrary",), collective_id=4, has_side_effects=True,
-            vmem_limit_bytes=52 * 2**20,
+            vmem_limit_bytes=62 * 2**20,
         ),
         name="backward_rule",
     )(
-        starts, decay_par, dn, mixed, og, gain, n, qe, tot, trans, qkv, inv, states, projected,
-        halo, projected, conv_w, hidden, ffn_part,
+        starts, decay_par, dn, mixed, og, o_gain, n, qe, tot, trans, qkv, inv, states, projected,
+        halo, projected, conv_w, hidden, hidden_grad, gain, ffn_gain_part, ffn_part, in_full,
+        gate_full, turned, x, late_grads,
     )
 
 
@@ -955,7 +1375,7 @@
 def mixer_kernel(
     peers, nin_hbm, mixed_hbm, weights_hbm, x_hbm, gain_ref, o_gain_ref,
     og_hbm, normed_hbm, nm_hbm, turned_hbm, hidden_ref,
-    nin, turned, mixed, weights, x_v, og_v, normed_v, nm, in_sem, out_sem,
+    nin, turned, mixed, weights, x_v, og_v, normed_v, nm, in_sem, x_sem, out_sem,
     send, recv, relay, sum_send, sum_recv, gather_send, gather_recv,
 ):
     me = lax.axis_index("head")
@@ -967,30 +1387,41 @@
         pltpu.make_async_copy(weights_hbm, weights, in_sem.at[0]),
         pltpu.make_async_copy(nin_hbm, nin, in_sem.at[1]),
         pltpu.make_async_copy(mixed_hbm, mixed, in_sem.at[2]),
-        pltpu.make_async_copy(part(x_hbm, me * own_rows, own_rows), x_v, in_sem.at[3]),
     ]
     for load in loads:
         load.start()
+    own_x = Pieces(x_hbm, x_v, total, subs, x_sem)
+    own_x.start(me)
+    stores = [
+        Pieces(source, target, total, subs, out_sem.at[i])
+        for i, (source, target) in enumerate(
+            ((og_v, og_hbm), (normed_v, normed_hbm), (nm, nm_hbm))
+        )
+    ]
     greet_heads(me, peers)
-    for load in loads[:3]:
+    for load in loads:
         load.wait()
     sums = Combine(send, recv, relay, me, sum_send, sum_recv, SUB)
 
     def project(i, carry):
         k = jnp.where(i == 0, peers - 1, lax.rem(i, peers - 1))
         owner = me ^ k
-        rows = pl.ds(pl.multiple_of(owner * own_rows, own_rows), own_rows)
-        og = mm(nin[rows, :], weights[:, 0:values])
-        og_v[rows, :] = og
+        og = mm(take(nin, owner, subs), weights[:, 0:values])
         gated = og * sigmoid(og)
+        own = take(mixed, owner, subs)
+        normed = []
         for first in range(0, values, DV):
-            at = pl.ds(first, DV)
-            own = mixed[rows, at]
-            inverse = lax.rsqrt(jnp.mean(own * own, axis=1, keepdims=True) + epsilon)
-            normed_v[rows, at] = (
-                own * inverse * o_gain_ref[0:1] * gated[:, first : first + DV]
-            ).astype(bf16)
-        send[k] = mm(normed_v[rows, :], weights[:, values:], NT).astype(bf16)
+            at = slice(first, first + DV)
+            inverse = lax.rsqrt(
+                jnp.mean(own[:, at] * own[:, at], axis=1, keepdims=True) + epsilon
+            )
+            normed.append((own[:, at] * inverse * o_gain_ref[0:1] * gated[:, at]).astype(bf16))
+        normed = jnp.concatenate(normed, axis=1)
+        send[k] = mm(normed, weights[:, values:], NT).astype(bf16)
+        for t in range(subs):
+            rows = piece_rows(owner, t, total, subs)
+            og_v[rows, :] = og[t * SUB : (t + 1) * SUB]
+            normed_v[rows, :] = normed[t * SUB : (t + 1) * SUB]
 
         for kk in range(1, peers):
 
@@ -999,8 +1430,8 @@
                 for t in range(subs):
                     sums.start(kk, t)
 
-        block_store(owner, own_rows, og_v, og_hbm, out_sem.at[0]).start()
-        block_store(owner, own_rows, normed_v, normed_hbm, out_sem.at[1]).start()
+        stores[0].start(owner)
+        stores[1].start(owner)
         return carry
 
     lax.fori_loop(0, peers, project, 0)
@@ -1009,17 +1440,17 @@
         turned[first : first + tile, :] = nin[:, first : first + tile].T
     for t in range(subs):
         sums.combine(t)
-    turned_store = pltpu.make_async_copy(turned, turned_hbm, in_sem.at[4])
+    turned_store = pltpu.make_async_copy(turned, turned_hbm, in_sem.at[3])
     turned_store.start()
-    loads[3].wait()
+    own_x.wait(me)
     gain = gain_ref[...]
-    ring = Spread(nm, own_rows, me, gather_send, gather_recv, SUB)
+    ring = Spread(nm, subs, me, gather_send, gather_recv)
     for t in range(subs):
         rows = rows_of(t)
         hidden = x_v[rows, :].astype(f32) + sums.collect(t)
         hidden_ref[rows, :] = hidden
         inverse = lax.rsqrt(jnp.mean(hidden * hidden, axis=1, keepdims=True) + epsilon)
-        part(nm, me * own_rows + t * SUB, SUB)[...] = (hidden * inverse * gain).astype(bf16)
+        ring.put(t, (hidden * inverse * gain).astype(bf16))
         ring.start(t)
     for t in range(subs):
         ring.forward(t)
@@ -1027,12 +1458,11 @@
         if k == peers - 1:
             for t in range(subs):
                 ring.finish(t)
-        block_store(me ^ k, own_rows, nm, nm_hbm, out_sem.at[2]).start()
+        stores[2].start(me ^ k)
     turned_store.wait()
     for i in range(peers):
-        block_store(i, own_rows, og_v, og_hbm, out_sem.at[0]).wait()
-        block_store(i, own_rows, normed_v, normed_hbm, out_sem.at[1]).wait()
-        block_store(i, own_rows, nm, nm_hbm, out_sem.at[2]).wait()
+        for store in stores:
+            store.wait(i)
     for t in range(subs):
         sums.drain(t)
         ring.drain(t)
@@ -1065,8 +1495,9 @@
             pltpu.VMEM((total, values), f32),
             pltpu.VMEM((total, values), bf16),
             pltpu.VMEM((total, width), bf16),
-            pltpu.SemaphoreType.DMA((5,)),
-            pltpu.SemaphoreType.DMA((3, peers)),
+            pltpu.SemaphoreType.DMA((4,)),
+            pltpu.SemaphoreType.DMA((peers, subs)),
+            pltpu.SemaphoreType.DMA((3, peers, subs)),
         ]
         + sum_buffers(own_rows, width, subs),
         compiler_params=pltpu.CompilerParams(
@@ -1079,8 +1510,8 @@
 def ffn_kernel(
     peers, places, cores, nm_hbm, ffn_hbm, ct_hbm, normed_hbm, weights_hbm, hidden_ref, gain_ref,
     grads_hbm, ffnp_hbm, ng_hbm, hgrad_ref, gpart_ref, down_ref,
-    nm, ffn_v, ct_v, normed_v, wout_v, act, dgu, dm, ffnp_v, grads_v, down_v, ng_v,
-    in_sem, out_sem, send, recv, relay, sum_send, sum_recv, gather_send, gather_recv,
+    nm_b, ct_b, dgu_b, nm, ffn_v, ct_v, normed_v, wout_v, act, dgu, dm, ffnp_v, grads_v, down_v, ng_v,
+    in_sem, out_sem, ng_sem, send, recv, relay, sum_send, sum_recv, gather_send, gather_recv,
     core_recv, seq_send, seq_recv, scatter_sems,
 ):
     me = lax.axis_index("head")
@@ -1107,30 +1538,36 @@
 
     def feed_forward(i, carry):
         k = jnp.where(i == 0, peers - 1, lax.rem(i, peers - 1))
-        rows = pl.ds(pl.multiple_of((me ^ k) * own_rows, own_rows), own_rows)
+        owner = me ^ k
+        nm_b[...] = take(nm, owner, subs)
+        ct_b[...] = take(ct_v, owner, subs)
 
         def cell_tile(j, carry):
             at = pl.ds(pl.multiple_of(j * tile, tile), tile)
             at_up = pl.ds(pl.multiple_of(cells + j * tile, tile), tile)
             at_down = pl.ds(pl.multiple_of(2 * cells + j * tile, tile), tile)
-            gate = mm(nm[rows, :], ffn_v[:, at])
-            up = mm(nm[rows, :], ffn_v[:, at_up])
-            dact = mm(ct_v[rows, :], ffn_v[:, at_down])
+            gate = mm(nm_b[...], ffn_v[:, at])
+            up = mm(nm_b[...], ffn_v[:, at_up])
+            dact = mm(ct_b[...], ffn_v[:, at_down])
             sig = sigmoid(gate)
             silu = gate * sig
-            act[rows, at] = (silu * up).astype(bf16)
-            dgu[rows, at] = (dact * up * sig * (1.0 + gate * (1.0 - sig))).astype(bf16)
-            dgu[rows, at_up] = (dact * silu).astype(bf16)
+            activated = (silu * up).astype(bf16)
+            dgu_b[:, at] = (dact * up * sig * (1.0 + gate * (1.0 - sig))).astype(bf16)
+            dgu_b[:, at_up] = (dact * silu).astype(bf16)
+            for t in range(subs):
+                act[piece_rows(owner, t, total, subs), at] = activated[t * SUB : (t + 1) * SUB]
             return carry
 
         lax.fori_loop(0, cells // tile, cell_tile, 0)
 
         def mid_tile(j, carry):
             at = pl.ds(pl.multiple_of(j * tile, tile), tile)
-            send[k, :, at] = mm(dgu[rows, :], ffn_v[at, 0 : 2 * cells], NT).astype(bf16)
+            send[k, :, at] = mm(dgu_b[...], ffn_v[at, 0 : 2 * cells], NT).astype(bf16)
             return carry
 
         lax.fori_loop(0, width // tile, mid_tile, 0)
+        for t in range(subs):
+            dgu[piece_rows(owner, t, total, subs), :] = dgu_b[rows_of(t), :]
 
         for kk in range(1, peers):
 
@@ -1168,7 +1605,7 @@
     for k in range(places - 1, -1, -1):
         scatter.pass_on(k)
     lax.fori_loop(half, width // tile, cell_grads, 0)
-    ring = Spread(dm, own_rows, me, gather_send, gather_recv, SUB)
+    ring = Spread(dm, subs, me, gather_send, gather_recv)
     gain_part = jnp.zeros((1, width), f32)
     for t in range(subs):
         rows = rows_of(t)
@@ -1177,11 +1614,11 @@
         inverse = lax.rsqrt(jnp.mean(hidden * hidden, axis=1, keepdims=True) + epsilon)
         scaled = hidden * inverse
         weighted = dmid * gain
-        grad = part(ct_v, me * own_rows + t * SUB, SUB)[...].astype(f32) + inverse * (
+        grad = ct_v[piece_rows(me, t, total, subs), :].astype(f32) + inverse * (
             weighted - scaled * jnp.mean(weighted * scaled, axis=1, keepdims=True)
         )
         hgrad_ref[rows, :] = grad
-        part(dm, me * own_rows + t * SUB, SUB)[...] = grad.astype(bf16)
+        ring.put(t, grad.astype(bf16))
         ring.start(t)
         gain_part = gain_part + jnp.sum(dmid * scaled, axis=0, keepdims=True)
     gpart_ref[...] = jnp.broadcast_to(gain_part, gpart_ref.shape)
@@ -1199,6 +1636,8 @@
         ring.forward(t)
     down_ref[...] = scatter.finish()
 
+    ng_store = Pieces(ng_v, ng_hbm, total, subs, ng_sem)
+
     def norm_rows(k, carry):
         owner = me ^ k
 
@@ -1207,9 +1646,10 @@
             for t in range(subs):
                 ring.finish(t)
 
-        rows = pl.ds(pl.multiple_of(owner * own_rows, own_rows), own_rows)
-        ng_v[rows, :] = mm(dm[rows, :], wout_v[...])
-        block_store(owner, own_rows, ng_v, ng_hbm, out_sem.at[1]).start()
+        grads = mm(take(dm, owner, subs), wout_v[...])
+        for t in range(subs):
+            ng_v[piece_rows(owner, t, total, subs), :] = grads[t * SUB : (t + 1) * SUB]
+        ng_store.start(owner)
         return carry
 
     lax.fori_loop(0, peers, norm_rows, 0)
@@ -1217,15 +1657,15 @@
     def out_grads(i, carry):
         at = pl.ds(pl.multiple_of(i * tile, tile), tile)
         grads_v[at, 2 * cells :] = mm(dm[:, at], normed_v[...], TN).astype(bf16)
-        block_store(i, tile, grads_v, grads_hbm, out_sem.at[2]).start()
+        block_store(i, tile, grads_v, grads_hbm, out_sem.at[1]).start()
         return carry
 
     lax.fori_loop(0, width // tile, out_grads, 0)
     for i in range(peers):
         block_store(i, own_rows, ffnp_v, ffnp_hbm, out_sem.at[0]).wait()
-        block_store(i, own_rows, ng_v, ng_hbm, out_sem.at[1]).wait()
+        ng_store.wait(i)
     for i in range(width // tile):
-        block_store(i, tile, grads_v, grads_hbm, out_sem.at[2]).wait()
+        block_store(i, tile, grads_v, grads_hbm, out_sem.at[1]).wait()
     for t in range(subs):
         sums.drain(t)
         ring.drain(t)
@@ -1254,6 +1694,9 @@
             shape((shard, cells), f32),
         ],
         scratch_shapes=[
+            pltpu.VMEM((own_rows, width), bf16),
+            pltpu.VMEM((own_rows, width), bf16),
+            pltpu.VMEM((own_rows, 2 * cells), bf16),
             pltpu.VMEM((total, width), bf16),
             pltpu.VMEM((width, 3 * cells), bf16),
             pltpu.VMEM((total, width), bf16),
@@ -1267,7 +1710,8 @@
             pltpu.VMEM((width, cells), bf16),
             pltpu.VMEM((total, values), f32),
             pltpu.SemaphoreType.DMA((5,)),
-            pltpu.SemaphoreType.DMA((3, max(peers, width // 256))),
+            pltpu.SemaphoreType.DMA((2, max(peers, width // 256))),
+            pltpu.SemaphoreType.DMA((peers, subs)),
         ]
         + sum_buffers(own_rows, width, subs)
         + scatter_buffers(places, shard, cells),
@@ -1276,199 +1720,6 @@
         ),
         name="feed_forward",
     )(nm, ffn_full, ct, normed, weights, hidden, gain)
-
-
-def input_grad_kernel(
-    peers, places, cores, heads, dp_hbm, win_hbm, wog_hbm, nin_hbm, x_hbm, hgrad_ref, gain_ref,
-    gains_ref, extras_ref,
-    out_hbm, gains_out, grad_out, small_out,
-    dp_v, win_v, wog_v, nin_v, x_v, whole, grads_v, gains_v, gains_recv, gains_sum, gains_all,
-    in_sem, out_sem,
-    send, recv, relay, sum_send, sum_recv, gather_send, gather_recv,
-    core_recv, seq_send, seq_recv, scatter_sems, hs, hr, gs, gr,
-):
-    me = lax.axis_index("head")
-    place, core = lax.axis_index("seq"), lax.axis_index("batch")
-    total, width = whole.shape
-    own_rows = total // peers
-    subs = own_rows // SUB
-    values = wog_v.shape[1]
-    conv_cols = win_v.shape[1] - PAD
-    cols = dp_v.shape[1]
-    group = places * cores
-    pair = cores * (width // group)
-    flat = place * cores + core
-    loads = [
-        pltpu.make_async_copy(dp_hbm, dp_v, in_sem.at[0]),
-        pltpu.make_async_copy(win_hbm, win_v, in_sem.at[1]),
-        pltpu.make_async_copy(wog_hbm.at[:, pl.ds(0, values)], wog_v, in_sem.at[2]),
-        pltpu.make_async_copy(nin_hbm, nin_v, in_sem.at[3]),
-        pltpu.make_async_copy(part(x_hbm, me * own_rows, own_rows), x_v, in_sem.at[4]),
-    ]
-    for load in loads:
-        load.start()
-    greet_group(me, peers, places, cores)
-    for load in loads[:3]:
-        load.wait()
-    sums = Combine(send, recv, relay, me, sum_send, sum_recv, SUB)
-
-    def project(i, carry):
-        k = jnp.where(i == 0, peers - 1, lax.rem(i, peers - 1))
-        rows = pl.ds(pl.multiple_of((me ^ k) * own_rows, own_rows), own_rows)
-        partial = mm(dp_v[rows, 0:conv_cols], win_v[:, 0:conv_cols], NT)
-        partial = partial + mm(
-            dp_v[rows, conv_cols : conv_cols + values], wog_v[...], NT
-        )
-        partial = partial + mm(dp_v[rows, conv_cols + values :], win_v[:, conv_cols:], NT)
-        send[k] = partial.astype(bf16)
-
-        for kk in range(1, peers):
-
-            @pl.when(k == kk)
-            def _():
-                for t in range(subs):
-                    sums.start(kk, t)
-
-        return carry
-
-    lax.fori_loop(0, peers - 1, project, 0)
-    loads[3].wait()
-    scatter = GroupScatter(grads_v, pl.ds(0, cols), core_recv, seq_send, seq_recv, scatter_sems)
-
-    def place_grads(i, carry):
-        k = places - 1 - i
-        rows = pl.ds(pl.multiple_of((place ^ k) * pair, pair), pair)
-        grads = mm(nin_v[rows, :], dp_v[...])
-        grads_v[rows, 0 : cols - PAD] = grads[:, : cols - PAD].astype(bf16)
-        grads_v[rows, cols - PAD :] = (grads[:, cols - PAD :] + extras_ref[rows, :]).astype(bf16)
-        scatter.core_copy(k).start()
-
-        @pl.when(i > 0)
-        def _():
-            scatter.pass_on(jnp.minimum(k + 1, places - 1))
-
-        return carry
-
-    lax.fori_loop(0, places, place_grads, 0)
-    scatter.pass_on(0)
-    for t in range(subs):
-        sums.combine(t)
-    project(peers - 1, 0)
-    loads[4].wait()
-    gain = gain_ref[...]
-    ring = Spread(whole, own_rows, me, gather_send, gather_recv, SUB)
-    gain_part = jnp.zeros((1, width), f32)
-    for t in range(subs):
-        rows = rows_of(t)
-        din = sums.collect(t)
-        x = x_v[rows, :].astype(f32)
-        inverse = lax.rsqrt(jnp.mean(x * x, axis=1, keepdims=True) + epsilon)
-        scaled = x * inverse
-        weighted = din * gain
-        grad = hgrad_ref[rows, :] + inverse * (
-            weighted - scaled * jnp.mean(weighted * scaled, axis=1, keepdims=True)
-        )
-        part(whole, me * own_rows + t * SUB, SUB)[...] = grad.astype(bf16)
-        ring.start(t)
-        gain_part = gain_part + jnp.sum(din * scaled, axis=0, keepdims=True)
-    gains_v[...] = gains_ref[...]
-    for r in range(width // 128):
-        gains_v[r : r + 1, :] = gain_part[:, r * 128 : (r + 1) * 128]
-
-    def gains_copy(k):
-        return head_copy(gains_v, gains_recv.at[k], hs.at[k], hr.at[k], me ^ k)
-
-    def to_group(d):
-        to = lax.rem(flat + d, group)
-        return pltpu.make_async_remote_copy(
-            src_ref=gains_sum, dst_ref=gains_all.at[d], send_sem=gs.at[d], recv_sem=gr.at[d],
-            device_id={"seq": to // cores, "batch": lax.rem(to, cores)}, device_id_type=MESH,
-        )
-
-    for k in range(1, peers):
-        gains_copy(k).start()
-    block_store(me, own_rows, whole, out_hbm, out_sem).start()
-    gathered = gains_v[...]
-    for k in range(1, peers):
-        gains_copy(k).wait_recv()
-        gathered = gathered + gains_recv[k]
-    gains_sum[...] = gathered
-    for d in range(1, group):
-        to_group(d).start()
-    for t in range(subs):
-        ring.forward(t)
-    block_store(me ^ 1, own_rows, whole, out_hbm, out_sem).start()
-    block_store(me ^ 2, own_rows, whole, out_hbm, out_sem).start()
-    for d in range(1, group):
-        to_group(d).wait_recv()
-        gathered = gathered + gains_all[d]
-    gains_out[...] = gathered
-    for t in range(subs):
-        ring.finish(t)
-    block_store(me ^ 3, own_rows, whole, out_hbm, out_sem).start()
-    grad = scatter.finish()
-    for head in range(heads):
-        at = head * (QKV + DV)
-        grad_out[:, at : at + QKV] = grad[:, head * QKV : (head + 1) * QKV]
-        gate_at = conv_cols + head * DV
-        grad_out[:, at + QKV : at + QKV + DV] = grad[:, gate_at : gate_at + DV]
-    small_out[...] = grad[:, conv_cols + values :]
-    for k in range(peers):
-        block_store(k, own_rows, whole, out_hbm, out_sem).wait()
-    for t in range(subs):
-        sums.drain(t)
-        ring.drain(t)
-    for k in range(1, peers):
-        gains_copy(k).wait_send()
-    scatter.drain()
-    for d in range(1, group):
-        to_group(d).wait_send()
-
-
-def input_grads(dp, in_full, gate_full, nin, x, hgrad, gain, gains, extras, heads):
-    peers, places, cores = lax.axis_size("head"), lax.axis_size("seq"), lax.axis_size("batch")
-    group = places * cores
-    total, width = x.shape
-    cols = dp.shape[1]
-    values = gate_full.shape[1] // 2
-    own_rows = total // peers
-    subs = own_rows // SUB
-    shard = width // group
-    shape = jax.ShapeDtypeStruct
-    per_peer = pltpu.SemaphoreType.DMA((peers,))
-    per_member = pltpu.SemaphoreType.DMA((group,))
-    return pl.pallas_call(
-        functools.partial(input_grad_kernel, peers, places, cores, heads),
-        in_specs=[anywhere()] * 5 + [vmem()] * 4,
-        out_specs=[anywhere()] + [vmem()] * 3,
-        out_shape=[
-            shape((total, width), bf16), shape(gains.shape, f32),
-            shape((shard, cols - PAD), f32), shape((shard, PAD), f32),
-        ],
-        scratch_shapes=[
-            pltpu.VMEM((total, cols), bf16),
-            pltpu.VMEM((width, cols - values), bf16),
-            pltpu.VMEM((width, values), bf16),
-            pltpu.VMEM((width, total), bf16),
-            pltpu.VMEM((own_rows, width), bf16),
-            pltpu.VMEM((total, width), bf16),
-            pltpu.VMEM((width, cols), bf16),
-            pltpu.VMEM(gains.shape, f32),
-            pltpu.VMEM((peers,) + gains.shape, f32),
-            pltpu.VMEM(gains.shape, f32),
-            pltpu.VMEM((group,) + gains.shape, f32),
-            pltpu.SemaphoreType.DMA((5,)),
-            pltpu.SemaphoreType.DMA((peers,)),
-        ]
-        + sum_buffers(own_rows, width, subs)
-        + scatter_buffers(places, shard, cols)
-        + [per_peer] * 2
-        + [per_member] * 2,
-        compiler_params=pltpu.CompilerParams(
-            collective_id=2, has_side_effects=True, vmem_limit_bytes=52 * 2**20
-        ),
-        name="input_grads",
-    )(dp, in_full, gate_full, nin, x, hgrad, gain, gains, extras)
 
 
 def late_kernel(units, cells, late_ref, down_in, gate_ref, up_ref, down_ref, out_ref):
@@ -1578,55 +1829,26 @@
     late_grads, ffn_part, normed_grad, hidden_grad, ffn_gain_part, down_own = feed_forward_block(
         nm, ffn_full, ct, normed, gate_full, hidden, ffn_gain_f
     )
-    late_own = lax.psum_scatter(late_grads, ALL, scatter_dimension=0, tiled=True)
-    projected_grad, dconv, ddecay, onorm_grads, result = backward_rule(
+    result, input_grad, gains, in_main, in_small, late_own = backward_rule(
         starts, decay_par, normed_grad, mixed, og, projected, o_gain_full, n, qe, tot, trans, qkv,
-        inv, states, halo, conv_full, hidden, ffn_part, seqs, heads,
+        inv, states, halo, conv_full, hidden, hidden_grad, attn_gain_f, ffn_gain_part, ffn_part,
+        in_full, gate_full, turned_in, x, late_grads, heads,
     )
     taps = CONV * heads
-    per_shard = taps * QKV // shards
-    conv_at = 2 * heads
-    conv_end = conv_at + per_shard // shard
-    onorm_grad = jnp.sum(onorm_grads[:, 0], axis=0)
-    decay_part = jnp.sum(ddecay[:, :2, 0].reshape(heads, seqs, 2), axis=1).T.reshape(1, 1, -1)
-    conv_grad = jnp.sum(dconv.reshape(heads, seqs, CONV, QKV), axis=1).transpose(1, 0, 2)
-    conv_grad = conv_grad.reshape(taps, shards, -1).transpose(1, 0, 2).reshape(shards, -1, shard)
-    decay_part = jnp.pad(decay_part, ((0, 0), (0, 0), (0, shard - 2 * heads)))
-    extras = jnp.concatenate(
-        [
-            jnp.zeros((shards, conv_at, shard), f32),
-            conv_grad,
-            jnp.broadcast_to(decay_part, (shards, 1, shard)),
-            jnp.zeros((shards, PAD - conv_end - 1, shard), f32),
-        ],
-        axis=1,
-    ).transpose(0, 2, 1).reshape(width, PAD)
-    lane_rows = width // 128
-    gains = jnp.concatenate(
-        [
-            jnp.zeros((lane_rows, 128), f32),
-            ffn_gain_part[0].reshape(lane_rows, 128),
-            jnp.pad(onorm_grad, (0, width - DV)).reshape(lane_rows, 128),
-        ]
-    )
-    input_grad, gains, in_main, in_small = input_grads(
-        projected_grad, in_full, gate_full, turned_in, x, hidden_grad, attn_gain_f, gains, extras,
-        heads,
-    )
+    per = QKV // shards
     grad_gate, grad_up, grad_down, grad_out = late_outputs(late_own, down_own, units, cells)
     at = lax.axis_index(ALL)
     gains = gains.reshape(3, width)
     own_gains = lax.dynamic_slice(gains, (0, at * shard), (2, shard))
     onorm_own = lax.dynamic_slice(gains, (2, at * (DV // shards)), (1, DV // shards))
-    small_rows = in_small.T
     return (
         result.reshape(tokens.shape),
         input_grad.reshape(tokens.shape),
         own_gains[0],
         in_main.reshape(shard, heads, QKV + DV),
         in_small[:, : 2 * heads].reshape(shard, heads, 2),
-        small_rows[conv_at:conv_end].reshape(CONV, heads, -1),
-        small_rows[conv_end, : 2 * heads].reshape(2, heads),
+        in_small[:taps, PAD // 2 : PAD // 2 + per].reshape(CONV, heads, per),
+        in_small[0, 2 * heads : 4 * heads].reshape(2, heads),
         onorm_own[0],
         grad_out.reshape(heads, DV, -1),
         own_gains[1],

time: 312 us -> 303 us (0.971)
  Pallas kernels: 227 us -> 219 us
  waiting for transfers between devices: 15 us -> 10.4 us
  local copies, waits for them, and re-layouts: 20.1 us -> 24.5 us
    pallas_call x3 -> x2, Pallas kernels: 132 us -> 120 us  [the longest x1 94 us: backward_rule(): pl.pallas_call(functools.partial(backward_kernel, heads, places, peers, c...]
    all_gather x1, waiting for transfers between devices: 5.39 us -> 1.22 us  [per_device(): ffn_full = lax.all_gather(packed_ffn, ALL, axis=0, tiled=True)]
    unnamed x50 -> x67, local copies, waits for them, and re-layouts: 11.6 us -> 14.7 us
  transfers between devices with their start and end apart: 5 -> 4, of which waited for: 2 -> 2; matrix products, arithmetic and copies ran while one was open for 7% -> 5% of each run, Pallas kernels for 55% -> 22%
where the time goes in v5:
time: 303 us
  Pallas kernels  219 us (72%)
  local copies, waits for them, and re-layouts  24.5 us (8%)
  blocking collectives  14.3 us (5%)
  between operations  14.1 us (5%)
  waiting for transfers between devices  10.4 us (3%)
  matrix products  8.6 us (3%)
  other arithmetic  6.72 us (2%)
  starting transfers between devices  5.04 us (2%)
    pallas_call x1, Pallas kernels, backward_rule(): pl.pallas_call(functools.partial(backward_kernel, heads, places, peers, c...  94 us
    pallas_call x1, Pallas kernels, feed_forward_block(): pl.pallas_call(functools.partial(ffn_kernel, peers, places, cores), in_sp...  54.9 us
    pallas_call x1, Pallas kernels, mixer(): pl.pallas_call(functools.partial(mixer_kernel, peers), in_specs=[anywhere...  41.6 us
    pallas_call x1, Pallas kernels, forward_rule(): pl.pallas_call(functools.partial(forward_kernel, heads, places), grid=(2...  25.9 us
    unnamed x67, local copies, waits for them, and re-layouts  14.7 us
    all_gather x1, blocking collectives, per_device(): small_full = lax.all_gather(small, ALL, axis=0)  14.3 us
    all_gather x1, waiting for transfers between devices, per_device(): in_full = lax.all_gather(packed_in, ALL, axis=0, tiled=True)  9.14 us
    dot_general x2, matrix products, matmul(): return lax.dot_general(a, b, (dims, ((), ())), preferred_element_type=f32)  8.6 us
  transfers between devices with their start and end apart: 4, of which 2 were waited for; matrix products, arithmetic and copies ran while one was open for 5% of the time, Pallas kernels for 22%

profile of v5, /device:TPU:0, one launch (start us, length us, event | category | flops | bytes accessed | tf_op | source)
XLA Modules:
  0.0 302.7 jit_solution(4557362239883594506)
XLA Ops:
  7.2 1.4 convert.54
  11.3 1.1 copy.46
  12.8 4.9 %collective-permute-start = (bf16[2,16,1024]{2,1,0:T(8,128)(2,1)S(1)}, bf16[2,16,1024]{2,1,0:T(8,128)(2,1)S(1)}, u32[]{:S(2)}, u32[]{:S(2)}) collective-permute-start(bf16[2,16,1024]{2,1,0:T(8,128)(2,1)S(1)} %slice.46), channel_id=1, source_target_pairs={{0,8},{8,16},{16,24},{1,9},{9,17},{17,25},{2,10},{10,18},{18,26},{... | collective-permute-start | bytes 196616 | tf_op jit(solution)/shard_map/ppermute | solution.py:1751
  17.9 14.3 %all-gather = bf16[8,1,800]{2,1,0:T(2,128)(2,1)S(1)} all-gather(bf16[1,1,800]{2,1,0:T(2,128)(2,1)S(1)} %maximum_bitcast_fusion), channel_id=1, replica_groups=mesh['seq'=4,'batch'=2,'head'=4] {'seq','batch'}, dimensions={0}, use_global_device_ids=true | all-gather | bytes 14400 | tf_op jit(solution)/shard_map/all_gather | solution.py:1801
  33.4 1.9 multiply_convert_fusion.nin_hbm
  35.6 9.1 %all-gather.5.cloned.1.call-done.win_hbm = bf16[1024,1152]{1,0:T(8,128)(2,1)} async-done(((bf16[128,1152]{1,0:T(8,128)(2,1)}), bf16[1024,1152]{1,0:T(8,128)(2,1)}) %all-gather.5.cloned.1.call-update) | async-done | bytes 2359312 | tf_op jit(solution)/shard_map/all_gather | solution.py:1800
  44.8 2.2 fusion.halo_ref
  47.0 6.4 %fusion.11.main_ref.rate_ref = f32[1024,1152]{1,0:T(8,128)} fusion(bf16[1024,1024]{1,0:T(8,128)(2,1)S(1)} %copy-done.17, bf16[1024,1152]{1,0:T(8,128)(2,1)} %all-gather.5.cloned.1.call-done.win_hbm), kind=kOutput, calls=%fused_computation.36 | convolution fusion | flops 2415919104 | bytes 9175040 | tf_op jit(solution)/shard_map/dot_general | solution.py:1759
  53.4 25.9 %forward_rule.1 = (bf16[1024,1024]{1,0:T(8,128)(2,1)S(1)}, bf16[4,4,128,128]{3,2,1,0:T(8,128)(2,1)S(1)}, bf16[4,4,128,128]{3,2,1,0:T(8,128)(2,1)S(1)}, bf16[4,4,...) custom-call(s32[2]{0:T(128)S(1)} %copy-done.15, ...), custom_call_target="tpu_custom_call" | custom-call | tf_op jit(solution)/shard_map/forward_rule/pallas_call | solution.py:613
  79.3 1.3 copy-done.1
  80.7 1.0 copy-done.3
  85.4 41.6 %mixer.1 = (f32[1024,512]{1,0:T(8,128)S(1)}, bf16[1024,512]{1,0:T(8,128)(2,1)S(1)}, bf16[1024,1024]{1,0:T(8,128)(2,1)}, bf16[1024,1024]{1,0:T(8,128)(2,1)}, f32[256,1024]{1,0:T(8,128)S(1)}) custom-call(bf16[1024,1024]{1,0:T(8,128)(2,1)} %multiply_convert_fusion.nin_hbm, f32[1024,512]{1,0:T(8,128)} %get-tuple-element.41.mixed_hbm.mixed_ref, ...), custom_call_target="tpu_custom_call" | custom-call | tf_op jit(solution)/shard_map/mixer/pallas_call | solution.py:1478
  128.0 1.3 copy-done.2
  130.3 1.2 all-gather.9.cloned.1.call-done.ffn_hbm
  131.5 54.9 %feed_forward.1 = (bf16[1024,2048]{1,0:T(8,128)(2,1)}, bf16[1024,1024]{1,0:T(8,128)(2,1)}, f32[1024,512]{1,0:T(8,128)}, f32[256,1024]{1,0:T(8,128)}, f32[8,1024]{1,0:T(8,128)}, /*index=5*/f32[128,768]{1,0:T(8,128)}) custom-call(bf16[1024,1024]{1,0:T(8,128)(2,1)} %get-tuple-element.42.nm_hbm, bf16[1024,2304]{1,0:T(8,128)(2,1)} %all-gather.9.cloned.1.call-done.ffn_hbm, ...), custom_call_target="tpu_custom_call" | custom-call | tf_op jit(solution)/shard_map/feed_forward/pallas_call | solution.py:1684
  186.4 94.0 %backward_rule.1 = (bf16[1024,1024]{1,0:T(8,128)(2,1)}, bf16[1024,1024]{1,0:T(8,128)(2,1)}, f32[24,128]{1,0:T(8,128)}, f32[128,1536]{1,0:T(8,128)}, f32[128,128]{1,0:T(8,128)}, /*index=5*/f32[128,2048]{1,0:T(8,128)}) custom-call(s32[2]{0:T(128)} %start_ref.3, f32[2,2]{1,0:T(2,128)} %decay_ref.3, f32[1024,512]{1,0:T(8,128)} %get-tuple-element.45.dn_ref, ...), custom_call_target="tpu_custom_call" | custom-call | tf_op jit(solution)/shard_map/backward_rule/pallas_call | solution.py:1266
  280.4 1.3 slice.54
  282.5 2.6 late_outputs.1
  285.1 1.3 pad_maximum_fusion
  286.4 1.1 copy.48
  287.5 2.5 reshape.236
  292.5 1.3 copy.60
  293.8 1.0 copy-done.18
  294.8 1.3 copy.61
  (104 shorter events, 13.3 us)
Async XLA Ops:
  7.2 1.8 copy-start.26
  7.2 2.9 copy-start.22
  7.2 37.6 %all-gather.5.cloned.1.call-start = ((), (), s32[]{:S(2)}) async-start(), calls=%async_computation | async-start | bytes 2654208 | tf_op jit(solution)/shard_map/all_gather | solution.py:1800
  8.7 2.5 copy-start.20
  8.9 2.3 copy-start.21
  9.9 75.4 %all-gather.7.cloned.1.call-start = ((), (), s32[]{:S(2)}) async-start(), calls=%async_computation.1 | async-start | bytes 2359296 | tf_op jit(solution)/shard_map/all_gather | solution.py:1802
  11.0 1.8 copy-start.16
  11.0 6.7 %copy-start.25 = (f32[4,2,64]{2,1,0:T(2,128)S(1)}, f32[4,2,64]{2,1,0:T(2,128)}, u32[]{:S(2)}) copy-start(f32[4,2,64]{2,1,0:T(2,128)} %param.18) | copy-start | bytes 6148
  11.1 6.8 %copy-start.29 = (f32[32]{0:T(128)S(1)}, f32[32]{0:T(128)}, u32[]{:S(2)}) copy-start(f32[32]{0:T(128)} %param.20) | copy-start | bytes 388
  11.1 6.8 %copy-start.27 = (f32[128]{0:T(128)S(1)}, f32[128]{0:T(128)}, u32[]{:S(2)}) copy-start(f32[128]{0:T(128)} %param.22) | copy-start | bytes 1540
  11.1 6.8 %copy-start.28 = (f32[128]{0:T(128)S(1)}, f32[128]{0:T(128)}, u32[]{:S(2)}) copy-start(f32[128]{0:T(128)} %param.15) | copy-start | bytes 1540
  11.1 120.4 %all-gather.9.cloned.1.call-start = ((), (), s32[]{:S(2)}) async-start(), calls=%async_computation.2 | async-start | bytes 5308416 | tf_op jit(solution)/shard_map/all_gather | solution.py:1803
  12.8 22.7 %collective-permute-start = (bf16[2,16,1024]{2,1,0:T(8,128)(2,1)S(1)}, bf16[2,16,1024]{2,1,0:T(8,128)(2,1)S(1)}, u32[]{:S(2)}, u32[]{:S(2)}) collective-permute-start(bf16[2,16,1024]{2,1,0:T(8,128)(2,1)S(1)} %slice.46), channel_id=1, source_target_pairs={{0,8},{8,16},{16,24},{1,9},{9,17},{17,25},{2,10},{10,18},{18,26},{... | collective-permute-start | bytes 196616 | tf_op jit(solution)/shard_map/ppermute | solution.py:1751
  33.4 52.0 %copy-start.11 = (f32[8,128]{1,0:T(8,128)}, f32[8,128]{1,0:T(8,128)S(1)}, u32[]{:S(2)}) copy-start(f32[8,128]{1,0:T(8,128)S(1)} %get-tuple-element.120) | copy-start | bytes 12292
  35.4 18.0 %copy-start.9 = (f32[4,1024]{1,0:T(4,128)}, f32[4,1024]{1,0:T(4,128)S(1)}, u32[]{:S(2)}) copy-start(f32[4,1024]{1,0:T(4,128)S(1)} %reshape.241.conv_ref) | copy-start | bytes 49156
  35.5 49.8 %copy-start.12 = (f32[1,256]{1,0:T(1,128)}, f32[1,256]{1,0:T(1,128)S(1)}, u32[]{:S(2)}) copy-start(f32[1,256]{1,0:T(1,128)S(1)} %reshape.243.o_gain_ref) | copy-start | bytes 3076
  44.8 2.2 copy-start.17
  47.0 6.4 %copy-start.8 = (f32[2,16,1024]{2,1,0:T(8,128)}, f32[2,16,1024]{2,1,0:T(8,128)S(1)}, u32[]{:S(2)}) copy-start(f32[2,16,1024]{2,1,0:T(8,128)S(1)} %fusion.halo_ref) | copy-start | bytes 393220
  47.0 6.4 %copy-start.14 = (f32[2,2]{1,0:T(2,128)S(1)}, f32[2,2]{1,0:T(2,128)}, u32[]{:S(2)}) copy-start(f32[2,2]{1,0:T(2,128)} %decay_ref.3) | copy-start | bytes 52
  47.0 6.4 %copy-start.15 = (s32[2]{0:T(128)S(1)}, s32[2]{0:T(128)}, u32[]{:S(2)}) copy-start(s32[2]{0:T(128)} %start_ref.3) | copy-start | bytes 28
  285.0 5.0 %copy-start.24 = (f32[24,128]{1,0:T(8,128)S(1)}, f32[24,128]{1,0:T(8,128)}, u32[]{:S(2)}) copy-start(f32[24,128]{1,0:T(8,128)} %get-tuple-element.61) | copy-start | bytes 36868
  285.0 6.1 %copy-start.23 = (f32[128,128]{1,0:T(8,128)S(1)}, f32[128,128]{1,0:T(8,128)}, u32[]{:S(2)}) copy-start(f32[128,128]{1,0:T(8,128)} %get-tuple-element.63) | copy-start | bytes 196612
  285.1 7.4 %copy-start.19 = (bf16[1024,1024]{1,0:T(8,128)(2,1)S(1)}, bf16[1024,1024]{1,0:T(8,128)(2,1)}, u32[]{:S(2)}) copy-start(bf16[1024,1024]{1,0:T(8,128)(2,1)} %get-tuple-element.59) | copy-start | bytes 6291460
  292.5 2.3 copy-start.18
  (10 other events, 9.3 us)
Sparse Core Ops, SparseCore 0:
  10.2 34.4 all-gather.4
  46.9 28.3 all-gather.6
  77.5 53.9 all-gather.8

commit v6 on v5

--- a/solution.py
+++ b/solution.py
@@ -450,8 +450,12 @@
     pl.semaphore_wait(barrier, peers + group - 2)
 
 
+def in_hbm(dims, kind):
+    return pltpu.HBM(dims, kind)
+
+
 def anywhere():
-    return pl.BlockSpec(memory_space=pl.ANY)
+    return pl.BlockSpec(memory_space=pltpu.HBM)
 
 
 def vmem():
@@ -565,10 +569,13 @@
             at = pl.ds(c * CHUNK, CHUNK)
             mixed_ref[at, :] = o_scr[chain, at, :] + both[DK:]
 
-    def passed(chain):
+    half = DV // 2
+
+    def passed(chain, side):
+        at = pl.ds(side * half, half)
         return along(
-            "seq", send.at[chain], recv.at[chain], send_sem.at[chain], recv_sem.at[chain],
-            jnp.minimum(place + 1, places - 1),
+            "seq", send.at[chain, :, at], recv.at[chain, :, at], send_sem.at[chain, side],
+            recv_sem.at[chain, side], jnp.minimum(place + 1, places - 1),
         )
 
     relayed = step - lag
@@ -576,21 +583,24 @@
     @pl.when((relayed >= 0) & (relayed < chains))
     def _():
         chain = jnp.clip(relayed, 0, chains - 1)
-
-        @pl.when(place > 0)
-        def _():
-            passed(chain).wait_recv()
-
-        @pl.when(place < places - 1)
-        def _():
-            leaving = mm(trans_ref[chain], recv[chain]) + carried_scr[chain]
-            send[chain] = leaving.astype(bf16)
-            passed(chain).start()
+        for side in range(2):
+            at = slice(side * half, (side + 1) * half)
+
+            @pl.when(place > 0)
+            def _():
+                passed(chain, side).wait_recv()
+
+            @pl.when(place < places - 1)
+            def _():
+                leaving = mm(trans_ref[chain], recv[chain, :, at]) + carried_scr[chain, :, at]
+                send[chain, :, at] = leaving.astype(bf16)
+                passed(chain, side).start()
 
     @pl.when((step == 2 * chains - 1) & (place < places - 1))
     def _():
         for chain in range(chains):
-            passed(chain).wait_send()
+            for side in range(2):
+                passed(chain, side).wait_send()
 
 
 def early(chains, make):
@@ -609,7 +619,7 @@
     rates_at = heads * QKV // PAD
     row = lambda first: lambda i: (i // heads, first + i % heads)
     whole = lambda *dims: pl.BlockSpec(dims, lambda j: (0,) * len(dims))
-    shape = jax.ShapeDtypeStruct
+    shape = in_hbm
     return pl.pallas_call(
         functools.partial(forward_kernel, heads, places),
         grid=(2 * chains,),
@@ -648,8 +658,8 @@
             pltpu.VMEM((chains, DK, DV), f32),
             pltpu.VMEM((chains, DK, DV), bf16),
             pltpu.VMEM((chains, DK, DV), bf16),
-            pltpu.SemaphoreType.DMA((chains,)),
-            pltpu.SemaphoreType.DMA((chains,)),
+            pltpu.SemaphoreType.DMA((chains, 2)),
+            pltpu.SemaphoreType.DMA((chains, 2)),
         ],
         compiler_params=pltpu.CompilerParams(
             dimension_semantics=("arbitrary",), collective_id=3, has_side_effects=True,
@@ -739,10 +749,13 @@
             for t in range(subs)
         ]
 
-    def passed(chain):
+    half = DV // 2
+
+    def passed(chain, side):
+        at = pl.ds(side * half, half)
         return along(
-            "seq", send.at[chain], recv.at[chain], send_sem.at[chain], recv_sem.at[chain],
-            jnp.maximum(place - 1, 0),
+            "seq", send.at[chain, :, at], recv.at[chain, :, at], send_sem.at[chain, side],
+            recv_sem.at[chain, side], jnp.maximum(place - 1, 0),
         )
 
     def returned(chain):
@@ -841,6 +854,13 @@
         conv_total = [jnp.zeros((1, QKV), f32) for _ in range(CONV)]
         lanes = lax.broadcasted_iota(jnp.int32, (CHUNK, PAD), 1)
         for c in range(count):
+            for t in range(seqs - 1):
+                if c == count - 1:
+
+                    @pl.when(step == chains + (t + 1) * heads)
+                    def _():
+                        in_sums.combine(t)
+
             at = pl.ds(c * CHUNK, CHUNK)
             q, k, v = qkv_ref[at, 0:DK], qkv_ref[at, DK : 2 * DK], qkv_ref[at, 2 * DK :]
             kf, vf = k.astype(f32), v.astype(f32)
@@ -986,16 +1006,18 @@
     @pl.when((relayed >= 0) & (relayed < chains))
     def _():
         chain = jnp.clip(relayed, 0, chains - 1)
-
-        @pl.when(place < places - 1)
-        def _():
-            passed(chain).wait_recv()
-
-        @pl.when(place > 0)
-        def _():
-            earlier = mm(trans_ref[chain], recv[chain], TN) + own_scr[chain]
-            send[chain] = earlier.astype(bf16)
-            passed(chain).start()
+        for side in range(2):
+            at = slice(side * half, (side + 1) * half)
+
+            @pl.when(place < places - 1)
+            def _():
+                passed(chain, side).wait_recv()
+
+            @pl.when(place > 0)
+            def _():
+                earlier = mm(trans_ref[chain], recv[chain, :, at], TN) + own_scr[chain, :, at]
+                send[chain, :, at] = earlier.astype(bf16)
+                passed(chain, side).start()
 
     @pl.when(step == chains - 1)
     def _():
@@ -1080,10 +1102,6 @@
                 for load in loads[:2]:
                     load.wait()
             project(t)
-
-        @pl.when(step == chains + (t + 1) * heads)
-        def _():
-            in_sums.combine(t)
 
     def own_input_grads(t):
         rows = pl.ds(t * SUB, SUB)
@@ -1218,7 +1236,8 @@
         def _():
             for chain in range(chains):
                 returned(chain).wait_send()
-                passed(chain).wait_send()
+                for side in range(2):
+                    passed(chain, side).wait_send()
 
         sums.drain(0)
         for t in range(subs):
@@ -1333,7 +1352,9 @@
             pltpu.VMEM((peers, gain_rows, 128), f32),
             pltpu.VMEM((gain_rows, 128), f32),
             pltpu.VMEM((group, gain_rows, 128), f32),
-            per_chain, per_chain, per_chain, per_chain,
+            pltpu.SemaphoreType.DMA((chains, 2)),
+            pltpu.SemaphoreType.DMA((chains, 2)),
+            per_chain, per_chain,
             pieces,
             pltpu.SemaphoreType.DMA((3,)),
             pltpu.SemaphoreType.DMA((places,)),
@@ -1474,7 +1495,7 @@
     values = mixed.shape[1]
     own_rows = total // peers
     subs = own_rows // SUB
-    shape = jax.ShapeDtypeStruct
+    shape = in_hbm
     return pl.pallas_call(
         functools.partial(mixer_kernel, peers),
         in_specs=[anywhere()] * 4 + [vmem()] * 2,
@@ -1680,7 +1701,7 @@
     values = normed.shape[1]
     cells = ffn_full.shape[1] // 3
     shard = width // (places * cores)
-    shape = jax.ShapeDtypeStruct
+    shape = in_hbm
     return pl.pallas_call(
         functools.partial(ffn_kernel, peers, places, cores),
         in_specs=[anywhere()] * 5 + [vmem()] * 2,
@@ -1722,27 +1743,71 @@
     )(nm, ffn_full, ct, normed, weights, hidden, gain)
 
 
-def late_kernel(units, cells, late_ref, down_in, gate_ref, up_ref, down_ref, out_ref):
-    gate_ref[...] = late_ref[:, 0:units].astype(f32)
-    up_ref[...] = late_ref[:, cells : cells + units].astype(f32)
+def results_kernel(
+    units, cells, late_ref, down_in, main_in, small_in, out_hbm, igrad_hbm,
+    cells_ref, down_ref, mixer_ref, main_ref, rates_ref, conv_ref, decay_ref, out_ref, igrad_ref,
+    out_v, igrad_v, sems,
+):
+    loads = [
+        pltpu.make_async_copy(out_hbm, out_v, sems.at[0]),
+        pltpu.make_async_copy(igrad_hbm, igrad_v, sems.at[1]),
+    ]
+    copies = [
+        pltpu.make_async_copy(out_v, out_ref, sems.at[2]),
+        pltpu.make_async_copy(igrad_v, igrad_ref, sems.at[3]),
+    ]
+    for load in loads:
+        load.start()
+    taps, heads, per = conv_ref.shape
+    for part_at in range(2):
+        at = part_at * cells
+        cells_ref[part_at] = late_ref[:, at : at + cells].T[0:units]
     down_ref[...] = down_in[...].T[0:units]
-    out_ref[...] = late_ref[:, 2 * cells :].astype(f32).T
-
-
-def late_outputs(late, down, units, cells):
+    mixer_ref[...] = late_ref[:, 2 * cells :].T
+    for load, copy in zip(loads, copies):
+        load.wait()
+        copy.start()
+    wide = main_ref.shape[2]
+    for head in range(heads):
+        main_ref[:, head, :] = main_in[:, head * wide : (head + 1) * wide]
+    small = small_in[...]
+    rates_ref[...] = small.T[0 : 2 * heads]
+    for tap in range(taps):
+        conv_ref[tap] = small[tap * heads : (tap + 1) * heads, PAD // 2 : PAD // 2 + per]
+    for row in range(2):
+        at = (2 + row) * heads
+        decay_ref[row : row + 1, :] = small[0:1, at : at + heads]
+    for copy in copies:
+        copy.wait()
+
+
+def results(late, down, main, small, out, igrad, units, cells, heads, per):
     shard = late.shape[0]
     values = late.shape[1] - 2 * cells
     shape = jax.ShapeDtypeStruct
     return pl.pallas_call(
-        functools.partial(late_kernel, units, cells),
-        in_specs=[vmem()] * 2,
-        out_specs=[vmem()] * 4,
+        functools.partial(results_kernel, units, cells),
+        in_specs=[vmem()] * 4 + [anywhere()] * 2,
+        out_specs=[vmem()] * 7 + [anywhere()] * 2,
         out_shape=[
-            shape((shard, units), f32), shape((shard, units), f32), shape((units, shard), f32),
+            shape((2, units, shard), f32),
+            shape((units, shard), f32),
             shape((values, shard), f32),
+            shape((shard, heads, main.shape[1] // heads), f32),
+            shape((2 * heads, shard), f32),
+            shape((CONV, heads, per), f32),
+            shape((2, heads), f32),
+            in_hbm(out.shape, out.dtype),
+            in_hbm(igrad.shape, igrad.dtype),
         ],
-        name="late_outputs",
-    )(late, down)
+        scratch_shapes=[
+            pltpu.VMEM(out.shape, out.dtype),
+            pltpu.VMEM(igrad.shape, igrad.dtype),
+            pltpu.SemaphoreType.DMA((4,)),
+        ],
+        compiler_params=pltpu.CompilerParams(vmem_limit_bytes=32 * 2**20),
+        name="results",
+    )(late, down, main, small, out, igrad)
 
 
 def shifted(shard, axis, by):
@@ -1818,7 +1883,7 @@
         return (rows * root_scale(rows) * attn_gain_f).astype(bf16)
 
     normed_in = normed_rows(x)
-    projected = matmul(normed_in, in_full)
+    projected = pltpu.with_memory_space_constraint(matmul(normed_in, in_full), pltpu.HBM)
     halo = matmul(normed_rows(before), in_full[:, :conv_cols]).reshape(seqs, HALO, conv_cols)
     qkv, inv, n, qe, tot, trans, states, mixed = forward_rule(
         starts, decay_par, projected, halo, conv_full, seqs, heads
@@ -1834,25 +1899,28 @@
         inv, states, halo, conv_full, hidden, hidden_grad, attn_gain_f, ffn_gain_part, ffn_part,
         in_full, gate_full, turned_in, x, late_grads, heads,
     )
-    taps = CONV * heads
-    per = QKV // shards
-    grad_gate, grad_up, grad_down, grad_out = late_outputs(late_own, down_own, units, cells)
+    grad_cells, grad_down, grad_out, grad_in, grad_rates, grad_conv, grad_decay, out, input_grad = (
+        results(
+            late_own, down_own, in_main, in_small, result, input_grad, units, cells, heads,
+            QKV // shards,
+        )
+    )
     at = lax.axis_index(ALL)
     gains = gains.reshape(3, width)
     own_gains = lax.dynamic_slice(gains, (0, at * shard), (2, shard))
     onorm_own = lax.dynamic_slice(gains, (2, at * (DV // shards)), (1, DV // shards))
     return (
-        result.reshape(tokens.shape),
+        out.reshape(tokens.shape),
         input_grad.reshape(tokens.shape),
         own_gains[0],
-        in_main.reshape(shard, heads, QKV + DV),
-        in_small[:, : 2 * heads].reshape(shard, heads, 2),
-        in_small[:taps, PAD // 2 : PAD // 2 + per].reshape(CONV, heads, per),
-        in_small[0, 2 * heads : 4 * heads].reshape(2, heads),
+        grad_in,
+        grad_rates.reshape(heads, 2, shard).transpose(2, 0, 1),
+        grad_conv,
+        grad_decay,
         onorm_own[0],
         grad_out.reshape(heads, DV, -1),
         own_gains[1],
-        jnp.stack([grad_gate, grad_up], axis=1),
+        grad_cells.transpose(2, 0, 1),
         grad_down,
     )
 

time: 303 us -> 295 us (0.974)
  local copies, waits for them, and re-layouts: 24.5 us -> 13.1 us
  waiting for transfers between devices: 10.4 us -> 18.6 us
    all_gather x1, waiting for transfers between devices: 1.22 us -> 8.26 us  [per_device(): ffn_full = lax.all_gather(packed_ffn, ALL, axis=0, tiled=True)]
    unnamed x67 -> x50, local copies, waits for them, and re-layouts: 14.7 us -> 8.56 us
  transfers between devices with their start and end apart: 4 -> 4, of which waited for: 2 -> 2; matrix products, arithmetic and copies ran while one was open for 5% -> 4% of each run, Pallas kernels for 22% -> 23%
where the time goes in v6:
time: 295 us
  Pallas kernels  217 us (74%)
  waiting for transfers between devices  18.6 us (6%)
  blocking collectives  14.5 us (5%)
  between operations  14.2 us (5%)
  local copies, waits for them, and re-layouts  13.1 us (4%)
  matrix products  8.47 us (3%)
  starting transfers between devices  5.04 us (2%)
  other arithmetic  4.08 us (1%)
    pallas_call x1, Pallas kernels, backward_rule(): pl.pallas_call(functools.partial(backward_kernel, heads, places, peers, c...  92.1 us
    pallas_call x1, Pallas kernels, feed_forward_block(): pl.pallas_call(functools.partial(ffn_kernel, peers, places, cores), in_sp...  52.3 us
    pallas_call x1, Pallas kernels, mixer(): pl.pallas_call(functools.partial(mixer_kernel, peers), in_specs=[anywhere...  41.1 us
    pallas_call x1, Pallas kernels, forward_rule(): pl.pallas_call(functools.partial(forward_kernel, heads, places), grid=(2...  27.2 us
    all_gather x1, blocking collectives, per_device(): small_full = lax.all_gather(small, ALL, axis=0)  14.5 us
    all_gather x1, waiting for transfers between devices, per_device(): in_full = lax.all_gather(packed_in, ALL, axis=0, tiled=True)  10.3 us
    unnamed x50, local copies, waits for them, and re-layouts  8.56 us
    dot_general x2, matrix products, matmul(): return lax.dot_general(a, b, (dims, ((), ())), preferred_element_type=f32)  8.47 us
  transfers between devices with their start and end apart: 4, of which 2 were waited for; matrix products, arithmetic and copies ran while one was open for 4% of the time, Pallas kernels for 23%

profile of v6, /device:TPU:0, one launch (start us, length us, event | category | flops | bytes accessed | tf_op | source)
XLA Modules:
  0.0 294.8 jit_solution(17898503530367949757)
XLA Ops:
  7.2 1.4 convert.54
  9.1 0.8 concatenate.32
  10.3 0.7 pad_maximum_fusion
  11.3 1.1 copy.40
  12.8 4.9 %collective-permute-start = (bf16[2,16,1024]{2,1,0:T(8,128)(2,1)S(1)}, bf16[2,16,1024]{2,1,0:T(8,128)(2,1)S(1)}, u32[]{:S(2)}, u32[]{:S(2)}) collective-permute-start(bf16[2,16,1024]{2,1,0:T(8,128)(2,1)S(1)} %slice.37), channel_id=1, source_target_pairs={{0,8},{8,16},{16,24},{1,9},{9,17},{17,25},{2,10},{10,18},{18,26},{... | collective-permute-start | bytes 196616 | tf_op jit(solution)/shard_map/ppermute | solution.py:1816
  17.9 14.5 %all-gather = bf16[8,1,800]{2,1,0:T(2,128)(2,1)S(1)} all-gather(bf16[1,1,800]{2,1,0:T(2,128)(2,1)S(1)} %maximum_bitcast_fusion), channel_id=1, replica_groups=mesh['seq'=4,'batch'=2,'head'=4] {'seq','batch'}, dimensions={0}, use_global_device_ids=true | all-gather | bytes 14400 | tf_op jit(solution)/shard_map/all_gather | solution.py:1866
  33.0 0.6 slice_convert_fusion.3
  34.5 10.3 %all-gather.5.cloned.1.call-done.win_hbm = bf16[1024,1152]{1,0:T(8,128)(2,1)} async-done(((bf16[128,1152]{1,0:T(8,128)(2,1)}), bf16[1024,1152]{1,0:T(8,128)(2,1)}) %all-gather.5.cloned.1.call-update) | async-done | bytes 2359312 | tf_op jit(solution)/shard_map/all_gather | solution.py:1865
  44.8 2.1 fusion.halo_ref
  46.9 6.4 %fusion.11.main_ref.rate_ref = f32[1024,1152]{1,0:T(8,128)} fusion(bf16[1024,1024]{1,0:T(8,128)(2,1)S(1)} %multiply_convert_fusion.nin_hbm, bf16[1024,1152]{1,0:T(8,128)(2,1)} %all-gather.5.cloned.1.call-done.win_hbm), kind=kOutput, calls=%fused_computation.34 | convolution fusion | flops 2415919104 | bytes 9175040 | tf_op jit(solution)/shard_map/dot_general | solution.py:1824
  53.3 27.2 %forward_rule.1 = (bf16[1024,1024]{1,0:T(8,128)(2,1)}, bf16[4,4,128,128]{3,2,1,0:T(8,128)(2,1)}, bf16[4,4,128,128]{3,2,1,0:T(8,128)(2,1)}, bf16[4,4,128,128]{3,2...) custom-call(s32[2]{0:T(128)S(1)} %copy-done.12, ...), custom_call_target="tpu_custom_call" | custom-call | tf_op jit(solution)/shard_map/forward_rule/pallas_call | solution.py:623
  80.6 1.6 copy-done
  82.2 41.1 %mixer.1 = (f32[1024,512]{1,0:T(8,128)}, bf16[1024,512]{1,0:T(8,128)(2,1)}, bf16[1024,1024]{1,0:T(8,128)(2,1)}, bf16[1024,1024]{1,0:T(8,128)(2,1)}, f32[256,1024]{1,0:T(8,128)}) custom-call(bf16[1024,1024]{1,0:T(8,128)(2,1)S(1)} %multiply_convert_fusion.nin_hbm, f32[1024,512]{1,0:T(8,128)S(1)} %copy-done, ...), custom_call_target="tpu_custom_call" | custom-call | tf_op jit(solution)/shard_map/mixer/pallas_call | solution.py:1499
  123.2 8.3 %all-gather.9.cloned.1.call-done.ffn_hbm = bf16[1024,2304]{1,0:T(8,128)(2,1)} async-done(((bf16[128,2304]{1,0:T(8,128)(2,1)}), bf16[1024,2304]{1,0:T(8,128)(2,1)}) %all-gather.9.cloned.1.call-update) | async-done | bytes 4718608 | tf_op jit(solution)/shard_map/all_gather | solution.py:1868
  131.5 52.3 %feed_forward.1 = (bf16[1024,2048]{1,0:T(8,128)(2,1)}, bf16[1024,1024]{1,0:T(8,128)(2,1)}, f32[1024,512]{1,0:T(8,128)}, f32[256,1024]{1,0:T(8,128)}, f32[8,1024]{1,0:T(8,128)}, /*index=5*/f32[128,768]{1,0:T(8,128)}) custom-call(bf16[1024,1024]{1,0:T(8,128)(2,1)} %get-tuple-element.47.nm_hbm, bf16[1024,2304]{1,0:T(8,128)(2,1)} %all-gather.9.cloned.1.call-done.ffn_hbm, ...), custom_call_target="tpu_custom_call" | custom-call | tf_op jit(solution)/shard_map/feed_forward/pallas_call | solution.py:1705
  183.8 92.1 %backward_rule.1 = (bf16[1024,1024]{1,0:T(8,128)(2,1)}, bf16[1024,1024]{1,0:T(8,128)(2,1)}, f32[24,128]{1,0:T(8,128)}, f32[128,1536]{1,0:T(8,128)}, f32[128,128]{1,0:T(8,128)}, /*index=5*/f32[128,2048]{1,0:T(8,128)}) custom-call(s32[2]{0:T(128)} %start_ref.3, f32[2,2]{1,0:T(2,128)} %decay_ref.3, f32[1024,512]{1,0:T(8,128)} %get-tuple-element.50.dn_ref, ...), custom_call_target="tpu_custom_call" | custom-call | tf_op jit(solution)/shard_map/backward_rule/pallas_call | solution.py:1285
  275.9 0.7 reshape.229
  277.2 0.6 dynamic-slice_bitcast_fusion
  277.7 1.6 copy-done.1
  279.3 1.6 copy-done.2
  280.9 1.2 copy-done.3
  282.1 1.1 copy-done.4
  283.3 0.8 copy-done.8
  284.1 4.1 %results.1 = (f32[2,704,128]{2,1,0:T(8,128)}, f32[704,128]{1,0:T(8,128)}, f32[512,128]{1,0:T(8,128)}, f32[128,2,768]{2,1,0:T(2,128)}, f32[4,128]{1,0:T(4,128)}, ...) custom-call(f32[128,2048]{1,0:T(8,128)S(1)} %copy-done.3, ...), custom_call_target="tpu_custom_call" | custom-call | tf_op jit(solution)/shard_map/results/pallas_call | solution.py:1788
  (81 shorter events, 3.5 us)
Async XLA Ops:
  7.2 1.8 copy-start.19
  7.2 2.9 copy-start.17
  7.2 37.6 %all-gather.5.cloned.1.call-start = ((), (), s32[]{:S(2)}) async-start(), calls=%async_computation | async-start | bytes 2654208 | tf_op jit(solution)/shard_map/all_gather | solution.py:1865
  8.7 2.5 copy-start.15
  8.9 2.3 copy-start.16
  9.9 70.6 %all-gather.7.cloned.1.call-start = ((), (), s32[]{:S(2)}) async-start(), calls=%async_computation.1 | async-start | bytes 2359296 | tf_op jit(solution)/shard_map/all_gather | solution.py:1867
  11.0 1.8 copy-start.13
  11.0 6.7 %copy-start.18 = (f32[4,2,64]{2,1,0:T(2,128)S(1)}, f32[4,2,64]{2,1,0:T(2,128)}, u32[]{:S(2)}) copy-start(f32[4,2,64]{2,1,0:T(2,128)} %param.18) | copy-start | bytes 6148
  11.1 6.8 %copy-start.22 = (f32[32]{0:T(128)S(1)}, f32[32]{0:T(128)}, u32[]{:S(2)}) copy-start(f32[32]{0:T(128)} %param.20) | copy-start | bytes 388
  11.1 6.8 %copy-start.20 = (f32[128]{0:T(128)S(1)}, f32[128]{0:T(128)}, u32[]{:S(2)}) copy-start(f32[128]{0:T(128)} %param.22) | copy-start | bytes 1540
  11.1 6.8 %copy-start.21 = (f32[128]{0:T(128)S(1)}, f32[128]{0:T(128)}, u32[]{:S(2)}) copy-start(f32[128]{0:T(128)} %param.15) | copy-start | bytes 1540
  11.1 120.4 %all-gather.9.cloned.1.call-start = ((), (), s32[]{:S(2)}) async-start(), calls=%async_computation.2 | async-start | bytes 5308416 | tf_op jit(solution)/shard_map/all_gather | solution.py:1868
  12.8 21.6 %collective-permute-start = (bf16[2,16,1024]{2,1,0:T(8,128)(2,1)S(1)}, bf16[2,16,1024]{2,1,0:T(8,128)(2,1)S(1)}, u32[]{:S(2)}, u32[]{:S(2)}) collective-permute-start(bf16[2,16,1024]{2,1,0:T(8,128)(2,1)S(1)} %slice.37), channel_id=1, source_target_pairs={{0,8},{8,16},{16,24},{1,9},{9,17},{17,25},{2,10},{10,18},{18,26},{... | collective-permute-start | bytes 196616 | tf_op jit(solution)/shard_map/ppermute | solution.py:1816
  17.9 15.7 %copy-start.14 = (bf16[2,512,1024]{2,1,0:T(8,128)(2,1)S(1)}, bf16[2,512,1024]{2,1,0:T(8,128)(2,1)}, u32[]{:S(2)}) copy-start(bf16[2,512,1024]{2,1,0:T(8,128)(2,1)} %param.13) | copy-start | bytes 6291460
  33.6 47.0 %copy-start.9 = (f32[8,128]{1,0:T(8,128)}, f32[8,128]{1,0:T(8,128)S(1)}, u32[]{:S(2)}) copy-start(f32[8,128]{1,0:T(8,128)S(1)} %get-tuple-element.82) | copy-start | bytes 12292
  34.4 18.9 %copy-start.7 = (f32[4,1024]{1,0:T(4,128)}, f32[4,1024]{1,0:T(4,128)S(1)}, u32[]{:S(2)}) copy-start(f32[4,1024]{1,0:T(4,128)S(1)} %reshape.233.conv_ref) | copy-start | bytes 49156
  34.4 46.1 %copy-start.10 = (f32[1,256]{1,0:T(1,128)}, f32[1,256]{1,0:T(1,128)S(1)}, u32[]{:S(2)}) copy-start(f32[1,256]{1,0:T(1,128)S(1)} %reshape.235.o_gain_ref) | copy-start | bytes 3076
  46.9 6.4 %copy-start.5 = (f32[2,16,1024]{2,1,0:T(8,128)}, f32[2,16,1024]{2,1,0:T(8,128)S(1)}, u32[]{:S(2)}) copy-start(f32[2,16,1024]{2,1,0:T(8,128)S(1)} %fusion.halo_ref) | copy-start | bytes 393220
  46.9 6.4 %copy-start.11 = (f32[2,2]{1,0:T(2,128)S(1)}, f32[2,2]{1,0:T(2,128)}, u32[]{:S(2)}) copy-start(f32[2,2]{1,0:T(2,128)} %decay_ref.3) | copy-start | bytes 52
  46.9 6.4 %copy-start.12 = (s32[2]{0:T(128)S(1)}, s32[2]{0:T(128)}, u32[]{:S(2)}) copy-start(s32[2]{0:T(128)} %start_ref.3) | copy-start | bytes 28
  80.6 1.6 copy-start
  183.8 93.9 %copy-start.6 = (f32[128,768]{1,0:T(8,128)S(1)}, f32[128,768]{1,0:T(8,128)}, u32[]{:S(2)}) copy-start(f32[128,768]{1,0:T(8,128)} %get-tuple-element.65.down_in) | copy-start | bytes 1179652
  277.7 1.6 copy-start.1
  279.3 1.6 copy-start.2
  (3 other events, 3.2 us)
Sparse Core Ops, SparseCore 0:
  10.2 34.5 all-gather.4
  47.0 28.2 all-gather.6
  77.5 53.9 all-gather.8

commit v7 on v6

--- a/solution.py
+++ b/solution.py
@@ -435,7 +435,7 @@
     ]
 
 
-def greet_group(me, peers, places, cores):
+def call_group(me, peers, places, cores):
     barrier = pltpu.get_barrier_semaphore()
     group = places * cores
     flat = lax.axis_index("seq") * cores + lax.axis_index("batch")
@@ -447,7 +447,15 @@
             barrier, inc=1, device_id={"seq": to // cores, "batch": lax.rem(to, cores)},
             device_id_type=MESH,
         )
-    pl.semaphore_wait(barrier, peers + group - 2)
+
+
+def meet_group(peers, places, cores):
+    pl.semaphore_wait(pltpu.get_barrier_semaphore(), peers + places * cores - 2)
+
+
+def greet_group(me, peers, places, cores):
+    call_group(me, peers, places, cores)
+    meet_group(peers, places, cores)
 
 
 def in_hbm(dims, kind):
@@ -494,10 +502,6 @@
         @pl.when(place == 0)
         def _():
             recv[...] = jnp.zeros_like(recv)
-
-        @pl.when(place < places - 1)
-        def _():
-            pl.semaphore_wait(barrier, 1)
 
     @pl.when(step < chains)
     def _():
@@ -578,6 +582,10 @@
             recv_sem.at[chain, side], jnp.minimum(place + 1, places - 1),
         )
 
+    @pl.when((step == 0) & (place < places - 1))
+    def _():
+        pl.semaphore_wait(pltpu.get_barrier_semaphore(), 1)
+
     relayed = step - lag
 
     @pl.when((relayed >= 0) & (relayed < chains))
@@ -611,12 +619,11 @@
     return lambda j: make(jnp.maximum(j - chains, 0))
 
 
-def forward_rule(starts, decay_par, projected, halo, conv_w, seqs, heads):
+def forward_rule(starts, decay_par, projected, halo, rates, conv_w, seqs, heads):
     places = lax.axis_size("seq")
     chains = seqs * heads
     length = projected.shape[0] // seqs
     count = length // CHUNK
-    rates_at = heads * QKV // PAD
     row = lambda first: lambda i: (i // heads, first + i % heads)
     whole = lambda *dims: pl.BlockSpec(dims, lambda j: (0,) * len(dims))
     shape = in_hbm
@@ -628,7 +635,7 @@
             smem(),
             pl.BlockSpec((length, QKV), early(chains, row(0))),
             pl.BlockSpec((1, HALO, QKV), early(chains, lambda i: (i // heads, 0, i % heads))),
-            pl.BlockSpec((length, PAD), early(chains, lambda i: (i // heads, rates_at))),
+            pl.BlockSpec((length, PAD), early(chains, lambda i: (i // heads, 0))),
             pl.BlockSpec((CONV, QKV), early(chains, lambda i: (0, i % heads))),
         ],
         out_specs=[
@@ -663,17 +670,17 @@
         ],
         compiler_params=pltpu.CompilerParams(
             dimension_semantics=("arbitrary",), collective_id=3, has_side_effects=True,
-            vmem_limit_bytes=48 * 2**20,
+            vmem_limit_bytes=62 * 2**20,
         ),
         name="forward_rule",
-    )(starts, decay_par, projected, halo, projected, conv_w)
+    )(starts, decay_par, projected, halo, rates, conv_w)
 
 
 def backward_kernel(
     heads, places, peers, cores, start_ref, decay_ref,
     dn_ref, mixed_ref, og_ref, o_gain_ref, n_ref, qe_ref, tot_ref, trans_ref,
     qkv_ref, inv_ref, s_ref, main_ref, halo_ref, rate_ref, conv_ref,
-    hidden_ref, hgrad_ref, gain_ref, ffn_gain_ref, ffnp_hbm, win_hbm, wog_hbm, nin_hbm, x_hbm,
+    hidden_ref, hgrad_ref, gain_ref, ffn_gain_ref, ffnp_hbm, win_hbm, wog_hbm, wrates_hbm, nin_hbm, x_hbm,
     late_hbm,
     out_hbm, igrad_hbm, gains_out, grad_out, small_out, late_out,
     dp_ref, x_scr, g_scr, do_scr, own_scr, send, recv, tail_scr, halo_send, halo_recv,
@@ -735,9 +742,10 @@
     in_store = Pieces(whole_in, igrad_hbm, total, subs, out_sem.at[1])
     own_x = Pieces(x_hbm, x_v, total, subs, x_sem)
     loads = [
-        pltpu.make_async_copy(win_hbm, win_v, in_sem.at[0]),
-        pltpu.make_async_copy(wog_hbm.at[:, pl.ds(0, values)], wog_v, in_sem.at[1]),
-        pltpu.make_async_copy(nin_hbm, nin_v, in_sem.at[2]),
+        pltpu.make_async_copy(win_hbm, win_v.at[:, pl.ds(0, conv_cols)], in_sem.at[0]),
+        pltpu.make_async_copy(wrates_hbm, win_v.at[:, pl.ds(conv_cols, PAD)], in_sem.at[1]),
+        pltpu.make_async_copy(wog_hbm.at[:, pl.ds(0, values)], wog_v, in_sem.at[2]),
+        pltpu.make_async_copy(nin_hbm, nin_v, in_sem.at[3]),
     ]
 
     def ffn_loads(k):
@@ -785,15 +793,7 @@
         for load in loads:
             load.start()
         own_x.start(me)
-        greet_group(me, peers, places, cores)
-        for k in range(peers - 1, 0, -1):
-            for load in ffn_loads(k):
-                load.wait()
-            sums.start(k, 0)
-        for load in ffn_loads(0):
-            load.wait()
-        for d in range(places):
-            late_line.core_copy(d, late_source(d)).start()
+        call_group(me, peers, places, cores)
 
     @pl.when(step < chains)
     def _():
@@ -826,6 +826,18 @@
             )
         o_gain_scr[0:1, :] = o_gain_scr[0:1, :] + gain_total
         own_scr[step] = state
+
+    @pl.when(step == 0)
+    def _():
+        meet_group(peers, places, cores)
+        for k in range(peers - 1, 0, -1):
+            for load in ffn_loads(k):
+                load.wait()
+            sums.start(k, 0)
+        for load in ffn_loads(0):
+            load.wait()
+        for d in range(places):
+            late_line.core_copy(d, late_source(d)).start()
 
     @pl.when(step >= chains)
     def _():
@@ -985,7 +997,7 @@
 
     @pl.when(step == chains - 1)
     def _():
-        loads[2].wait()
+        loads[3].wait()
 
         def gate_grads(i, carry):
             d = far_first(i)
@@ -1099,7 +1111,7 @@
         def _():
             mend_ends(t)
             if t == 0:
-                for load in loads[:2]:
+                for load in loads[:3]:
                     load.wait()
             project(t)
 
@@ -1136,7 +1148,7 @@
             kept = jnp.where((lanes >= PAD // 2) & (lanes < PAD // 2 + per), moved, 0.0)
             extras_v[q * shard : q * shard + taps, :] = kept + decay_scr[...]
         if seqs == 1:
-            for load in loads[:2]:
+            for load in loads[:3]:
                 load.wait()
 
         def place_grads(i, carry):
@@ -1254,9 +1266,9 @@
 
 
 def backward_rule(
-    starts, decay_par, dn, mixed, og, projected, o_gain, n, qe, tot, trans, qkv, inv, states, halo,
-    conv_w, hidden, hidden_grad, gain, ffn_gain_part, ffn_part, in_full, gate_full, turned, x, late_grads,
-    heads,
+    starts, decay_par, dn, mixed, og, projected, rates, o_gain, n, qe, tot, trans, qkv, inv, states, halo,
+    conv_w, hidden, hidden_grad, gain, ffn_gain_part, ffn_part, in_full, gate_full,
+    rates_full, turned, x, late_grads, heads,
 ):
     places, peers, cores = lax.axis_size("seq"), lax.axis_size("head"), lax.axis_size("batch")
     chains, count = n.shape[:2]
@@ -1266,7 +1278,6 @@
     width = hidden.shape[1]
     own_rows = hidden.shape[0]
     subs = own_rows // SUB
-    rates_at = heads * QKV // PAD
     values = heads * DV
     cols = heads * (QKV + DV) + PAD
     group = places * cores
@@ -1301,14 +1312,14 @@
             pl.BlockSpec((1, count, DK, DV), late(chains, chain4)),
             pl.BlockSpec((length, QKV), late(chains, row(0))),
             pl.BlockSpec((1, HALO, QKV), late(chains, lambda i: (i // heads, 0, i % heads))),
-            pl.BlockSpec((length, PAD), late(chains, lambda i: (i // heads, rates_at))),
+            pl.BlockSpec((length, PAD), late(chains, lambda i: (i // heads, 0))),
             pl.BlockSpec((CONV, QKV), late(chains, lambda i: (0, i % heads))),
             whole(own_rows, width),
             whole(own_rows, width),
             whole(1, width),
             whole(8, width),
         ]
-        + [anywhere()] * 6,
+        + [anywhere()] * 7,
         out_specs=[
             anywhere(),
             anywhere(),
@@ -1356,7 +1367,7 @@
             pltpu.SemaphoreType.DMA((chains, 2)),
             per_chain, per_chain,
             pieces,
-            pltpu.SemaphoreType.DMA((3,)),
+            pltpu.SemaphoreType.DMA((4,)),
             pltpu.SemaphoreType.DMA((places,)),
             pieces,
             pltpu.SemaphoreType.DMA((2, peers, subs)),
@@ -1374,8 +1385,8 @@
         name="backward_rule",
     )(
         starts, decay_par, dn, mixed, og, o_gain, n, qe, tot, trans, qkv, inv, states, projected,
-        halo, projected, conv_w, hidden, hidden_grad, gain, ffn_gain_part, ffn_part, in_full,
-        gate_full, turned, x, late_grads,
+        halo, rates, conv_w, hidden, hidden_grad, gain, ffn_gain_part, ffn_part, in_full,
+        gate_full, rates_full, turned, x, late_grads,
     )
 
 
@@ -1522,7 +1533,7 @@
         ]
         + sum_buffers(own_rows, width, subs),
         compiler_params=pltpu.CompilerParams(
-            collective_id=1, has_side_effects=True, vmem_limit_bytes=48 * 2**20
+            collective_id=1, has_side_effects=True, vmem_limit_bytes=62 * 2**20
         ),
         name="mixer",
     )(nin, mixed, weights, x, gain, o_gain)
@@ -1531,7 +1542,7 @@
 def ffn_kernel(
     peers, places, cores, nm_hbm, ffn_hbm, ct_hbm, normed_hbm, weights_hbm, hidden_ref, gain_ref,
     grads_hbm, ffnp_hbm, ng_hbm, hgrad_ref, gpart_ref, down_ref,
-    nm_b, ct_b, dgu_b, nm, ffn_v, ct_v, normed_v, wout_v, act, dgu, dm, ffnp_v, grads_v, down_v, ng_v,
+    nm_b, ct_b, dgu_b, nm, ffn_v, ends_v, ct_v, normed_v, wout_v, act, dgu, dm, ffnp_v, grads_v, down_v, ng_v,
     in_sem, out_sem, ng_sem, send, recv, relay, sum_send, sum_recv, gather_send, gather_recv,
     core_recv, seq_send, seq_recv, scatter_sems,
 ):
@@ -1542,8 +1553,21 @@
     subs = own_rows // SUB
     cells = act.shape[1]
     tile = 256
+    whole_cells = cells - PAD
     loads = [
-        pltpu.make_async_copy(ffn_hbm, ffn_v, in_sem.at[0]),
+        pltpu.make_async_copy(
+            ffn_hbm.at[:, pl.ds(p * whole_cells, whole_cells)],
+            ffn_v.at[:, pl.ds(p * cells, whole_cells)], in_sem.at[5 + p],
+        )
+        for p in range(3)
+    ] + [
+        pltpu.make_async_copy(
+            ffn_hbm.at[:, pl.ds(3 * whole_cells, PAD)], ends_v, in_sem.at[0]
+        ),
+        pltpu.make_async_copy(
+            ffn_hbm.at[:, pl.ds(3 * whole_cells + PAD, PAD)],
+            ffn_v.at[:, pl.ds(3 * cells - PAD, PAD)], in_sem.at[8],
+        ),
         pltpu.make_async_copy(nm_hbm, nm, in_sem.at[1]),
         pltpu.make_async_copy(ct_hbm, ct_v, in_sem.at[2]),
         pltpu.make_async_copy(normed_hbm, normed_v, in_sem.at[3]),
@@ -1552,8 +1576,14 @@
     for load in loads:
         load.start()
     greet_group(me, peers, places, cores)
-    for load in loads[:3]:
+    for load in loads[:7]:
         load.wait()
+    low = lax.broadcasted_iota(jnp.int32, ends_v.shape, 1) < PAD // 2
+    ends = ends_v[...].astype(f32)
+    ffn_v[:, whole_cells:cells] = jnp.where(low, ends, 0.0).astype(bf16)
+    ffn_v[:, cells + whole_cells : 2 * cells] = jnp.where(
+        low, pltpu.roll(ends, PAD // 2, 1), 0.0
+    ).astype(bf16)
     gain = gain_ref[...]
     sums = Combine(send, recv, relay, me, sum_send, sum_recv, SUB)
 
@@ -1651,8 +1681,8 @@
         return carry
 
     lax.fori_loop(0, peers, ffn_rows, 0)
-    loads[3].wait()
-    loads[4].wait()
+    loads[7].wait()
+    loads[8].wait()
     for t in range(subs):
         ring.forward(t)
     down_ref[...] = scatter.finish()
@@ -1693,13 +1723,12 @@
     scatter.drain()
 
 
-def feed_forward_block(nm, ffn_full, ct, normed, weights, hidden, gain):
+def feed_forward_block(nm, ffn_full, ct, normed, weights, hidden, gain, cells):
     peers, places, cores = lax.axis_size("head"), lax.axis_size("seq"), lax.axis_size("batch")
     total, width = ct.shape
     own_rows = total // peers
     subs = own_rows // SUB
     values = normed.shape[1]
-    cells = ffn_full.shape[1] // 3
     shard = width // (places * cores)
     shape = in_hbm
     return pl.pallas_call(
@@ -1720,6 +1749,7 @@
             pltpu.VMEM((own_rows, 2 * cells), bf16),
             pltpu.VMEM((total, width), bf16),
             pltpu.VMEM((width, 3 * cells), bf16),
+            pltpu.VMEM((width, PAD), bf16),
             pltpu.VMEM((total, width), bf16),
             pltpu.VMEM((total, values), bf16),
             pltpu.VMEM((width, values), bf16),
@@ -1730,23 +1760,23 @@
             pltpu.VMEM((width, 2 * cells + values), bf16),
             pltpu.VMEM((width, cells), bf16),
             pltpu.VMEM((total, values), f32),
-            pltpu.SemaphoreType.DMA((5,)),
+            pltpu.SemaphoreType.DMA((9,)),
             pltpu.SemaphoreType.DMA((2, max(peers, width // 256))),
             pltpu.SemaphoreType.DMA((peers, subs)),
         ]
         + sum_buffers(own_rows, width, subs)
         + scatter_buffers(places, shard, cells),
         compiler_params=pltpu.CompilerParams(
-            collective_id=5, has_side_effects=True, vmem_limit_bytes=56 * 2**20
+            collective_id=5, has_side_effects=True, vmem_limit_bytes=62 * 2**20
         ),
         name="feed_forward",
     )(nm, ffn_full, ct, normed, weights, hidden, gain)
 
 
 def results_kernel(
-    units, cells, late_ref, down_in, main_in, small_in, out_hbm, igrad_hbm,
+    units, cells, late_hbm, down_hbm, main_hbm, small_hbm, out_hbm, igrad_hbm,
     cells_ref, down_ref, mixer_ref, main_ref, rates_ref, conv_ref, decay_ref, out_ref, igrad_ref,
-    out_v, igrad_v, sems,
+    late_ref, down_in, main_in, small_in, out_v, igrad_v, sems,
 ):
     loads = [
         pltpu.make_async_copy(out_hbm, out_v, sems.at[0]),
@@ -1756,17 +1786,27 @@
         pltpu.make_async_copy(out_v, out_ref, sems.at[2]),
         pltpu.make_async_copy(igrad_v, igrad_ref, sems.at[3]),
     ]
-    for load in loads:
+    firsts = [
+        pltpu.make_async_copy(late_hbm, late_ref, sems.at[4]),
+        pltpu.make_async_copy(down_hbm, down_in, sems.at[5]),
+        pltpu.make_async_copy(main_hbm, main_in, sems.at[6]),
+        pltpu.make_async_copy(small_hbm, small_in, sems.at[7]),
+    ]
+    for load in firsts + loads:
         load.start()
+    firsts[0].wait()
     taps, heads, per = conv_ref.shape
     for part_at in range(2):
         at = part_at * cells
         cells_ref[part_at] = late_ref[:, at : at + cells].T[0:units]
+    firsts[1].wait()
     down_ref[...] = down_in[...].T[0:units]
     mixer_ref[...] = late_ref[:, 2 * cells :].T
     for load, copy in zip(loads, copies):
         load.wait()
         copy.start()
+    firsts[2].wait()
+    firsts[3].wait()
     wide = main_ref.shape[2]
     for head in range(heads):
         main_ref[:, head, :] = main_in[:, head * wide : (head + 1) * wide]
@@ -1787,7 +1827,7 @@
     shape = jax.ShapeDtypeStruct
     return pl.pallas_call(
         functools.partial(results_kernel, units, cells),
-        in_specs=[vmem()] * 4 + [anywhere()] * 2,
+        in_specs=[anywhere()] * 6,
         out_specs=[vmem()] * 7 + [anywhere()] * 2,
         out_shape=[
             shape((2, units, shard), f32),
@@ -1801,11 +1841,15 @@
             in_hbm(igrad.shape, igrad.dtype),
         ],
         scratch_shapes=[
+            pltpu.VMEM(late.shape, f32),
+            pltpu.VMEM(down.shape, f32),
+            pltpu.VMEM(main.shape, f32),
+            pltpu.VMEM(small.shape, f32),
             pltpu.VMEM(out.shape, out.dtype),
             pltpu.VMEM(igrad.shape, igrad.dtype),
-            pltpu.SemaphoreType.DMA((4,)),
+            pltpu.SemaphoreType.DMA((8,)),
         ],
-        compiler_params=pltpu.CompilerParams(vmem_limit_bytes=32 * 2**20),
+        compiler_params=pltpu.CompilerParams(vmem_limit_bytes=62 * 2**20),
         name="results",
     )(late, down, main, small, out, igrad)
 
@@ -1839,25 +1883,28 @@
     value_cols = heads * DV
     units = w_down.shape[0]
     cells = -(-units // 256) * 256
-    spare = cells - units
-
-    packed_in = jnp.concatenate(
-        [
-            w_in[:, :, :QKV].reshape(shard, conv_cols),
-            w_rates.reshape(shard, 2 * heads),
-            jnp.zeros((shard, PAD - 2 * heads), f32),
-        ],
-        axis=1,
-    ).astype(bf16)
+
+    packed_in = w_in[:, :, :QKV].reshape(shard, conv_cols).astype(bf16)
     packed_gate = jnp.concatenate(
         [w_in[:, :, QKV:].reshape(shard, value_cols), w_out.reshape(value_cols, -1).T], axis=1
     ).astype(bf16)
-    packed_ffn = jnp.pad(
-        jnp.stack([w_gu[:, 0], w_gu[:, 1], w_down.T], axis=1).astype(bf16),
-        ((0, 0), (0, 0), (0, spare)),
-    ).reshape(shard, 3 * cells)
+    whole_cells = cells - PAD
+    gate, up, down = w_gu[:, 0], w_gu[:, 1], w_down.T
+    ends = jnp.zeros((shard, PAD // 2 - (units - whole_cells)), f32)
+    packed_ffn = jnp.concatenate(
+        [part[:, :whole_cells] for part in (gate, up, down)]
+        + [
+            piece
+            for part in (gate, up, down)
+            for piece in (part[:, whole_cells:], ends)
+        ]
+        + [jnp.zeros((shard, PAD // 2), f32)],
+        axis=1,
+    ).astype(bf16)
     conv_flat = conv_w.reshape(-1)
-    small = jnp.concatenate([attn_gain, ffn_gain, conv_flat, o_gain]).astype(bf16)
+    small = jnp.concatenate(
+        [attn_gain, ffn_gain, conv_flat, o_gain, w_rates.reshape(-1)]
+    ).astype(bf16)
 
     x = tokens.reshape(total, width)
     ct = cotangent.reshape(total, width)
@@ -1876,28 +1923,33 @@
         .reshape(CONV, conv_cols)
         .astype(f32)
     )
-    o_gain_full = small_full[:, conv_end:].reshape(1, DV).astype(f32)
+    rates_at = conv_end + o_gain.shape[0]
+    o_gain_full = small_full[:, conv_end:rates_at].reshape(1, DV).astype(f32)
+    rates_full = jnp.pad(
+        small_full[:, rates_at:].reshape(width, 2 * heads), ((0, 0), (0, PAD - 2 * heads))
+    )
 
     def normed_rows(rows):
         rows = rows.astype(f32)
         return (rows * root_scale(rows) * attn_gain_f).astype(bf16)
 
     normed_in = normed_rows(x)
+    rates = matmul(normed_in, rates_full)
     projected = pltpu.with_memory_space_constraint(matmul(normed_in, in_full), pltpu.HBM)
-    halo = matmul(normed_rows(before), in_full[:, :conv_cols]).reshape(seqs, HALO, conv_cols)
+    halo = matmul(normed_rows(before), in_full).reshape(seqs, HALO, conv_cols)
     qkv, inv, n, qe, tot, trans, states, mixed = forward_rule(
-        starts, decay_par, projected, halo, conv_full, seqs, heads
+        starts, decay_par, projected, halo, rates, conv_full, seqs, heads
     )
     og, normed, nm, turned_in, hidden = mixer(
         normed_in, mixed, gate_full, x, ffn_gain_f, o_gain_full
     )
     late_grads, ffn_part, normed_grad, hidden_grad, ffn_gain_part, down_own = feed_forward_block(
-        nm, ffn_full, ct, normed, gate_full, hidden, ffn_gain_f
+        nm, ffn_full, ct, normed, gate_full, hidden, ffn_gain_f, cells
     )
     result, input_grad, gains, in_main, in_small, late_own = backward_rule(
-        starts, decay_par, normed_grad, mixed, og, projected, o_gain_full, n, qe, tot, trans, qkv,
+        starts, decay_par, normed_grad, mixed, og, projected, rates, o_gain_full, n, qe, tot, trans, qkv,
         inv, states, halo, conv_full, hidden, hidden_grad, attn_gain_f, ffn_gain_part, ffn_part,
-        in_full, gate_full, turned_in, x, late_grads, heads,
+        in_full, gate_full, rates_full, turned_in, x, late_grads, heads,
     )
     grad_cells, grad_down, grad_out, grad_in, grad_rates, grad_conv, grad_decay, out, input_grad = (
         results(

time: 295 us -> 288 us (0.976)
  waiting for transfers between devices: 18.6 us -> 8.48 us
  Pallas kernels: 217 us -> 222 us
  local copies, waits for them, and re-layouts: 13.1 us -> 9.17 us
    all_gather x1, waiting for transfers between devices: 10.3 us -> 2.24 us  [per_device(): in_full = lax.all_gather(packed_in, ALL, axis=0, tiled=True)]
    unnamed x50 -> x28, local copies, waits for them, and re-layouts: 8.56 us -> 2.47 us
    dot_general x2 -> x3, matrix products: 8.47 us -> 10.2 us  [matmul(): return lax.dot_general(a, b, (dims, ((), ())), preferred_element_type=f32)]
  transfers between devices with their start and end apart: 4 -> 4, of which waited for: 2 -> 2; matrix products, arithmetic and copies ran while one was open for 4% -> 6% of each run, Pallas kernels for 23% -> 24%
where the time goes in v7:
time: 288 us; the launch traced here: 287 us
  Pallas kernels  222 us (77%)
  blocking collectives  14.5 us (5%)
  between operations  14.2 us (5%)
  matrix products  10.2 us (4%)
  local copies, waits for them, and re-layouts  9.17 us (3%)
  waiting for transfers between devices  8.48 us (3%)
  starting transfers between devices  5.04 us (2%)
  other arithmetic  4.08 us (1%)
    pallas_call x1, Pallas kernels, backward_rule(): pl.pallas_call(functools.partial(backward_kernel, heads, places, peers, c...  93.4 us
    pallas_call x1, Pallas kernels, feed_forward_block(): pl.pallas_call(functools.partial(ffn_kernel, peers, places, cores), in_sp...  52.6 us
    pallas_call x1, Pallas kernels, mixer(): pl.pallas_call(functools.partial(mixer_kernel, peers), in_specs=[anywhere...  43.2 us
    pallas_call x1, Pallas kernels, forward_rule(): pl.pallas_call(functools.partial(forward_kernel, heads, places), grid=(2...  26.7 us
    all_gather x1, blocking collectives, per_device(): small_full = lax.all_gather(small, ALL, axis=0)  14.5 us
    dot_general x3, matrix products, matmul(): return lax.dot_general(a, b, (dims, ((), ())), preferred_element_type=f32)  10.2 us
    all_gather x1, waiting for transfers between devices, per_device(): ffn_full = lax.all_gather(packed_ffn, ALL, axis=0, tiled=True)  6.17 us
  transfers between devices with their start and end apart: 4, of which 2 were waited for; matrix products, arithmetic and copies ran while one was open for 6% of the time, Pallas kernels for 24%

profile of v7, /device:TPU:0, one launch (start us, length us, event | category | flops | bytes accessed | tf_op | source)
XLA Modules:
  0.0 287.2 jit_solution(17942062310972687557)
XLA Ops:
  7.2 1.5 convert.63
  8.9 0.7 copy.59
  10.0 0.7 pad_maximum_fusion
  11.6 1.0 concatenate.36
  12.7 4.9 %collective-permute-start = (bf16[2,16,1024]{2,1,0:T(8,128)(2,1)S(1)}, bf16[2,16,1024]{2,1,0:T(8,128)(2,1)S(1)}, u32[]{:S(2)}, u32[]{:S(2)}) collective-permute-start(bf16[2,16,1024]{2,1,0:T(8,128)(2,1)S(1)} %slice.64), channel_id=1, source_target_pairs={{0,8},{8,16},{16,24},{1,9},{9,17},{17,25},{2,10},{10,18},{18,26},{... | collective-permute-start | bytes 196616 | tf_op jit(solution)/shard_map/ppermute | solution.py:1860
  18.1 14.5 %all-gather = bf16[8,1,1312]{2,1,0:T(2,128)(2,1)S(1)} all-gather(bf16[1,1,1312]{2,1,0:T(2,128)(2,1)S(1)} %bitcast.78), channel_id=1, replica_groups=mesh['seq'=4,'batch'=2,'head'=4] {'seq','batch'}, dimensions={0}, use_global_device_ids=true | all-gather | bytes 23616 | tf_op jit(solution)/shard_map/all_gather | solution.py:1913
  33.2 0.6 reshape.231
  33.8 0.6 slice_convert_fusion.3
  34.9 1.3 copy-done.1
  36.2 1.5 fusion.9.rate_ref
  37.8 0.8 pad.4.wrates_hbm
  38.6 0.7 reshape.241.conv_ref
  39.3 0.6 reshape.243.o_gain_ref
  40.1 2.2 all-gather.5.cloned.1.call-done.win_hbm
  42.3 2.8 fusion.halo_ref
  45.0 6.0 %fusion.13.main_ref = f32[1024,1024]{1,0:T(8,128)} fusion(bf16[1024,1024]{1,0:T(8,128)(2,1)S(1)} %copy-done.2, bf16[1024,1024]{1,0:T(8,128)(2,1)} %all-gather.5.cloned.1.call-done.win_hbm), kind=kOutput, calls=%fused_computation.34 | convolution fusion | flops 2147483648 | bytes 8388608 | tf_op jit(solution)/shard_map/dot_general | solution.py:1868
  51.0 26.7 %forward_rule.1 = (bf16[1024,1024]{1,0:T(8,128)(2,1)}, bf16[4,4,128,128]{3,2,1,0:T(8,128)(2,1)}, bf16[4,4,128,128]{3,2,1,0:T(8,128)(2,1)}, bf16[4,4,128,128]{3,2...) custom-call(s32[2]{0:T(128)} %start_ref.3, ...), custom_call_target="tpu_custom_call" | custom-call | tf_op jit(solution)/shard_map/forward_rule/pallas_call | solution.py:630
  77.8 43.2 %mixer.1 = (f32[1024,512]{1,0:T(8,128)}, bf16[1024,512]{1,0:T(8,128)(2,1)}, bf16[1024,1024]{1,0:T(8,128)(2,1)}, bf16[1024,1024]{1,0:T(8,128)(2,1)}, f32[256,1024]{1,0:T(8,128)}) custom-call(bf16[1024,1024]{1,0:T(8,128)(2,1)} %copy-done.1, f32[1024,512]{1,0:T(8,128)} %get-tuple-element.46.mixed_hbm.mixed_ref, ...), custom_call_target="tpu_custom_call" | custom-call | tf_op jit(solution)/shard_map/mixer/pallas_call | solution.py:1510
  121.0 6.2 %all-gather.9.cloned.1.call-done.ffn_hbm = bf16[1024,2176]{1,0:T(8,128)(2,1)} async-done(((bf16[128,2176]{1,0:T(8,128)(2,1)}), bf16[1024,2176]{1,0:T(8,128)(2,1)}) %all-gather.9.cloned.1.call-update) | async-done | bytes 4456464 | tf_op jit(solution)/shard_map/all_gather | solution.py:1915
  127.2 52.6 %feed_forward.1 = (bf16[1024,2048]{1,0:T(8,128)(2,1)}, bf16[1024,1024]{1,0:T(8,128)(2,1)}, f32[1024,512]{1,0:T(8,128)}, f32[256,1024]{1,0:T(8,128)}, f32[8,1024]{1,0:T(8,128)}, /*index=5*/f32[128,768]{1,0:T(8,128)}) custom-call(bf16[1024,1024]{1,0:T(8,128)(2,1)} %get-tuple-element.47.nm_hbm, bf16[1024,2176]{1,0:T(8,128)(2,1)} %all-gather.9.cloned.1.call-done.ffn_hbm, ...), custom_call_target="tpu_custom_call" | custom-call | tf_op jit(solution)/shard_map/feed_forward/pallas_call | solution.py:1734
  179.7 93.4 %backward_rule.1 = (bf16[1024,1024]{1,0:T(8,128)(2,1)}, bf16[1024,1024]{1,0:T(8,128)(2,1)}, f32[24,128]{1,0:T(8,128)}, f32[128,1536]{1,0:T(8,128)}, f32[128,128]{1,0:T(8,128)}, /*index=5*/f32[128,2048]{1,0:T(8,128)}) custom-call(s32[2]{0:T(128)} %start_ref.3, f32[2,2]{1,0:T(2,128)} %decay_ref.3, f32[1024,512]{1,0:T(8,128)} %get-tuple-element.50.dn_ref, ...), custom_call_target="tpu_custom_call" | custom-call | tf_op jit(solution)/shard_map/backward_rule/pallas_call | solution.py:1296
  273.1 0.7 reshape.237
  274.4 0.6 dynamic-slice_bitcast_fusion
  274.9 5.7 %results.1 = (f32[2,704,128]{2,1,0:T(8,128)}, f32[704,128]{1,0:T(8,128)}, f32[512,128]{1,0:T(8,128)}, f32[128,2,768]{2,1,0:T(2,128)}, f32[4,128]{1,0:T(4,128)}, ...) custom-call(f32[128,2048]{1,0:T(8,128)} %get-tuple-element.64.late_hbm, ...), custom_call_target="tpu_custom_call" | custom-call | tf_op jit(solution)/shard_map/results/pallas_call | solution.py:1828
  (68 shorter events, 3.7 us)
Async XLA Ops:
  7.2 2.7 copy-start.4
  7.2 3.6 %copy-start.5 = (f32[128,2,704]{0,2,1:T(8,128)S(1)}, f32[128,2,704]{0,2,1:T(8,128)}, u32[]{:S(2)}) copy-start(f32[128,2,704]{0,2,1:T(8,128)} %param.23) | copy-start | bytes 2162692
  7.2 35.1 %all-gather.5.cloned.1.call-start = ((), (), s32[]{:S(2)}) async-start(), calls=%async_computation | async-start | bytes 2359296 | tf_op jit(solution)/shard_map/all_gather | solution.py:1912
  9.7 1.7 copy-start.3
  9.7 68.1 %all-gather.7.cloned.1.call-start = ((), (), s32[]{:S(2)}) async-start(), calls=%async_computation.1 | async-start | bytes 2359296 | tf_op jit(solution)/shard_map/all_gather | solution.py:1914
  10.8 116.4 %all-gather.9.cloned.1.call-start = ((), (), s32[]{:S(2)}) async-start(), calls=%async_computation.2 | async-start | bytes 5013504 | tf_op jit(solution)/shard_map/all_gather | solution.py:1915
  11.1 1.6 copy-start
  11.1 6.5 %copy-start.7 = (f32[128,2,2]{0,2,1:T(2,128)S(1)}, f32[128,2,2]{0,2,1:T(2,128)}, u32[]{:S(2)}) copy-start(f32[128,2,2]{0,2,1:T(2,128)} %param.17) | copy-start | bytes 6148
  11.1 6.8 %copy-start.6 = (f32[4,2,64]{2,1,0:T(2,128)S(1)}, f32[4,2,64]{2,1,0:T(2,128)}, u32[]{:S(2)}) copy-start(f32[4,2,64]{2,1,0:T(2,128)} %param.18) | copy-start | bytes 6148
  11.1 6.9 %copy-start.10 = (f32[32]{0:T(128)S(1)}, f32[32]{0:T(128)}, u32[]{:S(2)}) copy-start(f32[32]{0:T(128)} %param.20) | copy-start | bytes 388
  11.1 6.9 %copy-start.8 = (f32[128]{0:T(128)S(1)}, f32[128]{0:T(128)}, u32[]{:S(2)}) copy-start(f32[128]{0:T(128)} %param.22) | copy-start | bytes 1540
  11.1 6.9 %copy-start.9 = (f32[128]{0:T(128)S(1)}, f32[128]{0:T(128)}, u32[]{:S(2)}) copy-start(f32[128]{0:T(128)} %param.15) | copy-start | bytes 1540
  12.7 27.3 %collective-permute-start = (bf16[2,16,1024]{2,1,0:T(8,128)(2,1)S(1)}, bf16[2,16,1024]{2,1,0:T(8,128)(2,1)S(1)}, u32[]{:S(2)}, u32[]{:S(2)}) collective-permute-start(bf16[2,16,1024]{2,1,0:T(8,128)(2,1)S(1)} %slice.64), channel_id=1, source_target_pairs={{0,8},{8,16},{16,24},{1,9},{9,17},{17,25},{2,10},{10,18},{18,26},{... | collective-permute-start | bytes 196616 | tf_op jit(solution)/shard_map/ppermute | solution.py:1860
  34.9 1.3 copy-start.1
  37.8 7.3 %copy-start.2 = (bf16[1024,1024]{1,0:T(8,128)(2,1)S(1)}, bf16[1024,1024]{1,0:T(8,128)(2,1)}, u32[]{:S(2)}) copy-start(bf16[1024,1024]{1,0:T(8,128)(2,1)} %copy-done.1) | copy-start | bytes 6291460
Sparse Core Ops, SparseCore 0:
  10.2 32.0 all-gather.4
  44.5 28.7 all-gather.6
  75.4 51.7 all-gather.8

commit v8 on v7

--- a/solution.py
+++ b/solution.py
@@ -670,7 +670,7 @@
         ],
         compiler_params=pltpu.CompilerParams(
             dimension_semantics=("arbitrary",), collective_id=3, has_side_effects=True,
-            vmem_limit_bytes=62 * 2**20,
+            vmem_limit_bytes=48 * 2**20,
         ),
         name="forward_rule",
     )(starts, decay_par, projected, halo, rates, conv_w)
@@ -1542,7 +1542,7 @@
 def ffn_kernel(
     peers, places, cores, nm_hbm, ffn_hbm, ct_hbm, normed_hbm, weights_hbm, hidden_ref, gain_ref,
     grads_hbm, ffnp_hbm, ng_hbm, hgrad_ref, gpart_ref, down_ref,
-    nm_b, ct_b, dgu_b, nm, ffn_v, ends_v, ct_v, normed_v, wout_v, act, dgu, dm, ffnp_v, grads_v, down_v, ng_v,
+    nm_b, ct_b, dgu_b, nm, ffn_v, ends_v, ct_v, normed_v, wout_v, act, dgu, dm, ffnp_v, grads_v, down_v, ng_v, out_acc,
     in_sem, out_sem, ng_sem, send, recv, relay, sum_send, sum_recv, gather_send, gather_recv,
     core_recv, seq_send, seq_recv, scatter_sems,
 ):
@@ -1638,17 +1638,18 @@
 
     def down_grads(i, carry):
         at = pl.ds(pl.multiple_of(i * tile, tile), tile)
-        down_v[at, :] = mm(ct_v[:, at], act[...], TN).astype(bf16)
+        down_v[at, 0:cells] = mm(ct_v[:, at], act[...], TN).astype(bf16)
+        down_v[at, cells:] = mm(nm[:, at], dgu[:, 0:tile], TN).astype(bf16)
         return carry
 
     lax.fori_loop(0, width // tile, down_grads, 0)
-    scatter = GroupScatter(down_v, pl.ds(0, cells), core_recv, seq_send, seq_recv, scatter_sems)
+    scatter = GroupScatter(down_v, pl.ds(0, cells + tile), core_recv, seq_send, seq_recv, scatter_sems)
     for k in range(places - 1, -1, -1):
         scatter.core_copy(k).start()
 
     def cell_grads(i, carry):
         at = pl.ds(pl.multiple_of(i * tile, tile), tile)
-        grads_v[at, 0 : 2 * cells] = mm(nm[:, at], dgu[...], TN).astype(bf16)
+        grads_v[at, 0 : 2 * cells - tile] = mm(nm[:, at], dgu[:, tile:], TN).astype(bf16)
         return carry
 
     half = width // tile // 2
@@ -1685,7 +1686,6 @@
     loads[8].wait()
     for t in range(subs):
         ring.forward(t)
-    down_ref[...] = scatter.finish()
 
     ng_store = Pieces(ng_v, ng_hbm, total, subs, ng_sem)
 
@@ -1697,21 +1697,28 @@
             for t in range(subs):
                 ring.finish(t)
 
-        grads = mm(take(dm, owner, subs), wout_v[...])
+        block = take(dm, owner, subs)
+        grads = mm(block, wout_v[...])
         for t in range(subs):
             ng_v[piece_rows(owner, t, total, subs), :] = grads[t * SUB : (t + 1) * SUB]
         ng_store.start(owner)
+        rows = take(normed_v, owner, subs)
+        for first in range(0, width, tile):
+            at = slice(first, first + tile)
+            before = jnp.where(k == 0, 0.0, out_acc[at, :])
+            out_acc[at, :] = before + mm(block[:, at], rows, TN)
         return carry
 
     lax.fori_loop(0, peers, norm_rows, 0)
 
     def out_grads(i, carry):
         at = pl.ds(pl.multiple_of(i * tile, tile), tile)
-        grads_v[at, 2 * cells :] = mm(dm[:, at], normed_v[...], TN).astype(bf16)
+        grads_v[at, 2 * cells - tile :] = out_acc[at, :].astype(bf16)
         block_store(i, tile, grads_v, grads_hbm, out_sem.at[1]).start()
         return carry
 
     lax.fori_loop(0, width // tile, out_grads, 0)
+    down_ref[...] = scatter.finish()
     for i in range(peers):
         block_store(i, own_rows, ffnp_v, ffnp_hbm, out_sem.at[0]).wait()
         ng_store.wait(i)
@@ -1736,12 +1743,12 @@
         in_specs=[anywhere()] * 5 + [vmem()] * 2,
         out_specs=[anywhere()] * 3 + [vmem()] * 3,
         out_shape=[
-            shape((width, 2 * cells + values), bf16),
+            shape((width, 2 * cells - 256 + values), bf16),
             shape((total, width), bf16),
             shape((total, values), f32),
             shape((own_rows, width), f32),
             shape((8, width), f32),
-            shape((shard, cells), f32),
+            shape((shard, cells + 256), f32),
         ],
         scratch_shapes=[
             pltpu.VMEM((own_rows, width), bf16),
@@ -1757,15 +1764,16 @@
             pltpu.VMEM((total, 2 * cells), bf16),
             pltpu.VMEM((total, width), bf16),
             pltpu.VMEM((total, width), bf16),
-            pltpu.VMEM((width, 2 * cells + values), bf16),
-            pltpu.VMEM((width, cells), bf16),
+            pltpu.VMEM((width, 2 * cells - 256 + values), bf16),
+            pltpu.VMEM((width, cells + 256), bf16),
             pltpu.VMEM((total, values), f32),
+            pltpu.VMEM((width, values), f32),
             pltpu.SemaphoreType.DMA((9,)),
             pltpu.SemaphoreType.DMA((2, max(peers, width // 256))),
             pltpu.SemaphoreType.DMA((peers, subs)),
         ]
         + sum_buffers(own_rows, width, subs)
-        + scatter_buffers(places, shard, cells),
+        + scatter_buffers(places, shard, cells + 256),
         compiler_params=pltpu.CompilerParams(
             collective_id=5, has_side_effects=True, vmem_limit_bytes=62 * 2**20
         ),
@@ -1792,19 +1800,21 @@
         pltpu.make_async_copy(main_hbm, main_in, sems.at[6]),
         pltpu.make_async_copy(small_hbm, small_in, sems.at[7]),
     ]
-    for load in firsts + loads:
+    for load in loads + firsts:
         load.start()
-    firsts[0].wait()
-    taps, heads, per = conv_ref.shape
-    for part_at in range(2):
-        at = part_at * cells
-        cells_ref[part_at] = late_ref[:, at : at + cells].T[0:units]
-    firsts[1].wait()
-    down_ref[...] = down_in[...].T[0:units]
-    mixer_ref[...] = late_ref[:, 2 * cells :].T
     for load, copy in zip(loads, copies):
         load.wait()
         copy.start()
+    firsts[0].wait()
+    taps, heads, per = conv_ref.shape
+    firsts[1].wait()
+    early = down_in.shape[1] - cells
+    up_at = cells - early
+    cells_ref[0, 0:early] = down_in[:, cells:].T
+    cells_ref[0, early:units] = late_ref[:, 0:up_at].T[0 : units - early]
+    cells_ref[1] = late_ref[:, up_at : up_at + cells].T[0:units]
+    down_ref[...] = down_in[:, 0:cells].T[0:units]
+    mixer_ref[...] = late_ref[:, up_at + cells :].T
     firsts[2].wait()
     firsts[3].wait()
     wide = main_ref.shape[2]
@@ -1823,7 +1833,7 @@
 
 def results(late, down, main, small, out, igrad, units, cells, heads, per):
     shard = late.shape[0]
-    values = late.shape[1] - 2 * cells
+    values = late.shape[1] + down.shape[1] - 3 * cells
     shape = jax.ShapeDtypeStruct
     return pl.pallas_call(
         functools.partial(results_kernel, units, cells),

time: 288 us -> 285 us (0.990)
  Pallas kernels: 222 us -> 219 us
  transfers between devices with their start and end apart: 4 -> 4, of which waited for: 2 -> 2; matrix products, arithmetic and copies ran while one was open for 6% -> 6% of each run, Pallas kernels for 24% -> 25%
where the time goes in v8:
time: 285 us
  Pallas kernels  219 us (77%)
  blocking collectives  14.5 us (5%)
  between operations  14.2 us (5%)
  waiting for transfers between devices  10.7 us (4%)
  matrix products  8.94 us (3%)
  local copies, waits for them, and re-layouts  8.72 us (3%)
  starting transfers between devices  5.04 us (2%)
  other arithmetic  4.09 us (1%)
    pallas_call x1, Pallas kernels, backward_rule(): pl.pallas_call(functools.partial(backward_kernel, heads, places, peers, c...  91.3 us
    pallas_call x1, Pallas kernels, feed_forward_block(): pl.pallas_call(functools.partial(ffn_kernel, peers, places, cores), in_sp...  52.4 us
    pallas_call x1, Pallas kernels, mixer(): pl.pallas_call(functools.partial(mixer_kernel, peers), in_specs=[anywhere...  43.4 us
    pallas_call x1, Pallas kernels, forward_rule(): pl.pallas_call(functools.partial(forward_kernel, heads, places), grid=(2...  26.5 us
    all_gather x1, blocking collectives, per_device(): small_full = lax.all_gather(small, ALL, axis=0)  14.5 us
    dot_general x3, matrix products, matmul(): return lax.dot_general(a, b, (dims, ((), ())), preferred_element_type=f32)  8.94 us
    all_gather x1, waiting for transfers between devices, per_device(): ffn_full = lax.all_gather(packed_ffn, ALL, axis=0, tiled=True)  7.14 us
  transfers between devices with their start and end apart: 4, of which 2 were waited for; matrix products, arithmetic and copies ran while one was open for 6% of the time, Pallas kernels for 25%

profile of v8, /device:TPU:0, one launch (start us, length us, event | category | flops | bytes accessed | tf_op | source)
XLA Modules:
  0.0 284.9 jit_solution(2361368389064262208)
XLA Ops:
  7.2 1.5 convert.63
  8.9 0.7 copy.59
  10.0 0.7 pad_maximum_fusion
  11.6 1.0 concatenate.36
  12.7 4.9 %collective-permute-start = (bf16[2,16,1024]{2,1,0:T(8,128)(2,1)S(1)}, bf16[2,16,1024]{2,1,0:T(8,128)(2,1)S(1)}, u32[]{:S(2)}, u32[]{:S(2)}) collective-permute-start(bf16[2,16,1024]{2,1,0:T(8,128)(2,1)S(1)} %slice.64), channel_id=1, source_target_pairs={{0,8},{8,16},{16,24},{1,9},{9,17},{17,25},{2,10},{10,18},{18,26},{... | collective-permute-start | bytes 196616 | tf_op jit(solution)/shard_map/ppermute | solution.py:1870
  18.1 14.5 %all-gather = bf16[8,1,1312]{2,1,0:T(2,128)(2,1)S(1)} all-gather(bf16[1,1,1312]{2,1,0:T(2,128)(2,1)S(1)} %bitcast.78), channel_id=1, replica_groups=mesh['seq'=4,'batch'=2,'head'=4] {'seq','batch'}, dimensions={0}, use_global_device_ids=true | all-gather | bytes 23616 | tf_op jit(solution)/shard_map/all_gather | solution.py:1923
  33.2 0.6 reshape.231
  33.8 0.6 slice_convert_fusion.3
  34.4 0.5 multiply_convert_fusion.nin_hbm
  34.9 1.3 copy-done.6
  36.2 0.7 fusion.9.rate_ref
  37.0 0.9 pad.4.wrates_hbm
  38.0 0.6 reshape.243.o_gain_ref
  38.8 3.5 %all-gather.5.cloned.1.call-done.win_hbm = bf16[1024,1024]{1,0:T(8,128)(2,1)} async-done(((bf16[128,1024]{1,0:T(8,128)(2,1)}), bf16[1024,1024]{1,0:T(8,128)(2,1)}) %all-gather.5.cloned.1.call-update) | async-done | bytes 2097168 | tf_op jit(solution)/shard_map/all_gather | solution.py:1922
  42.3 2.2 fusion.halo_ref
  44.6 6.0 %fusion.13.main_ref = f32[1024,1024]{1,0:T(8,128)} fusion(bf16[1024,1024]{1,0:T(8,128)(2,1)S(1)} %copy-done.7, bf16[1024,1024]{1,0:T(8,128)(2,1)} %all-gather.5.cloned.1.call-done.win_hbm), kind=kOutput, calls=%fused_computation.34 | convolution fusion | flops 2147483648 | bytes 8388608 | tf_op jit(solution)/shard_map/dot_general | solution.py:1878
  50.6 26.5 %forward_rule.1 = (bf16[1024,1024]{1,0:T(8,128)(2,1)}, bf16[4,4,128,128]{3,2,1,0:T(8,128)(2,1)}, bf16[4,4,128,128]{3,2,1,0:T(8,128)(2,1)}, bf16[4,4,128,128]{3,2...) custom-call(s32[2]{0:T(128)S(1)} %copy-done.4, ...), custom_call_target="tpu_custom_call" | custom-call | tf_op jit(solution)/shard_map/forward_rule/pallas_call | solution.py:630
  77.1 43.4 %mixer.1 = (f32[1024,512]{1,0:T(8,128)}, bf16[1024,512]{1,0:T(8,128)(2,1)}, bf16[1024,1024]{1,0:T(8,128)(2,1)}, bf16[1024,1024]{1,0:T(8,128)(2,1)}, f32[256,1024]{1,0:T(8,128)}) custom-call(bf16[1024,1024]{1,0:T(8,128)(2,1)} %copy-done.6, f32[1024,512]{1,0:T(8,128)} %get-tuple-element.46.mixed_hbm.mixed_ref, ...), custom_call_target="tpu_custom_call" | custom-call | tf_op jit(solution)/shard_map/mixer/pallas_call | solution.py:1510
  120.5 7.1 %all-gather.9.cloned.1.call-done.ffn_hbm = bf16[1024,2176]{1,0:T(8,128)(2,1)} async-done(((bf16[128,2176]{1,0:T(8,128)(2,1)}), bf16[1024,2176]{1,0:T(8,128)(2,1)}) %all-gather.9.cloned.1.call-update) | async-done | bytes 4456464 | tf_op jit(solution)/shard_map/all_gather | solution.py:1925
  127.6 52.4 %feed_forward.1 = (bf16[1024,1792]{1,0:T(8,128)(2,1)}, bf16[1024,1024]{1,0:T(8,128)(2,1)}, f32[1024,512]{1,0:T(8,128)}, f32[256,1024]{1,0:T(8,128)}, f32[8,1024]{1,0:T(8,128)}, /*index=5*/f32[128,1024]{1,0:T(8,128)}) custom-call(bf16[1024,1024]{1,0:T(8,128)(2,1)} %get-tuple-element.47.nm_hbm, bf16[1024,2176]{1,0:T(8,128)(2,1)} %all-gather.9.cloned.1.call-done.ffn_hbm, ...), custom_call_target="tpu_custom_call" | custom-call | tf_op jit(solution)/shard_map/feed_forward/pallas_call | solution.py:1741
  180.0 91.3 %backward_rule.1 = (bf16[1024,1024]{1,0:T(8,128)(2,1)}, bf16[1024,1024]{1,0:T(8,128)(2,1)}, f32[24,128]{1,0:T(8,128)}, f32[128,1536]{1,0:T(8,128)}, f32[128,128]{1,0:T(8,128)}, /*index=5*/f32[128,1792]{1,0:T(8,128)}) custom-call(s32[2]{0:T(128)} %start_ref.3, f32[2,2]{1,0:T(2,128)} %decay_ref.3, f32[1024,512]{1,0:T(8,128)} %get-tuple-element.50.dn_ref, ...), custom_call_target="tpu_custom_call" | custom-call | tf_op jit(solution)/shard_map/backward_rule/pallas_call | solution.py:1296
  271.4 0.7 reshape.237
  272.6 0.6 dynamic-slice_bitcast_fusion
  273.2 5.2 %results.1 = (f32[2,704,128]{2,1,0:T(8,128)}, f32[704,128]{1,0:T(8,128)}, f32[512,128]{1,0:T(8,128)}, f32[128,2,768]{2,1,0:T(2,128)}, f32[4,128]{1,0:T(4,128)}, ...) custom-call(f32[128,1792]{1,0:T(8,128)} %get-tuple-element.64.late_hbm, ...), custom_call_target="tpu_custom_call" | custom-call | tf_op jit(solution)/shard_map/results/pallas_call | solution.py:1838
  (78 shorter events, 3.2 us)
Async XLA Ops:
  7.2 2.7 copy-start.9
  7.2 3.6 %copy-start.10 = (f32[128,2,704]{0,2,1:T(8,128)S(1)}, f32[128,2,704]{0,2,1:T(8,128)}, u32[]{:S(2)}) copy-start(f32[128,2,704]{0,2,1:T(8,128)} %param.23) | copy-start | bytes 2162692
  7.2 35.1 %all-gather.5.cloned.1.call-start = ((), (), s32[]{:S(2)}) async-start(), calls=%async_computation | async-start | bytes 2359296 | tf_op jit(solution)/shard_map/all_gather | solution.py:1922
  9.7 1.7 copy-start.8
  9.7 67.4 %all-gather.7.cloned.1.call-start = ((), (), s32[]{:S(2)}) async-start(), calls=%async_computation.1 | async-start | bytes 2359296 | tf_op jit(solution)/shard_map/all_gather | solution.py:1924
  10.8 116.9 %all-gather.9.cloned.1.call-start = ((), (), s32[]{:S(2)}) async-start(), calls=%async_computation.2 | async-start | bytes 5013504 | tf_op jit(solution)/shard_map/all_gather | solution.py:1925
  11.1 1.6 copy-start.5
  11.1 6.5 %copy-start.12 = (f32[128,2,2]{0,2,1:T(2,128)S(1)}, f32[128,2,2]{0,2,1:T(2,128)}, u32[]{:S(2)}) copy-start(f32[128,2,2]{0,2,1:T(2,128)} %param.17) | copy-start | bytes 6148
  11.1 6.8 %copy-start.11 = (f32[4,2,64]{2,1,0:T(2,128)S(1)}, f32[4,2,64]{2,1,0:T(2,128)}, u32[]{:S(2)}) copy-start(f32[4,2,64]{2,1,0:T(2,128)} %param.18) | copy-start | bytes 6148
  11.1 6.9 %copy-start.15 = (f32[32]{0:T(128)S(1)}, f32[32]{0:T(128)}, u32[]{:S(2)}) copy-start(f32[32]{0:T(128)} %param.20) | copy-start | bytes 388
  11.1 6.9 %copy-start.13 = (f32[128]{0:T(128)S(1)}, f32[128]{0:T(128)}, u32[]{:S(2)}) copy-start(f32[128]{0:T(128)} %param.22) | copy-start | bytes 1540
  11.1 6.9 %copy-start.14 = (f32[128]{0:T(128)S(1)}, f32[128]{0:T(128)}, u32[]{:S(2)}) copy-start(f32[128]{0:T(128)} %param.15) | copy-start | bytes 1540
  12.7 26.0 %collective-permute-start = (bf16[2,16,1024]{2,1,0:T(8,128)(2,1)S(1)}, bf16[2,16,1024]{2,1,0:T(8,128)(2,1)S(1)}, u32[]{:S(2)}, u32[]{:S(2)}) collective-permute-start(bf16[2,16,1024]{2,1,0:T(8,128)(2,1)S(1)} %slice.64), channel_id=1, source_target_pairs={{0,8},{8,16},{16,24},{1,9},{9,17},{17,25},{2,10},{10,18},{18,26},{... | collective-permute-start | bytes 196616 | tf_op jit(solution)/shard_map/ppermute | solution.py:1870
  34.9 1.3 copy-start.6
  37.0 13.6 %copy-start = (f32[1024,128]{1,0:T(8,128)}, f32[1024,128]{1,0:T(8,128)S(1)}, u32[]{:S(2)}) copy-start(f32[1024,128]{1,0:T(8,128)S(1)} %fusion.9.rate_ref) | copy-start | bytes 1572868
  38.0 12.5 %copy-start.2 = (f32[4,1024]{1,0:T(4,128)}, f32[4,1024]{1,0:T(4,128)S(1)}, u32[]{:S(2)}) copy-start(f32[4,1024]{1,0:T(4,128)S(1)} %reshape.241.conv_ref) | copy-start | bytes 49156
  42.3 2.2 copy-start.7
  44.5 6.0 %copy-start.1 = (f32[2,16,1024]{2,1,0:T(8,128)}, f32[2,16,1024]{2,1,0:T(8,128)S(1)}, u32[]{:S(2)}) copy-start(f32[2,16,1024]{2,1,0:T(8,128)S(1)} %fusion.halo_ref) | copy-start | bytes 393220
  44.6 6.0 %copy-start.3 = (f32[2,2]{1,0:T(2,128)S(1)}, f32[2,2]{1,0:T(2,128)}, u32[]{:S(2)}) copy-start(f32[2,2]{1,0:T(2,128)} %decay_ref.3) | copy-start | bytes 52
  44.6 6.0 %copy-start.4 = (s32[2]{0:T(128)S(1)}, s32[2]{0:T(128)}, u32[]{:S(2)}) copy-start(s32[2]{0:T(128)} %start_ref.3) | copy-start | bytes 28
Sparse Core Ops, SparseCore 0:
  10.2 32.0 all-gather.4
  44.5 29.2 all-gather.6
  76.0 51.6 all-gather.8
